TPU v7x, 32 devices: a whole 2x2x4 slice. The times are simulated.
32 devices in a mesh: grp: 2 (over y), fsdp: 8 (over z, x), tp: 2 (over core).
Axes of the slice: x: 2, y: 2, z: 4, core: 2. Of those that a mesh axis runs over, the one named last changes fastest.
Arguments:
- learn_hidden: bfloat16 [6144, 3840], P(('grp', 'fsdp'), 'tp'), parts along dimension 0, may hold values from -80 to 80
- learn_grad_out: bfloat16 [6144, 512], P(('grp', 'fsdp'), 'tp'), parts along dimension 0, may hold values from -320 to 320
- key_master: float32 [7680, 512], P(('grp', 'tp', 'fsdp')), parts along dimension 0, may hold values from -0.5 to 0.5
- key_first: float32 [7680, 512], P(('grp', 'tp', 'fsdp')), parts along dimension 0, may hold values from -0.3 to 0.3
- key_second: float32 [7680, 512], P(('grp', 'tp', 'fsdp')), parts along dimension 0, may hold values from 0.05 to 0.2
- rollout_hidden: bfloat16 [16, 8, 3840], P(('grp', 'fsdp')), parts along dimension 0, may hold values from -60 to 60
- query_base: bfloat16 [16, 8, 4096], P(('grp', 'fsdp'), None, 'tp'), parts along dimension 0, may hold values from -40 to 40
- cache_keys: bfloat16 [16, 1024, 512], P(('grp', 'fsdp'), None, 'tp'), parts along dimension 0, may hold values from -16 to 16
- cache_values: bfloat16 [16, 1024, 512], P(('grp', 'fsdp'), None, 'tp'), parts along dimension 0, may hold values from -6 to 6
- new_values: bfloat16 [16, 8, 512], P(('grp', 'fsdp'), None, 'tp'), parts along dimension 0, may hold values from -6 to 6
- cache_lengths: int32 [16], P(('grp', 'fsdp')), parts along dimension 0, may hold values from 129 to 1024, as said below
Outputs:
- grad_in: bfloat16 [6144, 3840], P(('grp', 'fsdp'), 'tp'), parts along dimension 0
- key_new: float32 [7680, 512], P(('grp', 'tp', 'fsdp')), parts along dimension 0
- key_first_new: float32 [7680, 512], P(('grp', 'tp', 'fsdp')), parts along dimension 0
- key_second_new: float32 [7680, 512], P(('grp', 'tp', 'fsdp')), parts along dimension 0
- step_keys: bfloat16 [16, 8, 512], P(('grp', 'fsdp'), None, 'tp'), parts along dimension 0
- attention: bfloat16 [16, 8, 4096], P(('grp', 'fsdp'), None, 'tp'), parts along dimension 0
There are 2 independent parts, one for each index of `grp`. A program takes and returns all parts, laid end to end along the dimension named above; each array names one. Nothing has to cross between parts.
Inputs may be any that keep to these rules, and one draw needn't show every extreme that they name: `cache_lengths`: each row holds more than one eighth of 1024; some row holds all 1024.
All inputs are finite; a program needn't handle non-finite values.
Results may differ from a plain program's by a relative error of at most 0.0049.
Values may be sent and summed in bfloat16 or wider, within the bound.
No kernel may reach another device: no remote copies, remote signals or barrier semaphores. Data moves between devices by JAX's collectives and lax.ppermute only.
A program may use at most 64 MiB of HBM per device.

v0:
```python
import math

import jax
import jax.numpy as jnp
from jax import lax
from jax.sharding import PartitionSpec as P

D = 3840
HQ = 32
KVH = 4
HD = 128
STEPS = 8
UPDATES = 20


beta_first = 0.9
beta_second = 0.95
learn_rate = 0.02
decay_rate = 0.1
adam_epsilon = 1e-08


def adamw_update(master, moment_one, moment_two, gradient, factor):
    clipped = factor * gradient
    first_new = beta_first * moment_one + (1.0 - beta_first) * clipped
    second_new = beta_second * moment_two + (1.0 - beta_second) * clipped * clipped
    first_hat = first_new / (1.0 - beta_first**UPDATES)
    second_hat = second_new / (1.0 - beta_second**UPDATES)
    master_new = master - learn_rate * (
        first_hat / (jnp.sqrt(second_hat) + adam_epsilon) + decay_rate * master
    )
    return (master_new, first_new, second_new)


def contract_rows(left, right):
    return lax.dot_general(
        left, right, (((0,), (0,)), ((), ())), preferred_element_type=jnp.float32
    )


def owner_order(blocks, shard_count, slice_count):
    block_rows = blocks.shape[0] // (shard_count * slice_count)
    width = blocks.shape[1]
    return (
        blocks.reshape(shard_count, slice_count, block_rows, width)
        .transpose(1, 0, 2, 3)
        .reshape(shard_count * slice_count * block_rows, width)
    )


def attend(queries, cache_keys, cache_values, fresh_keys, new_values, cache_lengths):
    row_count = queries.shape[0]
    cache_len = cache_keys.shape[1]
    local_heads = cache_keys.shape[2] // HD
    group_size = HQ // KVH
    span_total = cache_len + STEPS
    grouped = queries.reshape(row_count, STEPS, local_heads, group_size, HD)
    all_keys = jnp.concatenate([cache_keys, fresh_keys], axis=1).reshape(
        row_count, span_total, local_heads, HD
    )
    all_values = jnp.concatenate([cache_values, new_values], axis=1).reshape(
        row_count, span_total, local_heads, HD
    )
    scores = jnp.einsum(
        "rtkgd,rpkd->rtkgp", grouped, all_keys, preferred_element_type=jnp.float32
    ) / math.sqrt(HD)
    position = jnp.arange(span_total, dtype=jnp.int32)[None, None, :]
    step_index = jnp.arange(STEPS, dtype=jnp.int32)[None, :, None]
    length_limit = cache_lengths[:, None, None]
    visible = jnp.where(
        position < cache_len, position < length_limit, position - cache_len <= step_index
    )
    scores = jnp.where(visible[:, :, None, None, :], scores, jnp.float32(-1e30))
    largest = jnp.max(scores, axis=-1, keepdims=True)
    exponents = jnp.exp(scores - largest)
    weights = (exponents / jnp.sum(exponents, axis=-1, keepdims=True)).astype(jnp.bfloat16)
    blended = jnp.einsum(
        "rtkgp,rpkd->rtkgd", weights, all_values, preferred_element_type=jnp.float32
    )
    return blended.astype(jnp.bfloat16).reshape(row_count, STEPS, local_heads * group_size * HD)


def shards(
    learn_hidden,
    learn_grad_out,
    key_master,
    key_first,
    key_second,
    rollout_hidden,
    query_base,
    cache_keys,
    cache_values,
    new_values,
    cache_lengths,
):
    unit_scale = 1.0 / math.sqrt(D)
    shard_count = lax.axis_size("fsdp")
    slice_count = lax.axis_size("tp")
    cotangent = lax.all_gather(learn_grad_out, "tp", axis=1, tiled=True)
    weight_cast = key_master.astype(jnp.bfloat16)
    grad_in = (
        unit_scale
        * lax.dot_general(
            cotangent,
            lax.all_gather(weight_cast, "fsdp", axis=0, tiled=True),
            (((1,), (1,)), ((), ())),
            preferred_element_type=jnp.float32,
        )
    ).astype(jnp.bfloat16)
    grad_weight = lax.psum_scatter(
        unit_scale * contract_rows(learn_hidden, cotangent), "fsdp", scatter_dimension=0, tiled=True
    )
    square_sum = lax.psum(jnp.sum(grad_weight * grad_weight), ("fsdp", "tp"))
    tokens_all = learn_hidden.shape[0] * shard_count
    width_all = cotangent.shape[1]
    factor = jnp.minimum(1.0, math.sqrt(tokens_all * width_all) / jnp.sqrt(square_sum))
    key_new, key_first_new, key_second_new = adamw_update(
        key_master, key_first, key_second, grad_weight, factor
    )
    relay_cast = key_new.astype(jnp.bfloat16)
    column_count = width_all // slice_count
    every_row = lax.all_gather(relay_cast, ("fsdp", "tp"), axis=0, tiled=True)
    ordered = owner_order(every_row, shard_count, slice_count)
    relay_half = lax.dynamic_slice_in_dim(
        ordered, lax.axis_index("tp") * column_count, column_count, 1
    )
    projected = jnp.einsum(
        "rtd,dk->rtk", rollout_hidden, relay_half, preferred_element_type=jnp.float32
    )
    step_keys = (unit_scale * projected).astype(jnp.bfloat16)
    attention = attend(query_base, cache_keys, cache_values, step_keys, new_values, cache_lengths)
    return (grad_in, key_new, key_first_new, key_second_new, step_keys, attention)


def solution(mesh):
    in_specs = (
        P(("grp", "fsdp"), "tp"),
        P(("grp", "fsdp"), "tp"),
        P(("grp", "tp", "fsdp"), None),
        P(("grp", "tp", "fsdp"), None),
        P(("grp", "tp", "fsdp"), None),
        P(("grp", "fsdp"), None, None),
        P(("grp", "fsdp"), None, "tp"),
        P(("grp", "fsdp"), None, "tp"),
        P(("grp", "fsdp"), None, "tp"),
        P(("grp", "fsdp"), None, "tp"),
        P(("grp", "fsdp")),
    )
    out_specs = (
        P(("grp", "fsdp"), "tp"),
        P(("grp", "tp", "fsdp"), None),
        P(("grp", "tp", "fsdp"), None),
        P(("grp", "tp", "fsdp"), None),
        P(("grp", "fsdp"), None, "tp"),
        P(("grp", "fsdp"), None, "tp"),
    )
    return jax.shard_map(shards, mesh=mesh, in_specs=in_specs, out_specs=out_specs, check_vma=False)
```

profile of v0, /device:TPU:0, one launch (start us, length us, event | category | flops | bytes accessed | tf_op | source)
XLA Modules:
  0.0 245.0 jit_solution(10261284022544841565)
XLA Ops:
  7.2 0.0 copy-start
  7.2 0.0 reduce-scatter.2.cloned.1.call-start
  7.2 2.5 %all_gather.9 = bf16[384,512]{1,0:T(8,128)(2,1)S(1)} all-gather(bf16[384,256]{1,0:T(8,128)(2,1)} %param.12), channel_id=1, replica_groups=mesh['grp'=2,'fsdp'=8,'tp'=2] {'tp'}, dimensions={1}, use_global_device_ids=true | all-gather | bytes 589824 | tf_op jit(solution)/shard_map/all_gather | solution.py:99
  9.8 0.0 copy-done
  9.8 3.1 %convolution_multiply_fusion = f32[1920,512]{1,0:T(8,128)} fusion(bf16[384,1920]{1,0:T(8,128)(2,1)S(1)} %copy-done, bf16[384,512]{1,0:T(8,128)(2,1)S(1)} %all_gather.9), kind=kOutput, calls=%fused_computation | convolution fusion | flops 755957760 | bytes 5799936 | tf_op jit(solution)/shard_map/dot_general | solution.py:36
  12.9 0.0 copy-start.4
  12.9 0.0 copy-start.5
  12.9 0.0 reduce-scatter.2.cloned.1.call-update
  12.9 0.0 all-gather.3.cloned.1.call-start
  12.9 87.1 %reduce-scatter.2.cloned.1.call-done = f32[240,512]{1,0:T(8,128)} async-done(((f32[1920,512]{1,0:T(8,128)}), f32[240,512]{1,0:T(8,128)}) %reduce-scatter.2.cloned.1.call-update) | async-done | bytes 491536 | tf_op jit(solution)/shard_map/reduce_scatter | solution.py:110
  100.0 1.8 multiply_reduce_fusion
  101.8 32.7 %psum.7 = f32[]{:T(128)} all-reduce(f32[]{:T(128)} %multiply_reduce_fusion), channel_id=1, replica_groups=mesh['grp'=2,'fsdp'=8,'tp'=2] {'fsdp','tp'}, use_global_device_ids=true, to_apply=%region_2.0 | all-reduce | flops 1 | bytes 8 | tf_op jit(solution)/shard_map/psum | solution.py:113
  135.2 0.0 copy-done.4
  135.2 0.0 copy-done.5
  135.2 0.0 copy-start.1
  135.2 2.8 %fusion.24 = (bf16[240,512]{1,0:T(8,128)(2,1)}, f32[240,512]{1,0:T(8,128)}, f32[240,512]{1,0:T(8,128)}, f32[240,512]{1,0:T(8,128)}, bf16[240,512]{1,0:T(8,128)(2,1)}) fusion(f32[240,512]{1,0:T(8,128)S(1)} %copy-done.4, f32[240,512]{1,0:T(8,128)} %reduce-scatter.2.cloned.1.call-done, f32[]{:T(128)S(6)} %min_shard_map.3, f32[240,512]{1,0:T(8,128)S(1)} %copy-done.5, ...), kind=kLoop, calls=%fused_computation.36 | loop fusion | flops 2211840 | bytes 3932164 | tf_op jit(solution)/shard_map/convert_element_type | solution.py:120
  138.0 0.0 copy-start.2
  138.0 0.0 copy-start.7
  138.0 0.0 all-gather.3.cloned.1.call-update
  138.0 0.0 all-gather.5.cloned.1.call-start
  138.1 0.7 all-gather.5.cloned.1.call-update
  139.4 0.0 copy-done.1
  139.4 0.2 copy.19
  139.6 1.0 copy.20
  140.7 0.0 copy-done.2
  140.7 0.0 copy-done.7
  140.7 0.1 reshape.155
  140.9 42.1 %all-gather.3.cloned.1.call-done = bf16[1920,512]{1,0:T(8,128)(2,1)} async-done(((bf16[240,512]{1,0:T(8,128)(2,1)}), bf16[1920,512]{1,0:T(8,128)(2,1)}) %all-gather.3.cloned.1.call-update) | async-done | bytes 1966096 | tf_op jit(solution)/shard_map/all_gather | solution.py:105
  182.9 3.7 %fusion = bf16[384,1920]{1,0:T(8,128)(2,1)} fusion(bf16[384,512]{1,0:T(8,128)(2,1)S(1)} %all_gather.9, bf16[1920,512]{1,0:T(8,128)(2,1)} %all-gather.3.cloned.1.call-done), kind=kOutput, calls=%fused_computation.2 | convolution fusion | flops 756449280 | bytes 3833856 | tf_op jit(solution)/shard_map/dot_general | solution.py:103
  186.6 46.8 %all-gather.5.cloned.1.call-done = bf16[3840,512]{1,0:T(8,128)(2,1)} async-done(((bf16[240,512]{1,0:T(8,128)(2,1)}), bf16[3840,512]{1,0:T(8,128)(2,1)}) %all-gather.5.cloned.1.call-update) | async-done | bytes 3932176 | tf_op jit(solution)/shard_map/all_gather | solution.py:122
  233.4 0.0 copy-start.6
  233.4 2.4 copy.18
  235.8 0.0 copy-start.3
  235.8 0.0 copy-start.9
  235.8 0.0 copy-done.6
  235.8 0.4 fusion.9
  236.2 0.0 copy-start.8
  236.2 0.7 copy-done.3
  236.9 0.0 copy-done.9
  236.9 0.4 fusion.26
  237.2 0.2 fusion.15
  237.5 0.3 fusion.5
  237.8 0.0 copy-done.8
  237.8 0.6 reshape.159
  (5 shorter events, 0.1 us)
Async XLA Ops:
  7.2 2.6 %copy-start = (bf16[384,1920]{1,0:T(8,128)(2,1)S(1)}, bf16[384,1920]{1,0:T(8,128)(2,1)}, u32[]{:S(2)}) copy-start(bf16[384,1920]{1,0:T(8,128)(2,1)} %param.11) | copy-start | bytes 4423684
  7.2 92.8 %reduce-scatter.2.cloned.1.call-start = ((), (), s32[]{:S(2)}) async-start(), calls=%async_computation.2 | async-start | bytes 4423680 | tf_op jit(solution)/shard_map/reduce_scatter | solution.py:110
  12.9 122.3 %copy-start.4 = (f32[240,512]{1,0:T(8,128)S(1)}, f32[240,512]{1,0:T(8,128)}, u32[]{:S(2)}) copy-start(f32[240,512]{1,0:T(8,128)} %param.13) | copy-start | bytes 1474564
  12.9 122.3 %copy-start.5 = (f32[240,512]{1,0:T(8,128)S(1)}, f32[240,512]{1,0:T(8,128)}, u32[]{:S(2)}) copy-start(f32[240,512]{1,0:T(8,128)} %param.14) | copy-start | bytes 1474564
  12.9 170.0 %all-gather.3.cloned.1.call-start = ((), (), s32[]{:S(2)}) async-start(), calls=%async_computation.1 | async-start | bytes 2211840 | tf_op jit(solution)/shard_map/all_gather | solution.py:105
  135.2 4.2 %copy-start.1 = (bf16[1,1024,256]{2,1,0:T(8,128)(2,1)S(1)}, bf16[1,1024,256]{2,1,0:T(8,128)(2,1)}, u32[]{:S(2)}) copy-start(bf16[1,1024,256]{2,1,0:T(8,128)(2,1)} %param.18) | copy-start | bytes 1572868
  138.0 2.7 %copy-start.2 = (bf16[1,1024,256]{2,1,0:T(8,128)(2,1)S(1)}, bf16[1,1024,256]{2,1,0:T(8,128)(2,1)}, u32[]{:S(2)}) copy-start(bf16[1,1024,256]{2,1,0:T(8,128)(2,1)} %param.19) | copy-start | bytes 1572868
  138.0 2.7 %copy-start.7 = (bf16[1,8,256]{2,1,0:T(8,128)(2,1)S(1)}, bf16[1,8,256]{2,1,0:T(8,128)(2,1)}, u32[]{:S(2)}) copy-start(bf16[1,8,256]{2,1,0:T(8,128)(2,1)} %param.20) | copy-start | bytes 12292
  138.0 95.3 %all-gather.5.cloned.1.call-start = ((), (), s32[]{:S(2)}) async-start(), calls=%async_computation.3 | async-start | bytes 4177920 | tf_op jit(solution)/shard_map/all_gather | solution.py:122
  233.4 2.5 %copy-start.6 = (bf16[1,8,3840]{2,1,0:T(8,128)(2,1)S(1)}, bf16[1,8,3840]{2,1,0:T(8,128)(2,1)}, u32[]{:S(2)}) copy-start(bf16[1,8,3840]{2,1,0:T(8,128)(2,1)} %param.16) | copy-start | bytes 184324
  235.8 1.0 copy-start.3
  235.8 1.0 copy-start.9
  236.2 1.6 copy-start.8
Sparse Core Ops, SparseCore 0:
  13.0 86.9 reduce-scatter.1
  138.2 44.7 all-gather.2
  185.5 47.8 all-gather.4
where the time goes:
time: 245 us
  waiting for transfers between devices  177 us (72%)
  blocking collectives  35.3 us (14%)
  between operations  15.2 us (6%)
  matrix products  7.78 us (3%)
  local copies, waits for them, and re-layouts  5.13 us (2%)
  other arithmetic  4.83 us (2%)
    reduce_scatter x1, waiting for transfers between devices, shards(): lax.psum_scatter(unit_scale * contract_rows(learn_hidden, cotangent), 'fs...  87.1 us
    all_gather x1, waiting for transfers between devices, shards(): every_row = lax.all_gather(relay_cast, ('fsdp', 'tp'), axis=0, tiled=True)  46.8 us
    all_gather x1, waiting for transfers between devices, shards(): lax.all_gather(weight_cast, 'fsdp', axis=0, tiled=True)  42.1 us
    psum x1, blocking collectives, shards(): square_sum = lax.psum(jnp.sum(grad_weight * grad_weight), ('fsdp', 'tp'))  32.7 us
  transfers between devices with their start and end apart: 3, of which 3 were waited for; matrix products, arithmetic and copies ran while one was open for 2% of the time, Pallas kernels for 0%

commit v1 on v0

v1 whole, which is shorter than its diff:
```python
import math

import jax
import jax.numpy as jnp
from jax import lax
from jax.sharding import PartitionSpec as P

D = 3840
HQ = 32
KVH = 4
HD = 128
STEPS = 8
UPDATES = 20


beta_first = 0.9
beta_second = 0.95
learn_rate = 0.02
decay_rate = 0.1
adam_epsilon = 1e-08


def adamw_update(master, moment_one, moment_two, gradient, factor):
    clipped = factor * gradient
    first_new = beta_first * moment_one + (1.0 - beta_first) * clipped
    second_new = beta_second * moment_two + (1.0 - beta_second) * clipped * clipped
    first_hat = first_new / (1.0 - beta_first**UPDATES)
    second_hat = second_new / (1.0 - beta_second**UPDATES)
    master_new = master - learn_rate * (
        first_hat / (jnp.sqrt(second_hat) + adam_epsilon) + decay_rate * master
    )
    return (master_new, first_new, second_new)


def contract_rows(left, right):
    return lax.dot_general(
        left, right, (((0,), (0,)), ((), ())), preferred_element_type=jnp.float32
    )


def swap(value, axis, bit):
    size = lax.axis_size(axis)
    return lax.ppermute(value, axis, [(i, i ^ (1 << bit)) for i in range(size)])


def bit_of(axis, bit):
    return (lax.axis_index(axis) >> bit) & 1


def halves(value, axis, bit, at):
    mine = bit_of(axis, bit)
    keep = lax.dynamic_index_in_dim(value, mine, at, keepdims=False)
    give = lax.dynamic_index_in_dim(value, 1 - mine, at, keepdims=False)
    return keep, give


def bit_orders(bits, count):
    return [[(c * max(1, bits // count) + s) % bits for s in range(bits)] for c in range(count)]


def split_bits(value, bits):
    return value.reshape((2,) * bits + value.shape[1:])


def scatter_sum(parts, axis, link_type, chunks):
    size, rows, width = parts.shape
    bits = size.bit_length() - 1
    block = rows // chunks
    held = [split_bits(parts[:, c * block : (c + 1) * block], bits) for c in range(chunks)]
    left = [list(range(bits - 1, -1, -1)) for _ in range(chunks)]
    orders = bit_orders(bits, chunks)
    for stage in range(bits):
        for c in range(chunks):
            bit = orders[c][stage]
            at = left[c].index(bit)
            left[c].remove(bit)
            keep, give = halves(held[c], axis, bit, at)
            held[c] = keep + swap(give.astype(link_type), axis, bit).astype(jnp.float32)
    return jnp.concatenate(held, axis=0) if chunks > 1 else held[0]


def gather_blocks(block, axis, chunks):
    size = lax.axis_size(axis)
    bits = size.bit_length() - 1
    rows = block.shape[0] // chunks
    orders = [order[::-1] for order in bit_orders(bits, chunks)]
    held = [block[c * rows : (c + 1) * rows] for c in range(chunks)]
    have = [[] for _ in range(chunks)]
    for stage in range(bits):
        for c in range(chunks):
            bit = orders[c][stage]
            other = swap(held[c], axis, bit)
            at = sum(1 for b in have[c] if b > bit)
            have[c].append(bit)
            mine = bit_of(axis, bit)
            low = jnp.where(mine == 0, held[c], other)
            high = jnp.where(mine == 0, other, held[c])
            held[c] = jnp.stack([low, high], axis=at)
    held = [h.reshape((size, rows) + block.shape[1:]) for h in held]
    return jnp.concatenate(held, axis=1) if chunks > 1 else held[0]


def exchange_blocks(parts, axis):
    size = parts.shape[0]
    bits = size.bit_length() - 1
    held = split_bits(parts, bits)
    for stage in range(bits):
        bit = stage
        at = bits - 1 - stage
        keep, give = halves(held, axis, bit, at)
        other = swap(give, axis, bit)
        mine = bit_of(axis, bit)
        low = jnp.where(mine == 0, keep, other)
        high = jnp.where(mine == 0, other, keep)
        held = jnp.stack([low, high], axis=at)
    return held.reshape(parts.shape)


def total_sum(value, axes):
    for axis in axes:
        for bit in range(lax.axis_size(axis).bit_length() - 1):
            value = value + swap(value, axis, bit)
    return value


def attend_cache(grouped, cache_keys, cache_values, cache_lengths):
    row_count, _, local_heads, _, _ = grouped.shape
    cache_len = cache_keys.shape[1]
    keys = cache_keys.reshape(row_count, cache_len, local_heads, HD)
    values = cache_values.reshape(row_count, cache_len, local_heads, HD)
    scores = jnp.einsum(
        "rtkgd,rpkd->rtkgp", grouped, keys, preferred_element_type=jnp.float32
    ) / math.sqrt(HD)
    position = jnp.arange(cache_len, dtype=jnp.int32)
    visible = position[None, :] < cache_lengths[:, None]
    scores = jnp.where(visible[:, None, None, None, :], scores, jnp.float32(-1e30))
    largest = jnp.max(scores, axis=-1, keepdims=True)
    exponents = jnp.exp(scores - largest)
    total = jnp.sum(exponents, axis=-1, keepdims=True)
    blended = jnp.einsum(
        "rtkgp,rpkd->rtkgd",
        exponents.astype(jnp.bfloat16),
        values,
        preferred_element_type=jnp.float32,
    )
    return largest, total, blended


def attend_fresh(grouped, cached, fresh_keys, new_values):
    largest_old, total_old, blended_old = cached
    row_count, steps, local_heads, group_size, _ = grouped.shape
    keys = fresh_keys.reshape(row_count, steps, local_heads, HD)
    values = new_values.reshape(row_count, steps, local_heads, HD)
    scores = jnp.einsum(
        "rtkgd,rpkd->rtkgp", grouped, keys, preferred_element_type=jnp.float32
    ) / math.sqrt(HD)
    step = jnp.arange(steps, dtype=jnp.int32)
    visible = step[None, :] <= step[:, None]
    scores = jnp.where(visible[None, :, None, None, :], scores, jnp.float32(-1e30))
    largest = jnp.maximum(largest_old, jnp.max(scores, axis=-1, keepdims=True))
    exponents = jnp.exp(scores - largest)
    rescale = jnp.exp(largest_old - largest)
    total = rescale * total_old + jnp.sum(exponents, axis=-1, keepdims=True)
    blended = rescale * blended_old + jnp.einsum(
        "rtkgp,rpkd->rtkgd",
        exponents.astype(jnp.bfloat16),
        values,
        preferred_element_type=jnp.float32,
    )
    return (blended / total).astype(jnp.bfloat16).reshape(row_count, steps, -1)


def shards(
    learn_hidden,
    learn_grad_out,
    key_master,
    key_first,
    key_second,
    rollout_hidden,
    query_base,
    cache_keys,
    cache_values,
    new_values,
    cache_lengths,
):
    unit_scale = 1.0 / math.sqrt(D)
    shard_count = lax.axis_size("fsdp")
    slice_count = lax.axis_size("tp")
    owned, width_all = key_master.shape
    chunks = 3 if owned % 3 == 0 else 1
    row_count, steps, _ = rollout_hidden.shape
    cotangent = lax.all_gather(learn_grad_out, "tp", axis=1, tiled=True)
    partial_grad = unit_scale * contract_rows(learn_hidden, cotangent)
    grad_weight = scatter_sum(
        partial_grad.reshape(shard_count, owned, width_all), "fsdp", jnp.bfloat16, chunks
    )
    slices = rollout_hidden.reshape(row_count, steps, slice_count, shard_count, owned)
    half = lax.dynamic_index_in_dim(slices, lax.axis_index("tp"), 2, keepdims=False)
    hidden_rows = exchange_blocks(half.transpose(2, 0, 1, 3), "fsdp")
    hidden_rows = hidden_rows.reshape(shard_count * row_count * steps, owned)
    grouped = query_base.reshape(row_count, steps, -1, HQ // KVH, HD)
    cached = attend_cache(grouped, cache_keys, cache_values, cache_lengths)

    square_sum = total_sum(jnp.sum(grad_weight * grad_weight).reshape(1, 1), ("tp", "fsdp"))
    tokens_all = learn_hidden.shape[0] * shard_count
    factor = jnp.minimum(1.0, math.sqrt(tokens_all * width_all) / jnp.sqrt(square_sum))
    key_new, key_first_new, key_second_new = adamw_update(
        key_master, key_first, key_second, grad_weight, factor
    )
    relay_cast = key_new.astype(jnp.bfloat16)
    projected = lax.dot_general(
        hidden_rows, relay_cast, (((1,), (0,)), ((), ())), preferred_element_type=jnp.float32
    )
    column_count = width_all // slice_count
    keep, give = halves(projected.reshape(-1, slice_count, column_count), "tp", 0, 1)
    projected = keep + swap(give, "tp", 0)
    projected = scatter_sum(
        projected.reshape(shard_count, row_count * steps, column_count), "fsdp", jnp.float32, 1
    )
    step_keys = (unit_scale * projected).astype(jnp.bfloat16)
    step_keys = step_keys.reshape(row_count, steps, column_count)
    attention = attend_fresh(grouped, cached, step_keys, new_values)

    weight_all = gather_blocks(key_master.astype(jnp.bfloat16), "fsdp", chunks)
    grad_in = (
        unit_scale
        * lax.dot_general(
            cotangent,
            weight_all.reshape(-1, width_all),
            (((1,), (1,)), ((), ())),
            preferred_element_type=jnp.float32,
        )
    ).astype(jnp.bfloat16)
    return (grad_in, key_new, key_first_new, key_second_new, step_keys, attention)


def solution(mesh):
    in_specs = (
        P(("grp", "fsdp"), "tp"),
        P(("grp", "fsdp"), "tp"),
        P(("grp", "tp", "fsdp"), None),
        P(("grp", "tp", "fsdp"), None),
        P(("grp", "tp", "fsdp"), None),
        P(("grp", "fsdp"), None, None),
        P(("grp", "fsdp"), None, "tp"),
        P(("grp", "fsdp"), None, "tp"),
        P(("grp", "fsdp"), None, "tp"),
        P(("grp", "fsdp"), None, "tp"),
        P(("grp", "fsdp")),
    )
    out_specs = (
        P(("grp", "fsdp"), "tp"),
        P(("grp", "tp", "fsdp"), None),
        P(("grp", "tp", "fsdp"), None),
        P(("grp", "tp", "fsdp"), None),
        P(("grp", "fsdp"), None, "tp"),
        P(("grp", "fsdp"), None, "tp"),
    )
    return jax.shard_map(shards, mesh=mesh, in_specs=in_specs, out_specs=out_specs, check_vma=False)
```

time: 245 us -> 120 us (0.49)
  waiting for transfers between devices: 177 us -> 42.8 us
  blocking collectives: 35.3 us -> 2.55 us
  starting transfers between devices: 0.12 us -> 32.7 us
  local copies, waits for them, and re-layouts: 5.13 us -> 18.5 us
  between operations: 15.2 us -> 4.75 us
  other arithmetic: 4.83 us -> 11.9 us
    all_gather x2 -> x0, waiting for transfers between devices: 88.8 us -> none  [the longest x1 46.8 us: shards(): every_row = lax.all_gather(relay_cast, ('fsdp', 'tp'), axis=0, tiled=True)]
    reduce_scatter x1 -> x0, waiting for transfers between devices: 87.1 us -> none  [shards(): lax.psum_scatter(unit_scale * contract_rows(learn_hidden, cotangent), 'fs...]
    ppermute x0 -> x29, waiting for transfers between devices: none -> 42.8 us  [swap(): return lax.ppermute(value, axis, [(i, i ^ 1 << bit) for i in range(size)])]
    psum x1 -> x0, blocking collectives: 32.7 us -> none  [shards(): square_sum = lax.psum(jnp.sum(grad_weight * grad_weight), ('fsdp', 'tp'))]
    ppermute x0 -> x29, starting transfers between devices: none -> 32.7 us  [swap(): return lax.ppermute(value, axis, [(i, i ^ 1 << bit) for i in range(size)])]
    another operation x1 -> x4, local copies, waits for them, and re-layouts: 0.12 us -> 4.04 us
    convert_element_type x1 -> x10, local copies, waits for them, and re-layouts: 0.01 us -> 3.91 us  [the longest x9 3.9 us: scatter_sum(): held[c] = keep + swap(give.astype(link_type), axis, bit).astype(jnp.float32)]
    add x0 -> x13, other arithmetic: none -> 3.61 us  [the longest x11 3.59 us: scatter_sum(): held[c] = keep + swap(give.astype(link_type), axis, bit).astype(jnp.float32)]
  transfers between devices with their start and end apart: 3 -> 29, of which waited for: 3 -> 18; matrix products, arithmetic and copies ran while one was open for 2% -> 21% of each run, Pallas kernels for 0% -> 0%
where the time goes in v1:
time: 120 us; the launch traced here: 119 us
  waiting for transfers between devices  42.8 us (36%)
  starting transfers between devices  32.7 us (27%)
  local copies, waits for them, and re-layouts  18.5 us (15%)
  other arithmetic  11.9 us (10%)
  matrix products  5.48 us (5%)
  between operations  4.75 us (4%)
  blocking collectives  2.55 us (2%)
    ppermute x29, waiting for transfers between devices, swap(): return lax.ppermute(value, axis, [(i, i ^ 1 << bit) for i in range(size)])  42.8 us
    ppermute x29, starting transfers between devices, swap(): return lax.ppermute(value, axis, [(i, i ^ 1 << bit) for i in range(size)])  32.7 us
    another operation x2, local copies, waits for them, and re-layouts  3.95 us
    convert_element_type x9, local copies, waits for them, and re-layouts, scatter_sum(): held[c] = keep + swap(give.astype(link_type), axis, bit).astype(jnp.float32)  3.9 us
    add x11, other arithmetic, scatter_sum(): held[c] = keep + swap(give.astype(link_type), axis, bit).astype(jnp.float32)  3.59 us
    unnamed x33, local copies, waits for them, and re-layouts  3.38 us
    all_gather x1, blocking collectives, shards(): cotangent = lax.all_gather(learn_grad_out, 'tp', axis=1, tiled=True)  2.55 us
  transfers between devices with their start and end apart: 29, of which 18 were waited for; matrix products, arithmetic and copies ran while one was open for 21% of the time, Pallas kernels for 0%

profile of v1, /device:TPU:0, one launch (start us, length us, event | category | flops | bytes accessed | tf_op | source)
XLA Modules:
  0.0 118.6 jit_solution(1398689688898614000)
XLA Ops:
  0.7 2.5 %all_gather.3 = bf16[384,512]{1,0:T(8,128)(2,1)S(1)} all-gather(bf16[384,256]{1,0:T(8,128)(2,1)} %param.12), channel_id=1, replica_groups=mesh['grp'=2,'fsdp'=8,'tp'=2] {'tp'}, dimensions={1}, use_global_device_ids=true | all-gather | bytes 589824 | tf_op jit(solution)/shard_map/all_gather | solution.py:192
  3.2 1.2 %convolution_multiply_fusion = f32[1920,512]{1,0:T(8,128)S(1)} fusion(bf16[384,1920]{1,0:T(8,128)(2,1)S(1)} %copy-done, bf16[384,512]{1,0:T(8,128)(2,1)S(1)} %all_gather.3), kind=kOutput, calls=%fused_computation | convolution fusion | flops 755957760 | bytes 5799936 | tf_op jit(solution)/shard_map/dot_general | solution.py:36
  4.4 2.0 %fusion.57 = (f32[8,80,512]{2,1,0:T(8,128)S(1)}, f32[8,80,512]{2,1,0:T(8,128)}, f32[8,80,512]{2,1,0:T(8,128)}) fusion(f32[8,240,512]{2,1,0:T(8,128)S(1)} %bitcast.244), kind=kLoop, calls=%fused_computation.146 | loop fusion | bytes 7864320 | tf_op jit(solution)/shard_map/slice | solution.py:69
  6.4 1.1 fusion.17
  7.6 4.0 %collective-permute-start.15 = (bf16[2,2,80,512]{3,2,0,1:T(8,128)(2,1)S(1)}, bf16[2,2,80,512]{3,2,0,1:T(8,128)(2,1)}, u32[]{:S(2)}, u32[]{:S(2)}) collective-permute-start(bf16[2,2,80,512]{3,2,0,1:T(8,128)(2,1)S(1)} %fusion.17), channel_id=1, source_target_pairs={{0,8},{2,10},{4,12},{6,14},{8,0},{10,2},{12,4},{14,6},{1,9},{3,11}... | collective-permute-start | bytes 983048 | tf_op jit(solution)/shard_map/ppermute | solution.py:43
  11.6 1.9 %fusion.18 = bf16[2,2,80,512]{3,2,1,0:T(8,128)(2,1)} fusion(f32[2,2,2,80,512]{4,3,2,1,0:T(8,128)} %bitcast.247, s32[]{:T(128)S(6)} %select_n.234), kind=kLoop, calls=%fused_computation.40 | loop fusion | bytes 655364 | tf_op jit(solution)/shard_map/convert_element_type | solution.py:78
  13.4 1.6 %collective-permute-start.12 = (bf16[2,2,80,512]{3,2,1,0:T(8,128)(2,1)}, bf16[2,2,80,512]{3,2,1,0:T(8,128)(2,1)}, u32[]{:S(2)}, u32[]{:S(2)}) collective-permute-start(bf16[2,2,80,512]{3,2,1,0:T(8,128)(2,1)} %fusion.18), channel_id=1, source_target_pairs={{0,4},{2,6},{4,0},{6,2},{8,12},{10,14},{12,8},{14,10},{1,5},{3,7},... | collective-permute-start | bytes 983048 | tf_op jit(solution)/shard_map/ppermute | solution.py:43
  15.7 1.5 %collective-permute-start.9 = (bf16[2,2,80,512]{3,2,1,0:T(8,128)(2,1)}, bf16[2,2,80,512]{3,2,1,0:T(8,128)(2,1)}, u32[]{:S(2)}, u32[]{:S(2)}) collective-permute-start(bf16[2,2,80,512]{3,2,1,0:T(8,128)(2,1)} %fusion.16), channel_id=1, source_target_pairs={{0,2},{2,0},{4,6},{6,4},{8,10},{10,8},{12,14},{14,12},{1,3},{3,1},... | collective-permute-start | bytes 983048 | tf_op jit(solution)/shard_map/ppermute | solution.py:43
  17.2 1.6 %reshape.193 = bf16[1,8,2,8,240]{4,3,2,1,0:T(8,128)(2,1)} reshape(bf16[1,8,3840]{2,1,0:T(8,128)(2,1)} %param.16) | data formatting | bytes 122880 | tf_op jit(solution)/shard_map/reshape | solution.py:197
  18.9 1.4 %dynamic-slice_bitcast_fusion.2 = bf16[8,1,8,240]{3,0,2,1:T(8,128)(2,1)} fusion(bf16[1,8,2,8,240]{4,3,2,1,0:T(8,128)(2,1)} %reshape.193, s32[]{:T(128)S(6)} %select_n.240), kind=kLoop, calls=%fused_computation.106 | loop fusion | bytes 61444 | tf_op jit(solution)/shard_map/transpose | solution.py:199
  22.2 2.0 %reshape.196 = bf16[1024,2,128]{2,1,0:T(2,128)(2,1)} reshape(bf16[1,1024,256]{2,1,0:T(8,128)(2,1)} %param.18) | data formatting | bytes 1048576 | tf_op jit(solution)/shard_map/reshape.2
  24.9 2.1 %fusion.59 = (f32[8,2,8]{2,0,1:T(8,128)S(1)}, f32[1,8,2,8,1024]{4,3,1,2,0:T(8,128)}) fusion(bf16[8,2,8,128]{3,0,2,1:T(8,128)(2,1)} %bitcast.261, bf16[1024,2,128,1]{2,1,0,3:T(2,128)(2,1)} %bitcast.257, pred[1024]{0:T(1024)(128)(4,1)S(1)} %iota_compare_fusion.1), kind=kOutput, calls=%fused_computation.148 | convolution fusion | flops 33947520 | bytes 1082880 | tf_op jit(solution)/shard_map/rtkgd,rpkd->rtkgp/dot_general | solution.py:131
  27.6 0.8 fusion.47
  29.5 1.9 %fusion.14 = f32[8,2,8]{2,0,1:T(8,128)} fusion(f32[1,8,2,8,1024]{4,3,1,2,0:T(8,128)} %get-tuple-element.68, f32[8,2,8]{2,0,1:T(8,128)S(1)} %get-tuple-element.67), kind=kLoop, calls=%fused_computation.36 | loop fusion | flops 262016 | bytes 525312 | tf_op jit(solution)/shard_map/reduce_sum | solution.py:139
  31.4 1.7 %collective-permute-done.23 = bf16[2,2,1,8,240]{4,3,1,0,2:T(8,128)(2,1)} collective-permute-done((bf16[2,2,1,8,240]{4,3,1,0,2:T(8,128)(2,1)}, bf16[2,2,1,8,240]{4,3,1,0,2:T(8,128)(2,1)}, u32[]{:S(2)}, u32[]{:S(2)}) %collective-permute-start.23) | collective-permute-done | bytes 15392 | tf_op jit(solution)/shard_map/ppermute | solution.py:43
  35.4 2.0 %reshape.200 = bf16[1024,2,128]{2,1,0:T(2,128)(2,1)} reshape(bf16[1,1024,256]{2,1,0:T(8,128)(2,1)} %param.19) | data formatting | bytes 1048576 | tf_op jit(solution)/shard_map/reshape.11
  37.4 1.9 %collective-permute-done.24 = bf16[2,2,1,8,240]{4,3,1,0,2:T(8,128)(2,1)} collective-permute-done((bf16[2,2,1,8,240]{4,3,1,0,2:T(8,128)(2,1)S(1)}, bf16[2,2,1,8,240]{4,3,1,0,2:T(8,128)(2,1)}, u32[]{:S(2)}, u32[]{:S(2)}) %collective-permute-start.24) | collective-permute-done | bytes 15392 | tf_op jit(solution)/shard_map/ppermute | solution.py:43
  40.1 1.3 %bitcast_add_fusion = f32[2,2,80,512]{3,2,0,1:T(8,128)S(1)} fusion(bf16[2,2,80,512]{3,2,0,1:T(8,128)(2,1)} %collective-permute-done.15, f32[2,2,2,80,512]{4,3,2,1,0:T(8,128)} %bitcast.250, s32[]{:T(128)S(6)} %select_n.235), kind=kLoop, calls=%fused_computation.24 | loop fusion | flops 327680 | bytes 1638404 | tf_op jit(solution)/shard_map/add | solution.py:78
  41.5 1.6 %collective-permute-start.16 = (bf16[2,80,512]{2,1,0:T(8,128)(2,1)S(1)}, bf16[2,80,512]{2,1,0:T(8,128)(2,1)S(1)}, u32[]{:S(2)}, u32[]{:S(2)}) collective-permute-start(bf16[2,80,512]{2,1,0:T(8,128)(2,1)S(1)} %fusion.27), channel_id=1, source_target_pairs={{0,2},{2,0},{4,6},{6,4},{8,10},{10,8},{12,14},{14,12},{1,3},{3,1},... | collective-permute-start | bytes 491528 | tf_op jit(solution)/shard_map/ppermute | solution.py:43
  43.0 1.1 bitcast_add_fusion.1
  44.2 0.8 collective-permute-start.13
  45.0 1.1 bitcast_add_fusion.2
  47.0 1.4 %collective-permute-start.17 = (bf16[80,512]{1,0:T(8,128)(2,1)S(1)}, bf16[80,512]{1,0:T(8,128)(2,1)S(1)}, u32[]{:S(2)}, u32[]{:S(2)}) collective-permute-start(bf16[80,512]{1,0:T(8,128)(2,1)S(1)} %fusion.30), channel_id=1, source_target_pairs={{0,4},{2,6},{4,0},{6,2},{8,12},{10,14},{12,8},{14,10},{1,5},{3,7},... | collective-permute-start | bytes 245768 | tf_op jit(solution)/shard_map/ppermute | solution.py:43
  48.3 3.9 %collective-permute-done.13 = bf16[2,80,512]{2,1,0:T(8,128)(2,1)S(1)} collective-permute-done((bf16[2,80,512]{2,1,0:T(8,128)(2,1)S(1)}, bf16[2,80,512]{2,1,0:T(8,128)(2,1)S(1)}, u32[]{:S(2)}, u32[]{:S(2)}) %collective-permute-start.13) | collective-permute-done | bytes 163872 | tf_op jit(solution)/shard_map/ppermute | solution.py:43
  52.9 0.8 collective-permute-done.10
  53.8 0.8 collective-permute-start.11
  55.2 1.6 %collective-permute-done.14 = bf16[80,512]{1,0:T(8,128)(2,1)S(1)} collective-permute-done((bf16[80,512]{1,0:T(8,128)(2,1)S(1)}, bf16[80,512]{1,0:T(8,128)(2,1)S(1)}, u32[]{:S(2)}, u32[]{:S(2)}) %collective-permute-start.14) | collective-permute-done | bytes 81952 | tf_op jit(solution)/shard_map/ppermute | solution.py:43
  56.8 2.3 %collective-permute-done.11 = bf16[80,512]{1,0:T(8,128)(2,1)S(1)} collective-permute-done((bf16[80,512]{1,0:T(8,128)(2,1)S(1)}, bf16[80,512]{1,0:T(8,128)(2,1)S(1)}, u32[]{:S(2)}, u32[]{:S(2)}) %collective-permute-start.11) | collective-permute-done | bytes 81952 | tf_op jit(solution)/shard_map/ppermute | solution.py:43
  59.9 1.4 %collective-permute-done.18 = f32[1,1]{1,0:T(1,128)} collective-permute-done((f32[1,1]{1,0:T(1,128)}, f32[1,1]{1,0:T(1,128)}, u32[]{:S(2)}, u32[]{:S(2)}) %collective-permute-start.18) | collective-permute-done | bytes 36 | tf_op jit(solution)/shard_map/ppermute | solution.py:43
  62.5 2.1 %collective-permute-start.19 = (f32[1,1]{1,0:T(1,128)}, f32[1,1]{1,0:T(1,128)}, u32[]{:S(2)}, u32[]{:S(2)}) collective-permute-start(f32[1,1]{1,0:T(1,128)} %add.161), channel_id=1, source_target_pairs={{0,2},{2,0},{4,6},{6,4},{8,10},{10,8},{12,14},{14,12},{1,3},{3,1},... | collective-permute-start | bytes 20 | tf_op jit(solution)/shard_map/ppermute | solution.py:43
  64.6 1.7 %collective-permute-done.19 = f32[1,1]{1,0:T(1,128)} collective-permute-done((f32[1,1]{1,0:T(1,128)}, f32[1,1]{1,0:T(1,128)}, u32[]{:S(2)}, u32[]{:S(2)}) %collective-permute-start.19) | collective-permute-done | bytes 36 | tf_op jit(solution)/shard_map/ppermute | solution.py:43
  66.8 1.4 %collective-permute-start.20 = (f32[1,1]{1,0:T(1,128)}, f32[1,1]{1,0:T(1,128)}, u32[]{:S(2)}, u32[]{:S(2)}) collective-permute-start(f32[1,1]{1,0:T(1,128)} %add.162), channel_id=1, source_target_pairs={{0,4},{2,6},{4,0},{6,2},{8,12},{10,14},{12,8},{14,10},{1,5},{3,7},... | collective-permute-start | bytes 20 | tf_op jit(solution)/shard_map/ppermute | solution.py:43
  68.2 2.3 %collective-permute-done.20 = f32[1,1]{1,0:T(1,128)} collective-permute-done((f32[1,1]{1,0:T(1,128)}, f32[1,1]{1,0:T(1,128)}, u32[]{:S(2)}, u32[]{:S(2)}) %collective-permute-start.20) | collective-permute-done | bytes 36 | tf_op jit(solution)/shard_map/ppermute | solution.py:43
  71.0 2.1 %collective-permute-start.21 = (f32[1,1]{1,0:T(1,128)}, f32[1,1]{1,0:T(1,128)}, u32[]{:S(2)}, u32[]{:S(2)}) collective-permute-start(f32[1,1]{1,0:T(1,128)} %add.163), channel_id=1, source_target_pairs={{0,8},{2,10},{4,12},{6,14},{8,0},{10,2},{12,4},{14,6},{1,9},{3,11}... | collective-permute-start | bytes 20 | tf_op jit(solution)/shard_map/ppermute | solution.py:43
  73.2 2.5 %collective-permute-done.21 = f32[1,1]{1,0:T(1,128)} collective-permute-done((f32[1,1]{1,0:T(1,128)}, f32[1,1]{1,0:T(1,128)}, u32[]{:S(2)}, u32[]{:S(2)}) %collective-permute-start.21) | collective-permute-done | bytes 36 | tf_op jit(solution)/shard_map/ppermute | solution.py:43
  76.3 1.4 %fusion.55 = (bf16[240,512]{1,0:T(8,128)(2,1)S(1)}, f32[240,512]{1,0:T(8,128)}, f32[240,512]{1,0:T(8,128)}, f32[240,512]{1,0:T(8,128)}, bf16[240,512]{1,0:T(8,128)(2,1)S(1)}) fusion(f32[240,512]{1,0:T(8,128)S(1)} %copy-done.4, f32[80,512]{1,0:T(8,128)S(1)} %bitcast_add_fusion.6, f32[80,512]{1,0:T(8,128)S(1)} %bitcast_add_fusion.7, ...), kind=kLoop, calls=%fused_computation.145 | loop fusion | flops 2457600 | bytes 3932164 | tf_op jit(solution)/shard_map/convert_element_type | solution.py:210
  78.0 0.8 collective-permute-start
  79.5 1.6 %collective-permute-start.6 = (bf16[80,512]{1,0:T(8,128)(2,1)S(1)}, bf16[80,512]{1,0:T(8,128)(2,1)S(1)}, u32[]{:S(2)}, u32[]{:S(2)}) collective-permute-start(bf16[80,512]{1,0:T(8,128)(2,1)S(1)} %get-tuple-element.57), channel_id=1, source_target_pairs={{0,4},{2,6},{4,0},{6,2},{8,12},{10,14},{12,8},{14,10},{1,5},{3,7},... | collective-permute-start | bytes 245768 | tf_op jit(solution)/shard_map/ppermute | solution.py:43
  81.3 3.8 %collective-permute-done = bf16[80,512]{1,0:T(8,128)(2,1)S(1)} collective-permute-done((bf16[80,512]{1,0:T(8,128)(2,1)S(1)}, bf16[80,512]{1,0:T(8,128)(2,1)S(1)}, u32[]{:S(2)}, u32[]{:S(2)}) %collective-permute-start) | collective-permute-done | bytes 81952 | tf_op jit(solution)/shard_map/ppermute | solution.py:43
  85.6 1.3 %collective-permute-start.7 = (bf16[2,80,512]{2,1,0:T(8,128)(2,1)S(1)}, bf16[2,80,512]{2,1,0:T(8,128)(2,1)S(1)}, u32[]{:S(2)}, u32[]{:S(2)}) collective-permute-start(bf16[2,80,512]{2,1,0:T(8,128)(2,1)S(1)} %pad_maximum_fusion.10), channel_id=1, source_target_pairs={{0,2},{2,0},{4,6},{6,4},{8,10},{10,8},{12,14},{14,12},{1,3},{3,1},... | collective-permute-start | bytes 491528 | tf_op jit(solution)/shard_map/ppermute | solution.py:43
  87.1 2.5 %collective-permute-start.4 = (bf16[2,80,512]{2,1,0:T(8,128)(2,1)S(1)}, bf16[2,80,512]{2,1,0:T(8,128)(2,1)S(1)}, u32[]{:S(2)}, u32[]{:S(2)}) collective-permute-start(bf16[2,80,512]{2,1,0:T(8,128)(2,1)S(1)} %pad_maximum_fusion.9), channel_id=1, source_target_pairs={{0,8},{2,10},{4,12},{6,14},{8,0},{10,2},{12,4},{14,6},{1,9},{3,11}... | collective-permute-start | bytes 491528 | tf_op jit(solution)/shard_map/ppermute | solution.py:43
  89.6 1.6 %collective-permute-done.27 = f32[2,8,256]{2,1,0:T(8,128)S(1)} collective-permute-done((f32[2,8,256]{2,1,0:T(8,128)S(1)}, f32[2,8,256]{2,1,0:T(8,128)S(1)}, u32[]{:S(2)}, u32[]{:S(2)}) %collective-permute-start.27) | collective-permute-done | bytes 16416 | tf_op jit(solution)/shard_map/ppermute | solution.py:43
  91.5 2.4 %collective-permute-start.1 = (bf16[2,80,512]{2,1,0:T(8,128)(2,1)S(1)}, bf16[2,80,512]{2,1,0:T(8,128)(2,1)S(1)}, u32[]{:S(2)}, u32[]{:S(2)}) collective-permute-start(bf16[2,80,512]{2,1,0:T(8,128)(2,1)S(1)} %pad_maximum_fusion.8), channel_id=1, source_target_pairs={{0,4},{2,6},{4,0},{6,2},{8,12},{10,14},{12,8},{14,10},{1,5},{3,7},... | collective-permute-start | bytes 491528 | tf_op jit(solution)/shard_map/ppermute | solution.py:43
  93.8 3.4 %collective-permute-done.28 = f32[8,256]{1,0:T(8,128)S(1)} collective-permute-done((f32[8,256]{1,0:T(8,128)S(1)}, f32[8,256]{1,0:T(8,128)S(1)}, u32[]{:S(2)}, u32[]{:S(2)}) %collective-permute-start.28) | collective-permute-done | bytes 8224 | tf_op jit(solution)/shard_map/ppermute | solution.py:43
  99.0 2.6 %collective-permute-start.5 = (bf16[2,2,80,512]{3,2,1,0:T(8,128)(2,1)S(1)}, bf16[2,2,80,512]{3,2,1,0:T(8,128)(2,1)S(1)}, u32[]{:S(2)}, u32[]{:S(2)}) collective-permute-start(bf16[2,2,80,512]{3,2,1,0:T(8,128)(2,1)S(1)} %pad_maximum_fusion.6), channel_id=1, source_target_pairs={{0,4},{2,6},{4,0},{6,2},{8,12},{10,14},{12,8},{14,10},{1,5},{3,7},... | collective-permute-start | bytes 983048 | tf_op jit(solution)/shard_map/ppermute | solution.py:43
  102.2 12.3 %collective-permute-done.8 = bf16[2,2,80,512]{3,2,0,1:T(8,128)(2,1)S(1)} collective-permute-done((bf16[2,2,80,512]{3,2,0,1:T(8,128)(2,1)S(1)}, bf16[2,2,80,512]{3,2,0,1:T(8,128)(2,1)S(1)}, u32[]{:S(2)}, u32[]{:S(2)}) %collective-permute-start.8) | collective-permute-done | bytes 327712 | tf_op jit(solution)/shard_map/ppermute | solution.py:43
  115.3 1.2 %fusion.1 = bf16[384,1920]{0,1:T(8,128)(2,1)S(1)} fusion(bf16[1920,512]{1,0:T(8,128)(2,1)S(1)} %bitcast.254, bf16[384,512]{1,0:T(8,128)(2,1)S(1)} %all_gather.3), kind=kOutput, calls=%fused_computation.3 | convolution fusion | flops 756449280 | bytes 3833856 | tf_op jit(solution)/shard_map/dot_general | solution.py:227
  116.5 2.1 %copy.68 = bf16[384,1920]{1,0:T(8,128)(2,1)} copy(bf16[384,1920]{0,1:T(8,128)(2,1)S(1)} %fusion.1) | data formatting | bytes 2949120
  (121 shorter events, 15.6 us)
Async XLA Ops:
  0.6 2.6 %copy-start = (bf16[384,1920]{1,0:T(8,128)(2,1)S(1)}, bf16[384,1920]{1,0:T(8,128)(2,1)}, u32[]{:S(2)}) copy-start(bf16[384,1920]{1,0:T(8,128)(2,1)} %param.11) | copy-start | bytes 4423684
  7.6 32.6 %collective-permute-start.15 = (bf16[2,2,80,512]{3,2,0,1:T(8,128)(2,1)S(1)}, bf16[2,2,80,512]{3,2,0,1:T(8,128)(2,1)}, u32[]{:S(2)}, u32[]{:S(2)}) collective-permute-start(bf16[2,2,80,512]{3,2,0,1:T(8,128)(2,1)S(1)} %fusion.17), channel_id=1, source_target_pairs={{0,8},{2,10},{4,12},{6,14},{8,0},{10,2},{12,4},{14,6},{1,9},{3,11}... | collective-permute-start | bytes 983048 | tf_op jit(solution)/shard_map/ppermute | solution.py:43
  13.4 29.6 %collective-permute-start.12 = (bf16[2,2,80,512]{3,2,1,0:T(8,128)(2,1)}, bf16[2,2,80,512]{3,2,1,0:T(8,128)(2,1)}, u32[]{:S(2)}, u32[]{:S(2)}) collective-permute-start(bf16[2,2,80,512]{3,2,1,0:T(8,128)(2,1)} %fusion.18), channel_id=1, source_target_pairs={{0,4},{2,6},{4,0},{6,2},{8,12},{10,14},{12,8},{14,10},{1,5},{3,7},... | collective-permute-start | bytes 983048 | tf_op jit(solution)/shard_map/ppermute | solution.py:43
  15.7 29.2 %collective-permute-start.9 = (bf16[2,2,80,512]{3,2,1,0:T(8,128)(2,1)}, bf16[2,2,80,512]{3,2,1,0:T(8,128)(2,1)}, u32[]{:S(2)}, u32[]{:S(2)}) collective-permute-start(bf16[2,2,80,512]{3,2,1,0:T(8,128)(2,1)} %fusion.16), channel_id=1, source_target_pairs={{0,2},{2,0},{4,6},{6,4},{8,10},{10,8},{12,14},{14,12},{1,3},{3,1},... | collective-permute-start | bytes 983048 | tf_op jit(solution)/shard_map/ppermute | solution.py:43
  21.7 5.3 %collective-permute-start.22 = (bf16[2,2,1,8,240]{4,3,0,1,2:T(8,128)(2,1)S(1)}, bf16[2,2,1,8,240]{4,3,0,1,2:T(8,128)(2,1)S(1)}, u32[]{:S(2)}, u32[]{:S(2)}) collective-permute-start(bf16[2,2,1,8,240]{4,3,0,1,2:T(8,128)(2,1)S(1)} %bitcast.264), channel_id=1, source_target_pairs={{0,2},{2,0},{4,6},{6,4},{8,10},{10,8},{12,14},{14,12},{1,3},{3,1},... | collective-permute-start | bytes 46088 | tf_op jit(solution)/shard_map/ppermute | solution.py:43
  27.0 4.3 %copy-start.8 = (f32[8,2,8]{2,0,1:T(8,128)}, f32[8,2,8]{2,0,1:T(8,128)S(1)}, u32[]{:S(2)}) copy-start(f32[8,2,8]{2,0,1:T(8,128)S(1)} %get-tuple-element.67) | copy-start | bytes 1540
  27.0 0.6 copy-start.13
  29.1 4.1 %collective-permute-start.23 = (bf16[2,2,1,8,240]{4,3,1,0,2:T(8,128)(2,1)}, bf16[2,2,1,8,240]{4,3,1,0,2:T(8,128)(2,1)}, u32[]{:S(2)}, u32[]{:S(2)}) collective-permute-start(bf16[2,2,1,8,240]{4,3,1,0,2:T(8,128)(2,1)} %fusion.43), channel_id=1, source_target_pairs={{0,4},{2,6},{4,0},{6,2},{8,12},{10,14},{12,8},{14,10},{1,5},{3,7},... | collective-permute-start | bytes 46088 | tf_op jit(solution)/shard_map/ppermute | solution.py:43
  33.8 0.6 copy-start.7
  34.5 4.9 %collective-permute-start.24 = (bf16[2,2,1,8,240]{4,3,1,0,2:T(8,128)(2,1)S(1)}, bf16[2,2,1,8,240]{4,3,1,0,2:T(8,128)(2,1)}, u32[]{:S(2)}, u32[]{:S(2)}) collective-permute-start(bf16[2,2,1,8,240]{4,3,1,0,2:T(8,128)(2,1)S(1)} %fusion.39), channel_id=1, source_target_pairs={{0,8},{2,10},{4,12},{6,14},{8,0},{10,2},{12,4},{14,6},{1,9},{3,11}... | collective-permute-start | bytes 46088 | tf_op jit(solution)/shard_map/ppermute | solution.py:43
  37.4 5.6 %copy-start.1 = (f32[8,80,512]{2,1,0:T(8,128)S(1)}, f32[8,80,512]{2,1,0:T(8,128)}, u32[]{:S(2)}) copy-start(f32[8,80,512]{2,1,0:T(8,128)} %get-tuple-element.32) | copy-start | bytes 3932164
  41.5 5.4 %collective-permute-start.16 = (bf16[2,80,512]{2,1,0:T(8,128)(2,1)S(1)}, bf16[2,80,512]{2,1,0:T(8,128)(2,1)S(1)}, u32[]{:S(2)}, u32[]{:S(2)}) collective-permute-start(bf16[2,80,512]{2,1,0:T(8,128)(2,1)S(1)} %fusion.27), channel_id=1, source_target_pairs={{0,2},{2,0},{4,6},{6,4},{8,10},{10,8},{12,14},{14,12},{1,3},{3,1},... | collective-permute-start | bytes 491528 | tf_op jit(solution)/shard_map/ppermute | solution.py:43
  44.2 8.1 %collective-permute-start.13 = (bf16[2,80,512]{2,1,0:T(8,128)(2,1)S(1)}, bf16[2,80,512]{2,1,0:T(8,128)(2,1)S(1)}, u32[]{:S(2)}, u32[]{:S(2)}) collective-permute-start(bf16[2,80,512]{2,1,0:T(8,128)(2,1)S(1)} %fusion.26), channel_id=1, source_target_pairs={{0,8},{2,10},{4,12},{6,14},{8,0},{10,2},{12,4},{14,6},{1,9},{3,11}... | collective-permute-start | bytes 491528 | tf_op jit(solution)/shard_map/ppermute | solution.py:43
  46.1 7.6 %collective-permute-start.10 = (bf16[2,80,512]{2,1,0:T(8,128)(2,1)S(1)}, bf16[2,80,512]{2,1,0:T(8,128)(2,1)S(1)}, u32[]{:S(2)}, u32[]{:S(2)}) collective-permute-start(bf16[2,80,512]{2,1,0:T(8,128)(2,1)S(1)} %fusion.25), channel_id=1, source_target_pairs={{0,4},{2,6},{4,0},{6,2},{8,12},{10,14},{12,8},{14,10},{1,5},{3,7},... | collective-permute-start | bytes 491528 | tf_op jit(solution)/shard_map/ppermute | solution.py:43
  46.9 29.3 %copy-start.4 = (f32[240,512]{1,0:T(8,128)S(1)}, f32[240,512]{1,0:T(8,128)}, u32[]{:S(2)}) copy-start(f32[240,512]{1,0:T(8,128)} %param.13) | copy-start | bytes 1474564
  46.9 29.3 %copy-start.5 = (f32[240,512]{1,0:T(8,128)S(1)}, f32[240,512]{1,0:T(8,128)}, u32[]{:S(2)}) copy-start(f32[240,512]{1,0:T(8,128)} %param.14) | copy-start | bytes 1474564
  46.9 29.3 %copy-start.6 = (f32[240,512]{1,0:T(8,128)S(1)}, f32[240,512]{1,0:T(8,128)}, u32[]{:S(2)}) copy-start(f32[240,512]{1,0:T(8,128)} %param.15) | copy-start | bytes 1474564
  47.0 8.2 %collective-permute-start.17 = (bf16[80,512]{1,0:T(8,128)(2,1)S(1)}, bf16[80,512]{1,0:T(8,128)(2,1)S(1)}, u32[]{:S(2)}, u32[]{:S(2)}) collective-permute-start(bf16[80,512]{1,0:T(8,128)(2,1)S(1)} %fusion.30), channel_id=1, source_target_pairs={{0,4},{2,6},{4,0},{6,2},{8,12},{10,14},{12,8},{14,10},{1,5},{3,7},... | collective-permute-start | bytes 245768 | tf_op jit(solution)/shard_map/ppermute | solution.py:43
  52.3 4.5 %collective-permute-start.14 = (bf16[80,512]{1,0:T(8,128)(2,1)S(1)}, bf16[80,512]{1,0:T(8,128)(2,1)S(1)}, u32[]{:S(2)}, u32[]{:S(2)}) collective-permute-start(bf16[80,512]{1,0:T(8,128)(2,1)S(1)} %fusion.29), channel_id=1, source_target_pairs={{0,2},{2,0},{4,6},{6,4},{8,10},{10,8},{12,14},{14,12},{1,3},{3,1},... | collective-permute-start | bytes 245768 | tf_op jit(solution)/shard_map/ppermute | solution.py:43
  53.8 5.4 %collective-permute-start.11 = (bf16[80,512]{1,0:T(8,128)(2,1)S(1)}, bf16[80,512]{1,0:T(8,128)(2,1)S(1)}, u32[]{:S(2)}, u32[]{:S(2)}) collective-permute-start(bf16[80,512]{1,0:T(8,128)(2,1)S(1)} %fusion.28), channel_id=1, source_target_pairs={{0,8},{2,10},{4,12},{6,14},{8,0},{10,2},{12,4},{14,6},{1,9},{3,11}... | collective-permute-start | bytes 245768 | tf_op jit(solution)/shard_map/ppermute | solution.py:43
  59.9 1.4 %collective-permute-start.18 = (f32[1,1]{1,0:T(1,128)}, f32[1,1]{1,0:T(1,128)}, u32[]{:S(2)}, u32[]{:S(2)}) collective-permute-start(f32[1,1]{1,0:T(1,128)} %bitcast.47), channel_id=1, source_target_pairs={{0,1},{1,0},{2,3},{3,2},{4,5},{5,4},{6,7},{7,6},{8,9},{9,8},{10,11... | collective-permute-start | bytes 20 | tf_op jit(solution)/shard_map/ppermute | solution.py:43
  62.5 3.7 %collective-permute-start.19 = (f32[1,1]{1,0:T(1,128)}, f32[1,1]{1,0:T(1,128)}, u32[]{:S(2)}, u32[]{:S(2)}) collective-permute-start(f32[1,1]{1,0:T(1,128)} %add.161), channel_id=1, source_target_pairs={{0,2},{2,0},{4,6},{6,4},{8,10},{10,8},{12,14},{14,12},{1,3},{3,1},... | collective-permute-start | bytes 20 | tf_op jit(solution)/shard_map/ppermute | solution.py:43
  66.8 3.7 %collective-permute-start.20 = (f32[1,1]{1,0:T(1,128)}, f32[1,1]{1,0:T(1,128)}, u32[]{:S(2)}, u32[]{:S(2)}) collective-permute-start(f32[1,1]{1,0:T(1,128)} %add.162), channel_id=1, source_target_pairs={{0,4},{2,6},{4,0},{6,2},{8,12},{10,14},{12,8},{14,10},{1,5},{3,7},... | collective-permute-start | bytes 20 | tf_op jit(solution)/shard_map/ppermute | solution.py:43
  71.0 4.6 %collective-permute-start.21 = (f32[1,1]{1,0:T(1,128)}, f32[1,1]{1,0:T(1,128)}, u32[]{:S(2)}, u32[]{:S(2)}) collective-permute-start(f32[1,1]{1,0:T(1,128)} %add.163), channel_id=1, source_target_pairs={{0,8},{2,10},{4,12},{6,14},{8,0},{10,2},{12,4},{14,6},{1,9},{3,11}... | collective-permute-start | bytes 20 | tf_op jit(solution)/shard_map/ppermute | solution.py:43
  77.7 19.5 %copy-start.11 = (bf16[1,8,2048]{2,1,0:T(8,128)(2,1)S(1)}, bf16[1,8,2048]{2,1,0:T(8,128)(2,1)}, u32[]{:S(2)}) copy-start(bf16[1,8,2048]{2,1,0:T(8,128)(2,1)} %param.17) | copy-start | bytes 98308
  77.7 19.5 %copy-start.15 = (pred[8,8]{1,0:T(8,128)(4,1)S(1)}, pred[8,8]{1,0:T(8,128)(4,1)}, u32[]{:S(2)}) copy-start(pred[8,8]{1,0:T(8,128)(4,1)} %iota_compare_fusion) | copy-start | bytes 196
  77.7 19.8 %copy-start.9 = (f32[8,2,8]{2,0,1:T(8,128)S(1)}, f32[8,2,8]{2,0,1:T(8,128)}, u32[]{:S(2)}) copy-start(f32[8,2,8]{2,0,1:T(8,128)} %copy-done.8) | copy-start | bytes 1540
  77.7 19.9 %copy-start.14 = (bf16[1,8,256]{2,1,0:T(8,128)(2,1)S(1)}, bf16[1,8,256]{2,1,0:T(8,128)(2,1)}, u32[]{:S(2)}) copy-start(bf16[1,8,256]{2,1,0:T(8,128)(2,1)} %param.20) | copy-start | bytes 12292
  77.7 20.1 %copy-start.10 = (f32[8,2,8]{2,0,1:T(8,128)S(1)}, f32[8,2,8]{2,0,1:T(8,128)}, u32[]{:S(2)}) copy-start(f32[8,2,8]{2,0,1:T(8,128)} %fusion.14) | copy-start | bytes 1540
  77.7 20.1 %copy-start.2 = (f32[1,8,2,8,1024]{4,3,1,2,0:T(8,128)S(1)}, f32[1,8,2,8,1024]{4,3,1,2,0:T(8,128)}, u32[]{:S(2)}) copy-start(f32[1,8,2,8,1024]{4,3,1,2,0:T(8,128)} %get-tuple-element.68) | copy-start | bytes 1572868
  77.7 20.1 %copy-start.3 = (bf16[1024,2,128]{2,1,0:T(2,128)(2,1)S(1)}, bf16[1024,2,128]{2,1,0:T(2,128)(2,1)}, u32[]{:S(2)}) copy-start(bf16[1024,2,128]{2,1,0:T(2,128)(2,1)} %reshape.200) | copy-start | bytes 1572868
  77.9 3.2 %collective-permute-start.25 = (f32[64,256]{1,0:T(8,128)S(1)}, f32[64,256]{1,0:T(8,128)S(1)}, u32[]{:S(2)}, u32[]{:S(2)}) collective-permute-start(f32[64,256]{1,0:T(8,128)S(1)} %dynamic-slice_bitcast_fusion), channel_id=1, source_target_pairs={{0,1},{1,0},{2,3},{3,2},{4,5},{5,4},{6,7},{7,6},{8,9},{9,8},{10,11... | collective-permute-start | bytes 196616 | tf_op jit(solution)/shard_map/ppermute | solution.py:43
  78.0 7.1 %collective-permute-start = (bf16[80,512]{1,0:T(8,128)(2,1)S(1)}, bf16[80,512]{1,0:T(8,128)(2,1)S(1)}, u32[]{:S(2)}, u32[]{:S(2)}) collective-permute-start(bf16[80,512]{1,0:T(8,128)(2,1)S(1)} %get-tuple-element.56), channel_id=1, source_target_pairs={{0,8},{2,10},{4,12},{6,14},{8,0},{10,2},{12,4},{14,6},{1,9},{3,11}... | collective-permute-start | bytes 245768 | tf_op jit(solution)/shard_map/ppermute | solution.py:43
  78.8 6.3 %collective-permute-start.3 = (bf16[80,512]{1,0:T(8,128)(2,1)S(1)}, bf16[80,512]{1,0:T(8,128)(2,1)S(1)}, u32[]{:S(2)}, u32[]{:S(2)}) collective-permute-start(bf16[80,512]{1,0:T(8,128)(2,1)S(1)} %get-tuple-element.58), channel_id=1, source_target_pairs={{0,2},{2,0},{4,6},{6,4},{8,10},{10,8},{12,14},{14,12},{1,3},{3,1},... | collective-permute-start | bytes 245768 | tf_op jit(solution)/shard_map/ppermute | solution.py:43
  79.5 6.1 %collective-permute-start.6 = (bf16[80,512]{1,0:T(8,128)(2,1)S(1)}, bf16[80,512]{1,0:T(8,128)(2,1)S(1)}, u32[]{:S(2)}, u32[]{:S(2)}) collective-permute-start(bf16[80,512]{1,0:T(8,128)(2,1)S(1)} %get-tuple-element.57), channel_id=1, source_target_pairs={{0,4},{2,6},{4,0},{6,2},{8,12},{10,14},{12,8},{14,10},{1,5},{3,7},... | collective-permute-start | bytes 245768 | tf_op jit(solution)/shard_map/ppermute | solution.py:43
  81.1 5.9 %collective-permute-start.26 = (f32[2,2,8,256]{3,2,1,0:T(8,128)S(1)}, f32[2,2,8,256]{3,2,1,0:T(8,128)S(1)}, u32[]{:S(2)}, u32[]{:S(2)}) collective-permute-start(f32[2,2,8,256]{3,2,1,0:T(8,128)S(1)} %dynamic-slice_bitcast_fusion.1), channel_id=1, source_target_pairs={{0,2},{2,0},{4,6},{6,4},{8,10},{10,8},{12,14},{14,12},{1,3},{3,1},... | collective-permute-start | bytes 98312 | tf_op jit(solution)/shard_map/ppermute | solution.py:43
  85.6 13.1 %collective-permute-start.7 = (bf16[2,80,512]{2,1,0:T(8,128)(2,1)S(1)}, bf16[2,80,512]{2,1,0:T(8,128)(2,1)S(1)}, u32[]{:S(2)}, u32[]{:S(2)}) collective-permute-start(bf16[2,80,512]{2,1,0:T(8,128)(2,1)S(1)} %pad_maximum_fusion.10), channel_id=1, source_target_pairs={{0,2},{2,0},{4,6},{6,4},{8,10},{10,8},{12,14},{14,12},{1,3},{3,1},... | collective-permute-start | bytes 491528 | tf_op jit(solution)/shard_map/ppermute | solution.py:43
  87.0 4.2 %collective-permute-start.27 = (f32[2,8,256]{2,1,0:T(8,128)S(1)}, f32[2,8,256]{2,1,0:T(8,128)S(1)}, u32[]{:S(2)}, u32[]{:S(2)}) collective-permute-start(f32[2,8,256]{2,1,0:T(8,128)S(1)} %dynamic-slice_bitcast_fusion.3), channel_id=1, source_target_pairs={{0,4},{2,6},{4,0},{6,2},{8,12},{10,14},{12,8},{14,10},{1,5},{3,7},... | collective-permute-start | bytes 49160 | tf_op jit(solution)/shard_map/ppermute | solution.py:43
  87.1 11.8 %collective-permute-start.4 = (bf16[2,80,512]{2,1,0:T(8,128)(2,1)S(1)}, bf16[2,80,512]{2,1,0:T(8,128)(2,1)S(1)}, u32[]{:S(2)}, u32[]{:S(2)}) collective-permute-start(bf16[2,80,512]{2,1,0:T(8,128)(2,1)S(1)} %pad_maximum_fusion.9), channel_id=1, source_target_pairs={{0,8},{2,10},{4,12},{6,14},{8,0},{10,2},{12,4},{14,6},{1,9},{3,11}... | collective-permute-start | bytes 491528 | tf_op jit(solution)/shard_map/ppermute | solution.py:43
  91.2 6.0 %collective-permute-start.28 = (f32[8,256]{1,0:T(8,128)S(1)}, f32[8,256]{1,0:T(8,128)S(1)}, u32[]{:S(2)}, u32[]{:S(2)}) collective-permute-start(f32[8,256]{1,0:T(8,128)S(1)} %fusion.52), channel_id=1, source_target_pairs={{0,8},{2,10},{4,12},{6,14},{8,0},{10,2},{12,4},{14,6},{1,9},{3,11}... | collective-permute-start | bytes 24584 | tf_op jit(solution)/shard_map/ppermute | solution.py:43
  91.5 10.1 %collective-permute-start.1 = (bf16[2,80,512]{2,1,0:T(8,128)(2,1)S(1)}, bf16[2,80,512]{2,1,0:T(8,128)(2,1)S(1)}, u32[]{:S(2)}, u32[]{:S(2)}) collective-permute-start(bf16[2,80,512]{2,1,0:T(8,128)(2,1)S(1)} %pad_maximum_fusion.8), channel_id=1, source_target_pairs={{0,4},{2,6},{4,0},{6,2},{8,12},{10,14},{12,8},{14,10},{1,5},{3,7},... | collective-permute-start | bytes 491528 | tf_op jit(solution)/shard_map/ppermute | solution.py:43
  97.2 1.8 %copy-start.12 = (bf16[8,256]{1,0:T(8,128)(2,1)}, bf16[8,256]{1,0:T(8,128)(2,1)S(1)}, u32[]{:S(2)}) copy-start(bf16[8,256]{1,0:T(8,128)(2,1)S(1)} %fusion.51) | copy-start | bytes 12292
  98.8 15.7 %collective-permute-start.8 = (bf16[2,2,80,512]{3,2,0,1:T(8,128)(2,1)S(1)}, bf16[2,2,80,512]{3,2,0,1:T(8,128)(2,1)S(1)}, u32[]{:S(2)}, u32[]{:S(2)}) collective-permute-start(bf16[2,2,80,512]{3,2,0,1:T(8,128)(2,1)S(1)} %pad_maximum_fusion.7), channel_id=1, source_target_pairs={{0,8},{2,10},{4,12},{6,14},{8,0},{10,2},{12,4},{14,6},{1,9},{3,11}... | collective-permute-start | bytes 983048 | tf_op jit(solution)/shard_map/ppermute | solution.py:43
  99.0 15.8 %collective-permute-start.5 = (bf16[2,2,80,512]{3,2,1,0:T(8,128)(2,1)S(1)}, bf16[2,2,80,512]{3,2,1,0:T(8,128)(2,1)S(1)}, u32[]{:S(2)}, u32[]{:S(2)}) collective-permute-start(bf16[2,2,80,512]{3,2,1,0:T(8,128)(2,1)S(1)} %pad_maximum_fusion.6), channel_id=1, source_target_pairs={{0,4},{2,6},{4,0},{6,2},{8,12},{10,14},{12,8},{14,10},{1,5},{3,7},... | collective-permute-start | bytes 983048 | tf_op jit(solution)/shard_map/ppermute | solution.py:43
  101.6 13.4 %collective-permute-start.2 = (bf16[2,2,80,512]{3,2,1,0:T(8,128)(2,1)S(1)}, bf16[2,2,80,512]{3,2,1,0:T(8,128)(2,1)S(1)}, u32[]{:S(2)}, u32[]{:S(2)}) collective-permute-start(bf16[2,2,80,512]{3,2,1,0:T(8,128)(2,1)S(1)} %pad_maximum_fusion.5), channel_id=1, source_target_pairs={{0,2},{2,0},{4,6},{6,4},{8,10},{10,8},{12,14},{14,12},{1,3},{3,1},... | collective-permute-start | bytes 983048 | tf_op jit(solution)/shard_map/ppermute | solution.py:43

commit v2 on v0

v2 whole, which is shorter than its diff:
```python
import functools
import math

import jax
import jax.numpy as jnp
from jax import lax
from jax.experimental import pallas as pl
from jax.experimental.pallas import tpu as pltpu
from jax.sharding import PartitionSpec as P

D = 3840
HQ = 32
KVH = 4
HD = 128
STEPS = 8
UPDATES = 20


beta_first = 0.9
beta_second = 0.95
learn_rate = 0.02
decay_rate = 0.1
adam_epsilon = 1e-08

unit_scale = 1.0 / math.sqrt(D)
MASKED = -1e30
VMEM = pl.BlockSpec(memory_space=pltpu.VMEM)
SMEM = pl.BlockSpec(memory_space=pltpu.SMEM)
SMALL = pltpu.CompilerParams(vmem_limit_bytes=16 * 1024 * 1024)


def tied(*values):
    return lax.optimization_barrier(values)


def swap(value, axis, bit):
    size = lax.axis_size(axis)
    return lax.ppermute(value, axis, [(i, i ^ (1 << bit)) for i in range(size)])


def bit_of(axis, bit):
    return (lax.axis_index(axis) >> bit) & 1


def halves(value, axis, bit, at):
    mine = bit_of(axis, bit)
    keep = lax.dynamic_index_in_dim(value, mine, at, keepdims=False)
    give = lax.dynamic_index_in_dim(value, 1 - mine, at, keepdims=False)
    return keep, give


def joined(held, other, axis, bit, at):
    mine = bit_of(axis, bit)
    low = jnp.where(mine == 0, held, other)
    high = jnp.where(mine == 0, other, held)
    return jnp.stack([low, high], axis=at)


def split_bits(value, bits):
    return value.reshape((2,) * bits + value.shape[1:])


def owner_with(bit, value, index):
    return ((index >> bit) << (bit + 1)) | (value << bit) | (index & ((1 << bit) - 1))


def gradient_kernel(cuts, size, where_ref, hidden_ref, cot_ref, *refs):
    outs, total = refs[:-1], refs[-1]
    rows = hidden_ref.shape[1]
    owned = rows // size
    step = 384 if rows % 384 == 0 else rows
    for at in range(0, rows, step):
        total[at : at + step, :] = unit_scale * lax.dot_general(
            hidden_ref[:, at : at + step],
            cot_ref[...],
            (((0,), (0,)), ((), ())),
            preferred_element_type=jnp.float32,
        )
    here = where_ref[0]
    for c, (start, width, bit) in enumerate(cuts):
        mine = (here >> bit) & 1
        for index in range(size // 2):
            keep = pl.multiple_of(owner_with(bit, mine, index) * owned, 16)
            give = pl.multiple_of(owner_with(bit, 1 - mine, index) * owned, 16)
            outs[2 * c][index] = total[pl.ds(keep, owned), start : start + width]
            outs[2 * c + 1][index] = total[pl.ds(give, owned), start : start + width].astype(
                jnp.bfloat16
            )


def gradient_parts(hidden, cot, cuts, size):
    rows = hidden.shape[1]
    owned = rows // size
    here = lax.axis_index("fsdp")
    if owned % 16 == 0:
        shapes = []
        for _, width, _ in cuts:
            shapes.append(jax.ShapeDtypeStruct((size // 2, owned, width), jnp.float32))
            shapes.append(jax.ShapeDtypeStruct((size // 2, owned, width), jnp.bfloat16))
        outs = pl.pallas_call(
            functools.partial(gradient_kernel, cuts, size),
            out_shape=shapes,
            in_specs=[SMEM, VMEM, VMEM],
            out_specs=[VMEM] * len(shapes),
            scratch_shapes=[pltpu.VMEM((rows, cot.shape[1]), jnp.float32)],
            compiler_params=pltpu.CompilerParams(vmem_limit_bytes=24 * 1024 * 1024),
            cost_estimate=pl.CostEstimate(
                flops=2 * rows * cot.size,
                bytes_accessed=2 * (hidden.size + cot.size) + 6 * rows * cot.shape[1],
                transcendentals=0,
            ),
        )(here.astype(jnp.int32).reshape(1), hidden, cot)
        return [(outs[2 * c], outs[2 * c + 1]) for c in range(len(cuts))]
    product = unit_scale * lax.dot_general(
        hidden, cot, (((0,), (0,)), ((), ())), preferred_element_type=jnp.float32
    )
    product = product.reshape(size, owned, -1)
    bits = size.bit_length() - 1
    parts = []
    for start, width, bit in cuts:
        cut = split_bits(product[:, :, start : start + width], bits)
        keep, give = halves(cut, "fsdp", bit, bits - 1 - bit)
        parts.append(
            (
                keep.reshape(size // 2, owned, width),
                give.astype(jnp.bfloat16).reshape(size // 2, owned, width),
            )
        )
    return parts


def rows_kernel(slices, here_ref, hidden_ref, out_ref):
    size, _, owned = out_ref.shape
    for half in range(slices):

        @pl.when(here_ref[0] == half)
        def _():
            for index in range(size):
                at = (half * size + index) * owned
                out_ref[index] = hidden_ref[:, at : at + owned]


def rows_by_owner(hidden, slices, size):
    tokens, width = hidden.shape
    owned = width // slices // size
    if owned % 16 != 0:
        cut = hidden.reshape(tokens, slices, size, owned)
        cut = lax.dynamic_index_in_dim(cut, lax.axis_index("tp"), 1, keepdims=False)
        return cut.transpose(1, 0, 2)
    return pl.pallas_call(
        functools.partial(rows_kernel, slices),
        out_shape=jax.ShapeDtypeStruct((size, tokens, owned), hidden.dtype),
        in_specs=[SMEM, VMEM],
        out_specs=VMEM,
        compiler_params=SMALL,
    )(lax.axis_index("tp").astype(jnp.int32).reshape(1), hidden)


def stacked_heads(query, head, group):
    return jnp.concatenate(
        [query[:, (head * group + g) * HD : (head * group + g + 1) * HD] for g in range(group)],
        axis=0,
    )


def contract_last(left, right):
    return lax.dot_general(
        left, right, (((1,), (1,)), ((), ())), preferred_element_type=jnp.float32
    )


def cache_kernel(
    length_ref, query_ref, keys_ref, values_ref, gate_ref, largest_ref, total_ref, blend_ref
):
    group = HQ // KVH
    rows, span, width = keys_ref.shape
    for r in range(rows):
        for head in range(width // HD):
            lanes = slice(head * HD, (head + 1) * HD)
            queries = stacked_heads(query_ref[r], head, group)
            scores = contract_last(queries, keys_ref[r, :, lanes]) / math.sqrt(HD)
            position = lax.broadcasted_iota(jnp.int32, scores.shape, 1)
            scores = jnp.where(position < length_ref[r], scores, jnp.float32(MASKED))
            largest = jnp.max(scores, axis=1, keepdims=True)
            exponents = jnp.exp(scores - largest)
            total = jnp.sum(exponents, axis=1, keepdims=True)
            largest_ref[r, head] = jnp.broadcast_to(largest, (queries.shape[0], HD))
            total_ref[r, head] = jnp.broadcast_to(total, (queries.shape[0], HD))
            blend_ref[r, head] = jnp.dot(
                exponents.astype(jnp.bfloat16),
                values_ref[r, :, lanes],
                preferred_element_type=jnp.float32,
            )


def attend_cache(query, keys, values, lengths, gate):
    rows, steps, _ = query.shape
    heads = keys.shape[2] // HD
    shape = jax.ShapeDtypeStruct((rows, heads, steps * (HQ // KVH), HD), jnp.float32)
    return pl.pallas_call(
        cache_kernel,
        out_shape=[shape] * 3,
        in_specs=[SMEM, VMEM, VMEM, VMEM, pl.BlockSpec(memory_space=pl.ANY)],
        out_specs=[VMEM] * 3,
        compiler_params=SMALL,
        cost_estimate=pl.CostEstimate(
            flops=4 * rows * heads * steps * (HQ // KVH) * keys.shape[1] * HD,
            bytes_accessed=4 * keys.size,
            transcendentals=rows * heads * steps * (HQ // KVH) * keys.shape[1],
        ),
    )(lengths, query, keys, values, gate)


def fresh_kernel(
    query_ref, keep_ref, other_ref, values_ref, largest_ref, total_ref, blend_ref, keys_ref, out_ref
):
    group = HQ // KVH
    rows, steps, width = keys_ref.shape
    for r in range(rows):
        fresh = unit_scale * (keep_ref[r] + other_ref[r])
        fresh = fresh.astype(jnp.bfloat16)
        keys_ref[r] = fresh
        values = values_ref[r].astype(jnp.float32)
        for head in range(width // HD):
            lanes = slice(head * HD, (head + 1) * HD)
            queries = stacked_heads(query_ref[r], head, group).astype(jnp.float32)
            keys = fresh[:, lanes].astype(jnp.float32)
            step = lax.broadcasted_iota(jnp.int32, (group * steps, 1), 0) % steps
            scores = []
            for s in range(steps):
                score = jnp.sum(queries * keys[s : s + 1], axis=1, keepdims=True) / math.sqrt(HD)
                scores.append(jnp.where(step >= s, score, jnp.float32(MASKED)))
            largest_old = largest_ref[r, head][:, :1]
            largest = functools.reduce(jnp.maximum, scores, largest_old)
            rescale = jnp.exp(largest_old - largest)
            total = rescale * total_ref[r, head][:, :1]
            blend = rescale * blend_ref[r, head]
            for s in range(steps):
                exponent = jnp.exp(scores[s] - largest)
                total = total + exponent
                blend = blend + exponent * values[s : s + 1, lanes]
            result = (blend / total).astype(jnp.bfloat16)
            for g in range(group):
                at = (head * group + g) * HD
                out_ref[r, :, at : at + HD] = result[g * steps : (g + 1) * steps]


def attend_fresh(query, keep, other, values, cached):
    rows, steps, width = values.shape
    return pl.pallas_call(
        fresh_kernel,
        out_shape=[
            jax.ShapeDtypeStruct((rows, steps, width), jnp.bfloat16),
            jax.ShapeDtypeStruct(query.shape, jnp.bfloat16),
        ],
        in_specs=[VMEM] * 7,
        out_specs=[VMEM] * 2,
        compiler_params=SMALL,
    )(query, keep, other, values, *cached)


def sum_kernel(here_ref, *refs):
    cuts, grad_ref, square_ref = refs[:-2], refs[-2], refs[-1]
    pieces = [cuts[2 * c][...] + cuts[2 * c + 1][...].astype(jnp.float32) for c in range(3)]
    own = jnp.concatenate(pieces[:2], axis=1)
    far = pieces[2]
    half = own.shape[1]

    @pl.when(here_ref[0] == 0)
    def _():
        grad_ref[:, :half] = own
        grad_ref[:, half:] = far

    @pl.when(here_ref[0] != 0)
    def _():
        grad_ref[:, :half] = far
        grad_ref[:, half:] = own

    square = jnp.sum(own * own + far * far)
    square_ref[...] = jnp.full(square_ref.shape, square, jnp.float32)


def summed(pairs):
    rows = pairs[0][0].shape[0]
    width = sum(keep.shape[1] for keep, _ in pairs)
    flat = [a for pair in pairs for a in pair]
    return pl.pallas_call(
        sum_kernel,
        out_shape=[
            jax.ShapeDtypeStruct((rows, width), jnp.float32),
            jax.ShapeDtypeStruct((8, 128), jnp.float32),
        ],
        in_specs=[SMEM] + [VMEM] * len(flat),
        out_specs=[VMEM] * 2,
        compiler_params=SMALL,
    )(lax.axis_index("tp").astype(jnp.int32).reshape(1), *flat)


def adamw(factor, grad, master, first, second):
    clipped = factor * grad
    first_new = beta_first * first + (1.0 - beta_first) * clipped
    second_new = beta_second * second + (1.0 - beta_second) * clipped * clipped
    first_hat = first_new / (1.0 - beta_first**UPDATES)
    second_hat = second_new / (1.0 - beta_second**UPDATES)
    master_new = master - learn_rate * (
        first_hat / (jnp.sqrt(second_hat) + adam_epsilon) + decay_rate * master
    )
    return master_new, first_new, second_new


def project_kernel(limit, square_ref, other_ref, grad_ref, master_ref, first_ref, second_ref, hidden_ref, out_ref):
    square = square_ref[:1, :1] + other_ref[:1, :1]
    factor = jnp.minimum(1.0, limit / jnp.sqrt(square))
    relay = adamw(factor, grad_ref[...], master_ref[...], first_ref[...], second_ref[...])[0]
    out_ref[...] = jnp.dot(
        hidden_ref[...], relay.astype(jnp.bfloat16), preferred_element_type=jnp.float32
    )


def project(limit, square, other, grad, master, first, second, hidden):
    return pl.pallas_call(
        functools.partial(project_kernel, limit),
        out_shape=jax.ShapeDtypeStruct((hidden.shape[0], master.shape[1]), jnp.float32),
        in_specs=[VMEM] * 7,
        out_specs=VMEM,
        compiler_params=SMALL,
    )(square, other, grad, master, first, second, hidden)


def bit_orders(bits):
    if bits == 3:
        return [[2, 0, 1], [1, 2, 0], [0, 1, 2]]
    return [[(c * max(1, bits // 3) + s) % bits for s in range(bits)] for c in range(3)]


def exchange_blocks(parts, axis):
    bits = parts.shape[0].bit_length() - 1
    held = split_bits(parts, bits)
    for bit in range(bits):
        at = bits - 1 - bit
        keep, give = halves(held, axis, bit, at)
        held = joined(keep, swap(give, axis, bit), axis, bit, at)
    return held.reshape(parts.shape)


def shards(
    learn_hidden,
    learn_grad_out,
    key_master,
    key_first,
    key_second,
    rollout_hidden,
    query_base,
    cache_keys,
    cache_values,
    new_values,
    cache_lengths,
):
    size = lax.axis_size("fsdp")
    slice_count = lax.axis_size("tp")
    bits = size.bit_length() - 1
    owned, width_all = key_master.shape
    column_count = width_all // slice_count
    row_count, steps, _ = rollout_hidden.shape
    orders = bit_orders(bits)
    tp_here = lax.axis_index("tp")

    other_cot = swap(learn_grad_out, "tp", 0)
    near = column_count // 2
    parts = gradient_parts(
        learn_hidden, learn_grad_out, [(0, near, orders[0][0]), (near, near, orders[1][0])], size
    )
    parts += gradient_parts(learn_hidden, other_cot, [(0, column_count, orders[2][0])], size)
    held = [keep for keep, _ in parts]
    sent = [swap(give, "fsdp", orders[c][0]) for c, (_, give) in enumerate(parts)]
    cached = attend_cache(query_base, cache_keys, cache_values, cache_lengths, held[2])

    held[2], gated_master, gated_hidden = tied(held[2], key_master, rollout_hidden)
    weight_cast = gated_master.astype(jnp.bfloat16)
    mine = jnp.where(tp_here == 0, weight_cast[:, :column_count], weight_cast[:, column_count:])
    far = jnp.where(tp_here == 0, weight_cast[:, column_count:], weight_cast[:, :column_count])
    blocks = [mine[:, :near], mine[:, near:], far]
    have = [[], [], []]

    def gather_stage(c):
        bit = orders[c][bits - 1 - len(have[c])]
        at = sum(1 for b in have[c] if b > bit)
        have[c].append(bit)
        blocks[c] = joined(blocks[c], swap(blocks[c], "fsdp", bit), "fsdp", bit, at)

    for c in range(3):
        gather_stage(c)

    left = [[b for b in range(bits - 1, -1, -1) if b != order[0]] for order in orders]
    for stage in range(1, bits):
        for c in range(3):
            bit = orders[c][stage]
            at = left[c].index(bit)
            left[c].remove(bit)
            whole = held[c] + sent[c].astype(jnp.float32)
            whole = whole.reshape((2,) * (len(left[c]) + 1) + (owned, whole.shape[-1]))
            held[c], give = halves(whole, "fsdp", bit, at)
            sent[c] = swap(give.astype(jnp.bfloat16), "fsdp", bit)
        if stage < bits - 1:
            for c in range(3):
                held[c], blocks[c] = tied(held[c], blocks[c])
                gather_stage(c)
    grad_weight, square = summed(
        [(held[c].reshape(owned, -1), sent[c].reshape(owned, -1)) for c in range(3)]
    )

    by_owner = rows_by_owner(gated_hidden.reshape(row_count * steps, -1), slice_count, size)
    rows = split_bits(by_owner, bits)
    square = square + swap(square, "tp", 0)
    for bit in range(bits):
        at = bits - 1 - bit
        keep, give = halves(rows, "fsdp", bit, at)
        give, square = tied(give, square)
        other, come = tied(swap(square, "fsdp", bit), swap(give, "fsdp", bit))
        rows = joined(keep, come, "fsdp", bit, at)
        if bit == 0:
            for c in range(3):
                if orders[c][0] == 0:
                    other, blocks[c] = tied(other, blocks[c])
                    gather_stage(c)
        if bit < bits - 1:
            square = square + other
    for c in range(3):
        if orders[c][0] != 0:
            other, blocks[c] = tied(other, blocks[c])
            gather_stage(c)
    hidden_rows = rows.reshape(size * row_count * steps, owned)
    limit = math.sqrt(learn_hidden.shape[0] * size * width_all)
    projected = project(
        limit, square, other, grad_weight, key_master, key_first, key_second, hidden_rows
    )

    projected = split_bits(projected.reshape(size, row_count * steps, width_all), bits)
    left = list(range(bits - 1, -1, -1))
    for bit in range(bits):
        at = left.index(bit)
        left.remove(bit)
        keep, give = halves(projected, "fsdp", bit, at)
        for c in range(3):
            if orders[c][0] == bit:
                give, blocks[c] = tied(give, blocks[c])
        other_keys = swap(give, "fsdp", bit)
        if bit == 0:
            other_keys, gated_grad = tied(other_keys, grad_weight)
            projected = keep + other_keys
            projected = projected.reshape((-1, slice_count, column_count))
            keep, give = halves(projected, "tp", 0, 1)
            projected = keep + swap(give, "tp", 0)
            projected = projected.reshape((2,) * len(left) + (row_count * steps, column_count))
        else:
            projected = keep + other_keys
    shape = (row_count, steps, column_count)
    step_keys, attention = attend_fresh(
        query_base, keep.reshape(shape), other_keys.reshape(shape), new_values, cached
    )

    total = square[:1, :1] + other[:1, :1]
    factor = jnp.minimum(1.0, limit / jnp.sqrt(total))
    key_new, key_first_new, key_second_new = adamw(
        factor, gated_grad, key_master, key_first, key_second
    )

    blocks = [b.reshape(size * owned, -1) for b in blocks]
    grad_in = contract_last(learn_grad_out, jnp.concatenate(blocks[:2], axis=1))
    grad_in = grad_in + contract_last(other_cot, blocks[2])
    grad_in = (unit_scale * grad_in).astype(jnp.bfloat16)
    return (grad_in, key_new, key_first_new, key_second_new, step_keys, attention)


def solution(mesh):
    in_specs = (
        P(("grp", "fsdp"), "tp"),
        P(("grp", "fsdp"), "tp"),
        P(("grp", "tp", "fsdp"), None),
        P(("grp", "tp", "fsdp"), None),
        P(("grp", "tp", "fsdp"), None),
        P(("grp", "fsdp"), None, None),
        P(("grp", "fsdp"), None, "tp"),
        P(("grp", "fsdp"), None, "tp"),
        P(("grp", "fsdp"), None, "tp"),
        P(("grp", "fsdp"), None, "tp"),
        P(("grp", "fsdp")),
    )
    out_specs = (
        P(("grp", "fsdp"), "tp"),
        P(("grp", "tp", "fsdp"), None),
        P(("grp", "tp", "fsdp"), None),
        P(("grp", "tp", "fsdp"), None),
        P(("grp", "fsdp"), None, "tp"),
        P(("grp", "fsdp"), None, "tp"),
    )
    return jax.shard_map(shards, mesh=mesh, in_specs=in_specs, out_specs=out_specs, check_vma=False)
```

time: 245 us -> 100 us (0.41)
  waiting for transfers between devices: 177 us -> 43.9 us
  blocking collectives: 35.3 us -> 0 us
  starting transfers between devices: 0.12 us -> 32.5 us
  between operations: 15.2 us -> 3.25 us
  matrix products: 7.78 us -> 1.4 us
  Pallas kernels: 0 us -> 5.29 us
    all_gather x2 -> x0, waiting for transfers between devices: 88.8 us -> none  [the longest x1 46.8 us: shards(): every_row = lax.all_gather(relay_cast, ('fsdp', 'tp'), axis=0, tiled=True)]
    reduce_scatter x1 -> x0, waiting for transfers between devices: 87.1 us -> none  [shards(): lax.psum_scatter(unit_scale * contract_rows(learn_hidden, cotangent), 'fs...]
    ppermute x0 -> x30, waiting for transfers between devices: none -> 43.9 us  [swap(): return lax.ppermute(value, axis, [(i, i ^ 1 << bit) for i in range(size)])]
    psum x1 -> x0, blocking collectives: 32.7 us -> none  [shards(): square_sum = lax.psum(jnp.sum(grad_weight * grad_weight), ('fsdp', 'tp'))]
    ppermute x0 -> x30, starting transfers between devices: none -> 32.5 us  [swap(): return lax.ppermute(value, axis, [(i, i ^ 1 << bit) for i in range(size)])]
    dot_general x5 -> x2, matrix products: 7.78 us -> 1.4 us  [contract_last(): lax.dot_general(left, right, (((1,), (1,)), ((), ())), preferred_element_...]
    pallas_call x0 -> x7, Pallas kernels: none -> 5.29 us  [the longest x2 2.53 us: gradient_parts(): pl.pallas_call(functools.partial(gradient_kernel, cuts, size), out_shape=...]
    unnamed x21 -> x28, local copies, waits for them, and re-layouts: 0.91 us -> 5.83 us
  transfers between devices with their start and end apart: 3 -> 30, of which waited for: 3 -> 16; matrix products, arithmetic and copies ran while one was open for 2% -> 11% of each run, Pallas kernels for 0% -> 4%
where the time goes in v2:
time: 100 us; the launch traced here: 99.7 us
  waiting for transfers between devices  43.9 us (44%)
  starting transfers between devices  32.5 us (32%)
  local copies, waits for them, and re-layouts  7.4 us (7%)
  other arithmetic  5.98 us (6%)
  Pallas kernels  5.29 us (5%)
  between operations  3.25 us (3%)
  matrix products  1.4 us (1%)
    ppermute x30, waiting for transfers between devices, swap(): return lax.ppermute(value, axis, [(i, i ^ 1 << bit) for i in range(size)])  43.9 us
    ppermute x30, starting transfers between devices, swap(): return lax.ppermute(value, axis, [(i, i ^ 1 << bit) for i in range(size)])  32.5 us
    unnamed x28, local copies, waits for them, and re-layouts  5.83 us
    another operation x21, other arithmetic, joined(): return jnp.stack([low, high], axis=at)  3.28 us
    pallas_call x2, Pallas kernels, gradient_parts(): pl.pallas_call(functools.partial(gradient_kernel, cuts, size), out_shape=...  2.53 us
  transfers between devices with their start and end apart: 30, of which 16 were waited for; matrix products, arithmetic and copies ran while one was open for 11% of the time, Pallas kernels for 4%

profile of v2, /device:TPU:0, one launch (start us, length us, event | category | flops | bytes accessed | tf_op | source)
XLA Modules:
  0.0 99.7 jit_solution(17178008623907305926)
XLA Ops:
  1.2 1.4 %copy-done = bf16[384,1920]{1,0:T(8,128)(2,1)S(1)} copy-done((bf16[384,1920]{1,0:T(8,128)(2,1)S(1)}, bf16[384,1920]{1,0:T(8,128)(2,1)}, u32[]{:S(2)}) %copy-start) | copy-done | bytes 1474584
  2.5 0.9 copy-done.5
  3.5 1.6 %shard_map.156 = (f32[4,240,128]{2,1,0:T(8,128)S(1)}, bf16[4,240,128]{2,1,0:T(8,128)(2,1)}, f32[4,240,128]{2,1,0:T(8,128)S(1)}, bf16[4,240,128]{2,1,0:T(8,128)(2,1)S(1)}) custom-call(s32[1]{0:T(128)} %bitcast.1.where_ref, bf16[384,1920]{1,0:T(8,128)(2,1)S(1)} %copy-done, bf16[384,256]{1,0:T(8,128)(2,1)S(1)} %copy-done.5), custom_call_target="tpu_custom_call" | custom-call | flops 377487360 | bytes 4620288 | tf_op jit(solution)/shard_map/pallas_call | solution.py:100
  5.1 3.6 %collective-permute-start.1 = (bf16[4,240,128]{2,1,0:T(8,128)(2,1)}, bf16[4,240,128]{2,1,0:T(8,128)(2,1)}, u32[]{:S(2)}, u32[]{:S(2)}) collective-permute-start(bf16[4,240,128]{2,1,0:T(8,128)(2,1)} %get-tuple-element.57), channel_id=1, source_target_pairs={{0,8},{2,10},{4,12},{6,14},{8,0},{10,2},{12,4},{14,6},{1,9},{3,11}... | collective-permute-start | bytes 737288 | tf_op jit(solution)/shard_map/ppermute | solution.py:38
  8.7 1.6 %collective-permute-start.5 = (bf16[4,240,128]{2,1,0:T(8,128)(2,1)S(1)}, bf16[4,240,128]{2,1,0:T(8,128)(2,1)S(1)}, u32[]{:S(2)}, u32[]{:S(2)}) collective-permute-start(bf16[4,240,128]{2,1,0:T(8,128)(2,1)S(1)} %get-tuple-element.61), channel_id=1, source_target_pairs={{0,4},{2,6},{4,0},{6,2},{8,12},{10,14},{12,8},{14,10},{1,5},{3,7},... | collective-permute-start | bytes 737288 | tf_op jit(solution)/shard_map/ppermute | solution.py:38
  11.0 1.4 %copy-done.1 = bf16[384,1920]{1,0:T(8,128)(2,1)S(1)} copy-done((bf16[384,1920]{1,0:T(8,128)(2,1)S(1)}, bf16[384,1920]{1,0:T(8,128)(2,1)}, u32[]{:S(2)}) %copy-start.1) | copy-done | bytes 1474584
  12.3 0.9 shard_map.154
  13.3 1.6 %collective-permute-start.6 = (bf16[240,128]{1,0:T(8,128)(2,1)S(1)}, bf16[240,128]{1,0:T(8,128)(2,1)S(1)}, u32[]{:S(2)}, u32[]{:S(2)}) collective-permute-start(bf16[240,128]{1,0:T(8,128)(2,1)S(1)} %get-tuple-element.145), channel_id=1, source_target_pairs={{0,2},{2,0},{4,6},{6,4},{8,10},{10,8},{12,14},{14,12},{1,3},{3,1},... | collective-permute-start | bytes 184328 | tf_op jit(solution)/shard_map/ppermute | solution.py:38
  16.0 0.8 shard_map.159
  16.8 4.2 %collective-permute-done.1 = bf16[4,240,128]{2,1,0:T(8,128)(2,1)} collective-permute-done((bf16[4,240,128]{2,1,0:T(8,128)(2,1)}, bf16[4,240,128]{2,1,0:T(8,128)(2,1)}, u32[]{:S(2)}, u32[]{:S(2)}) %collective-permute-start.1) | collective-permute-done | bytes 245792 | tf_op jit(solution)/shard_map/ppermute | solution.py:38
  21.0 1.0 convert_add_fusion.3
  22.1 1.6 %collective-permute-start.3 = (bf16[2,240,128]{2,1,0:T(8,128)(2,1)S(1)}, bf16[2,240,128]{2,1,0:T(8,128)(2,1)S(1)}, u32[]{:S(2)}, u32[]{:S(2)}) collective-permute-start(bf16[2,240,128]{2,1,0:T(8,128)(2,1)S(1)} %fusion.11), channel_id=1, source_target_pairs={{0,2},{2,0},{4,6},{6,4},{8,10},{10,8},{12,14},{14,12},{1,3},{3,1},... | collective-permute-start | bytes 368648 | tf_op jit(solution)/shard_map/ppermute | solution.py:38
  23.8 3.0 %collective-permute-start.7 = (bf16[2,240,128]{2,1,0:T(8,128)(2,1)S(1)}, bf16[2,240,128]{2,1,0:T(8,128)(2,1)S(1)}, u32[]{:S(2)}, u32[]{:S(2)}) collective-permute-start(bf16[2,240,128]{2,1,0:T(8,128)(2,1)S(1)} %fusion.9), channel_id=1, source_target_pairs={{0,8},{2,10},{4,12},{6,14},{8,0},{10,2},{12,4},{14,6},{1,9},{3,11}... | collective-permute-start | bytes 368648 | tf_op jit(solution)/shard_map/ppermute | solution.py:38
  26.9 0.5 collective-permute-start.21
  27.4 7.3 %collective-permute-done.10 = bf16[240,256]{1,0:T(8,128)(2,1)S(1)} collective-permute-done((bf16[240,256]{1,0:T(8,128)(2,1)S(1)}, bf16[240,256]{1,0:T(8,128)(2,1)S(1)}, u32[]{:S(2)}, u32[]{:S(2)}) %collective-permute-start.10) | collective-permute-done | bytes 122912 | tf_op jit(solution)/shard_map/ppermute | solution.py:38
  34.8 1.4 %collective-permute-start.4 = (bf16[240,128]{1,0:T(8,128)(2,1)S(1)}, bf16[240,128]{1,0:T(8,128)(2,1)S(1)}, u32[]{:S(2)}, u32[]{:S(2)}) collective-permute-start(bf16[240,128]{1,0:T(8,128)(2,1)S(1)} %fusion.12), channel_id=1, source_target_pairs={{0,4},{2,6},{4,0},{6,2},{8,12},{10,14},{12,8},{14,10},{1,5},{3,7},... | collective-permute-start | bytes 184328 | tf_op jit(solution)/shard_map/ppermute | solution.py:38
  36.2 2.5 %collective-permute-done.7 = bf16[2,240,128]{2,1,0:T(8,128)(2,1)S(1)} collective-permute-done((bf16[2,240,128]{2,1,0:T(8,128)(2,1)S(1)}, bf16[2,240,128]{2,1,0:T(8,128)(2,1)S(1)}, u32[]{:S(2)}, u32[]{:S(2)}) %collective-permute-start.7) | collective-permute-done | bytes 122912 | tf_op jit(solution)/shard_map/ppermute | solution.py:38
  38.7 1.7 %collective-permute-start.8 = (bf16[240,128]{1,0:T(8,128)(2,1)S(1)}, bf16[240,128]{1,0:T(8,128)(2,1)S(1)}, u32[]{:S(2)}, u32[]{:S(2)}) collective-permute-start(bf16[240,128]{1,0:T(8,128)(2,1)S(1)} %fusion.13), channel_id=1, source_target_pairs={{0,2},{2,0},{4,6},{6,4},{8,10},{10,8},{12,14},{14,12},{1,3},{3,1},... | collective-permute-start | bytes 184328 | tf_op jit(solution)/shard_map/ppermute | solution.py:38
  40.8 2.1 %collective-permute-start.16 = (bf16[2,240,256]{2,1,0:T(8,128)(2,1)S(1)}, bf16[2,240,256]{2,1,0:T(8,128)(2,1)S(1)}, u32[]{:S(2)}, u32[]{:S(2)}) collective-permute-start(bf16[2,240,256]{2,1,0:T(8,128)(2,1)S(1)} %pad_maximum_fusion.4), channel_id=1, source_target_pairs={{0,4},{2,6},{4,0},{6,2},{8,12},{10,14},{12,8},{14,10},{1,5},{3,7},... | collective-permute-start | bytes 737288 | tf_op jit(solution)/shard_map/ppermute | solution.py:38
  42.8 7.2 %collective-permute-done.11 = bf16[2,240,256]{2,1,0:T(8,128)(2,1)S(1)} collective-permute-done((bf16[2,240,256]{2,1,0:T(8,128)(2,1)S(1)}, bf16[2,240,256]{2,1,0:T(8,128)(2,1)S(1)}, u32[]{:S(2)}, u32[]{:S(2)}) %collective-permute-start.11) | collective-permute-done | bytes 245792 | tf_op jit(solution)/shard_map/ppermute | solution.py:38
  50.3 6.0 %collective-permute-done.12.refs_5_ = bf16[240,256]{1,0:T(8,128)(2,1)S(1)} collective-permute-done((bf16[240,256]{1,0:T(8,128)(2,1)S(1)}, bf16[240,256]{1,0:T(8,128)(2,1)S(1)}, u32[]{:S(2)}, u32[]{:S(2)}) %collective-permute-start.12) | collective-permute-done | bytes 122912 | tf_op jit(solution)/shard_map/ppermute | solution.py:38
  56.7 1.1 %collective-permute-done.13 = f32[8,128]{1,0:T(8,128)S(1)} collective-permute-done((f32[8,128]{1,0:T(8,128)S(1)}, f32[8,128]{1,0:T(8,128)S(1)}, u32[]{:S(2)}, u32[]{:S(2)}) %collective-permute-start.13) | collective-permute-done | bytes 4128 | tf_op jit(solution)/shard_map/ppermute | solution.py:38
  57.8 0.6 collective-permute-start.14
  58.4 1.4 %collective-permute-start.15 = (bf16[2,2,8,240]{3,2,1,0:T(8,128)(2,1)S(1)}, bf16[2,2,8,240]{3,2,1,0:T(8,128)(2,1)S(1)}, u32[]{:S(2)}, u32[]{:S(2)}) collective-permute-start(bf16[2,2,8,240]{3,2,1,0:T(8,128)(2,1)S(1)} %dynamic-slice_bitcast_fusion.8), channel_id=1, source_target_pairs={{0,2},{2,0},{4,6},{6,4},{8,10},{10,8},{12,14},{14,12},{1,3},{3,1},... | collective-permute-start | bytes 46088 | tf_op jit(solution)/shard_map/ppermute | solution.py:38
  59.9 1.5 %collective-permute-done.14 = f32[8,128]{1,0:T(8,128)S(1)} collective-permute-done((f32[8,128]{1,0:T(8,128)S(1)}, f32[8,128]{1,0:T(8,128)S(1)}, u32[]{:S(2)}, u32[]{:S(2)}) %collective-permute-start.14) | collective-permute-done | bytes 4128 | tf_op jit(solution)/shard_map/ppermute | solution.py:38
  61.4 0.7 collective-permute-done.15
  62.2 2.0 %collective-permute-start.18 = (bf16[2,2,8,240]{3,2,1,0:T(8,128)(2,1)S(1)}, bf16[2,2,8,240]{3,2,1,0:T(8,128)(2,1)S(1)}, u32[]{:S(2)}, u32[]{:S(2)}) collective-permute-start(bf16[2,2,8,240]{3,2,1,0:T(8,128)(2,1)S(1)} %bitcast.167), channel_id=1, source_target_pairs={{0,4},{2,6},{4,0},{6,2},{8,12},{10,14},{12,8},{14,10},{1,5},{3,7},... | collective-permute-start | bytes 46088 | tf_op jit(solution)/shard_map/ppermute | solution.py:38
  64.3 1.6 %collective-permute-done.17 = f32[8,128]{1,0:T(8,128)S(1)} collective-permute-done((f32[8,128]{1,0:T(8,128)S(1)}, f32[8,128]{1,0:T(8,128)S(1)}, u32[]{:S(2)}, u32[]{:S(2)}) %collective-permute-start.17) | collective-permute-done | bytes 4128 | tf_op jit(solution)/shard_map/ppermute | solution.py:38
  66.1 2.0 %collective-permute-start.19 = (f32[8,128]{1,0:T(8,128)S(1)}, f32[8,128]{1,0:T(8,128)S(1)}, u32[]{:S(2)}, u32[]{:S(2)}) collective-permute-start(f32[8,128]{1,0:T(8,128)S(1)} %add.130.square_ref), channel_id=1, source_target_pairs={{0,8},{2,10},{4,12},{6,14},{8,0},{10,2},{12,4},{14,6},{1,9},{3,11}... | collective-permute-start | bytes 12296 | tf_op jit(solution)/shard_map/ppermute | solution.py:38
  68.0 1.0 %collective-permute-start.20 = (bf16[2,2,8,240]{3,2,1,0:T(8,128)(2,1)S(1)}, bf16[2,2,8,240]{3,2,1,0:T(8,128)(2,1)S(1)}, u32[]{:S(2)}, u32[]{:S(2)}) collective-permute-start(bf16[2,2,8,240]{3,2,1,0:T(8,128)(2,1)S(1)} %fusion.17), channel_id=1, source_target_pairs={{0,8},{2,10},{4,12},{6,14},{8,0},{10,2},{12,4},{14,6},{1,9},{3,11}... | collective-permute-start | bytes 46088 | tf_op jit(solution)/shard_map/ppermute | solution.py:38
  69.1 1.5 %collective-permute-start.23 = (bf16[2,2,240,256]{3,2,0,1:T(8,128)(2,1)S(1)}, bf16[2,2,240,256]{3,2,0,1:T(8,128)(2,1)S(1)}, u32[]{:S(2)}, u32[]{:S(2)}) collective-permute-start(bf16[2,2,240,256]{3,2,0,1:T(8,128)(2,1)S(1)} %pad_maximum_fusion.1), channel_id=1, source_target_pairs={{0,2},{2,0},{4,6},{6,4},{8,10},{10,8},{12,14},{14,12},{1,3},{3,1},... | collective-permute-start | bytes 1474568 | tf_op jit(solution)/shard_map/ppermute | solution.py:38
  71.1 1.7 %collective-permute-done.20 = bf16[2,2,8,240]{3,2,1,0:T(8,128)(2,1)S(1)} collective-permute-done((bf16[2,2,8,240]{3,2,1,0:T(8,128)(2,1)S(1)}, bf16[2,2,8,240]{3,2,1,0:T(8,128)(2,1)S(1)}, u32[]{:S(2)}, u32[]{:S(2)}) %collective-permute-start.20) | collective-permute-done | bytes 15392 | tf_op jit(solution)/shard_map/ppermute | solution.py:38
  73.1 3.0 %collective-permute-start.28 = (bf16[2,2,240,128]{3,2,1,0:T(8,128)(2,1)S(1)}, bf16[2,2,240,128]{3,2,1,0:T(8,128)(2,1)S(1)}, u32[]{:S(2)}, u32[]{:S(2)}) collective-permute-start(bf16[2,2,240,128]{3,2,1,0:T(8,128)(2,1)S(1)} %pad_maximum_fusion.5), channel_id=1, source_target_pairs={{0,8},{2,10},{4,12},{6,14},{8,0},{10,2},{12,4},{14,6},{1,9},{3,11}... | collective-permute-start | bytes 737288 | tf_op jit(solution)/shard_map/ppermute | solution.py:38
  77.9 0.6 shard_map.158
  78.5 3.1 %collective-permute-done.26 = bf16[2,2,240,128]{3,2,1,0:T(8,128)(2,1)S(1)} collective-permute-done((bf16[2,2,240,128]{3,2,1,0:T(8,128)(2,1)S(1)}, bf16[2,2,240,128]{3,2,1,0:T(8,128)(2,1)S(1)}, u32[]{:S(2)}, u32[]{:S(2)}) %collective-permute-start.26) | collective-permute-done | bytes 245792 | tf_op jit(solution)/shard_map/ppermute | solution.py:38
  81.7 1.8 %collective-permute-done.28 = bf16[2,2,240,128]{3,2,1,0:T(8,128)(2,1)S(1)} collective-permute-done((bf16[2,2,240,128]{3,2,1,0:T(8,128)(2,1)S(1)}, bf16[2,2,240,128]{3,2,1,0:T(8,128)(2,1)S(1)}, u32[]{:S(2)}, u32[]{:S(2)}) %collective-permute-start.28) | collective-permute-done | bytes 245792 | tf_op jit(solution)/shard_map/ppermute | solution.py:38
  83.4 0.8 select_bitcast_fusion.3
  84.4 1.1 %collective-permute-start.24 = (f32[2,2,8,512]{3,2,1,0:T(8,128)S(1)}, f32[2,2,8,512]{3,2,1,0:T(8,128)S(1)}, u32[]{:S(2)}, u32[]{:S(2)}) collective-permute-start(f32[2,2,8,512]{3,2,1,0:T(8,128)S(1)} %dynamic-slice_bitcast_fusion.6), channel_id=1, source_target_pairs={{0,2},{2,0},{4,6},{6,4},{8,10},{10,8},{12,14},{14,12},{1,3},{3,1},... | collective-permute-start | bytes 196616 | tf_op jit(solution)/shard_map/ppermute | solution.py:38
  85.5 0.8 pad_maximum_fusion.2
  86.3 2.4 %collective-permute-done.24 = f32[2,2,8,512]{3,2,1,0:T(8,128)S(1)} collective-permute-done((f32[2,2,8,512]{3,2,1,0:T(8,128)S(1)}, f32[2,2,8,512]{3,2,1,0:T(8,128)S(1)}, u32[]{:S(2)}, u32[]{:S(2)}) %collective-permute-start.24) | collective-permute-done | bytes 65568 | tf_op jit(solution)/shard_map/ppermute | solution.py:38
  89.0 1.1 %pad_maximum_fusion.3 = bf16[2,2,2,240,128]{4,3,2,1,0:T(8,128)(2,1)S(1)} fusion(bf16[1,2,2,240,128]{4,3,2,1,0:T(8,128)(2,1)} %get-tuple-element.126, bf16[1,2,2,240,128]{4,3,2,1,0:T(8,128)(2,1)} %get-tuple-element.125), kind=kLoop, calls=%fused_computation.14 | loop fusion | flops 245760 | bytes 983040 | tf_op jit(solution)/shard_map/stack | solution.py:56
  90.3 1.4 %multiply_subtract_fusion = (f32[240,512]{1,0:T(8,128)}, f32[240,512]{1,0:T(8,128)}, f32[240,512]{1,0:T(8,128)}) fusion(f32[240,512]{1,0:T(8,128)S(1)} %copy-done.2, f32[240,512]{1,0:T(8,128)S(1)} %get-tuple-element.95.grad_ref, f32[]{:T(128)} %bitcast.63, f32[240,512]{1,0:T(8,128)S(1)} %copy-done.3, f32[240,512]{1,0:T(8,128)S(1)} %copy-done.4), kind=kLoop, calls=%fused_computation.16 | loop fusion | flops 1966080 | bytes 3440644 | tf_op jit(solution)/shard_map/sub | solution.py:305
  91.7 2.3 %collective-permute-done.27 = f32[2,8,256]{2,1,0:T(8,128)S(1)} collective-permute-done((f32[2,8,256]{2,1,0:T(8,128)S(1)}, f32[2,8,256]{2,1,0:T(8,128)S(1)}, u32[]{:S(2)}, u32[]{:S(2)}) %collective-permute-start.27) | collective-permute-done | bytes 16416 | tf_op jit(solution)/shard_map/ppermute | solution.py:38
  94.0 0.7 collective-permute-start.29
  94.7 0.7 fusion.3
  95.4 0.7 fusion.2
  96.1 2.1 %copy.38 = bf16[384,1920]{1,0:T(8,128)(2,1)} copy(bf16[384,1920]{0,1:T(8,128)(2,1)S(1)} %fusion.2) | data formatting | bytes 2949120
  98.6 1.0 %shard_map.160 = (bf16[1,8,256]{2,1,0:T(8,128)(2,1)}, bf16[1,8,2048]{2,1,0:T(8,128)(2,1)}) custom-call(bf16[1,8,2048]{2,1,0:T(8,128)(2,1)S(1)} %copy-done.9, f32[1,8,256]{2,1,0:T(8,128)S(1)} %get-tuple-element.157.keep_ref, f32[1,8,256]{2,1,0:T(8,128)S(1)} %bitcast.154, bf16[1,8,256]{2,1,0:T(8,128)(2,1)S(1)} %copy-done.11, ...), custom_call_target="tpu_custom_call" | custom-call | tf_op jit(solution)/shard_map/pallas_call | solution.py:250
  (110 shorter events, 5.7 us)
Async XLA Ops:
  0.6 10.3 %collective-permute-start = (bf16[384,256]{1,0:T(8,128)(2,1)}, bf16[384,256]{1,0:T(8,128)(2,1)S(1)}, u32[]{:S(2)}, u32[]{:S(2)}) collective-permute-start(bf16[384,256]{1,0:T(8,128)(2,1)} %cot_ref.1), channel_id=1, source_target_pairs={{0,1},{1,0},{2,3},{3,2},{4,5},{5,4},{6,7},{7,6},{8,9},{9,8},{10,11... | collective-permute-start | bytes 589832 | tf_op jit(solution)/shard_map/ppermute | solution.py:38
  1.2 1.4 %copy-start = (bf16[384,1920]{1,0:T(8,128)(2,1)S(1)}, bf16[384,1920]{1,0:T(8,128)(2,1)}, u32[]{:S(2)}) copy-start(bf16[384,1920]{1,0:T(8,128)(2,1)} %hidden_ref.3) | copy-start | bytes 4423684
  2.5 0.9 copy-start.5
  3.5 9.8 %copy-start.2 = (f32[240,512]{1,0:T(8,128)S(1)}, f32[240,512]{1,0:T(8,128)}, u32[]{:S(2)}) copy-start(f32[240,512]{1,0:T(8,128)} %master_ref.1) | copy-start | bytes 1474564
  3.5 12.4 %copy-start.10 = (bf16[1,8,3840]{2,1,0:T(8,128)(2,1)S(1)}, bf16[1,8,3840]{2,1,0:T(8,128)(2,1)}, u32[]{:S(2)}) copy-start(bf16[1,8,3840]{2,1,0:T(8,128)(2,1)} %param.16) | copy-start | bytes 184324
  3.5 12.5 %copy-start.7 = (bf16[1,1024,256]{2,1,0:T(8,128)(2,1)S(1)}, bf16[1,1024,256]{2,1,0:T(8,128)(2,1)}, u32[]{:S(2)}) copy-start(bf16[1,1024,256]{2,1,0:T(8,128)(2,1)} %keys_ref.1) | copy-start | bytes 1572868
  3.5 12.5 %copy-start.8 = (bf16[1,1024,256]{2,1,0:T(8,128)(2,1)S(1)}, bf16[1,1024,256]{2,1,0:T(8,128)(2,1)}, u32[]{:S(2)}) copy-start(bf16[1,1024,256]{2,1,0:T(8,128)(2,1)} %values_ref.2) | copy-start | bytes 1572868
  3.5 12.5 %copy-start.9 = (bf16[1,8,2048]{2,1,0:T(8,128)(2,1)S(1)}, bf16[1,8,2048]{2,1,0:T(8,128)(2,1)}, u32[]{:S(2)}) copy-start(bf16[1,8,2048]{2,1,0:T(8,128)(2,1)} %query_ref.3) | copy-start | bytes 98308
  5.1 15.9 %collective-permute-start.1 = (bf16[4,240,128]{2,1,0:T(8,128)(2,1)}, bf16[4,240,128]{2,1,0:T(8,128)(2,1)}, u32[]{:S(2)}, u32[]{:S(2)}) collective-permute-start(bf16[4,240,128]{2,1,0:T(8,128)(2,1)} %get-tuple-element.57), channel_id=1, source_target_pairs={{0,8},{2,10},{4,12},{6,14},{8,0},{10,2},{12,4},{14,6},{1,9},{3,11}... | collective-permute-start | bytes 737288 | tf_op jit(solution)/shard_map/ppermute | solution.py:38
  8.7 13.4 %collective-permute-start.5 = (bf16[4,240,128]{2,1,0:T(8,128)(2,1)S(1)}, bf16[4,240,128]{2,1,0:T(8,128)(2,1)S(1)}, u32[]{:S(2)}, u32[]{:S(2)}) collective-permute-start(bf16[4,240,128]{2,1,0:T(8,128)(2,1)S(1)} %get-tuple-element.61), channel_id=1, source_target_pairs={{0,4},{2,6},{4,0},{6,2},{8,12},{10,14},{12,8},{14,10},{1,5},{3,7},... | collective-permute-start | bytes 737288 | tf_op jit(solution)/shard_map/ppermute | solution.py:38
  11.0 1.4 %copy-start.1 = (bf16[384,1920]{1,0:T(8,128)(2,1)S(1)}, bf16[384,1920]{1,0:T(8,128)(2,1)}, u32[]{:S(2)}) copy-start(bf16[384,1920]{1,0:T(8,128)(2,1)} %hidden_ref.3) | copy-start | bytes 4423684
  13.3 10.5 %collective-permute-start.6 = (bf16[240,128]{1,0:T(8,128)(2,1)S(1)}, bf16[240,128]{1,0:T(8,128)(2,1)S(1)}, u32[]{:S(2)}, u32[]{:S(2)}) collective-permute-start(bf16[240,128]{1,0:T(8,128)(2,1)S(1)} %get-tuple-element.145), channel_id=1, source_target_pairs={{0,2},{2,0},{4,6},{6,4},{8,10},{10,8},{12,14},{14,12},{1,3},{3,1},... | collective-permute-start | bytes 184328 | tf_op jit(solution)/shard_map/ppermute | solution.py:38
  14.9 11.9 %collective-permute-start.2 = (bf16[240,128]{1,0:T(8,128)(2,1)S(1)}, bf16[240,128]{1,0:T(8,128)(2,1)S(1)}, u32[]{:S(2)}, u32[]{:S(2)}) collective-permute-start(bf16[240,128]{1,0:T(8,128)(2,1)S(1)} %get-tuple-element.146), channel_id=1, source_target_pairs={{0,4},{2,6},{4,0},{6,2},{8,12},{10,14},{12,8},{14,10},{1,5},{3,7},... | collective-permute-start | bytes 184328 | tf_op jit(solution)/shard_map/ppermute | solution.py:38
  15.3 25.1 %collective-permute-start.9 = (bf16[4,240,256]{2,1,0:T(8,128)(2,1)S(1)}, bf16[4,240,256]{2,1,0:T(8,128)(2,1)S(1)}, u32[]{:S(2)}, u32[]{:S(2)}) collective-permute-start(bf16[4,240,256]{2,1,0:T(8,128)(2,1)S(1)} %get-tuple-element.64), channel_id=1, source_target_pairs={{0,2},{2,0},{4,6},{6,4},{8,10},{10,8},{12,14},{14,12},{1,3},{3,1},... | collective-permute-start | bytes 1474568 | tf_op jit(solution)/shard_map/ppermute | solution.py:38
  21.0 13.7 %collective-permute-start.10 = (bf16[240,256]{1,0:T(8,128)(2,1)S(1)}, bf16[240,256]{1,0:T(8,128)(2,1)S(1)}, u32[]{:S(2)}, u32[]{:S(2)}) collective-permute-start(bf16[240,256]{1,0:T(8,128)(2,1)S(1)} %get-tuple-element.137), channel_id=1, source_target_pairs={{0,8},{2,10},{4,12},{6,14},{8,0},{10,2},{12,4},{14,6},{1,9},{3,11}... | collective-permute-start | bytes 368648 | tf_op jit(solution)/shard_map/ppermute | solution.py:38
  22.1 12.7 %collective-permute-start.3 = (bf16[2,240,128]{2,1,0:T(8,128)(2,1)S(1)}, bf16[2,240,128]{2,1,0:T(8,128)(2,1)S(1)}, u32[]{:S(2)}, u32[]{:S(2)}) collective-permute-start(bf16[2,240,128]{2,1,0:T(8,128)(2,1)S(1)} %fusion.11), channel_id=1, source_target_pairs={{0,2},{2,0},{4,6},{6,4},{8,10},{10,8},{12,14},{14,12},{1,3},{3,1},... | collective-permute-start | bytes 368648 | tf_op jit(solution)/shard_map/ppermute | solution.py:38
  23.8 14.8 %collective-permute-start.7 = (bf16[2,240,128]{2,1,0:T(8,128)(2,1)S(1)}, bf16[2,240,128]{2,1,0:T(8,128)(2,1)S(1)}, u32[]{:S(2)}, u32[]{:S(2)}) collective-permute-start(bf16[2,240,128]{2,1,0:T(8,128)(2,1)S(1)} %fusion.9), channel_id=1, source_target_pairs={{0,8},{2,10},{4,12},{6,14},{8,0},{10,2},{12,4},{14,6},{1,9},{3,11}... | collective-permute-start | bytes 368648 | tf_op jit(solution)/shard_map/ppermute | solution.py:38
  26.9 13.8 %collective-permute-start.21 = (bf16[2,240,128]{2,1,0:T(8,128)(2,1)S(1)}, bf16[2,240,128]{2,1,0:T(8,128)(2,1)S(1)}, u32[]{:S(2)}, u32[]{:S(2)}) collective-permute-start(bf16[2,240,128]{2,1,0:T(8,128)(2,1)S(1)} %get-tuple-element.80), channel_id=1, source_target_pairs={{0,2},{2,0},{4,6},{6,4},{8,10},{10,8},{12,14},{14,12},{1,3},{3,1},... | collective-permute-start | bytes 368648 | tf_op jit(solution)/shard_map/ppermute | solution.py:38
  34.7 15.5 %collective-permute-start.22 = (bf16[2,240,128]{2,1,0:T(8,128)(2,1)S(1)}, bf16[2,240,128]{2,1,0:T(8,128)(2,1)S(1)}, u32[]{:S(2)}, u32[]{:S(2)}) collective-permute-start(bf16[2,240,128]{2,1,0:T(8,128)(2,1)S(1)} %get-tuple-element.82), channel_id=1, source_target_pairs={{0,8},{2,10},{4,12},{6,14},{8,0},{10,2},{12,4},{14,6},{1,9},{3,11}... | collective-permute-start | bytes 368648 | tf_op jit(solution)/shard_map/ppermute | solution.py:38
  34.8 15.5 %collective-permute-start.4 = (bf16[240,128]{1,0:T(8,128)(2,1)S(1)}, bf16[240,128]{1,0:T(8,128)(2,1)S(1)}, u32[]{:S(2)}, u32[]{:S(2)}) collective-permute-start(bf16[240,128]{1,0:T(8,128)(2,1)S(1)} %fusion.12), channel_id=1, source_target_pairs={{0,4},{2,6},{4,0},{6,2},{8,12},{10,14},{12,8},{14,10},{1,5},{3,7},... | collective-permute-start | bytes 184328 | tf_op jit(solution)/shard_map/ppermute | solution.py:38
  38.7 11.6 %collective-permute-start.8 = (bf16[240,128]{1,0:T(8,128)(2,1)S(1)}, bf16[240,128]{1,0:T(8,128)(2,1)S(1)}, u32[]{:S(2)}, u32[]{:S(2)}) collective-permute-start(bf16[240,128]{1,0:T(8,128)(2,1)S(1)} %fusion.13), channel_id=1, source_target_pairs={{0,2},{2,0},{4,6},{6,4},{8,10},{10,8},{12,14},{14,12},{1,3},{3,1},... | collective-permute-start | bytes 184328 | tf_op jit(solution)/shard_map/ppermute | solution.py:38
  40.6 9.4 %collective-permute-start.11 = (bf16[2,240,256]{2,1,0:T(8,128)(2,1)S(1)}, bf16[2,240,256]{2,1,0:T(8,128)(2,1)S(1)}, u32[]{:S(2)}, u32[]{:S(2)}) collective-permute-start(bf16[2,240,256]{2,1,0:T(8,128)(2,1)S(1)} %fusion.8), channel_id=1, source_target_pairs={{0,4},{2,6},{4,0},{6,2},{8,12},{10,14},{12,8},{14,10},{1,5},{3,7},... | collective-permute-start | bytes 737288 | tf_op jit(solution)/shard_map/ppermute | solution.py:38
  40.8 15.9 %collective-permute-start.16 = (bf16[2,240,256]{2,1,0:T(8,128)(2,1)S(1)}, bf16[2,240,256]{2,1,0:T(8,128)(2,1)S(1)}, u32[]{:S(2)}, u32[]{:S(2)}) collective-permute-start(bf16[2,240,256]{2,1,0:T(8,128)(2,1)S(1)} %pad_maximum_fusion.4), channel_id=1, source_target_pairs={{0,4},{2,6},{4,0},{6,2},{8,12},{10,14},{12,8},{14,10},{1,5},{3,7},... | collective-permute-start | bytes 737288 | tf_op jit(solution)/shard_map/ppermute | solution.py:38
  50.1 27.8 %copy-start.3 = (f32[240,512]{1,0:T(8,128)S(1)}, f32[240,512]{1,0:T(8,128)}, u32[]{:S(2)}) copy-start(f32[240,512]{1,0:T(8,128)} %first_ref.1) | copy-start | bytes 1474564
  50.1 27.8 %copy-start.4 = (f32[240,512]{1,0:T(8,128)S(1)}, f32[240,512]{1,0:T(8,128)}, u32[]{:S(2)}) copy-start(f32[240,512]{1,0:T(8,128)} %second_ref.1) | copy-start | bytes 1474564
  50.1 6.1 %collective-permute-start.12 = (bf16[240,256]{1,0:T(8,128)(2,1)S(1)}, bf16[240,256]{1,0:T(8,128)(2,1)S(1)}, u32[]{:S(2)}, u32[]{:S(2)}) collective-permute-start(bf16[240,256]{1,0:T(8,128)(2,1)S(1)} %fusion.10), channel_id=1, source_target_pairs={{0,8},{2,10},{4,12},{6,14},{8,0},{10,2},{12,4},{14,6},{1,9},{3,11}... | collective-permute-start | bytes 368648 | tf_op jit(solution)/shard_map/ppermute | solution.py:38
  56.5 1.2 %collective-permute-start.13 = (f32[8,128]{1,0:T(8,128)S(1)}, f32[8,128]{1,0:T(8,128)S(1)}, u32[]{:S(2)}, u32[]{:S(2)}) collective-permute-start(f32[8,128]{1,0:T(8,128)S(1)} %get-tuple-element.66), channel_id=1, source_target_pairs={{0,1},{1,0},{2,3},{3,2},{4,5},{5,4},{6,7},{7,6},{8,9},{9,8},{10,11... | collective-permute-start | bytes 12296 | tf_op jit(solution)/shard_map/ppermute | solution.py:38
  57.8 3.6 %collective-permute-start.14 = (f32[8,128]{1,0:T(8,128)S(1)}, f32[8,128]{1,0:T(8,128)S(1)}, u32[]{:S(2)}, u32[]{:S(2)}) collective-permute-start(f32[8,128]{1,0:T(8,128)S(1)} %add.128), channel_id=1, source_target_pairs={{0,2},{2,0},{4,6},{6,4},{8,10},{10,8},{12,14},{14,12},{1,3},{3,1},... | collective-permute-start | bytes 12296 | tf_op jit(solution)/shard_map/ppermute | solution.py:38
  58.4 3.7 %collective-permute-start.15 = (bf16[2,2,8,240]{3,2,1,0:T(8,128)(2,1)S(1)}, bf16[2,2,8,240]{3,2,1,0:T(8,128)(2,1)S(1)}, u32[]{:S(2)}, u32[]{:S(2)}) collective-permute-start(bf16[2,2,8,240]{3,2,1,0:T(8,128)(2,1)S(1)} %dynamic-slice_bitcast_fusion.8), channel_id=1, source_target_pairs={{0,2},{2,0},{4,6},{6,4},{8,10},{10,8},{12,14},{14,12},{1,3},{3,1},... | collective-permute-start | bytes 46088 | tf_op jit(solution)/shard_map/ppermute | solution.py:38
  62.2 3.7 %collective-permute-start.17 = (f32[8,128]{1,0:T(8,128)S(1)}, f32[8,128]{1,0:T(8,128)S(1)}, u32[]{:S(2)}, u32[]{:S(2)}) collective-permute-start(f32[8,128]{1,0:T(8,128)S(1)} %add.129), channel_id=1, source_target_pairs={{0,4},{2,6},{4,0},{6,2},{8,12},{10,14},{12,8},{14,10},{1,5},{3,7},... | collective-permute-start | bytes 12296 | tf_op jit(solution)/shard_map/ppermute | solution.py:38
  62.2 3.8 %collective-permute-start.18 = (bf16[2,2,8,240]{3,2,1,0:T(8,128)(2,1)S(1)}, bf16[2,2,8,240]{3,2,1,0:T(8,128)(2,1)S(1)}, u32[]{:S(2)}, u32[]{:S(2)}) collective-permute-start(bf16[2,2,8,240]{3,2,1,0:T(8,128)(2,1)S(1)} %bitcast.167), channel_id=1, source_target_pairs={{0,4},{2,6},{4,0},{6,2},{8,12},{10,14},{12,8},{14,10},{1,5},{3,7},... | collective-permute-start | bytes 46088 | tf_op jit(solution)/shard_map/ppermute | solution.py:38
  66.1 5.0 %collective-permute-start.19 = (f32[8,128]{1,0:T(8,128)S(1)}, f32[8,128]{1,0:T(8,128)S(1)}, u32[]{:S(2)}, u32[]{:S(2)}) collective-permute-start(f32[8,128]{1,0:T(8,128)S(1)} %add.130.square_ref), channel_id=1, source_target_pairs={{0,8},{2,10},{4,12},{6,14},{8,0},{10,2},{12,4},{14,6},{1,9},{3,11}... | collective-permute-start | bytes 12296 | tf_op jit(solution)/shard_map/ppermute | solution.py:38
  68.0 4.7 %collective-permute-start.20 = (bf16[2,2,8,240]{3,2,1,0:T(8,128)(2,1)S(1)}, bf16[2,2,8,240]{3,2,1,0:T(8,128)(2,1)S(1)}, u32[]{:S(2)}, u32[]{:S(2)}) collective-permute-start(bf16[2,2,8,240]{3,2,1,0:T(8,128)(2,1)S(1)} %fusion.17), channel_id=1, source_target_pairs={{0,8},{2,10},{4,12},{6,14},{8,0},{10,2},{12,4},{14,6},{1,9},{3,11}... | collective-permute-start | bytes 46088 | tf_op jit(solution)/shard_map/ppermute | solution.py:38
  69.1 15.1 %collective-permute-start.23 = (bf16[2,2,240,256]{3,2,0,1:T(8,128)(2,1)S(1)}, bf16[2,2,240,256]{3,2,0,1:T(8,128)(2,1)S(1)}, u32[]{:S(2)}, u32[]{:S(2)}) collective-permute-start(bf16[2,2,240,256]{3,2,0,1:T(8,128)(2,1)S(1)} %pad_maximum_fusion.1), channel_id=1, source_target_pairs={{0,2},{2,0},{4,6},{6,4},{8,10},{10,8},{12,14},{14,12},{1,3},{3,1},... | collective-permute-start | bytes 1474568 | tf_op jit(solution)/shard_map/ppermute | solution.py:38
  72.8 8.8 %collective-permute-start.26 = (bf16[2,2,240,128]{3,2,1,0:T(8,128)(2,1)S(1)}, bf16[2,2,240,128]{3,2,1,0:T(8,128)(2,1)S(1)}, u32[]{:S(2)}, u32[]{:S(2)}) collective-permute-start(bf16[2,2,240,128]{3,2,1,0:T(8,128)(2,1)S(1)} %pad_maximum_fusion.6), channel_id=1, source_target_pairs={{0,4},{2,6},{4,0},{6,2},{8,12},{10,14},{12,8},{14,10},{1,5},{3,7},... | collective-permute-start | bytes 737288 | tf_op jit(solution)/shard_map/ppermute | solution.py:38
  73.1 10.3 %collective-permute-start.28 = (bf16[2,2,240,128]{3,2,1,0:T(8,128)(2,1)S(1)}, bf16[2,2,240,128]{3,2,1,0:T(8,128)(2,1)S(1)}, u32[]{:S(2)}, u32[]{:S(2)}) collective-permute-start(bf16[2,2,240,128]{3,2,1,0:T(8,128)(2,1)S(1)} %pad_maximum_fusion.5), channel_id=1, source_target_pairs={{0,8},{2,10},{4,12},{6,14},{8,0},{10,2},{12,4},{14,6},{1,9},{3,11}... | collective-permute-start | bytes 737288 | tf_op jit(solution)/shard_map/ppermute | solution.py:38
  84.4 4.3 %collective-permute-start.24 = (f32[2,2,8,512]{3,2,1,0:T(8,128)S(1)}, f32[2,2,8,512]{3,2,1,0:T(8,128)S(1)}, u32[]{:S(2)}, u32[]{:S(2)}) collective-permute-start(f32[2,2,8,512]{3,2,1,0:T(8,128)S(1)} %dynamic-slice_bitcast_fusion.6), channel_id=1, source_target_pairs={{0,2},{2,0},{4,6},{6,4},{8,10},{10,8},{12,14},{14,12},{1,3},{3,1},... | collective-permute-start | bytes 196616 | tf_op jit(solution)/shard_map/ppermute | solution.py:38
  88.9 1.3 %collective-permute-start.25 = (f32[32,256]{1,0:T(8,128)S(1)}, f32[32,256]{1,0:T(8,128)S(1)}, u32[]{:S(2)}, u32[]{:S(2)}) collective-permute-start(f32[32,256]{1,0:T(8,128)S(1)} %bitcast.166), channel_id=1, source_target_pairs={{0,1},{1,0},{2,3},{3,2},{4,5},{5,4},{6,7},{7,6},{8,9},{9,8},{10,11... | collective-permute-start | bytes 98312 | tf_op jit(solution)/shard_map/ppermute | solution.py:38
  90.1 1.6 %copy-start.12 = (bf16[2,2,2,240,128]{4,3,2,0,1:T(8,128)(2,1)S(1)}, bf16[2,2,2,240,128]{4,3,2,0,1:T(8,128)(2,1)}, u32[]{:S(2)}) copy-start(bf16[2,2,2,240,128]{4,3,2,0,1:T(8,128)(2,1)} %pad_maximum_fusion.2) | copy-start | bytes 1474564
  90.1 4.6 %copy-start.6 = (bf16[384,256]{1,0:T(8,128)(2,1)S(1)}, bf16[384,256]{1,0:T(8,128)(2,1)}, u32[]{:S(2)}) copy-start(bf16[384,256]{1,0:T(8,128)(2,1)} %cot_ref.1) | copy-start | bytes 589828
  90.2 3.8 %collective-permute-start.27 = (f32[2,8,256]{2,1,0:T(8,128)S(1)}, f32[2,8,256]{2,1,0:T(8,128)S(1)}, u32[]{:S(2)}, u32[]{:S(2)}) collective-permute-start(f32[2,8,256]{2,1,0:T(8,128)S(1)} %dynamic-slice_bitcast_fusion.7), channel_id=1, source_target_pairs={{0,4},{2,6},{4,0},{6,2},{8,12},{10,14},{12,8},{14,10},{1,5},{3,7},... | collective-permute-start | bytes 49160 | tf_op jit(solution)/shard_map/ppermute | solution.py:38
  94.0 4.6 %collective-permute-start.29 = (f32[8,256]{1,0:T(8,128)S(1)}, f32[8,256]{1,0:T(8,128)S(1)}, u32[]{:S(2)}, u32[]{:S(2)}) collective-permute-start(f32[8,256]{1,0:T(8,128)S(1)} %get-tuple-element.96), channel_id=1, source_target_pairs={{0,8},{2,10},{4,12},{6,14},{8,0},{10,2},{12,4},{14,6},{1,9},{3,11}... | collective-permute-start | bytes 24584 | tf_op jit(solution)/shard_map/ppermute | solution.py:38
  95.4 3.2 %copy-start.11 = (bf16[1,8,256]{2,1,0:T(8,128)(2,1)S(1)}, bf16[1,8,256]{2,1,0:T(8,128)(2,1)}, u32[]{:S(2)}) copy-start(bf16[1,8,256]{2,1,0:T(8,128)(2,1)} %values_ref.3) | copy-start | bytes 12292

commit v3 on v0

v3 whole, which is shorter than its diff:
```python
import functools
import math

import jax
import jax.numpy as jnp
from jax import lax
from jax.experimental import pallas as pl
from jax.experimental.pallas import tpu as pltpu
from jax.sharding import PartitionSpec as P

D = 3840
HQ = 32
KVH = 4
HD = 128
STEPS = 8
UPDATES = 20


beta_first = 0.9
beta_second = 0.95
learn_rate = 0.02
decay_rate = 0.1
adam_epsilon = 1e-08

unit_scale = 1.0 / math.sqrt(D)
MASKED = -1e30
VMEM = pl.BlockSpec(memory_space=pltpu.VMEM)
SMEM = pl.BlockSpec(memory_space=pltpu.SMEM)
TOKEN = jax.ShapeDtypeStruct((8, 128), jnp.float32)
TINY = pl.CostEstimate(flops=1, bytes_accessed=1, transcendentals=0)
SMALL = pltpu.CompilerParams(vmem_limit_bytes=16 * 1024 * 1024)


def tied(*values):
    return lax.optimization_barrier(values)


def swap(value, axis, bit):
    size = lax.axis_size(axis)
    return lax.ppermute(value, axis, [(i, i ^ (1 << bit)) for i in range(size)])


def with_bit(blocks, bits, bit, value):
    split = blocks.reshape((2,) * bits + blocks.shape[1:])
    return lax.index_in_dim(split, value, bits - 1 - bit, keepdims=False)


def pick(blocks, names, bit, value):
    return jnp.stack([blocks[i] for i, name in enumerate(names) if (name >> bit) & 1 == value])


units = (1, 1, 2)
widths = (1, 1, 1, 1)


def sum_orders(bits):
    if bits == 3:
        return [[2, 0, 1], [1, 2, 0], [0, 1, 2]]
    return [[(c * max(1, bits // 3) + s) % bits for s in range(bits)] for c in range(3)]


def gather_orders(bits):
    up = list(range(1, bits))
    return [up[-1:] + [0] + up[:-1], up[::-1] + [0], up + [0], up + [0]]


def sum_names(order, stage):
    names = [0]
    for bit in sorted(order[stage:]):
        names = names + [name | (1 << bit) for name in names]
    return names


def gather_names(order, stage):
    names = [0]
    for bit in order[:stage]:
        names = names + [name | (1 << bit) for name in names]
    return names


def bit_units(bits, stage, bit):
    out = []
    for c, order in enumerate(sum_orders(bits)):
        if order[stage] == bit:
            count = len(sum_names(order, stage)) // 2
            out += [("sum", c, i, u) for i in range(count) for u in range(units[c])]
    for g, order in enumerate(gather_orders(bits)):
        if stage < bits - 1:
            if order[stage] == bit:
                count = len(gather_names(order, stage))
                out += [("gather", g, i, u) for i in range(count) for u in range(widths[g])]
    return out


def messages_of(bits, stage):
    out = []
    for bit in range(bits - 1, -1, -1):
        what = bit_units(bits, stage, bit)
        if stage == 0 and bit == 0 and bits == 3:
            out.append((bit, what[: len(what) // 2]))
            out.append((bit, what[len(what) // 2 :]))
        elif what:
            out.append((bit, what))
    return out


def kept(order, stage):
    names = sum_names(order, stage)
    return [i for i, name in enumerate(names) if not (name >> order[stage]) & 1]


def given(order, stage):
    names = sum_names(order, stage)
    return [i for i, name in enumerate(names) if (name >> order[stage]) & 1]


def start_of(cuts, c):
    return sum(cuts[:c])


def next_stage(bits, stage, unit, came, keeps, helds):
    orders, spreads = sum_orders(bits), gather_orders(bits)
    place = {}
    for m, (_, what) in enumerate(messages_of(bits, stage)):
        for i, key in enumerate(what):
            place[key] = (m, i)
    sums, gathered = [], []
    for c, order in enumerate(orders):
        blocks = []
        for i in range(len(kept(order, stage))):
            block = keeps(c, i)
            parts = []
            for u in range(units[c]):
                add = came(*place[("sum", c, i, u)]).astype(jnp.float32)
                parts.append(block[:, u * unit : (u + 1) * unit] + add)
            blocks.append(parts)
        sums.append(blocks)
    for g, order in enumerate(spreads):
        old, new = [], []
        for i in range(len(gather_names(order, stage))):
            block = helds(g, i)
            old.append([block[:, u * unit : (u + 1) * unit] for u in range(widths[g])])
            new.append([came(*place[("gather", g, i, u)]) for u in range(widths[g])])
        gathered.append(old + new)
    messages = []
    for _, what in messages_of(bits, stage + 1):
        out = []
        for kind, c, i, u in what:
            if kind == "sum":
                out.append(sums[c][given(orders[c], stage + 1)[i]][u].astype(jnp.bfloat16))
            else:
                out.append(gathered[c][i][u])
        messages.append(out)
    keep_out = [[sums[c][i] for i in kept(orders[c], stage + 1)] for c in range(len(units))]
    return messages, keep_out, gathered


def stage_shapes(bits, stage, rows, unit):
    messages = [
        jax.ShapeDtypeStruct((len(what), rows, unit), jnp.bfloat16)
        for _, what in messages_of(bits, stage)
    ]
    keeps = [
        jax.ShapeDtypeStruct((len(kept(order, stage)), rows, units[c] * unit), jnp.float32)
        for c, order in enumerate(sum_orders(bits))
    ]
    helds = [
        jax.ShapeDtypeStruct((len(gather_names(order, stage)), rows, widths[g] * unit), jnp.bfloat16)
        for g, order in enumerate(gather_orders(bits))
    ]
    return messages, keeps, helds


def put_blocks(ref, blocks, unit):
    for i, parts in enumerate(blocks):
        for u, part in enumerate(parts):
            ref[i, :, u * unit : (u + 1) * unit] = part


def first_kernel(bits, cuts, unit, over, where_ref, hidden_ref, cot_ref, master_ref, gate_ref, *refs):
    outs, token_ref, total = refs[:-2], refs[-2], refs[-1]
    token_ref[...] = jnp.zeros(token_ref.shape, jnp.float32)
    orders = sum_orders(bits)
    columns = hidden_ref.shape[1]
    owned = columns >> bits
    half = 2 * unit
    step = 384 if columns % 384 == 0 else columns
    for at in range(0, columns, step):
        total[at : at + step, :] = unit_scale * lax.dot_general(
            hidden_ref[:, at : at + step],
            cot_ref[...],
            (((0,), (0,)), ((), ())),
            preferred_element_type=jnp.float32,
        )
    here, core = where_ref[0], where_ref[1]
    sums = [c for c, order in enumerate(orders) if order[0] in over]
    origin = start_of(units, sums[0])
    at = 0
    for low, high in cuts:
        rows = high - low
        whats = [what for bit, what in messages_of(bits, 0) if bit in over]
        messages = outs[at : at + len(whats)]
        at += len(whats)
        keeps = dict(zip(sums, outs[at : at + len(sums)]))
        at += len(sums)
        helds = outs[at : at + len(widths)] if 0 in over else []
        at += len(helds)

        def block(c, index):
            name = sum_names(orders[c], 0)[index]
            start = pl.multiple_of((here ^ name) * owned + low, 16)
            first = (start_of(units, c) - origin) * unit
            return total[pl.ds(start, rows), first : first + units[c] * unit]

        weight = master_ref[low:high, :].astype(jnp.bfloat16)
        near = jnp.where(core == 0, weight[:, :half], weight[:, half:])
        far = jnp.where(core == 0, weight[:, half:], weight[:, :half])
        weight = jnp.concatenate([near, far], axis=1)
        for c in sums:
            for i, index in enumerate(kept(orders[c], 0)):
                keeps[c][i] = block(c, index)
        for g, held in enumerate(helds):
            first = start_of(widths, g) * unit
            held[0] = weight[:, first : first + widths[g] * unit]
        for message, what in zip(messages, whats):
            for j, (kind, c, i, u) in enumerate(what):
                if kind == "sum":
                    if j == 0 or what[j - 1][:3] != (kind, c, i):
                        give = block(c, given(orders[c], 0)[i]).astype(jnp.bfloat16)
                    message[j] = give[:, u * unit : (u + 1) * unit]
                else:
                    first = (start_of(widths, c) + u) * unit
                    message[j] = weight[:, first : first + unit]


def first_stage(bits, cuts, unit, hidden, near, far, master):
    orders = sum_orders(bits)
    owned = hidden.shape[1] >> bits
    here = lax.axis_index("fsdp").astype(jnp.int32)
    core = lax.axis_index("tp").astype(jnp.int32)
    token = jnp.zeros(TOKEN.shape, TOKEN.dtype)
    if bits == 3 and owned % 16 == 0:
        result = [([], [None] * len(units), []) for _ in cuts]
        for over, cot in (((2, 1), near), ((0,), far)):
            sums = [c for c, order in enumerate(orders) if order[0] in over]
            which = [m for m, (bit, _) in enumerate(messages_of(bits, 0)) if bit in over]
            shapes = []
            for low, high in cuts:
                messages, keeps, helds = stage_shapes(bits, 0, high - low, unit)
                shapes += [messages[m] for m in which] + [keeps[c] for c in sums]
                shapes += helds if 0 in over else []
            outs = pl.pallas_call(
                functools.partial(first_kernel, bits, cuts, unit, over),
                out_shape=shapes + [TOKEN],
                in_specs=[SMEM] + [VMEM] * 4,
                out_specs=[VMEM] * (len(shapes) + 1),
                scratch_shapes=[pltpu.VMEM((hidden.shape[1], cot.shape[1]), jnp.float32)],
                compiler_params=SMALL,
                cost_estimate=TINY,
            )(jnp.stack([here, core]), hidden, cot, master, token)
            token, outs = outs[-1], list(outs[:-1])
            for messages, keeps, helds in result:
                messages += [outs.pop(0) for _ in which]
                for c in sums:
                    keeps[c] = outs.pop(0)
                if 0 in over:
                    helds += [outs.pop(0) for _ in widths]
        return result, token
    product = unit_scale * lax.dot_general(
        hidden,
        jnp.concatenate([near, far], axis=1),
        (((0,), (0,)), ((), ())),
        preferred_element_type=jnp.float32,
    ).reshape(1 << bits, owned, -1)
    weight = master.astype(jnp.bfloat16)
    weight = jnp.where(core == 0, weight, jnp.roll(weight, near.shape[1], axis=1))
    result = []
    for low, high in cuts:

        def block(c, index):
            name = sum_names(orders[c], 0)[index]
            whole = lax.dynamic_index_in_dim(product, here ^ name, 0, keepdims=False)
            first = start_of(units, c) * unit
            return whole[low:high, first : first + units[c] * unit]

        messages = []
        for _, what in messages_of(bits, 0):
            blocks = []
            for kind, c, i, u in what:
                if kind == "sum":
                    give = block(c, given(orders[c], 0)[i])
                    blocks.append(give[:, u * unit : (u + 1) * unit].astype(jnp.bfloat16))
                else:
                    first = (start_of(widths, c) + u) * unit
                    blocks.append(weight[low:high, first : first + unit])
            messages.append(jnp.stack(blocks))
        keeps = [
            jnp.stack([block(c, index) for index in kept(order, 0)])
            for c, order in enumerate(orders)
        ]
        helds = []
        for g, width in enumerate(widths):
            first = start_of(widths, g) * unit
            helds.append(weight[None, low:high, first : first + width * unit])
        result.append((messages, keeps, helds))
    return result, token


def stage_kernel(bits, stage, unit, counts, *refs):
    refs = list(refs)
    came, keeps, helds = (tuple(refs.pop(0) for _ in range(n)) for n in counts)
    token_ref = refs.pop()
    token_ref[...] = jnp.zeros(token_ref.shape, jnp.float32)
    outs = refs[1:]
    messages, keep_out, gathered = next_stage(
        bits,
        stage,
        unit,
        lambda m, i: came[m][i],
        lambda c, i: keeps[c][i],
        lambda g, i: helds[g][i],
    )
    for ref, blocks in zip(outs, messages):
        for i, block in enumerate(blocks):
            ref[i] = block
    for ref, blocks in zip(outs[len(messages) :], keep_out + gathered):
        put_blocks(ref, blocks, unit)


def run_stage(bits, stage, unit, came, keeps, helds, gate):
    rows = keeps[0].shape[1]
    groups = stage_shapes(bits, stage + 1, rows, unit)
    if rows % 16 == 0:
        shapes = [shape for group in groups for shape in group]
        counts = (len(came), len(keeps), len(helds))
        outs = pl.pallas_call(
            functools.partial(stage_kernel, bits, stage, unit, counts),
            out_shape=shapes + [TOKEN],
            in_specs=[VMEM] * (sum(counts) + 1),
            out_specs=[VMEM] * (len(shapes) + 1),
            compiler_params=SMALL,
            cost_estimate=TINY,
        )(*came, *keeps, *helds, gate)
        outs = list(outs)
        return [[outs.pop(0) for _ in group] for group in groups] + [outs[-1]]
    messages, keep_out, gathered = next_stage(
        bits,
        stage,
        unit,
        lambda m, i: came[m][i],
        lambda c, i: keeps[c][i],
        lambda g, i: helds[g][i],
    )
    whole = lambda blocks: jnp.stack([jnp.concatenate(parts, axis=1) for parts in blocks])
    return (
        [jnp.stack(blocks) for blocks in messages],
        [whole(blocks) for blocks in keep_out],
        [whole(blocks) for blocks in gathered],
        gate,
    )


def stacked_heads(query, head, group):
    return jnp.concatenate(
        [query[:, (head * group + g) * HD : (head * group + g + 1) * HD] for g in range(group)],
        axis=0,
    )


def contract_last(left, right):
    return lax.dot_general(
        left, right, (((1,), (1,)), ((), ())), preferred_element_type=jnp.float32
    )


def cache_kernel(
    length_ref, query_ref, keys_ref, values_ref, gate_ref, largest_ref, total_ref, blend_ref
):
    group = HQ // KVH
    rows, span, width = keys_ref.shape
    for r in range(rows):
        for head in range(width // HD):
            lanes = slice(head * HD, (head + 1) * HD)
            queries = stacked_heads(query_ref[r], head, group)
            scores = contract_last(queries, keys_ref[r, :, lanes]) / math.sqrt(HD)
            position = lax.broadcasted_iota(jnp.int32, scores.shape, 1)
            scores = jnp.where(position < length_ref[r], scores, jnp.float32(MASKED))
            largest = jnp.max(scores, axis=1, keepdims=True)
            exponents = jnp.exp(scores - largest)
            total = jnp.sum(exponents, axis=1, keepdims=True)
            largest_ref[r, head] = jnp.broadcast_to(largest, (queries.shape[0], HD))
            total_ref[r, head] = jnp.broadcast_to(total, (queries.shape[0], HD))
            blend_ref[r, head] = jnp.dot(
                exponents.astype(jnp.bfloat16),
                values_ref[r, :, lanes],
                preferred_element_type=jnp.float32,
            )


def attend_cache(query, keys, values, lengths, gate):
    rows, steps, _ = query.shape
    heads = keys.shape[2] // HD
    shape = jax.ShapeDtypeStruct((rows, heads, steps * (HQ // KVH), HD), jnp.float32)
    outs = pl.pallas_call(
        cache_kernel,
        out_shape=[shape] * 3,
        in_specs=[SMEM, VMEM, VMEM, VMEM, VMEM],
        out_specs=[VMEM] * 3,
        compiler_params=SMALL,
        cost_estimate=TINY,
    )(lengths, query, keys, values, gate)
    return list(outs)


def fresh_kernel(
    query_ref, keep_ref, other_ref, values_ref, largest_ref, total_ref, blend_ref,
    near_ref, far_ref, updated_ref, keys_ref, out_ref
):
    group = HQ // KVH
    rows, steps, width = keys_ref.shape
    for r in range(rows):
        fresh = unit_scale * (keep_ref[r] + other_ref[r])
        fresh = fresh.astype(jnp.bfloat16)
        keys_ref[r] = fresh
        values = values_ref[r].astype(jnp.float32)
        for head in range(width // HD):
            lanes = slice(head * HD, (head + 1) * HD)
            queries = stacked_heads(query_ref[r], head, group).astype(jnp.float32)
            keys = fresh[:, lanes].astype(jnp.float32)
            step = lax.broadcasted_iota(jnp.int32, (group * steps, 1), 0) % steps
            scores = []
            for s in range(steps):
                score = jnp.sum(queries * keys[s : s + 1], axis=1, keepdims=True) / math.sqrt(HD)
                scores.append(jnp.where(step >= s, score, jnp.float32(MASKED)))
            largest_old = largest_ref[r, head][:, :1]
            largest = functools.reduce(jnp.maximum, scores, largest_old)
            rescale = jnp.exp(largest_old - largest)
            total = rescale * total_ref[r, head][:, :1]
            blend = rescale * blend_ref[r, head]
            for s in range(steps):
                exponent = jnp.exp(scores[s] - largest)
                total = total + exponent
                blend = blend + exponent * values[s : s + 1, lanes]
            result = (blend / total).astype(jnp.bfloat16)
            for g in range(group):
                at = (head * group + g) * HD
                out_ref[r, :, at : at + HD] = result[g * steps : (g + 1) * steps]


def attend_fresh(query, keep, other, values, cached, gates):
    rows, steps, width = values.shape
    return pl.pallas_call(
        fresh_kernel,
        out_shape=[
            jax.ShapeDtypeStruct((rows, steps, width), jnp.bfloat16),
            jax.ShapeDtypeStruct(query.shape, jnp.bfloat16),
        ],
        in_specs=[VMEM] * 10,
        out_specs=[VMEM] * 2,
        compiler_params=SMALL,
        cost_estimate=TINY,
    )(query, keep, other, values, *cached, *gates)


def rows_kernel(slices, where_ref, hidden_ref, gate_ref, out_ref):
    size, _, owned = out_ref.shape
    for half in range(slices):

        @pl.when(where_ref[1] == half)
        def _():
            for index in range(size):
                at = (half * size + index) * owned
                out_ref[where_ref[0] ^ index] = hidden_ref[:, at : at + owned]


def rows_by_owner(hidden, slices, size, gate):
    tokens, width = hidden.shape
    owned = width // slices // size
    here = lax.axis_index("fsdp").astype(jnp.int32)
    core = lax.axis_index("tp").astype(jnp.int32)
    if owned % 16 != 0:
        cut = hidden.reshape(tokens, slices, size, owned)
        cut = lax.dynamic_index_in_dim(cut, core, 1, keepdims=False).transpose(1, 0, 2)
        return cut[here ^ jnp.arange(size, dtype=jnp.int32)]
    return pl.pallas_call(
        functools.partial(rows_kernel, slices),
        out_shape=jax.ShapeDtypeStruct((size, tokens, owned), hidden.dtype),
        in_specs=[SMEM, VMEM, VMEM],
        out_specs=VMEM,
        compiler_params=SMALL,
        cost_estimate=TINY,
    )(jnp.stack([here, core]), hidden, gate)


def sum_kernel(bits, unit, parts, here_ref, *refs):
    inputs, grad_ref, square_ref = list(refs[:-2]), refs[-2], refs[-1]
    half = 2 * unit
    square = jnp.zeros((1, 1), jnp.float32)
    place = {}
    for m, (_, what) in enumerate(messages_of(bits, bits - 1)):
        for i, key in enumerate(what):
            place[key] = (m, i)
    low = 0
    for came_count, keep_count in parts:
        came = [inputs.pop(0) for _ in range(came_count)]
        keeps = [inputs.pop(0) for _ in range(keep_count)]
        rows = keeps[0].shape[1]
        pieces = []
        for c in range(len(units)):
            where = [place[("sum", c, 0, u)] for u in range(units[c])]
            add = [came[m][i] for m, i in where]
            add = add[0] if len(add) == 1 else jnp.concatenate(add, axis=1)
            pieces.append(keeps[c][0] + add.astype(jnp.float32))
        near = jnp.concatenate(pieces[:2], axis=1)
        far = pieces[2]
        here = here_ref[0]
        grad_ref[low : low + rows, :half] = jnp.where(here == 0, near, far)
        grad_ref[low : low + rows, half:] = jnp.where(here == 0, far, near)
        square = square + jnp.sum(near * near + far * far, keepdims=True)
        low += rows
    square_ref[...] = jnp.broadcast_to(square, square_ref.shape)


def summed(bits, unit, parts):
    flat = [a for came, keeps in parts for a in list(came) + list(keeps)]
    rows = sum(keeps[0].shape[1] for _, keeps in parts)
    counts = [(len(came), len(keeps)) for came, keeps in parts]
    return pl.pallas_call(
        functools.partial(sum_kernel, bits, unit, counts),
        out_shape=[
            jax.ShapeDtypeStruct((rows, 4 * unit), jnp.float32),
            jax.ShapeDtypeStruct((8, 128), jnp.float32),
        ],
        in_specs=[SMEM] + [VMEM] * len(flat),
        out_specs=[VMEM] * 2,
        compiler_params=SMALL,
        cost_estimate=TINY,
    )(lax.axis_index("tp").astype(jnp.int32).reshape(1), *flat)


def lay_out(bits, cuts, unit, which, here, blocks, weight):
    owned = cuts[-1][1]
    at = 0
    for low, high in cuts:
        for lane, g in enumerate(which):
            order = gather_orders(bits)[g]
            lanes = slice(lane * unit, (lane + 1) * unit)
            old = gather_names(order, bits - 1)
            for names in (old, [name | (1 << order[-1]) for name in old]):
                for i, name in enumerate(names):
                    start = pl.multiple_of((here ^ name) * owned + low, 16)
                    weight[pl.ds(start, high - low), lanes] = blocks[at][i]
                at += 1


def near_kernel(bits, cuts, unit, which, here_ref, cot_ref, *refs):
    blocks, out_ref, token_ref, weight = refs[:-3], refs[-3], refs[-2], refs[-1]
    token_ref[...] = jnp.zeros(token_ref.shape, jnp.float32)
    lay_out(bits, cuts, unit, which, here_ref[0], blocks, weight)
    columns = out_ref.shape[1]
    tile = 384 if columns % 384 == 0 else columns
    for at in range(0, columns, tile):
        out_ref[:, at : at + tile] = contract_last(cot_ref[...], weight[at : at + tile, :])


def far_kernel(bits, cuts, unit, which, here_ref, cot_ref, near_ref, *refs):
    blocks, out_ref, token_ref, weight, result, done = refs[:-5], *refs[-5:]
    token_ref[...] = jnp.zeros(token_ref.shape, jnp.float32)
    lay_out(bits, cuts, unit, which, here_ref[0], blocks, weight)
    count = result.shape[0]
    tile = count // done.shape[0]
    copies = []
    for i in range(done.shape[0]):
        rows = slice(i * tile, (i + 1) * tile)
        product = near_ref[rows, :] + contract_last(cot_ref[rows, :], weight[...])
        result[rows, :] = (unit_scale * product).astype(jnp.bfloat16)
        copy = pltpu.make_async_copy(result.at[rows, :], out_ref.at[rows, :], done.at[i])
        copy.start()
        copies.append(copy)
    for copy in copies:
        copy.wait()


INPUT = pltpu.CompilerParams(vmem_limit_bytes=24 * 1024 * 1024)


def gathered_columns(bits, which, helds, came):
    here = lax.axis_index("fsdp").astype(jnp.int32)
    place = here ^ jnp.arange(1 << bits, dtype=jnp.int32)
    weight = []
    for g in which:
        order = gather_orders(bits)[g]
        old = gather_names(order, bits - 1)
        names = old + [name | (1 << order[-1]) for name in old]
        blocks = jnp.concatenate([helds[g], came[g]], axis=0)[jnp.argsort(jnp.array(names))]
        weight.append(blocks[place].reshape(-1, blocks.shape[-1]))
    return jnp.concatenate(weight, axis=1)


def input_near(bits, cuts, unit, cot, helds, came):
    columns = cuts[-1][1] << bits
    if cuts[-1][1] % 16 != 0:
        product = contract_last(cot, gathered_columns(bits, (0, 1), helds, came))
        return product, jnp.zeros(TOKEN.shape, TOKEN.dtype)
    blocks = [a for g in (0, 1) for a in (helds[g], came[g])]
    return pl.pallas_call(
        functools.partial(near_kernel, bits, cuts, unit, (0, 1)),
        out_shape=[jax.ShapeDtypeStruct((cot.shape[0], columns), jnp.float32), TOKEN],
        in_specs=[SMEM] + [VMEM] * (1 + len(blocks)),
        out_specs=[VMEM] * 2,
        scratch_shapes=[pltpu.VMEM((columns, 2 * unit), jnp.bfloat16)],
        compiler_params=INPUT,
        cost_estimate=TINY,
    )(lax.axis_index("fsdp").astype(jnp.int32).reshape(1), cot, *blocks)


def input_far(bits, cuts, unit, cot, near, helds, came):
    columns = cuts[-1][1] << bits
    if cuts[-1][1] % 16 != 0:
        product = near + contract_last(cot, gathered_columns(bits, (2, 3), helds, came))
        return (unit_scale * product).astype(jnp.bfloat16), jnp.zeros(TOKEN.shape, TOKEN.dtype)
    blocks = [a for g in (2, 3) for a in (helds[g], came[g])]
    tokens = cot.shape[0]
    pieces = 4 if tokens % 64 == 0 else 1
    return pl.pallas_call(
        functools.partial(far_kernel, bits, cuts, unit, (2, 3)),
        out_shape=[jax.ShapeDtypeStruct((tokens, columns), jnp.bfloat16), TOKEN],
        in_specs=[SMEM] + [VMEM] * (2 + len(blocks)),
        out_specs=[pl.BlockSpec(memory_space=pl.ANY), VMEM],
        scratch_shapes=[
            pltpu.VMEM((columns, 2 * unit), jnp.bfloat16),
            pltpu.VMEM((tokens, columns), jnp.bfloat16),
            pltpu.SemaphoreType.DMA((pieces,)),
        ],
        compiler_params=INPUT,
        cost_estimate=TINY,
    )(lax.axis_index("fsdp").astype(jnp.int32).reshape(1), cot, near, *blocks)


def adamw(factor, grad, master, first, second):
    clipped = factor * grad
    first_new = beta_first * first + (1.0 - beta_first) * clipped
    second_new = beta_second * second + (1.0 - beta_second) * clipped * clipped
    first_hat = first_new / (1.0 - beta_first**UPDATES)
    second_hat = second_new / (1.0 - beta_second**UPDATES)
    master_new = master - learn_rate * (
        first_hat / (jnp.sqrt(second_hat) + adam_epsilon) + decay_rate * master
    )
    return master_new, first_new, second_new


def project_kernel(
    limit, bit, where_ref, square_ref, other_ref, grad_ref, master_ref, first_ref, second_ref,
    hidden_ref, keep_ref, give_ref
):
    square = square_ref[:1, :1] + other_ref[:1, :1]
    factor = jnp.minimum(1.0, limit / jnp.sqrt(square))
    relay = adamw(factor, grad_ref[...], master_ref[...], first_ref[...], second_ref[...])[0]
    product = jnp.dot(
        hidden_ref[...], relay.astype(jnp.bfloat16), preferred_element_type=jnp.float32
    )
    core = where_ref[0]
    half = product.shape[1] // 2
    near = jnp.where(core == 0, product[:, :half], product[:, half:])
    far = jnp.where(core == 0, product[:, half:], product[:, :half])
    _, tokens, _ = keep_ref.shape
    names = range(2 * keep_ref.shape[0])
    for ref, value in ((keep_ref, 0), (give_ref, 1)):
        for i, name in enumerate(name for name in names if (name >> bit) & 1 == value):
            rows = slice(name * tokens, (name + 1) * tokens)
            ref[i, :, :half] = near[rows]
            ref[i, :, half:] = far[rows]


def project(limit, bit, square, other, grad, master, first, second, hidden, tokens):
    count = hidden.shape[0] // tokens // 2
    shape = jax.ShapeDtypeStruct((count, tokens, master.shape[1]), jnp.float32)
    return pl.pallas_call(
        functools.partial(project_kernel, limit, bit),
        out_shape=[shape] * 2,
        in_specs=[SMEM] + [VMEM] * 7,
        out_specs=[VMEM] * 2,
        compiler_params=SMALL,
        cost_estimate=TINY,
    )(
        lax.axis_index("tp").astype(jnp.int32).reshape(1),
        square, other, grad, master, first, second, hidden,
    )


def update_kernel(
    limit, square_ref, other_ref, grad_ref, master_ref, first_ref, second_ref,
    master_out, first_out, second_out, token_ref
):
    token_ref[...] = jnp.zeros(token_ref.shape, jnp.float32)
    factor = jnp.minimum(1.0, limit / jnp.sqrt(square_ref[:1, :1] + other_ref[:1, :1]))
    master_out[...], first_out[...], second_out[...] = adamw(
        factor, grad_ref[...], master_ref[...], first_ref[...], second_ref[...]
    )


def updated(limit, square, other, grad, master, first, second):
    return pl.pallas_call(
        functools.partial(update_kernel, limit),
        out_shape=[jax.ShapeDtypeStruct(master.shape, jnp.float32)] * 3 + [TOKEN],
        in_specs=[VMEM] * 6,
        out_specs=[VMEM] * 4,
        compiler_params=SMALL,
        cost_estimate=TINY,
    )(square, other, grad, master, first, second)


def shards(
    learn_hidden,
    learn_grad_out,
    key_master,
    key_first,
    key_second,
    rollout_hidden,
    query_base,
    cache_keys,
    cache_values,
    new_values,
    cache_lengths,
):
    size = lax.axis_size("fsdp")
    slice_count = lax.axis_size("tp")
    bits = size.bit_length() - 1
    owned, width_all = key_master.shape
    column_count = width_all // slice_count
    row_count, steps, _ = rollout_hidden.shape
    unit = column_count // 2
    cuts = [(0, owned)]

    other_cot = swap(learn_grad_out, "tp", 0)
    parts, gate = first_stage(
        bits, cuts, unit, learn_hidden, learn_grad_out, other_cot, key_master
    )

    def send(messages, stage):
        over = [bit for bit, _ in messages_of(bits, stage)]
        return [swap(message, "fsdp", bit) for message, bit in zip(messages, over)]

    rows = rows_by_owner(rollout_hidden.reshape(row_count * steps, -1), slice_count, size, gate)
    row_bits = [0, 2, 1] if bits == 3 else list(range(bits))

    def send_rows(stage, messages):
        give, messages[-1] = tied(with_bit(rows, bits, row_bits[stage], 1), messages[-1])
        return swap(give, "fsdp", row_bits[stage])

    def take_rows(stage, come, sent):
        come, sent[0] = tied(come, sent[0])
        bit = row_bits[stage]
        out = jnp.stack([with_bit(rows, bits, bit, 0), come], axis=bits - 1 - bit)
        return out.reshape((size,) + out.shape[bits:])

    keeps = [k for _, k, _ in parts]
    helds = [h for _, _, h in parts]
    come = send_rows(0, parts[0][0])
    sent = [send(messages, 0) for messages, _, _ in parts]
    cached = attend_cache(query_base, cache_keys, cache_values, cache_lengths, gate)
    cached[0], sent[0][0] = tied(cached[0], sent[0][0])
    came = [[None] * len(widths) for _ in cuts]
    for stage in range(bits - 1):
        for p in range(len(cuts)):
            if p == 0:
                rows = take_rows(stage, come, sent[0])
            messages, keeps[p], helds[p], gate = run_stage(
                bits, stage, unit, sent[p], keeps[p], helds[p], gate
            )
            if p == 0 and stage < bits - 2:
                come = send_rows(stage + 1, messages)
            sent[p] = send(messages, stage + 1)
    grad_weight, square = summed(bits, unit, list(zip(sent, keeps)))

    spreads = gather_orders(bits)

    def last_gather(value, g):
        value, helds[0][g] = tied(value, helds[0][g])
        came[0][g] = swap(helds[0][g], "fsdp", spreads[g][-1])
        return value

    give, square = tied(with_bit(rows, bits, row_bits[-1], 1), square)
    come = swap(give, "fsdp", row_bits[-1])
    if spreads[0][-1] != 0:
        square = last_gather(square, 0)
    square = square + swap(square, "tp", 0)
    far_bits = list(range(1, bits))
    later = {0: [g for g in (0, 1, 2) if spreads[g][-1] == 0], 1: [3]}
    for bit in [0] + far_bits:
        if bit == spreads[0][-1]:
            square, came[0][0] = tied(square, came[0][0])
        other = swap(square, "fsdp", bit)
        for g in later.get(bit, []):
            other = last_gather(other, g)
        if bit != bits - 1:
            square = square + other
    rows = jnp.stack([with_bit(rows, bits, row_bits[-1], 0), come], axis=bits - 1 - row_bits[-1])
    near_sum, near_token = input_near(bits, cuts, unit, learn_grad_out, helds[0], came[0])
    other, near_token = tied(other, near_token)
    hidden_rows = rows.reshape(size * row_count * steps, owned)
    limit = math.sqrt(learn_hidden.shape[0] * size * width_all)
    keep, give = project(
        limit, 1, square, other, grad_weight, key_master, key_first, key_second, hidden_rows,
        row_count * steps,
    )

    give, gated_grad = tied(give, grad_weight)
    key_new, key_first_new, key_second_new, updated_token = updated(
        limit, square, other, gated_grad, key_master, key_first, key_second
    )

    names = list(range(size))
    for bit in far_bits + [0]:
        if bit != 1:
            keep, give = pick(projected, names, bit, 0), pick(projected, names, bit, 1)
        if bit == 0:
            near, far = projected[..., :column_count], projected[..., column_count:]
            projected = near + swap(far, "tp", 0)
            keep, give = pick(projected, names, bit, 0), pick(projected, names, bit, 1)
        names = [name for name in names if not (name >> bit) & 1]
        come = swap(give, "fsdp", bit)
        if bit == 1:
            come, updated_token, came[0][2] = tied(come, updated_token, came[0][2])
        if bit == 2:
            come, came[0][3] = tied(come, came[0][3])
        projected = keep + come
    shape = (row_count, steps, column_count)
    grad_in, far_token = input_far(bits, cuts, unit, other_cot, near_sum, helds[0], came[0])
    step_keys, attention = attend_fresh(
        query_base, keep.reshape(shape), come.reshape(shape), new_values, cached,
        (updated_token, near_token, far_token),
    )
    return (grad_in, key_new, key_first_new, key_second_new, step_keys, attention)


def solution(mesh):
    in_specs = (
        P(("grp", "fsdp"), "tp"),
        P(("grp", "fsdp"), "tp"),
        P(("grp", "tp", "fsdp"), None),
        P(("grp", "tp", "fsdp"), None),
        P(("grp", "tp", "fsdp"), None),
        P(("grp", "fsdp"), None, None),
        P(("grp", "fsdp"), None, "tp"),
        P(("grp", "fsdp"), None, "tp"),
        P(("grp", "fsdp"), None, "tp"),
        P(("grp", "fsdp"), None, "tp"),
        P(("grp", "fsdp")),
    )
    out_specs = (
        P(("grp", "fsdp"), "tp"),
        P(("grp", "tp", "fsdp"), None),
        P(("grp", "tp", "fsdp"), None),
        P(("grp", "tp", "fsdp"), None),
        P(("grp", "fsdp"), None, "tp"),
        P(("grp", "fsdp"), None, "tp"),
    )
    return jax.shard_map(shards, mesh=mesh, in_specs=in_specs, out_specs=out_specs, check_vma=False)
```

time: 245 us -> 90.5 us (0.37)
  waiting for transfers between devices: 177 us -> 40.3 us
  blocking collectives: 35.3 us -> 0 us
  starting transfers between devices: 0.12 us -> 33 us
  between operations: 15.2 us -> 1.51 us
  Pallas kernels: 0 us -> 12 us
  matrix products: 7.78 us -> 0 us
  other arithmetic: 4.83 us -> 0.13 us
    all_gather x2 -> x0, waiting for transfers between devices: 88.8 us -> none  [the longest x1 46.8 us: shards(): every_row = lax.all_gather(relay_cast, ('fsdp', 'tp'), axis=0, tiled=True)]
    reduce_scatter x1 -> x0, waiting for transfers between devices: 87.1 us -> none  [shards(): lax.psum_scatter(unit_scale * contract_rows(learn_hidden, cotangent), 'fs...]
    ppermute x0 -> x26, waiting for transfers between devices: none -> 40.3 us  [swap(): return lax.ppermute(value, axis, [(i, i ^ 1 << bit) for i in range(size)])]
    ppermute x0 -> x26, starting transfers between devices: none -> 33 us  [swap(): return lax.ppermute(value, axis, [(i, i ^ 1 << bit) for i in range(size)])]
    psum x1 -> x0, blocking collectives: 32.7 us -> none  [shards(): square_sum = lax.psum(jnp.sum(grad_weight * grad_weight), ('fsdp', 'tp'))]
    pallas_call x0 -> x12, Pallas kernels: none -> 12 us  [the longest x2 2.84 us: first_stage(): pl.pallas_call(functools.partial(first_kernel, bits, cuts, unit, over), o...]
    dot_general x5 -> x0, matrix products: 7.78 us -> none  [the longest x1 3.66 us: shards(): lax.dot_general(cotangent, lax.all_gather(weight_cast, 'fsdp', axis=0, ti...]
    reshape x2 -> x0, local copies, waits for them, and re-layouts: 3.07 us -> none  [the longest x1 2.44 us: owner_order(): blocks.reshape(shard_count, slice_count, block_rows, width)]
  transfers between devices with their start and end apart: 3 -> 26, of which waited for: 3 -> 15; matrix products, arithmetic and copies ran while one was open for 2% -> 0% of each run, Pallas kernels for 0% -> 11%
where the time goes in v3:
time: 90.5 us; the launch traced here: 90.3 us
  waiting for transfers between devices  40.3 us (45%)
  starting transfers between devices  33 us (36%)
  Pallas kernels  12 us (13%)
  local copies, waits for them, and re-layouts  3.39 us (4%)
  between operations  1.51 us (2%)
    ppermute x26, waiting for transfers between devices, swap(): return lax.ppermute(value, axis, [(i, i ^ 1 << bit) for i in range(size)])  40.3 us
    ppermute x26, starting transfers between devices, swap(): return lax.ppermute(value, axis, [(i, i ^ 1 << bit) for i in range(size)])  33 us
    unnamed x24, local copies, waits for them, and re-layouts  3.37 us
    pallas_call x2, Pallas kernels, first_stage(): pl.pallas_call(functools.partial(first_kernel, bits, cuts, unit, over), o...  2.84 us
    pallas_call x1, Pallas kernels, input_far(): pl.pallas_call(functools.partial(far_kernel, bits, cuts, unit, (2, 3)), o...  2.23 us
  transfers between devices with their start and end apart: 26, of which 15 were waited for; matrix products, arithmetic and copies ran while one was open for 0% of the time, Pallas kernels for 11%

profile of v3, /device:TPU:0, one launch (start us, length us, event | category | flops | bytes accessed | tf_op | source)
XLA Modules:
  0.0 90.3 jit_solution(9949136088737955559)
XLA Ops:
  0.6 0.5 collective-permute-start
  1.2 1.0 %copy-done = f32[240,512]{1,0:T(8,128)S(1)} copy-done((f32[240,512]{1,0:T(8,128)S(1)}, f32[240,512]{1,0:T(8,128)}, u32[]{:S(2)}) %copy-start) | copy-done | bytes 491544
  2.3 1.4 %copy-done.2 = bf16[384,1920]{1,0:T(8,128)(2,1)S(1)} copy-done((bf16[384,1920]{1,0:T(8,128)(2,1)S(1)}, bf16[384,1920]{1,0:T(8,128)(2,1)}, u32[]{:S(2)}) %copy-start.2) | copy-done | bytes 1474584
  3.6 0.9 %copy-done.5 = bf16[384,256]{1,0:T(8,128)(2,1)S(1)} copy-done((bf16[384,256]{1,0:T(8,128)(2,1)S(1)}, bf16[384,256]{1,0:T(8,128)(2,1)}, u32[]{:S(2)}) %copy-start.5) | copy-done | bytes 196632
  4.6 1.4 %shard_map.154 = (bf16[6,240,128]{2,1,0:T(8,128)(2,1)S(1)}, bf16[6,240,128]{2,1,0:T(8,128)(2,1)S(1)}, f32[4,240,128]{2,1,0:T(8,128)S(1)}, f32[4,240,128]{2,1,0:T(8,128)S(1)}, f32[8,128]{1,0:T(8,128)S(1)}) custom-call(s32[2]{0:T(128)S(1)} %pad_add_fusion.where_ref, bf16[384,1920]{1,0:T(8,128)(2,1)S(1)} %copy-done.2, bf16[384,256]{1,0:T(8,128)(2,1)S(1)} %copy-done.5, ...), custom_call_target="tpu_custom_call" | custom-call | flops 1 | bytes 1 | tf_op jit(solution)/shard_map/pallas_call | solution.py:252
  6.0 3.7 %collective-permute-start.2 = (bf16[6,240,128]{2,1,0:T(8,128)(2,1)S(1)}, bf16[6,240,128]{2,1,0:T(8,128)(2,1)S(1)}, u32[]{:S(2)}, u32[]{:S(2)}) collective-permute-start(bf16[6,240,128]{2,1,0:T(8,128)(2,1)S(1)} %get-tuple-element.93), channel_id=1, source_target_pairs={{0,8},{2,10},{4,12},{6,14},{8,0},{10,2},{12,4},{14,6},{1,9},{3,11}... | collective-permute-start | bytes 1105928 | tf_op jit(solution)/shard_map/ppermute | solution.py:40
  9.7 1.6 %collective-permute-start.3 = (bf16[6,240,128]{2,1,0:T(8,128)(2,1)S(1)}, bf16[6,240,128]{2,1,0:T(8,128)(2,1)S(1)}, u32[]{:S(2)}, u32[]{:S(2)}) collective-permute-start(bf16[6,240,128]{2,1,0:T(8,128)(2,1)S(1)} %get-tuple-element.97), channel_id=1, source_target_pairs={{0,4},{2,6},{4,0},{6,2},{8,12},{10,14},{12,8},{14,10},{1,5},{3,7},... | collective-permute-start | bytes 1105928 | tf_op jit(solution)/shard_map/ppermute | solution.py:40
  11.3 1.4 %shard_map.155 = (bf16[4,240,128]{2,1,0:T(8,128)(2,1)S(1)}, bf16[4,240,128]{2,1,0:T(8,128)(2,1)S(1)}, f32[4,240,256]{2,1,0:T(8,128)S(1)}, bf16[1,240,128]{2,1,0:...) custom-call(s32[2]{0:T(128)S(1)} %pad_add_fusion.where_ref, ...), custom_call_target="tpu_custom_call" | custom-call | flops 1 | bytes 1 | tf_op jit(solution)/shard_map/pallas_call | solution.py:252
  12.7 0.6 shard_map.156
  13.4 1.6 %collective-permute-start.5 = (bf16[4,240,128]{2,1,0:T(8,128)(2,1)S(1)}, bf16[4,240,128]{2,1,0:T(8,128)(2,1)S(1)}, u32[]{:S(2)}, u32[]{:S(2)}) collective-permute-start(bf16[4,240,128]{2,1,0:T(8,128)(2,1)S(1)} %get-tuple-element.99), channel_id=1, source_target_pairs={{0,2},{2,0},{4,6},{6,4},{8,10},{10,8},{12,14},{14,12},{1,3},{3,1},... | collective-permute-start | bytes 737288 | tf_op jit(solution)/shard_map/ppermute | solution.py:40
  14.9 0.5 collective-permute-start.4
  15.5 1.5 %collective-permute-start.1 = (bf16[2,2,8,240]{3,2,1,0:T(8,128)(2,1)S(1)}, bf16[2,2,8,240]{3,2,1,0:T(8,128)(2,1)S(1)}, u32[]{:S(2)}, u32[]{:S(2)}) collective-permute-start(bf16[2,2,8,240]{3,2,1,0:T(8,128)(2,1)S(1)} %get-tuple-element.91), channel_id=1, source_target_pairs={{0,2},{2,0},{4,6},{6,4},{8,10},{10,8},{12,14},{14,12},{1,3},{3,1},... | collective-permute-start | bytes 46088 | tf_op jit(solution)/shard_map/ppermute | solution.py:40
  17.6 0.8 shard_map.157
  18.4 8.5 %collective-permute-done.2.refs_0_ = bf16[6,240,128]{2,1,0:T(8,128)(2,1)S(1)} collective-permute-done((bf16[6,240,128]{2,1,0:T(8,128)(2,1)S(1)}, bf16[6,240,128]{2,1,0:T(8,128)(2,1)S(1)}, u32[]{:S(2)}, u32[]{:S(2)}) %collective-permute-start.2) | collective-permute-done | bytes 368672 | tf_op jit(solution)/shard_map/ppermute | solution.py:40
  27.5 1.4 %collective-permute-start.7 = (bf16[6,240,128]{2,1,0:T(8,128)(2,1)S(1)}, bf16[6,240,128]{2,1,0:T(8,128)(2,1)S(1)}, u32[]{:S(2)}, u32[]{:S(2)}) collective-permute-start(bf16[6,240,128]{2,1,0:T(8,128)(2,1)S(1)} %get-tuple-element.109), channel_id=1, source_target_pairs={{0,8},{2,10},{4,12},{6,14},{8,0},{10,2},{12,4},{14,6},{1,9},{3,11}... | collective-permute-start | bytes 1105928 | tf_op jit(solution)/shard_map/ppermute | solution.py:40
  28.9 2.5 %collective-permute-start.8 = (bf16[6,240,128]{2,1,0:T(8,128)(2,1)S(1)}, bf16[6,240,128]{2,1,0:T(8,128)(2,1)S(1)}, u32[]{:S(2)}, u32[]{:S(2)}) collective-permute-start(bf16[6,240,128]{2,1,0:T(8,128)(2,1)S(1)} %get-tuple-element.112), channel_id=1, source_target_pairs={{0,4},{2,6},{4,0},{6,2},{8,12},{10,14},{12,8},{14,10},{1,5},{3,7},... | collective-permute-start | bytes 1105928 | tf_op jit(solution)/shard_map/ppermute | solution.py:40
  31.4 1.6 %collective-permute-start.9 = (bf16[4,240,128]{2,1,0:T(8,128)(2,1)S(1)}, bf16[4,240,128]{2,1,0:T(8,128)(2,1)S(1)}, u32[]{:S(2)}, u32[]{:S(2)}) collective-permute-start(bf16[4,240,128]{2,1,0:T(8,128)(2,1)S(1)} %get-tuple-element.113), channel_id=1, source_target_pairs={{0,2},{2,0},{4,6},{6,4},{8,10},{10,8},{12,14},{14,12},{1,3},{3,1},... | collective-permute-start | bytes 737288 | tf_op jit(solution)/shard_map/ppermute | solution.py:40
  33.0 0.6 collective-permute-start.6
  33.6 13.6 %collective-permute-done.6 = bf16[2,2,8,240]{3,2,1,0:T(8,128)(2,1)S(1)} collective-permute-done((bf16[2,2,8,240]{3,2,1,0:T(8,128)(2,1)S(1)}, bf16[2,2,8,240]{3,2,1,0:T(8,128)(2,1)S(1)}, u32[]{:S(2)}, u32[]{:S(2)}) %collective-permute-start.6) | collective-permute-done | bytes 15392 | tf_op jit(solution)/shard_map/ppermute | solution.py:40
  47.1 0.8 shard_map.159
  47.9 1.3 %collective-permute-start.10 = (bf16[2,240,128]{2,1,0:T(8,128)(2,1)S(1)}, bf16[2,240,128]{2,1,0:T(8,128)(2,1)S(1)}, u32[]{:S(2)}, u32[]{:S(2)}) collective-permute-start(bf16[2,240,128]{2,1,0:T(8,128)(2,1)S(1)} %get-tuple-element.122), channel_id=1, source_target_pairs={{0,8},{2,10},{4,12},{6,14},{8,0},{10,2},{12,4},{14,6},{1,9},{3,11}... | collective-permute-start | bytes 368648 | tf_op jit(solution)/shard_map/ppermute | solution.py:40
  49.2 1.8 %collective-permute-start.11 = (bf16[1,240,128]{2,1,0:T(8,128)(2,1)S(1)}, bf16[1,240,128]{2,1,0:T(8,128)(2,1)S(1)}, u32[]{:S(2)}, u32[]{:S(2)}) collective-permute-start(bf16[1,240,128]{2,1,0:T(8,128)(2,1)S(1)} %get-tuple-element.123), channel_id=1, source_target_pairs={{0,4},{2,6},{4,0},{6,2},{8,12},{10,14},{12,8},{14,10},{1,5},{3,7},... | collective-permute-start | bytes 184328 | tf_op jit(solution)/shard_map/ppermute | solution.py:40
  51.1 1.5 %collective-permute-start.12 = (bf16[1,240,128]{2,1,0:T(8,128)(2,1)S(1)}, bf16[1,240,128]{2,1,0:T(8,128)(2,1)S(1)}, u32[]{:S(2)}, u32[]{:S(2)}) collective-permute-start(bf16[1,240,128]{2,1,0:T(8,128)(2,1)S(1)} %get-tuple-element.124), channel_id=1, source_target_pairs={{0,2},{2,0},{4,6},{6,4},{8,10},{10,8},{12,14},{14,12},{1,3},{3,1},... | collective-permute-start | bytes 184328 | tf_op jit(solution)/shard_map/ppermute | solution.py:40
  52.6 1.5 %collective-permute-done.11.refs_1_ = bf16[1,240,128]{2,1,0:T(8,128)(2,1)S(1)} collective-permute-done((bf16[1,240,128]{2,1,0:T(8,128)(2,1)S(1)}, bf16[1,240,128]{2,1,0:T(8,128)(2,1)S(1)}, u32[]{:S(2)}, u32[]{:S(2)}) %collective-permute-start.11) | collective-permute-done | bytes 61472 | tf_op jit(solution)/shard_map/ppermute | solution.py:40
  54.0 1.2 %collective-permute-done.12.refs_2_ = bf16[1,240,128]{2,1,0:T(8,128)(2,1)S(1)} collective-permute-done((bf16[1,240,128]{2,1,0:T(8,128)(2,1)S(1)}, bf16[1,240,128]{2,1,0:T(8,128)(2,1)S(1)}, u32[]{:S(2)}, u32[]{:S(2)}) %collective-permute-start.12) | collective-permute-done | bytes 61472 | tf_op jit(solution)/shard_map/ppermute | solution.py:40
  55.9 1.2 %collective-permute-done.13 = f32[8,128]{1,0:T(8,128)S(1)} collective-permute-done((f32[8,128]{1,0:T(8,128)S(1)}, f32[8,128]{1,0:T(8,128)S(1)}, u32[]{:S(2)}, u32[]{:S(2)}) %collective-permute-start.13) | collective-permute-done | bytes 4128 | tf_op jit(solution)/shard_map/ppermute | solution.py:40
  57.0 1.5 %collective-permute-start.14 = (f32[8,128]{1,0:T(8,128)S(1)}, f32[8,128]{1,0:T(8,128)S(1)}, u32[]{:S(2)}, u32[]{:S(2)}) collective-permute-start(f32[8,128]{1,0:T(8,128)S(1)} %add.18), channel_id=1, source_target_pairs={{0,2},{2,0},{4,6},{6,4},{8,10},{10,8},{12,14},{14,12},{1,3},{3,1},... | collective-permute-start | bytes 12296 | tf_op jit(solution)/shard_map/ppermute | solution.py:40
  58.5 2.2 %collective-permute-done.14 = f32[8,128]{1,0:T(8,128)S(1)} collective-permute-done((f32[8,128]{1,0:T(8,128)S(1)}, f32[8,128]{1,0:T(8,128)S(1)}, u32[]{:S(2)}, u32[]{:S(2)}) %collective-permute-start.14) | collective-permute-done | bytes 4128 | tf_op jit(solution)/shard_map/ppermute | solution.py:40
  60.6 1.5 %collective-permute-start.16 = (bf16[4,240,128]{2,1,0:T(8,128)(2,1)S(1)}, bf16[4,240,128]{2,1,0:T(8,128)(2,1)S(1)}, u32[]{:S(2)}, u32[]{:S(2)}) collective-permute-start(bf16[4,240,128]{2,1,0:T(8,128)(2,1)S(1)} %get-tuple-element.138.refs_2_), channel_id=1, source_target_pairs={{0,2},{2,0},{4,6},{6,4},{8,10},{10,8},{12,14},{14,12},{1,3},{3,1},... | collective-permute-start | bytes 737288 | tf_op jit(solution)/shard_map/ppermute | solution.py:40
  62.1 0.6 collective-permute-start.21
  62.7 2.0 %collective-permute-start.17 = (f32[8,128]{1,0:T(8,128)S(1)}, f32[8,128]{1,0:T(8,128)S(1)}, u32[]{:S(2)}, u32[]{:S(2)}) collective-permute-start(f32[8,128]{1,0:T(8,128)S(1)} %add.19), channel_id=1, source_target_pairs={{0,4},{2,6},{4,0},{6,2},{8,12},{10,14},{12,8},{14,10},{1,5},{3,7},... | collective-permute-start | bytes 12296 | tf_op jit(solution)/shard_map/ppermute | solution.py:40
  64.6 1.6 %collective-permute-done.17 = f32[8,128]{1,0:T(8,128)S(1)} collective-permute-done((f32[8,128]{1,0:T(8,128)S(1)}, f32[8,128]{1,0:T(8,128)S(1)}, u32[]{:S(2)}, u32[]{:S(2)}) %collective-permute-start.17) | collective-permute-done | bytes 4128 | tf_op jit(solution)/shard_map/ppermute | solution.py:40
  66.3 1.5 %collective-permute-start.23 = (bf16[4,240,128]{2,1,0:T(8,128)(2,1)S(1)}, bf16[4,240,128]{2,1,0:T(8,128)(2,1)S(1)}, u32[]{:S(2)}, u32[]{:S(2)}) collective-permute-start(bf16[4,240,128]{2,1,0:T(8,128)(2,1)S(1)} %get-tuple-element.153.refs_2_), channel_id=1, source_target_pairs={{0,2},{2,0},{4,6},{6,4},{8,10},{10,8},{12,14},{14,12},{1,3},{3,1},... | collective-permute-start | bytes 737288 | tf_op jit(solution)/shard_map/ppermute | solution.py:40
  67.7 1.8 %collective-permute-start.19 = (bf16[2,2,8,240]{3,2,1,0:T(8,128)(2,1)S(1)}, bf16[2,2,8,240]{3,2,1,0:T(8,128)(2,1)S(1)}, u32[]{:S(2)}, u32[]{:S(2)}) collective-permute-start(bf16[2,2,8,240]{3,2,1,0:T(8,128)(2,1)S(1)} %get-tuple-element.147), channel_id=1, source_target_pairs={{0,4},{2,6},{4,0},{6,2},{8,12},{10,14},{12,8},{14,10},{1,5},{3,7},... | collective-permute-start | bytes 46088 | tf_op jit(solution)/shard_map/ppermute | solution.py:40
  69.6 1.5 %collective-permute-start.18 = (f32[8,128]{1,0:T(8,128)S(1)}, f32[8,128]{1,0:T(8,128)S(1)}, u32[]{:S(2)}, u32[]{:S(2)}) collective-permute-start(f32[8,128]{1,0:T(8,128)S(1)} %add.20.square_ref), channel_id=1, source_target_pairs={{0,8},{2,10},{4,12},{6,14},{8,0},{10,2},{12,4},{14,6},{1,9},{3,11}... | collective-permute-start | bytes 12296 | tf_op jit(solution)/shard_map/ppermute | solution.py:40
  71.5 0.9 shard_map.161
  72.4 1.7 %collective-permute-done.18.other_ref = f32[8,128]{1,0:T(8,128)S(1)} collective-permute-done((f32[8,128]{1,0:T(8,128)S(1)}, f32[8,128]{1,0:T(8,128)S(1)}, u32[]{:S(2)}, u32[]{:S(2)}) %collective-permute-start.18) | collective-permute-done | bytes 4128 | tf_op jit(solution)/shard_map/ppermute | solution.py:40
  74.1 0.6 shard_map.162
  74.7 0.4 collective-permute-start.20
  75.1 1.6 %shard_map.163 = (f32[240,512]{1,0:T(8,128)}, f32[240,512]{1,0:T(8,128)}, f32[240,512]{1,0:T(8,128)}, f32[8,128]{1,0:T(8,128)S(1)}) custom-call(f32[8,128]{1,0:T(8,128)S(1)} %add.20.square_ref, f32[8,128]{1,0:T(8,128)S(1)} %collective-permute-done.18.other_ref, f32[240,512]{1,0:T(8,128)S(1)} %get-tuple-element.150.grad_ref, f32[240,512]{1,0:T(8,128)S(1)} %copy-done.1, ...), custom_call_target="tpu_custom_call" | custom-call | flops 1 | bytes 1 | tf_op jit(solution)/shard_map/pallas_call | solution.py:703
  76.8 2.3 %collective-permute-done.20 = f32[4,8,512]{2,1,0:T(8,128)S(1)} collective-permute-done((f32[4,8,512]{2,1,0:T(8,128)S(1)}, f32[4,8,512]{2,1,0:T(8,128)S(1)}, u32[]{:S(2)}, u32[]{:S(2)}) %collective-permute-start.20) | collective-permute-done | bytes 65568 | tf_op jit(solution)/shard_map/ppermute | solution.py:40
  79.1 1.5 %collective-permute-start.22 = (f32[2,8,512]{2,1,0:T(8,128)S(1)}, f32[2,8,512]{2,1,0:T(8,128)S(1)}, u32[]{:S(2)}, u32[]{:S(2)}) collective-permute-start(f32[2,8,512]{2,1,0:T(8,128)S(1)} %stack.47), channel_id=1, source_target_pairs={{0,8},{2,10},{4,12},{6,14},{8,0},{10,2},{12,4},{14,6},{1,9},{3,11}... | collective-permute-start | bytes 98312 | tf_op jit(solution)/shard_map/ppermute | solution.py:40
  80.6 3.7 %collective-permute-done.22 = f32[2,8,512]{2,1,0:T(8,128)S(1)} collective-permute-done((f32[2,8,512]{2,1,0:T(8,128)S(1)}, f32[2,8,512]{2,1,0:T(8,128)S(1)}, u32[]{:S(2)}, u32[]{:S(2)}) %collective-permute-start.22) | collective-permute-done | bytes 32800 | tf_op jit(solution)/shard_map/ppermute | solution.py:40
  84.4 1.2 %collective-permute-done.24 = f32[2,8,256]{2,1,0:T(8,128)S(1)} collective-permute-done((f32[2,8,256]{2,1,0:T(8,128)S(1)}, f32[2,8,256]{2,1,0:T(8,128)S(1)}, u32[]{:S(2)}, u32[]{:S(2)}) %collective-permute-start.24) | collective-permute-done | bytes 16416 | tf_op jit(solution)/shard_map/ppermute | solution.py:40
  85.6 0.6 collective-permute-start.25
  86.1 2.2 %shard_map.164 = (bf16[384,1920]{1,0:T(8,128)(2,1)}, f32[8,128]{1,0:T(8,128)S(1)}) custom-call(s32[1]{0:T(128)} %bitcast.here_ref, bf16[384,256]{1,0:T(8,128)(2,1)S(1)} %collective-permute-done.cot_ref, f32[384,1920]{1,0:T(8,128)S(1)} %get-tuple-element.139.near_ref, bf16[4,240,128]{2,1,0:T(8,128)(2,1)S(1)} %get-tuple-element.140.refs_0_, ...), custom_call_target="tpu_custom_call" | custom-call | flops 1 | bytes 1 | tf_op jit(solution)/shard_map/pallas_call | solution.py:625
  88.4 0.8 collective-permute-done.25.other_ref
  89.2 1.1 %shard_map.165 = (bf16[1,8,256]{2,1,0:T(8,128)(2,1)}, bf16[1,8,2048]{2,1,0:T(8,128)(2,1)}) custom-call(bf16[1,8,2048]{2,1,0:T(8,128)(2,1)S(1)} %copy-done.9, f32[1,8,256]{2,1,0:T(8,128)S(1)} %get-tuple-element.177.keep_ref, f32[1,8,256]{2,1,0:T(8,128)S(1)} %collective-permute-done.25.other_ref, bf16[1,8,256]{2,1,0:T(8,128)(2,1)S(1)} %copy-done.11, ...), custom_call_target="tpu_custom_call" | custom-call | flops 1 | bytes 1 | tf_op jit(solution)/shard_map/pallas_call | solution.py:452
  (55 shorter events, 1.9 us)
Async XLA Ops:
  0.6 10.7 %collective-permute-start = (bf16[384,256]{1,0:T(8,128)(2,1)}, bf16[384,256]{1,0:T(8,128)(2,1)S(1)}, u32[]{:S(2)}, u32[]{:S(2)}) collective-permute-start(bf16[384,256]{1,0:T(8,128)(2,1)} %cot_ref.3), channel_id=1, source_target_pairs={{0,1},{1,0},{2,3},{3,2},{4,5},{5,4},{6,7},{7,6},{8,9},{9,8},{10,11... | collective-permute-start | bytes 589832 | tf_op jit(solution)/shard_map/ppermute | solution.py:40
  1.2 1.0 %copy-start = (f32[240,512]{1,0:T(8,128)S(1)}, f32[240,512]{1,0:T(8,128)}, u32[]{:S(2)}) copy-start(f32[240,512]{1,0:T(8,128)} %master_ref.7) | copy-start | bytes 1474564
  2.3 1.4 %copy-start.2 = (bf16[384,1920]{1,0:T(8,128)(2,1)S(1)}, bf16[384,1920]{1,0:T(8,128)(2,1)}, u32[]{:S(2)}) copy-start(bf16[384,1920]{1,0:T(8,128)(2,1)} %hidden_ref.3) | copy-start | bytes 4423684
  3.6 0.9 %copy-start.5 = (bf16[384,256]{1,0:T(8,128)(2,1)S(1)}, bf16[384,256]{1,0:T(8,128)(2,1)}, u32[]{:S(2)}) copy-start(bf16[384,256]{1,0:T(8,128)(2,1)} %cot_ref.3) | copy-start | bytes 589828
  4.6 6.7 %copy-start.1 = (f32[240,512]{1,0:T(8,128)S(1)}, f32[240,512]{1,0:T(8,128)}, u32[]{:S(2)}) copy-start(f32[240,512]{1,0:T(8,128)} %master_ref.7) | copy-start | bytes 1474564
  6.0 6.7 %copy-start.10 = (bf16[1,8,3840]{2,1,0:T(8,128)(2,1)S(1)}, bf16[1,8,3840]{2,1,0:T(8,128)(2,1)}, u32[]{:S(2)}) copy-start(bf16[1,8,3840]{2,1,0:T(8,128)(2,1)} %param.16) | copy-start | bytes 184324
  6.0 11.6 %copy-start.7 = (bf16[1,1024,256]{2,1,0:T(8,128)(2,1)S(1)}, bf16[1,1024,256]{2,1,0:T(8,128)(2,1)}, u32[]{:S(2)}) copy-start(bf16[1,1024,256]{2,1,0:T(8,128)(2,1)} %keys_ref.1) | copy-start | bytes 1572868
  6.0 11.6 %copy-start.8 = (bf16[1,1024,256]{2,1,0:T(8,128)(2,1)S(1)}, bf16[1,1024,256]{2,1,0:T(8,128)(2,1)}, u32[]{:S(2)}) copy-start(bf16[1,1024,256]{2,1,0:T(8,128)(2,1)} %values_ref.2) | copy-start | bytes 1572868
  6.0 11.6 %copy-start.9 = (bf16[1,8,2048]{2,1,0:T(8,128)(2,1)S(1)}, bf16[1,8,2048]{2,1,0:T(8,128)(2,1)}, u32[]{:S(2)}) copy-start(bf16[1,8,2048]{2,1,0:T(8,128)(2,1)} %query_ref.3) | copy-start | bytes 98308
  6.0 20.9 %collective-permute-start.2 = (bf16[6,240,128]{2,1,0:T(8,128)(2,1)S(1)}, bf16[6,240,128]{2,1,0:T(8,128)(2,1)S(1)}, u32[]{:S(2)}, u32[]{:S(2)}) collective-permute-start(bf16[6,240,128]{2,1,0:T(8,128)(2,1)S(1)} %get-tuple-element.93), channel_id=1, source_target_pairs={{0,8},{2,10},{4,12},{6,14},{8,0},{10,2},{12,4},{14,6},{1,9},{3,11}... | collective-permute-start | bytes 1105928 | tf_op jit(solution)/shard_map/ppermute | solution.py:40
  9.7 17.4 %collective-permute-start.3 = (bf16[6,240,128]{2,1,0:T(8,128)(2,1)S(1)}, bf16[6,240,128]{2,1,0:T(8,128)(2,1)S(1)}, u32[]{:S(2)}, u32[]{:S(2)}) collective-permute-start(bf16[6,240,128]{2,1,0:T(8,128)(2,1)S(1)} %get-tuple-element.97), channel_id=1, source_target_pairs={{0,4},{2,6},{4,0},{6,2},{8,12},{10,14},{12,8},{14,10},{1,5},{3,7},... | collective-permute-start | bytes 1105928 | tf_op jit(solution)/shard_map/ppermute | solution.py:40
  13.4 13.8 %collective-permute-start.5 = (bf16[4,240,128]{2,1,0:T(8,128)(2,1)S(1)}, bf16[4,240,128]{2,1,0:T(8,128)(2,1)S(1)}, u32[]{:S(2)}, u32[]{:S(2)}) collective-permute-start(bf16[4,240,128]{2,1,0:T(8,128)(2,1)S(1)} %get-tuple-element.99), channel_id=1, source_target_pairs={{0,2},{2,0},{4,6},{6,4},{8,10},{10,8},{12,14},{14,12},{1,3},{3,1},... | collective-permute-start | bytes 737288 | tf_op jit(solution)/shard_map/ppermute | solution.py:40
  14.9 12.2 %collective-permute-start.4 = (bf16[4,240,128]{2,1,0:T(8,128)(2,1)S(1)}, bf16[4,240,128]{2,1,0:T(8,128)(2,1)S(1)}, u32[]{:S(2)}, u32[]{:S(2)}) collective-permute-start(bf16[4,240,128]{2,1,0:T(8,128)(2,1)S(1)} %get-tuple-element.98), channel_id=1, source_target_pairs={{0,2},{2,0},{4,6},{6,4},{8,10},{10,8},{12,14},{14,12},{1,3},{3,1},... | collective-permute-start | bytes 737288 | tf_op jit(solution)/shard_map/ppermute | solution.py:40
  15.5 11.5 %collective-permute-start.1 = (bf16[2,2,8,240]{3,2,1,0:T(8,128)(2,1)S(1)}, bf16[2,2,8,240]{3,2,1,0:T(8,128)(2,1)S(1)}, u32[]{:S(2)}, u32[]{:S(2)}) collective-permute-start(bf16[2,2,8,240]{3,2,1,0:T(8,128)(2,1)S(1)} %get-tuple-element.91), channel_id=1, source_target_pairs={{0,2},{2,0},{4,6},{6,4},{8,10},{10,8},{12,14},{14,12},{1,3},{3,1},... | collective-permute-start | bytes 46088 | tf_op jit(solution)/shard_map/ppermute | solution.py:40
  27.5 19.6 %collective-permute-start.7 = (bf16[6,240,128]{2,1,0:T(8,128)(2,1)S(1)}, bf16[6,240,128]{2,1,0:T(8,128)(2,1)S(1)}, u32[]{:S(2)}, u32[]{:S(2)}) collective-permute-start(bf16[6,240,128]{2,1,0:T(8,128)(2,1)S(1)} %get-tuple-element.109), channel_id=1, source_target_pairs={{0,8},{2,10},{4,12},{6,14},{8,0},{10,2},{12,4},{14,6},{1,9},{3,11}... | collective-permute-start | bytes 1105928 | tf_op jit(solution)/shard_map/ppermute | solution.py:40
  28.9 18.2 %collective-permute-start.8 = (bf16[6,240,128]{2,1,0:T(8,128)(2,1)S(1)}, bf16[6,240,128]{2,1,0:T(8,128)(2,1)S(1)}, u32[]{:S(2)}, u32[]{:S(2)}) collective-permute-start(bf16[6,240,128]{2,1,0:T(8,128)(2,1)S(1)} %get-tuple-element.112), channel_id=1, source_target_pairs={{0,4},{2,6},{4,0},{6,2},{8,12},{10,14},{12,8},{14,10},{1,5},{3,7},... | collective-permute-start | bytes 1105928 | tf_op jit(solution)/shard_map/ppermute | solution.py:40
  31.4 15.7 %collective-permute-start.9 = (bf16[4,240,128]{2,1,0:T(8,128)(2,1)S(1)}, bf16[4,240,128]{2,1,0:T(8,128)(2,1)S(1)}, u32[]{:S(2)}, u32[]{:S(2)}) collective-permute-start(bf16[4,240,128]{2,1,0:T(8,128)(2,1)S(1)} %get-tuple-element.113), channel_id=1, source_target_pairs={{0,2},{2,0},{4,6},{6,4},{8,10},{10,8},{12,14},{14,12},{1,3},{3,1},... | collective-permute-start | bytes 737288 | tf_op jit(solution)/shard_map/ppermute | solution.py:40
  33.0 14.1 %collective-permute-start.6 = (bf16[2,2,8,240]{3,2,1,0:T(8,128)(2,1)S(1)}, bf16[2,2,8,240]{3,2,1,0:T(8,128)(2,1)S(1)}, u32[]{:S(2)}, u32[]{:S(2)}) collective-permute-start(bf16[2,2,8,240]{3,2,1,0:T(8,128)(2,1)S(1)} %get-tuple-element.108), channel_id=1, source_target_pairs={{0,8},{2,10},{4,12},{6,14},{8,0},{10,2},{12,4},{14,6},{1,9},{3,11}... | collective-permute-start | bytes 46088 | tf_op jit(solution)/shard_map/ppermute | solution.py:40
  47.1 24.4 %copy-start.6 = (bf16[384,256]{1,0:T(8,128)(2,1)S(1)}, bf16[384,256]{1,0:T(8,128)(2,1)}, u32[]{:S(2)}) copy-start(bf16[384,256]{1,0:T(8,128)(2,1)} %cot_ref.3) | copy-start | bytes 589828
  47.9 26.2 %copy-start.3 = (f32[240,512]{1,0:T(8,128)S(1)}, f32[240,512]{1,0:T(8,128)}, u32[]{:S(2)}) copy-start(f32[240,512]{1,0:T(8,128)} %first_ref.3) | copy-start | bytes 1474564
  47.9 26.2 %copy-start.4 = (f32[240,512]{1,0:T(8,128)S(1)}, f32[240,512]{1,0:T(8,128)}, u32[]{:S(2)}) copy-start(f32[240,512]{1,0:T(8,128)} %second_ref.3) | copy-start | bytes 1474564
  47.9 7.5 %collective-permute-start.10 = (bf16[2,240,128]{2,1,0:T(8,128)(2,1)S(1)}, bf16[2,240,128]{2,1,0:T(8,128)(2,1)S(1)}, u32[]{:S(2)}, u32[]{:S(2)}) collective-permute-start(bf16[2,240,128]{2,1,0:T(8,128)(2,1)S(1)} %get-tuple-element.122), channel_id=1, source_target_pairs={{0,8},{2,10},{4,12},{6,14},{8,0},{10,2},{12,4},{14,6},{1,9},{3,11}... | collective-permute-start | bytes 368648 | tf_op jit(solution)/shard_map/ppermute | solution.py:40
  49.2 4.8 %collective-permute-start.11 = (bf16[1,240,128]{2,1,0:T(8,128)(2,1)S(1)}, bf16[1,240,128]{2,1,0:T(8,128)(2,1)S(1)}, u32[]{:S(2)}, u32[]{:S(2)}) collective-permute-start(bf16[1,240,128]{2,1,0:T(8,128)(2,1)S(1)} %get-tuple-element.123), channel_id=1, source_target_pairs={{0,4},{2,6},{4,0},{6,2},{8,12},{10,14},{12,8},{14,10},{1,5},{3,7},... | collective-permute-start | bytes 184328 | tf_op jit(solution)/shard_map/ppermute | solution.py:40
  51.1 4.2 %collective-permute-start.12 = (bf16[1,240,128]{2,1,0:T(8,128)(2,1)S(1)}, bf16[1,240,128]{2,1,0:T(8,128)(2,1)S(1)}, u32[]{:S(2)}, u32[]{:S(2)}) collective-permute-start(bf16[1,240,128]{2,1,0:T(8,128)(2,1)S(1)} %get-tuple-element.124), channel_id=1, source_target_pairs={{0,2},{2,0},{4,6},{6,4},{8,10},{10,8},{12,14},{14,12},{1,3},{3,1},... | collective-permute-start | bytes 184328 | tf_op jit(solution)/shard_map/ppermute | solution.py:40
  55.7 7.0 %collective-permute-start.15 = (bf16[4,240,128]{2,1,0:T(8,128)(2,1)S(1)}, bf16[4,240,128]{2,1,0:T(8,128)(2,1)S(1)}, u32[]{:S(2)}, u32[]{:S(2)}) collective-permute-start(bf16[4,240,128]{2,1,0:T(8,128)(2,1)S(1)} %get-tuple-element.131.refs_0_), channel_id=1, source_target_pairs={{0,4},{2,6},{4,0},{6,2},{8,12},{10,14},{12,8},{14,10},{1,5},{3,7},... | collective-permute-start | bytes 737288 | tf_op jit(solution)/shard_map/ppermute | solution.py:40
  55.8 1.2 %collective-permute-start.13 = (f32[8,128]{1,0:T(8,128)S(1)}, f32[8,128]{1,0:T(8,128)S(1)}, u32[]{:S(2)}, u32[]{:S(2)}) collective-permute-start(f32[8,128]{1,0:T(8,128)S(1)} %get-tuple-element.132), channel_id=1, source_target_pairs={{0,1},{1,0},{2,3},{3,2},{4,5},{5,4},{6,7},{7,6},{8,9},{9,8},{10,11... | collective-permute-start | bytes 12296 | tf_op jit(solution)/shard_map/ppermute | solution.py:40
  57.0 3.6 %collective-permute-start.14 = (f32[8,128]{1,0:T(8,128)S(1)}, f32[8,128]{1,0:T(8,128)S(1)}, u32[]{:S(2)}, u32[]{:S(2)}) collective-permute-start(f32[8,128]{1,0:T(8,128)S(1)} %add.18), channel_id=1, source_target_pairs={{0,2},{2,0},{4,6},{6,4},{8,10},{10,8},{12,14},{14,12},{1,3},{3,1},... | collective-permute-start | bytes 12296 | tf_op jit(solution)/shard_map/ppermute | solution.py:40
  60.6 10.9 %collective-permute-start.16 = (bf16[4,240,128]{2,1,0:T(8,128)(2,1)S(1)}, bf16[4,240,128]{2,1,0:T(8,128)(2,1)S(1)}, u32[]{:S(2)}, u32[]{:S(2)}) collective-permute-start(bf16[4,240,128]{2,1,0:T(8,128)(2,1)S(1)} %get-tuple-element.138.refs_2_), channel_id=1, source_target_pairs={{0,2},{2,0},{4,6},{6,4},{8,10},{10,8},{12,14},{14,12},{1,3},{3,1},... | collective-permute-start | bytes 737288 | tf_op jit(solution)/shard_map/ppermute | solution.py:40
  62.1 14.7 %collective-permute-start.21 = (bf16[4,240,128]{2,1,0:T(8,128)(2,1)S(1)}, bf16[4,240,128]{2,1,0:T(8,128)(2,1)S(1)}, u32[]{:S(2)}, u32[]{:S(2)}) collective-permute-start(bf16[4,240,128]{2,1,0:T(8,128)(2,1)S(1)} %get-tuple-element.140.refs_0_), channel_id=1, source_target_pairs={{0,2},{2,0},{4,6},{6,4},{8,10},{10,8},{12,14},{14,12},{1,3},{3,1},... | collective-permute-start | bytes 737288 | tf_op jit(solution)/shard_map/ppermute | solution.py:40
  62.7 3.6 %collective-permute-start.17 = (f32[8,128]{1,0:T(8,128)S(1)}, f32[8,128]{1,0:T(8,128)S(1)}, u32[]{:S(2)}, u32[]{:S(2)}) collective-permute-start(f32[8,128]{1,0:T(8,128)S(1)} %add.19), channel_id=1, source_target_pairs={{0,4},{2,6},{4,0},{6,2},{8,12},{10,14},{12,8},{14,10},{1,5},{3,7},... | collective-permute-start | bytes 12296 | tf_op jit(solution)/shard_map/ppermute | solution.py:40
  66.3 18.0 %collective-permute-start.23 = (bf16[4,240,128]{2,1,0:T(8,128)(2,1)S(1)}, bf16[4,240,128]{2,1,0:T(8,128)(2,1)S(1)}, u32[]{:S(2)}, u32[]{:S(2)}) collective-permute-start(bf16[4,240,128]{2,1,0:T(8,128)(2,1)S(1)} %get-tuple-element.153.refs_2_), channel_id=1, source_target_pairs={{0,2},{2,0},{4,6},{6,4},{8,10},{10,8},{12,14},{14,12},{1,3},{3,1},... | collective-permute-start | bytes 737288 | tf_op jit(solution)/shard_map/ppermute | solution.py:40
  67.7 3.7 %collective-permute-start.19 = (bf16[2,2,8,240]{3,2,1,0:T(8,128)(2,1)S(1)}, bf16[2,2,8,240]{3,2,1,0:T(8,128)(2,1)S(1)}, u32[]{:S(2)}, u32[]{:S(2)}) collective-permute-start(bf16[2,2,8,240]{3,2,1,0:T(8,128)(2,1)S(1)} %get-tuple-element.147), channel_id=1, source_target_pairs={{0,4},{2,6},{4,0},{6,2},{8,12},{10,14},{12,8},{14,10},{1,5},{3,7},... | collective-permute-start | bytes 46088 | tf_op jit(solution)/shard_map/ppermute | solution.py:40
  69.6 4.5 %collective-permute-start.18 = (f32[8,128]{1,0:T(8,128)S(1)}, f32[8,128]{1,0:T(8,128)S(1)}, u32[]{:S(2)}, u32[]{:S(2)}) collective-permute-start(f32[8,128]{1,0:T(8,128)S(1)} %add.20.square_ref), channel_id=1, source_target_pairs={{0,8},{2,10},{4,12},{6,14},{8,0},{10,2},{12,4},{14,6},{1,9},{3,11}... | collective-permute-start | bytes 12296 | tf_op jit(solution)/shard_map/ppermute | solution.py:40
  74.7 4.4 %collective-permute-start.20 = (f32[4,8,512]{2,1,0:T(8,128)S(1)}, f32[4,8,512]{2,1,0:T(8,128)S(1)}, u32[]{:S(2)}, u32[]{:S(2)}) collective-permute-start(f32[4,8,512]{2,1,0:T(8,128)S(1)} %get-tuple-element.149), channel_id=1, source_target_pairs={{0,4},{2,6},{4,0},{6,2},{8,12},{10,14},{12,8},{14,10},{1,5},{3,7},... | collective-permute-start | bytes 196616 | tf_op jit(solution)/shard_map/ppermute | solution.py:40
  79.1 5.2 %collective-permute-start.22 = (f32[2,8,512]{2,1,0:T(8,128)S(1)}, f32[2,8,512]{2,1,0:T(8,128)S(1)}, u32[]{:S(2)}, u32[]{:S(2)}) collective-permute-start(f32[2,8,512]{2,1,0:T(8,128)S(1)} %stack.47), channel_id=1, source_target_pairs={{0,8},{2,10},{4,12},{6,14},{8,0},{10,2},{12,4},{14,6},{1,9},{3,11}... | collective-permute-start | bytes 98312 | tf_op jit(solution)/shard_map/ppermute | solution.py:40
  84.3 1.2 %collective-permute-start.24 = (f32[2,8,256]{2,1,0:T(8,128)S(1)}, f32[2,8,256]{2,1,0:T(8,128)S(1)}, u32[]{:S(2)}, u32[]{:S(2)}) collective-permute-start(f32[2,8,256]{2,1,0:T(8,128)S(1)} %slice.53), channel_id=1, source_target_pairs={{0,1},{1,0},{2,3},{3,2},{4,5},{5,4},{6,7},{7,6},{8,9},{9,8},{10,11... | collective-permute-start | bytes 49160 | tf_op jit(solution)/shard_map/ppermute | solution.py:40
  85.6 3.7 %collective-permute-start.25 = (f32[1,8,256]{2,1,0:T(8,128)S(1)}, f32[1,8,256]{2,1,0:T(8,128)S(1)}, u32[]{:S(2)}, u32[]{:S(2)}) collective-permute-start(f32[1,8,256]{2,1,0:T(8,128)S(1)} %get-tuple-element.176), channel_id=1, source_target_pairs={{0,2},{2,0},{4,6},{6,4},{8,10},{10,8},{12,14},{14,12},{1,3},{3,1},... | collective-permute-start | bytes 24584 | tf_op jit(solution)/shard_map/ppermute | solution.py:40
  86.1 3.1 %copy-start.11 = (bf16[1,8,256]{2,1,0:T(8,128)(2,1)S(1)}, bf16[1,8,256]{2,1,0:T(8,128)(2,1)}, u32[]{:S(2)}) copy-start(bf16[1,8,256]{2,1,0:T(8,128)(2,1)} %values_ref.3) | copy-start | bytes 12292

commit v4 on v3

--- a/solution.py
+++ b/solution.py
@@ -35,14 +35,13 @@
     return lax.optimization_barrier(values)
 
 
+def swap_with(value, axis, mask):
+    size = lax.axis_size(axis)
+    return lax.ppermute(value, axis, [(i, i ^ mask) for i in range(size)])
+
+
 def swap(value, axis, bit):
-    size = lax.axis_size(axis)
-    return lax.ppermute(value, axis, [(i, i ^ (1 << bit)) for i in range(size)])
-
-
-def with_bit(blocks, bits, bit, value):
-    split = blocks.reshape((2,) * bits + blocks.shape[1:])
-    return lax.index_in_dim(split, value, bits - 1 - bit, keepdims=False)
+    return swap_with(value, axis, 1 << bit)
 
 
 def pick(blocks, names, bit, value):
@@ -92,6 +91,13 @@
     return out
 
 
+def held_groups(bits, stage):
+    if stage < bits - 1:
+        return [[g] for g in range(len(widths))]
+    low = [g for g, order in enumerate(gather_orders(bits)) if order[-1] == 0]
+    return [[g] for g in range(len(widths)) if g not in low] + [low]
+
+
 def messages_of(bits, stage):
     out = []
     for bit in range(bits - 1, -1, -1):
@@ -102,6 +108,24 @@
         elif what:
             out.append((bit, what))
     return out
+
+
+def row_bits(bits):
+    return [0, 2, 1] if bits == 3 else list(range(bits))
+
+
+def carrier(bits, stage):
+    over = [bit for bit, _ in messages_of(bits, stage)]
+    return len(over) - 1 - over[::-1].index(row_bits(bits)[stage])
+
+
+def names_with(bits, bit):
+    return [name for name in range(1 << bits) if (name >> bit) & 1]
+
+
+def packed_tokens(owned, unit, tokens):
+    fits = owned % 16 == 0 and unit < owned <= 2 * unit and unit % 128 == 0 and tokens % 8 == 0
+    return tokens if fits else 0
 
 
 def kept(order, stage):
@@ -152,23 +176,43 @@
                 out.append(gathered[c][i][u])
         messages.append(out)
     keep_out = [[sums[c][i] for i in kept(orders[c], stage + 1)] for c in range(len(units))]
-    return messages, keep_out, gathered
-
-
-def stage_shapes(bits, stage, rows, unit):
-    messages = [
-        jax.ShapeDtypeStruct((len(what), rows, unit), jnp.bfloat16)
-        for _, what in messages_of(bits, stage)
-    ]
+    held_out = [[b for g in group for b in gathered[g]] for group in held_groups(bits, stage + 1)]
+    return messages, keep_out, held_out
+
+
+def stage_shapes(bits, stage, rows, unit, tokens):
+    messages = []
+    for m, (_, what) in enumerate(messages_of(bits, stage)):
+        more = (tokens << bits) if tokens and m == carrier(bits, stage) else 0
+        messages.append(jax.ShapeDtypeStruct((len(what) * rows + more, unit), jnp.bfloat16))
     keeps = [
         jax.ShapeDtypeStruct((len(kept(order, stage)), rows, units[c] * unit), jnp.float32)
         for c, order in enumerate(sum_orders(bits))
     ]
     helds = [
-        jax.ShapeDtypeStruct((len(gather_names(order, stage)), rows, widths[g] * unit), jnp.bfloat16)
-        for g, order in enumerate(gather_orders(bits))
+        jax.ShapeDtypeStruct((len(group) << stage, rows, unit), jnp.bfloat16)
+        for group in held_groups(bits, stage)
     ]
-    return messages, keeps, helds
+    state = [jax.ShapeDtypeStruct((1 << bits, 2 * tokens, unit), jnp.bfloat16)] if tokens else []
+    return messages, keeps, helds, state
+
+
+def put_rows(bits, stage, rows, messages, state):
+    m = carrier(bits, stage)
+    base = len(messages_of(bits, stage)[m][1]) * rows
+    count = state[0].shape[0]
+    for j, name in enumerate(names_with(bits, row_bits(bits)[stage])):
+        messages[m][base + j * count : base + (j + 1) * count, :] = state[name]
+
+
+def take_rows(bits, stage, rows, came, state):
+    m = carrier(bits, stage)
+    base = len(messages_of(bits, stage)[m][1]) * rows
+    count = state[0].shape[0]
+    out = list(state)
+    for j, name in enumerate(names_with(bits, row_bits(bits)[stage])):
+        out[name] = came[m][base + j * count : base + (j + 1) * count, :]
+    return out
 
 
 def put_blocks(ref, blocks, unit):
@@ -177,22 +221,56 @@
             ref[i, :, u * unit : (u + 1) * unit] = part
 
 
-def first_kernel(bits, cuts, unit, over, where_ref, hidden_ref, cot_ref, master_ref, gate_ref, *refs):
-    outs, token_ref, total = refs[:-2], refs[-2], refs[-1]
-    token_ref[...] = jnp.zeros(token_ref.shape, jnp.float32)
+def first_kernel(bits, cuts, unit, over, slices, where_ref, *refs):
+    refs = list(refs)
     orders = sum_orders(bits)
+    here, core = where_ref[0], where_ref[1]
+    half = 2 * unit
+    if 0 in over:
+        hidden_ref, cot_ref, weight_ref, tokens_ref = refs[:4]
+        outs, token_ref, total = refs[5:-2], refs[-2], refs[-1]
+        waits = []
+    else:
+        cot_ref, weight_ref = refs[-3], None
+        outs, (hidden_ref, weight_out, tokens_ref, token_ref), (total, _, master_ref, done) = (
+            refs[5:-8], refs[-8:-4], refs[-4:]
+        )
     columns = hidden_ref.shape[1]
     owned = columns >> bits
-    half = 2 * unit
     step = 384 if columns % 384 == 0 else columns
+    if 0 not in over:
+        ends = [(refs[1], cot_ref)]
+        tokens = hidden_ref.shape[0]
+        ends += [
+            (refs[0].at[low : low + tokens // 2, at : at + step], hidden_ref.at[low : low + tokens // 2, at : at + step])
+            for at in range(0, columns, step)
+            for low in range(0, tokens, tokens // 2)
+        ]
+        ends += [(refs[2], master_ref), (refs[3], tokens_ref)]
+        waits = [pltpu.make_async_copy(a, b, done.at[i]) for i, (a, b) in enumerate(ends)]
+        for copy in waits:
+            copy.start()
+        waits.pop(0).wait()
     for at in range(0, columns, step):
+        for _ in range(2 if waits else 0):
+            waits.pop(0).wait()
         total[at : at + step, :] = unit_scale * lax.dot_general(
             hidden_ref[:, at : at + step],
             cot_ref[...],
             (((0,), (0,)), ((), ())),
             preferred_element_type=jnp.float32,
         )
-    here, core = where_ref[0], where_ref[1]
+    if waits:
+        waits.pop(0).wait()
+        weight = master_ref[...].astype(jnp.bfloat16)
+        near = jnp.where(core == 0, weight[:, :half], weight[:, half:])
+        far = jnp.where(core == 0, weight[:, half:], weight[:, :half])
+        weight = jnp.concatenate([near, far], axis=1)
+        weight_out[...] = weight
+        waits.pop(0).wait()
+    else:
+        weight = weight_ref[...]
+    token_ref[...] = jnp.zeros(token_ref.shape, jnp.float32)
     sums = [c for c, order in enumerate(orders) if order[0] in over]
     origin = start_of(units, sums[0])
     at = 0
@@ -205,6 +283,8 @@
         at += len(sums)
         helds = outs[at : at + len(widths)] if 0 in over else []
         at += len(helds)
+        state = outs[at] if 0 in over else None
+        at += 0 in over
 
         def block(c, index):
             name = sum_names(orders[c], 0)[index]
@@ -212,10 +292,6 @@
             first = (start_of(units, c) - origin) * unit
             return total[pl.ds(start, rows), first : first + units[c] * unit]
 
-        weight = master_ref[low:high, :].astype(jnp.bfloat16)
-        near = jnp.where(core == 0, weight[:, :half], weight[:, half:])
-        far = jnp.where(core == 0, weight[:, half:], weight[:, :half])
-        weight = jnp.concatenate([near, far], axis=1)
         for c in sums:
             for i, index in enumerate(kept(orders[c], 0)):
                 keeps[c][i] = block(c, index)
@@ -227,44 +303,79 @@
                 if kind == "sum":
                     if j == 0 or what[j - 1][:3] != (kind, c, i):
                         give = block(c, given(orders[c], 0)[i]).astype(jnp.bfloat16)
-                    message[j] = give[:, u * unit : (u + 1) * unit]
+                    message[j * rows : (j + 1) * rows, :] = give[:, u * unit : (u + 1) * unit]
                 else:
                     first = (start_of(widths, c) + u) * unit
-                    message[j] = weight[:, first : first + unit]
-
-
-def first_stage(bits, cuts, unit, hidden, near, far, master):
+                    message[j * rows : (j + 1) * rows, :] = weight[:, first : first + unit]
+        if 0 in over:
+            for part in range(slices):
+
+                @pl.when(core == part)
+                def _():
+                    wide = tokens_ref[...].astype(jnp.float32)
+                    for index in range(1 << bits):
+                        at = (part << bits) * owned + index * owned
+                        low = wide[:, at : at + unit]
+                        high = wide[:, at + unit : at + owned]
+                        blank = jnp.zeros((high.shape[0], 2 * unit - owned), jnp.float32)
+                        high = jnp.concatenate([high, blank], axis=1)
+                        state[here ^ index] = jnp.concatenate([low, high], axis=0).astype(
+                            jnp.bfloat16
+                        )
+
+            first = len(messages_of(bits, 0)) - len(messages)
+            padded = [None] * first + list(messages)
+            put_rows(bits, 0, rows, padded, [state[name] for name in range(1 << bits)])
+
+
+def first_stage(bits, cuts, unit, hidden, near, far, master, rollout, slices, tokens):
     orders = sum_orders(bits)
     owned = hidden.shape[1] >> bits
     here = lax.axis_index("fsdp").astype(jnp.int32)
     core = lax.axis_index("tp").astype(jnp.int32)
     token = jnp.zeros(TOKEN.shape, TOKEN.dtype)
-    if bits == 3 and owned % 16 == 0:
-        result = [([], [None] * len(units), []) for _ in cuts]
-        for over, cot in (((2, 1), near), ((0,), far)):
+    if bits == 3 and tokens:
+        result = [([], [None] * len(units), [], []) for _ in cuts]
+        reads = [
+            pltpu.with_memory_space_constraint(a, pltpu.HBM) for a in (hidden, near, master, rollout)
+        ]
+        for over in ((2, 1), (0,)):
             sums = [c for c, order in enumerate(orders) if order[0] in over]
             which = [m for m, (bit, _) in enumerate(messages_of(bits, 0)) if bit in over]
             shapes = []
             for low, high in cuts:
-                messages, keeps, helds = stage_shapes(bits, 0, high - low, unit)
+                messages, keeps, helds, state = stage_shapes(bits, 0, high - low, unit, tokens)
                 shapes += [messages[m] for m in which] + [keeps[c] for c in sums]
-                shapes += helds if 0 in over else []
+                shapes += helds + state if 0 in over else []
+            scratch = [pltpu.VMEM((hidden.shape[1], near.shape[1]), jnp.float32)]
+            if 0 not in over:
+                shapes.append(jax.ShapeDtypeStruct(hidden.shape, hidden.dtype))
+                shapes.append(jax.ShapeDtypeStruct(master.shape, jnp.bfloat16))
+                shapes.append(jax.ShapeDtypeStruct(rollout.shape, rollout.dtype))
+                step = 384 if hidden.shape[1] % 384 == 0 else hidden.shape[1]
+                scratch.append(pltpu.VMEM(near.shape, near.dtype))
+                scratch.append(pltpu.VMEM(master.shape, master.dtype))
+                scratch.append(pltpu.SemaphoreType.DMA((3 + 2 * (hidden.shape[1] // step),)))
+            place = VMEM if 0 in over else pl.BlockSpec(memory_space=pltpu.HBM)
             outs = pl.pallas_call(
-                functools.partial(first_kernel, bits, cuts, unit, over),
+                functools.partial(first_kernel, bits, cuts, unit, over, slices),
                 out_shape=shapes + [TOKEN],
-                in_specs=[SMEM] + [VMEM] * 4,
+                in_specs=[SMEM] + [place] * 4 + [VMEM],
                 out_specs=[VMEM] * (len(shapes) + 1),
-                scratch_shapes=[pltpu.VMEM((hidden.shape[1], cot.shape[1]), jnp.float32)],
+                scratch_shapes=scratch,
                 compiler_params=SMALL,
                 cost_estimate=TINY,
-            )(jnp.stack([here, core]), hidden, cot, master, token)
+            )(jnp.stack([here, core]), *reads, token)
             token, outs = outs[-1], list(outs[:-1])
-            for messages, keeps, helds in result:
+            for messages, keeps, helds, state in result:
                 messages += [outs.pop(0) for _ in which]
                 for c in sums:
                     keeps[c] = outs.pop(0)
                 if 0 in over:
                     helds += [outs.pop(0) for _ in widths]
+                    state += [outs.pop(0)]
+            if 0 not in over:
+                reads = [outs[0], far, outs[1], outs[2]]
         return result, token
     product = unit_scale * lax.dot_general(
         hidden,
@@ -293,7 +404,7 @@
                 else:
                     first = (start_of(widths, c) + u) * unit
                     blocks.append(weight[low:high, first : first + unit])
-            messages.append(jnp.stack(blocks))
+            messages.append(jnp.concatenate(blocks, axis=0))
         keeps = [
             jnp.stack([block(c, index) for index in kept(order, 0)])
             for c, order in enumerate(orders)
@@ -302,37 +413,42 @@
         for g, width in enumerate(widths):
             first = start_of(widths, g) * unit
             helds.append(weight[None, low:high, first : first + width * unit])
-        result.append((messages, keeps, helds))
+        result.append((messages, keeps, helds, []))
     return result, token
 
 
 def stage_kernel(bits, stage, unit, counts, *refs):
     refs = list(refs)
-    came, keeps, helds = (tuple(refs.pop(0) for _ in range(n)) for n in counts)
+    came, keeps, helds, state = (tuple(refs.pop(0) for _ in range(n)) for n in counts)
     token_ref = refs.pop()
     token_ref[...] = jnp.zeros(token_ref.shape, jnp.float32)
     outs = refs[1:]
+    rows = keeps[0].shape[1]
     messages, keep_out, gathered = next_stage(
         bits,
         stage,
         unit,
-        lambda m, i: came[m][i],
+        lambda m, i: came[m][i * rows : (i + 1) * rows, :],
         lambda c, i: keeps[c][i],
         lambda g, i: helds[g][i],
     )
     for ref, blocks in zip(outs, messages):
         for i, block in enumerate(blocks):
-            ref[i] = block
+            ref[i * rows : (i + 1) * rows, :] = block
     for ref, blocks in zip(outs[len(messages) :], keep_out + gathered):
         put_blocks(ref, blocks, unit)
-
-
-def run_stage(bits, stage, unit, came, keeps, helds, gate):
+    names = take_rows(bits, stage, rows, came, [state[0][name] for name in range(1 << bits)])
+    for name, block in enumerate(names):
+        outs[-1][name] = block
+    put_rows(bits, stage + 1, rows, outs, names)
+
+
+def run_stage(bits, stage, unit, came, keeps, helds, state, gate, tokens):
     rows = keeps[0].shape[1]
-    groups = stage_shapes(bits, stage + 1, rows, unit)
-    if rows % 16 == 0:
+    groups = stage_shapes(bits, stage + 1, rows, unit, tokens)
+    if tokens:
         shapes = [shape for group in groups for shape in group]
-        counts = (len(came), len(keeps), len(helds))
+        counts = (len(came), len(keeps), len(helds), len(state))
         outs = pl.pallas_call(
             functools.partial(stage_kernel, bits, stage, unit, counts),
             out_shape=shapes + [TOKEN],
@@ -340,22 +456,23 @@
             out_specs=[VMEM] * (len(shapes) + 1),
             compiler_params=SMALL,
             cost_estimate=TINY,
-        )(*came, *keeps, *helds, gate)
+        )(*came, *keeps, *helds, *state, gate)
         outs = list(outs)
         return [[outs.pop(0) for _ in group] for group in groups] + [outs[-1]]
     messages, keep_out, gathered = next_stage(
         bits,
         stage,
         unit,
-        lambda m, i: came[m][i],
+        lambda m, i: came[m][i * rows : (i + 1) * rows],
         lambda c, i: keeps[c][i],
         lambda g, i: helds[g][i],
     )
     whole = lambda blocks: jnp.stack([jnp.concatenate(parts, axis=1) for parts in blocks])
     return (
-        [jnp.stack(blocks) for blocks in messages],
+        [jnp.concatenate(blocks, axis=0) for blocks in messages],
         [whole(blocks) for blocks in keep_out],
         [whole(blocks) for blocks in gathered],
+        [],
         gate,
     )
 
@@ -462,112 +579,102 @@
     )(query, keep, other, values, *cached, *gates)
 
 
-def rows_kernel(slices, where_ref, hidden_ref, gate_ref, out_ref):
-    size, _, owned = out_ref.shape
-    for half in range(slices):
-
-        @pl.when(where_ref[1] == half)
-        def _():
-            for index in range(size):
-                at = (half * size + index) * owned
-                out_ref[where_ref[0] ^ index] = hidden_ref[:, at : at + owned]
-
-
-def rows_by_owner(hidden, slices, size, gate):
+def rows_by_owner(hidden, slices, size):
     tokens, width = hidden.shape
-    owned = width // slices // size
+    cut = hidden.reshape(tokens, slices, size, width // slices // size)
+    cut = lax.dynamic_index_in_dim(cut, lax.axis_index("tp"), 1, keepdims=False)
     here = lax.axis_index("fsdp").astype(jnp.int32)
-    core = lax.axis_index("tp").astype(jnp.int32)
-    if owned % 16 != 0:
-        cut = hidden.reshape(tokens, slices, size, owned)
-        cut = lax.dynamic_index_in_dim(cut, core, 1, keepdims=False).transpose(1, 0, 2)
-        return cut[here ^ jnp.arange(size, dtype=jnp.int32)]
-    return pl.pallas_call(
-        functools.partial(rows_kernel, slices),
-        out_shape=jax.ShapeDtypeStruct((size, tokens, owned), hidden.dtype),
-        in_specs=[SMEM, VMEM, VMEM],
-        out_specs=VMEM,
-        compiler_params=SMALL,
-        cost_estimate=TINY,
-    )(jnp.stack([here, core]), hidden, gate)
-
-
-def sum_kernel(bits, unit, parts, here_ref, *refs):
-    inputs, grad_ref, square_ref = list(refs[:-2]), refs[-2], refs[-1]
+    return cut.transpose(1, 0, 2)[here ^ jnp.arange(size, dtype=jnp.int32)]
+
+
+def sum_kernel(bits, unit, counts, here_ref, *refs):
+    refs = list(refs)
+    came, keeps, state = (tuple(refs.pop(0) for _ in range(n)) for n in counts)
+    grad_ref, square_ref = refs[:2]
     half = 2 * unit
-    square = jnp.zeros((1, 1), jnp.float32)
     place = {}
     for m, (_, what) in enumerate(messages_of(bits, bits - 1)):
         for i, key in enumerate(what):
             place[key] = (m, i)
-    low = 0
-    for came_count, keep_count in parts:
-        came = [inputs.pop(0) for _ in range(came_count)]
-        keeps = [inputs.pop(0) for _ in range(keep_count)]
-        rows = keeps[0].shape[1]
-        pieces = []
-        for c in range(len(units)):
-            where = [place[("sum", c, 0, u)] for u in range(units[c])]
-            add = [came[m][i] for m, i in where]
-            add = add[0] if len(add) == 1 else jnp.concatenate(add, axis=1)
-            pieces.append(keeps[c][0] + add.astype(jnp.float32))
-        near = jnp.concatenate(pieces[:2], axis=1)
-        far = pieces[2]
-        here = here_ref[0]
-        grad_ref[low : low + rows, :half] = jnp.where(here == 0, near, far)
-        grad_ref[low : low + rows, half:] = jnp.where(here == 0, far, near)
-        square = square + jnp.sum(near * near + far * far, keepdims=True)
-        low += rows
+    rows = keeps[0].shape[1]
+    pieces = []
+    for c in range(len(units)):
+        where = [place[("sum", c, 0, u)] for u in range(units[c])]
+        add = [came[m][i * rows : (i + 1) * rows, :] for m, i in where]
+        add = add[0] if len(add) == 1 else jnp.concatenate(add, axis=1)
+        pieces.append(keeps[c][0] + add.astype(jnp.float32))
+    near = jnp.concatenate(pieces[:2], axis=1)
+    far = pieces[2]
+    here = here_ref[0]
+    grad_ref[:, :half] = jnp.where(here == 0, near, far)
+    grad_ref[:, half:] = jnp.where(here == 0, far, near)
+    square = jnp.sum(near * near + far * far, keepdims=True)
     square_ref[...] = jnp.broadcast_to(square, square_ref.shape)
-
-
-def summed(bits, unit, parts):
-    flat = [a for came, keeps in parts for a in list(came) + list(keeps)]
-    rows = sum(keeps[0].shape[1] for _, keeps in parts)
-    counts = [(len(came), len(keeps)) for came, keeps in parts]
+    if state:
+        names = [state[0][name] for name in range(1 << bits)]
+        for name, block in enumerate(take_rows(bits, bits - 1, rows, came, names)):
+            refs[2][name] = block
+
+
+def summed(bits, unit, came, keeps, state):
+    rows = keeps[0].shape[1]
+    counts = (len(came), len(keeps), len(state))
     return pl.pallas_call(
         functools.partial(sum_kernel, bits, unit, counts),
         out_shape=[
             jax.ShapeDtypeStruct((rows, 4 * unit), jnp.float32),
             jax.ShapeDtypeStruct((8, 128), jnp.float32),
-        ],
-        in_specs=[SMEM] + [VMEM] * len(flat),
-        out_specs=[VMEM] * 2,
+        ]
+        + [jax.ShapeDtypeStruct(a.shape, a.dtype) for a in state],
+        in_specs=[SMEM] + [VMEM] * sum(counts),
+        out_specs=[VMEM] * (2 + len(state)),
         compiler_params=SMALL,
         cost_estimate=TINY,
-    )(lax.axis_index("tp").astype(jnp.int32).reshape(1), *flat)
-
-
-def lay_out(bits, cuts, unit, which, here, blocks, weight):
-    owned = cuts[-1][1]
-    at = 0
-    for low, high in cuts:
-        for lane, g in enumerate(which):
-            order = gather_orders(bits)[g]
-            lanes = slice(lane * unit, (lane + 1) * unit)
-            old = gather_names(order, bits - 1)
-            for names in (old, [name | (1 << order[-1]) for name in old]):
-                for i, name in enumerate(names):
-                    start = pl.multiple_of((here ^ name) * owned + low, 16)
-                    weight[pl.ds(start, high - low), lanes] = blocks[at][i]
-                at += 1
-
-
-def near_kernel(bits, cuts, unit, which, here_ref, cot_ref, *refs):
+    )(lax.axis_index("tp").astype(jnp.int32).reshape(1), *came, *keeps, *state)
+
+
+def lay_out(bits, unit, which, here, owned, held, weight):
+    for lane, g in enumerate(which):
+        order = gather_orders(bits)[g]
+        lanes = slice(lane * unit, (lane + 1) * unit)
+        for i, name in enumerate(gather_names(order, bits - 1)):
+            for late in (False, True):
+                owner = here ^ (name | (late << order[-1]))
+                start = pl.multiple_of(owner * owned, 16)
+                weight[pl.ds(start, owned), lanes] = held(g, i, late)
+
+
+def held_place(bits, g, i):
+    for at, group in enumerate(held_groups(bits, bits - 1)):
+        if g in group:
+            return at, (group.index(g) << (bits - 1)) + i
+
+
+def block_reader(bits, refs):
+    count = len(refs) // 2
+
+    def held(g, i, late):
+        at, index = held_place(bits, g, i)
+        return refs[at + count * late][index]
+
+    return held
+
+
+def near_kernel(bits, unit, which, here_ref, cot_ref, gate_ref, *refs):
     blocks, out_ref, token_ref, weight = refs[:-3], refs[-3], refs[-2], refs[-1]
     token_ref[...] = jnp.zeros(token_ref.shape, jnp.float32)
-    lay_out(bits, cuts, unit, which, here_ref[0], blocks, weight)
     columns = out_ref.shape[1]
+    lay_out(bits, unit, which, here_ref[0], columns >> bits, block_reader(bits, blocks), weight)
     tile = 384 if columns % 384 == 0 else columns
     for at in range(0, columns, tile):
         out_ref[:, at : at + tile] = contract_last(cot_ref[...], weight[at : at + tile, :])
 
 
-def far_kernel(bits, cuts, unit, which, here_ref, cot_ref, near_ref, *refs):
+def far_kernel(bits, unit, which, here_ref, cot_ref, near_ref, *refs):
     blocks, out_ref, token_ref, weight, result, done = refs[:-5], *refs[-5:]
     token_ref[...] = jnp.zeros(token_ref.shape, jnp.float32)
-    lay_out(bits, cuts, unit, which, here_ref[0], blocks, weight)
-    count = result.shape[0]
+    count, columns = result.shape
+    lay_out(bits, unit, which, here_ref[0], columns >> bits, block_reader(bits, blocks), weight)
     tile = count // done.shape[0]
     copies = []
     for i in range(done.shape[0]):
@@ -584,46 +691,46 @@
 INPUT = pltpu.CompilerParams(vmem_limit_bytes=24 * 1024 * 1024)
 
 
-def gathered_columns(bits, which, helds, came):
+def gathered_columns(bits, which, blocks):
     here = lax.axis_index("fsdp").astype(jnp.int32)
     place = here ^ jnp.arange(1 << bits, dtype=jnp.int32)
+    held = block_reader(bits, blocks)
     weight = []
     for g in which:
         order = gather_orders(bits)[g]
         old = gather_names(order, bits - 1)
         names = old + [name | (1 << order[-1]) for name in old]
-        blocks = jnp.concatenate([helds[g], came[g]], axis=0)[jnp.argsort(jnp.array(names))]
-        weight.append(blocks[place].reshape(-1, blocks.shape[-1]))
+        pieces = [held(g, i, late) for late in (False, True) for i in range(len(old))]
+        pieces = jnp.stack(pieces)[jnp.argsort(jnp.array(names))]
+        weight.append(pieces[place].reshape(-1, pieces.shape[-1]))
     return jnp.concatenate(weight, axis=1)
 
 
-def input_near(bits, cuts, unit, cot, helds, came):
-    columns = cuts[-1][1] << bits
-    if cuts[-1][1] % 16 != 0:
-        product = contract_last(cot, gathered_columns(bits, (0, 1), helds, came))
-        return product, jnp.zeros(TOKEN.shape, TOKEN.dtype)
-    blocks = [a for g in (0, 1) for a in (helds[g], came[g])]
+def input_near(bits, owned, unit, cot, blocks, gate):
+    columns = owned << bits
+    if owned % 16 != 0:
+        product = contract_last(cot, gathered_columns(bits, (0, 1), blocks))
+        return product, gate
     return pl.pallas_call(
-        functools.partial(near_kernel, bits, cuts, unit, (0, 1)),
+        functools.partial(near_kernel, bits, unit, (0, 1)),
         out_shape=[jax.ShapeDtypeStruct((cot.shape[0], columns), jnp.float32), TOKEN],
-        in_specs=[SMEM] + [VMEM] * (1 + len(blocks)),
+        in_specs=[SMEM] + [VMEM] * (2 + len(blocks)),
         out_specs=[VMEM] * 2,
         scratch_shapes=[pltpu.VMEM((columns, 2 * unit), jnp.bfloat16)],
         compiler_params=INPUT,
         cost_estimate=TINY,
-    )(lax.axis_index("fsdp").astype(jnp.int32).reshape(1), cot, *blocks)
-
-
-def input_far(bits, cuts, unit, cot, near, helds, came):
-    columns = cuts[-1][1] << bits
-    if cuts[-1][1] % 16 != 0:
-        product = near + contract_last(cot, gathered_columns(bits, (2, 3), helds, came))
+    )(lax.axis_index("fsdp").astype(jnp.int32).reshape(1), cot, gate, *blocks)
+
+
+def input_far(bits, owned, unit, cot, near, blocks):
+    columns = owned << bits
+    if owned % 16 != 0:
+        product = near + contract_last(cot, gathered_columns(bits, (2, 3), blocks))
         return (unit_scale * product).astype(jnp.bfloat16), jnp.zeros(TOKEN.shape, TOKEN.dtype)
-    blocks = [a for g in (2, 3) for a in (helds[g], came[g])]
     tokens = cot.shape[0]
     pieces = 4 if tokens % 64 == 0 else 1
     return pl.pallas_call(
-        functools.partial(far_kernel, bits, cuts, unit, (2, 3)),
+        functools.partial(far_kernel, bits, unit, (2, 3)),
         out_shape=[jax.ShapeDtypeStruct((tokens, columns), jnp.bfloat16), TOKEN],
         in_specs=[SMEM] + [VMEM] * (2 + len(blocks)),
         out_specs=[pl.BlockSpec(memory_space=pl.ANY), VMEM],
@@ -650,33 +757,39 @@
 
 
 def project_kernel(
-    limit, bit, where_ref, square_ref, other_ref, grad_ref, master_ref, first_ref, second_ref,
+    limit, where_ref, square_ref, other_ref, grad_ref, master_ref, first_ref, second_ref,
     hidden_ref, keep_ref, give_ref
 ):
     square = square_ref[:1, :1] + other_ref[:1, :1]
     factor = jnp.minimum(1.0, limit / jnp.sqrt(square))
     relay = adamw(factor, grad_ref[...], master_ref[...], first_ref[...], second_ref[...])[0]
-    product = jnp.dot(
-        hidden_ref[...], relay.astype(jnp.bfloat16), preferred_element_type=jnp.float32
-    )
+    relay = relay.astype(jnp.bfloat16)
+    tokens = keep_ref.shape[1]
+    if len(hidden_ref.shape) == 3:
+        unit = hidden_ref.shape[2]
+        blocks = [hidden_ref[i].astype(jnp.float32) for i in range(hidden_ref.shape[0])]
+        low = jnp.concatenate([block[:tokens] for block in blocks], axis=0)
+        high = jnp.concatenate([block[tokens:] for block in blocks], axis=0)
+        high = high[:, : relay.shape[0] - unit]
+        product = jnp.dot(
+            low.astype(jnp.bfloat16), relay[:unit], preferred_element_type=jnp.float32
+        ) + jnp.dot(high.astype(jnp.bfloat16), relay[unit:], preferred_element_type=jnp.float32)
+    else:
+        product = jnp.dot(hidden_ref[...], relay, preferred_element_type=jnp.float32)
     core = where_ref[0]
     half = product.shape[1] // 2
     near = jnp.where(core == 0, product[:, :half], product[:, half:])
     far = jnp.where(core == 0, product[:, half:], product[:, :half])
-    _, tokens, _ = keep_ref.shape
-    names = range(2 * keep_ref.shape[0])
-    for ref, value in ((keep_ref, 0), (give_ref, 1)):
-        for i, name in enumerate(name for name in names if (name >> bit) & 1 == value):
-            rows = slice(name * tokens, (name + 1) * tokens)
-            ref[i, :, :half] = near[rows]
-            ref[i, :, half:] = far[rows]
-
-
-def project(limit, bit, square, other, grad, master, first, second, hidden, tokens):
-    count = hidden.shape[0] // tokens // 2
-    shape = jax.ShapeDtypeStruct((count, tokens, master.shape[1]), jnp.float32)
+    for i in range(keep_ref.shape[0]):
+        keep_ref[i] = near[i * tokens : (i + 1) * tokens]
+        give_ref[i] = far[i * tokens : (i + 1) * tokens]
+
+
+def project(limit, square, other, grad, master, first, second, hidden, size, tokens):
+    half = master.shape[1] // 2
+    shape = jax.ShapeDtypeStruct((size, tokens, half), jnp.float32)
     return pl.pallas_call(
-        functools.partial(project_kernel, limit, bit),
+        functools.partial(project_kernel, limit),
         out_shape=[shape] * 2,
         in_specs=[SMEM] + [VMEM] * 7,
         out_specs=[VMEM] * 2,
@@ -731,78 +844,72 @@
     row_count, steps, _ = rollout_hidden.shape
     unit = column_count // 2
     cuts = [(0, owned)]
+    tokens = row_count * steps
+    packed = packed_tokens(owned, unit, tokens) if bits == 3 else 0
 
     other_cot = swap(learn_grad_out, "tp", 0)
+    rollout = rollout_hidden.reshape(tokens, -1)
     parts, gate = first_stage(
-        bits, cuts, unit, learn_hidden, learn_grad_out, other_cot, key_master
+        bits, cuts, unit, learn_hidden, learn_grad_out, other_cot, key_master, rollout,
+        slice_count, packed,
     )
 
     def send(messages, stage):
         over = [bit for bit, _ in messages_of(bits, stage)]
         return [swap(message, "fsdp", bit) for message, bit in zip(messages, over)]
 
-    rows = rows_by_owner(rollout_hidden.reshape(row_count * steps, -1), slice_count, size, gate)
-    row_bits = [0, 2, 1] if bits == 3 else list(range(bits))
-
-    def send_rows(stage, messages):
-        give, messages[-1] = tied(with_bit(rows, bits, row_bits[stage], 1), messages[-1])
-        return swap(give, "fsdp", row_bits[stage])
-
-    def take_rows(stage, come, sent):
-        come, sent[0] = tied(come, sent[0])
-        bit = row_bits[stage]
-        out = jnp.stack([with_bit(rows, bits, bit, 0), come], axis=bits - 1 - bit)
-        return out.reshape((size,) + out.shape[bits:])
-
-    keeps = [k for _, k, _ in parts]
-    helds = [h for _, _, h in parts]
-    come = send_rows(0, parts[0][0])
-    sent = [send(messages, 0) for messages, _, _ in parts]
+    messages, keeps, helds, state = parts[0]
+    sent = send(messages, 0)
     cached = attend_cache(query_base, cache_keys, cache_values, cache_lengths, gate)
-    cached[0], sent[0][0] = tied(cached[0], sent[0][0])
-    came = [[None] * len(widths) for _ in cuts]
+    cached[0], sent[0] = tied(cached[0], sent[0])
     for stage in range(bits - 1):
-        for p in range(len(cuts)):
-            if p == 0:
-                rows = take_rows(stage, come, sent[0])
-            messages, keeps[p], helds[p], gate = run_stage(
-                bits, stage, unit, sent[p], keeps[p], helds[p], gate
-            )
-            if p == 0 and stage < bits - 2:
-                come = send_rows(stage + 1, messages)
-            sent[p] = send(messages, stage + 1)
-    grad_weight, square = summed(bits, unit, list(zip(sent, keeps)))
-
-    spreads = gather_orders(bits)
-
-    def last_gather(value, g):
-        value, helds[0][g] = tied(value, helds[0][g])
-        came[0][g] = swap(helds[0][g], "fsdp", spreads[g][-1])
+        messages, keeps, helds, state, gate = run_stage(
+            bits, stage, unit, sent, keeps, helds, state, gate, packed
+        )
+        sent = send(messages, stage + 1)
+    grad_weight, square, *state = summed(bits, unit, sent, keeps, state)
+    if packed:
+        hidden_rows = state[0]
+    else:
+        rows = rows_by_owner(rollout, slice_count, size)
+        for bit in range(bits):
+            names = names_with(bits, bit)
+            come = swap(jnp.stack([rows[name] for name in names]), "fsdp", bit)
+            rows = rows.at[jnp.array(names)].set(come)
+        hidden_rows = rows.reshape(size * tokens, owned)
+
+    last_bits = [gather_orders(bits)[group[0]][-1] for group in held_groups(bits, bits - 1)]
+    blocks, late = list(helds), [None] * len(last_bits)
+
+    def last_gather(value, at):
+        value, blocks[at] = tied(value, blocks[at])
+        late[at] = swap(blocks[at], "fsdp", last_bits[at])
         return value
 
-    give, square = tied(with_bit(rows, bits, row_bits[-1], 1), square)
-    come = swap(give, "fsdp", row_bits[-1])
-    if spreads[0][-1] != 0:
-        square = last_gather(square, 0)
+    far_bits = list(range(1, bits))
+    if bits > 1:
+        others = [swap_with(square, "fsdp", mask) for mask in (1, 2, 3)]
+        others = list(tied(*others))
+        for at, bit in enumerate(last_bits):
+            if bit < 2:
+                others[bit] = last_gather(others[bit], at)
+        square = (square + others[0]) + (others[1] + others[2])
+    else:
+        square = square + swap(square, "fsdp", 0)
     square = square + swap(square, "tp", 0)
-    far_bits = list(range(1, bits))
-    later = {0: [g for g in (0, 1, 2) if spreads[g][-1] == 0], 1: [3]}
-    for bit in [0] + far_bits:
-        if bit == spreads[0][-1]:
-            square, came[0][0] = tied(square, came[0][0])
+    for bit in far_bits[1:]:
         other = swap(square, "fsdp", bit)
-        for g in later.get(bit, []):
-            other = last_gather(other, g)
         if bit != bits - 1:
             square = square + other
-    rows = jnp.stack([with_bit(rows, bits, row_bits[-1], 0), come], axis=bits - 1 - row_bits[-1])
-    near_sum, near_token = input_near(bits, cuts, unit, learn_grad_out, helds[0], came[0])
-    other, near_token = tied(other, near_token)
-    hidden_rows = rows.reshape(size * row_count * steps, owned)
+    for at, bit in enumerate(last_bits):
+        if bit >= 2:
+            other = last_gather(other, at)
+        if bit == 1:
+            other, late[at] = tied(other, late[at])
     limit = math.sqrt(learn_hidden.shape[0] * size * width_all)
     keep, give = project(
-        limit, 1, square, other, grad_weight, key_master, key_first, key_second, hidden_rows,
-        row_count * steps,
+        limit, square, other, grad_weight, key_master, key_first, key_second, hidden_rows,
+        size, tokens,
     )
 
     give, gated_grad = tied(give, grad_weight)
@@ -810,23 +917,23 @@
         limit, square, other, gated_grad, key_master, key_first, key_second
     )
 
+    projected = keep + swap(give, "tp", 0)
     names = list(range(size))
     for bit in far_bits + [0]:
-        if bit != 1:
-            keep, give = pick(projected, names, bit, 0), pick(projected, names, bit, 1)
-        if bit == 0:
-            near, far = projected[..., :column_count], projected[..., column_count:]
-            projected = near + swap(far, "tp", 0)
-            keep, give = pick(projected, names, bit, 0), pick(projected, names, bit, 1)
+        keep, give = pick(projected, names, bit, 0), pick(projected, names, bit, 1)
         names = [name for name in names if not (name >> bit) & 1]
         come = swap(give, "fsdp", bit)
         if bit == 1:
-            come, updated_token, came[0][2] = tied(come, updated_token, came[0][2])
+            come, updated_token = tied(come, updated_token)
         if bit == 2:
-            come, came[0][3] = tied(come, came[0][3])
+            near_sum, near_token = input_near(
+                bits, owned, unit, learn_grad_out, blocks + late, updated_token
+            )
+            come, near_token = tied(come, near_token)
+        if bit == 0:
+            grad_in, far_token = input_far(bits, owned, unit, other_cot, near_sum, blocks + late)
         projected = keep + come
     shape = (row_count, steps, column_count)
-    grad_in, far_token = input_far(bits, cuts, unit, other_cot, near_sum, helds[0], came[0])
     step_keys, attention = attend_fresh(
         query_base, keep.reshape(shape), come.reshape(shape), new_values, cached,
         (updated_token, near_token, far_token),

time: 90.5 us -> 85 us (0.939)
  starting transfers between devices: 33 us -> 27.4 us
  local copies, waits for them, and re-layouts: 3.39 us -> 0.06 us
  Pallas kernels: 12 us -> 13.9 us
  waiting for transfers between devices: 40.3 us -> 41.9 us
    ppermute x26 -> x22, starting transfers between devices: 33 us -> 27.4 us  [swap_with(): return lax.ppermute(value, axis, [(i, i ^ mask) for i in range(size)])]
    unnamed x24 -> x16, local copies, waits for them, and re-layouts: 3.37 us -> 0.04 us
    pallas_call x6 -> x5, Pallas kernels: 7.17 us -> 9.07 us  [the longest x2 5.38 us: first_stage(): pl.pallas_call(functools.partial(first_kernel, bits, cuts, unit, over, sl...]
    ppermute x26 -> x22, waiting for transfers between devices: 40.3 us -> 41.9 us  [swap_with(): return lax.ppermute(value, axis, [(i, i ^ mask) for i in range(size)])]
  transfers between devices with their start and end apart: 26 -> 22, of which waited for: 15 -> 17; matrix products, arithmetic and copies ran while one was open for 0% -> 0% of each run, Pallas kernels for 11% -> 14%
where the time goes in v4:
time: 85 us; the launch traced here: 84.8 us
  waiting for transfers between devices  41.9 us (49%)
  starting transfers between devices  27.4 us (32%)
  Pallas kernels  13.9 us (16%)
  between operations  1.45 us (2%)
    ppermute x22, waiting for transfers between devices, swap_with(): return lax.ppermute(value, axis, [(i, i ^ mask) for i in range(size)])  41.9 us
    ppermute x22, starting transfers between devices, swap_with(): return lax.ppermute(value, axis, [(i, i ^ mask) for i in range(size)])  27.4 us
    pallas_call x2, Pallas kernels, first_stage(): pl.pallas_call(functools.partial(first_kernel, bits, cuts, unit, over, sl...  5.38 us
    pallas_call x1, Pallas kernels, input_far(): pl.pallas_call(functools.partial(far_kernel, bits, unit, (2, 3)), out_sha...  2.23 us
  transfers between devices with their start and end apart: 22, of which 17 were waited for; matrix products, arithmetic and copies ran while one was open for 0% of the time, Pallas kernels for 14%

profile of v4, /device:TPU:0, one launch (start us, length us, event | category | flops | bytes accessed | tf_op | source)
XLA Modules:
  0.0 84.8 jit_solution(12582033354117905853)
XLA Ops:
  0.6 0.5 collective-permute-start
  1.2 3.7 %shard_map.154 = (bf16[1440,128]{1,0:T(8,128)(2,1)S(1)}, bf16[1440,128]{1,0:T(8,128)(2,1)S(1)}, f32[4,240,128]{2,1,0:T(8,128)S(1)}, f32[4,240,128]{2,1,0:T(8,128...) custom-call(s32[2]{0:T(128)S(1)} %pad_add_fusion.where_ref, ...), custom_call_target="tpu_custom_call" | custom-call | flops 1 | bytes 1 | tf_op jit(solution)/shard_map/pallas_call | solution.py:360
  5.0 3.7 %collective-permute-start.1 = (bf16[1440,128]{1,0:T(8,128)(2,1)S(1)}, bf16[1440,128]{1,0:T(8,128)(2,1)S(1)}, u32[]{:S(2)}, u32[]{:S(2)}) collective-permute-start(bf16[1440,128]{1,0:T(8,128)(2,1)S(1)} %get-tuple-element.85), channel_id=1, source_target_pairs={{0,8},{2,10},{4,12},{6,14},{8,0},{10,2},{12,4},{14,6},{1,9},{3,11}... | collective-permute-start | bytes 1105928 | tf_op jit(solution)/shard_map/ppermute | solution.py:40
  8.7 1.6 %collective-permute-start.2 = (bf16[1440,128]{1,0:T(8,128)(2,1)S(1)}, bf16[1440,128]{1,0:T(8,128)(2,1)S(1)}, u32[]{:S(2)}, u32[]{:S(2)}) collective-permute-start(bf16[1440,128]{1,0:T(8,128)(2,1)S(1)} %get-tuple-element.87), channel_id=1, source_target_pairs={{0,4},{2,6},{4,0},{6,2},{8,12},{10,14},{12,8},{14,10},{1,5},{3,7},... | collective-permute-start | bytes 1105928 | tf_op jit(solution)/shard_map/ppermute | solution.py:40
  10.3 1.6 %shard_map.155 = (bf16[960,128]{1,0:T(8,128)(2,1)S(1)}, bf16[1024,128]{1,0:T(8,128)(2,1)S(1)}, f32[4,240,256]{2,1,0:T(8,128)S(1)}, bf16[1,240,128]{2,1,0:T(8,128...) custom-call(s32[2]{0:T(128)S(1)} %pad_add_fusion.where_ref, ...), custom_call_target="tpu_custom_call" | custom-call | flops 1 | bytes 1 | tf_op jit(solution)/shard_map/pallas_call | solution.py:360
  11.9 1.6 %collective-permute-start.4 = (bf16[1024,128]{1,0:T(8,128)(2,1)S(1)}, bf16[1024,128]{1,0:T(8,128)(2,1)S(1)}, u32[]{:S(2)}, u32[]{:S(2)}) collective-permute-start(bf16[1024,128]{1,0:T(8,128)(2,1)S(1)} %get-tuple-element.89), channel_id=1, source_target_pairs={{0,2},{2,0},{4,6},{6,4},{8,10},{10,8},{12,14},{14,12},{1,3},{3,1},... | collective-permute-start | bytes 786440 | tf_op jit(solution)/shard_map/ppermute | solution.py:40
  13.5 0.5 collective-permute-start.3
  14.7 0.8 shard_map.156
  15.5 10.5 %collective-permute-done.1.refs_0_ = bf16[1440,128]{1,0:T(8,128)(2,1)S(1)} collective-permute-done((bf16[1440,128]{1,0:T(8,128)(2,1)S(1)}, bf16[1440,128]{1,0:T(8,128)(2,1)S(1)}, u32[]{:S(2)}, u32[]{:S(2)}) %collective-permute-start.1) | collective-permute-done | bytes 368672 | tf_op jit(solution)/shard_map/ppermute | solution.py:40
  25.9 0.2 collective-permute-done.2.refs_1_
  26.1 0.4 shard_map.157
  26.5 1.4 %collective-permute-start.5 = (bf16[1504,128]{1,0:T(8,128)(2,1)S(1)}, bf16[1504,128]{1,0:T(8,128)(2,1)S(1)}, u32[]{:S(2)}, u32[]{:S(2)}) collective-permute-start(bf16[1504,128]{1,0:T(8,128)(2,1)S(1)} %get-tuple-element.98), channel_id=1, source_target_pairs={{0,8},{2,10},{4,12},{6,14},{8,0},{10,2},{12,4},{14,6},{1,9},{3,11}... | collective-permute-start | bytes 1155080 | tf_op jit(solution)/shard_map/ppermute | solution.py:40
  27.9 2.4 %collective-permute-start.6 = (bf16[1440,128]{1,0:T(8,128)(2,1)S(1)}, bf16[1440,128]{1,0:T(8,128)(2,1)S(1)}, u32[]{:S(2)}, u32[]{:S(2)}) collective-permute-start(bf16[1440,128]{1,0:T(8,128)(2,1)S(1)} %get-tuple-element.99), channel_id=1, source_target_pairs={{0,4},{2,6},{4,0},{6,2},{8,12},{10,14},{12,8},{14,10},{1,5},{3,7},... | collective-permute-start | bytes 1105928 | tf_op jit(solution)/shard_map/ppermute | solution.py:40
  30.4 1.5 %collective-permute-start.7 = (bf16[960,128]{1,0:T(8,128)(2,1)S(1)}, bf16[960,128]{1,0:T(8,128)(2,1)S(1)}, u32[]{:S(2)}, u32[]{:S(2)}) collective-permute-start(bf16[960,128]{1,0:T(8,128)(2,1)S(1)} %get-tuple-element.100), channel_id=1, source_target_pairs={{0,2},{2,0},{4,6},{6,4},{8,10},{10,8},{12,14},{14,12},{1,3},{3,1},... | collective-permute-start | bytes 737288 | tf_op jit(solution)/shard_map/ppermute | solution.py:40
  31.9 5.9 %collective-permute-done.7.refs_2_ = bf16[960,128]{1,0:T(8,128)(2,1)S(1)} collective-permute-done((bf16[960,128]{1,0:T(8,128)(2,1)S(1)}, bf16[960,128]{1,0:T(8,128)(2,1)S(1)}, u32[]{:S(2)}, u32[]{:S(2)}) %collective-permute-start.7) | collective-permute-done | bytes 245792 | tf_op jit(solution)/shard_map/ppermute | solution.py:40
  37.8 6.2 %collective-permute-done.6.refs_1_ = bf16[1440,128]{1,0:T(8,128)(2,1)S(1)} collective-permute-done((bf16[1440,128]{1,0:T(8,128)(2,1)S(1)}, bf16[1440,128]{1,0:T(8,128)(2,1)S(1)}, u32[]{:S(2)}, u32[]{:S(2)}) %collective-permute-start.6) | collective-permute-done | bytes 368672 | tf_op jit(solution)/shard_map/ppermute | solution.py:40
  44.0 2.3 %collective-permute-done.5.refs_0_ = bf16[1504,128]{1,0:T(8,128)(2,1)S(1)} collective-permute-done((bf16[1504,128]{1,0:T(8,128)(2,1)S(1)}, bf16[1504,128]{1,0:T(8,128)(2,1)S(1)}, u32[]{:S(2)}, u32[]{:S(2)}) %collective-permute-start.5) | collective-permute-done | bytes 385056 | tf_op jit(solution)/shard_map/ppermute | solution.py:40
  46.2 0.8 shard_map.158
  47.0 1.3 %collective-permute-start.8 = (bf16[480,128]{1,0:T(8,128)(2,1)S(1)}, bf16[480,128]{1,0:T(8,128)(2,1)S(1)}, u32[]{:S(2)}, u32[]{:S(2)}) collective-permute-start(bf16[480,128]{1,0:T(8,128)(2,1)S(1)} %get-tuple-element.110), channel_id=1, source_target_pairs={{0,8},{2,10},{4,12},{6,14},{8,0},{10,2},{12,4},{14,6},{1,9},{3,11}... | collective-permute-start | bytes 368648 | tf_op jit(solution)/shard_map/ppermute | solution.py:40
  48.3 1.8 %collective-permute-start.9 = (bf16[304,128]{1,0:T(8,128)(2,1)S(1)}, bf16[304,128]{1,0:T(8,128)(2,1)S(1)}, u32[]{:S(2)}, u32[]{:S(2)}) collective-permute-start(bf16[304,128]{1,0:T(8,128)(2,1)S(1)} %get-tuple-element.111), channel_id=1, source_target_pairs={{0,4},{2,6},{4,0},{6,2},{8,12},{10,14},{12,8},{14,10},{1,5},{3,7},... | collective-permute-start | bytes 233480 | tf_op jit(solution)/shard_map/ppermute | solution.py:40
  50.1 1.5 %collective-permute-start.10 = (bf16[240,128]{1,0:T(8,128)(2,1)S(1)}, bf16[240,128]{1,0:T(8,128)(2,1)S(1)}, u32[]{:S(2)}, u32[]{:S(2)}) collective-permute-start(bf16[240,128]{1,0:T(8,128)(2,1)S(1)} %get-tuple-element.112), channel_id=1, source_target_pairs={{0,2},{2,0},{4,6},{6,4},{8,10},{10,8},{12,14},{14,12},{1,3},{3,1},... | collective-permute-start | bytes 184328 | tf_op jit(solution)/shard_map/ppermute | solution.py:40
  51.6 2.7 %collective-permute-done.10.refs_2_ = bf16[240,128]{1,0:T(8,128)(2,1)S(1)} collective-permute-done((bf16[240,128]{1,0:T(8,128)(2,1)S(1)}, bf16[240,128]{1,0:T(8,128)(2,1)S(1)}, u32[]{:S(2)}, u32[]{:S(2)}) %collective-permute-start.10) | collective-permute-done | bytes 61472 | tf_op jit(solution)/shard_map/ppermute | solution.py:40
  54.3 0.4 collective-permute-done.8.refs_0_
  54.7 0.3 shard_map.159
  55.0 1.2 %collective-permute-start.11 = (f32[8,128]{1,0:T(8,128)S(1)}, f32[8,128]{1,0:T(8,128)S(1)}, u32[]{:S(2)}, u32[]{:S(2)}) collective-permute-start(f32[8,128]{1,0:T(8,128)S(1)} %get-tuple-element.117), channel_id=1, source_target_pairs={{0,2},{2,0},{4,6},{6,4},{8,10},{10,8},{12,14},{14,12},{1,3},{3,1},... | collective-permute-start | bytes 12296 | tf_op jit(solution)/shard_map/ppermute | solution.py:40
  56.2 0.5 collective-permute-start.12
  56.7 1.9 %collective-permute-start.13 = (f32[8,128]{1,0:T(8,128)S(1)}, f32[8,128]{1,0:T(8,128)S(1)}, u32[]{:S(2)}, u32[]{:S(2)}) collective-permute-start(f32[8,128]{1,0:T(8,128)S(1)} %get-tuple-element.117), channel_id=1, source_target_pairs={{0,6},{2,4},{4,2},{6,0},{8,14},{10,12},{12,10},{14,8},{1,7},{3,5},... | collective-permute-start | bytes 12296 | tf_op jit(solution)/shard_map/ppermute | solution.py:40
  58.5 0.1 collective-permute-done.11
  58.7 1.2 %collective-permute-done.12 = f32[8,128]{1,0:T(8,128)S(1)} collective-permute-done((f32[8,128]{1,0:T(8,128)S(1)}, f32[8,128]{1,0:T(8,128)S(1)}, u32[]{:S(2)}, u32[]{:S(2)}) %collective-permute-start.12) | collective-permute-done | bytes 4128 | tf_op jit(solution)/shard_map/ppermute | solution.py:40
  59.8 1.4 %collective-permute-done.13 = f32[8,128]{1,0:T(8,128)S(1)} collective-permute-done((f32[8,128]{1,0:T(8,128)S(1)}, f32[8,128]{1,0:T(8,128)S(1)}, u32[]{:S(2)}, u32[]{:S(2)}) %collective-permute-start.13) | collective-permute-done | bytes 4128 | tf_op jit(solution)/shard_map/ppermute | solution.py:40
  61.2 1.6 %collective-permute-start.16 = (bf16[4,240,128]{2,1,0:T(8,128)(2,1)S(1)}, bf16[4,240,128]{2,1,0:T(8,128)(2,1)S(1)}, u32[]{:S(2)}, u32[]{:S(2)}) collective-permute-start(bf16[4,240,128]{2,1,0:T(8,128)(2,1)S(1)} %get-tuple-element.125.refs_0_), channel_id=1, source_target_pairs={{0,4},{2,6},{4,0},{6,2},{8,12},{10,14},{12,8},{14,10},{1,5},{3,7},... | collective-permute-start | bytes 737288 | tf_op jit(solution)/shard_map/ppermute | solution.py:40
  62.7 0.9 %collective-permute-start.19 = (bf16[12,240,128]{2,1,0:T(8,128)(2,1)S(1)}, bf16[12,240,128]{2,1,0:T(8,128)(2,1)S(1)}, u32[]{:S(2)}, u32[]{:S(2)}) collective-permute-start(bf16[12,240,128]{2,1,0:T(8,128)(2,1)S(1)} %get-tuple-element.135.refs_1_), channel_id=1, source_target_pairs={{0,2},{2,0},{4,6},{6,4},{8,10},{10,8},{12,14},{14,12},{1,3},{3,1},... | collective-permute-start | bytes 2211848 | tf_op jit(solution)/shard_map/ppermute | solution.py:40
  63.7 1.2 %collective-permute-done.14 = f32[8,128]{1,0:T(8,128)S(1)} collective-permute-done((f32[8,128]{1,0:T(8,128)S(1)}, f32[8,128]{1,0:T(8,128)S(1)}, u32[]{:S(2)}, u32[]{:S(2)}) %collective-permute-start.14) | collective-permute-done | bytes 4128 | tf_op jit(solution)/shard_map/ppermute | solution.py:40
  64.8 0.7 collective-permute-start.15
  65.5 3.8 %collective-permute-done.15.other_ref = f32[8,128]{1,0:T(8,128)S(1)} collective-permute-done((f32[8,128]{1,0:T(8,128)S(1)}, f32[8,128]{1,0:T(8,128)S(1)}, u32[]{:S(2)}, u32[]{:S(2)}) %collective-permute-start.15) | collective-permute-done | bytes 4128 | tf_op jit(solution)/shard_map/ppermute | solution.py:40
  69.4 0.6 shard_map.160
  70.1 1.2 %collective-permute-done.17 = f32[8,8,256]{2,1,0:T(8,128)S(1)} collective-permute-done((f32[8,8,256]{2,1,0:T(8,128)S(1)}, f32[8,8,256]{2,1,0:T(8,128)S(1)}, u32[]{:S(2)}, u32[]{:S(2)}) %collective-permute-start.17) | collective-permute-done | bytes 65568 | tf_op jit(solution)/shard_map/ppermute | solution.py:40
  71.3 0.8 collective-permute-start.18
  72.1 1.7 %shard_map.161 = (f32[240,512]{1,0:T(8,128)}, f32[240,512]{1,0:T(8,128)}, f32[240,512]{1,0:T(8,128)}, f32[8,128]{1,0:T(8,128)S(1)}) custom-call(f32[8,128]{1,0:T(8,128)S(1)} %add.24.square_ref, f32[8,128]{1,0:T(8,128)S(1)} %collective-permute-done.15.other_ref, f32[240,512]{1,0:T(8,128)S(1)} %get-tuple-element.132.grad_ref, f32[240,512]{1,0:T(8,128)S(1)} %copy-done, ...), custom_call_target="tpu_custom_call" | custom-call | flops 1 | bytes 1 | tf_op jit(solution)/shard_map/pallas_call | solution.py:816
  73.8 1.5 %collective-permute-done.18 = f32[4,8,256]{2,1,0:T(8,128)S(1)} collective-permute-done((f32[4,8,256]{2,1,0:T(8,128)S(1)}, f32[4,8,256]{2,1,0:T(8,128)S(1)}, u32[]{:S(2)}, u32[]{:S(2)}) %collective-permute-start.18) | collective-permute-done | bytes 32800 | tf_op jit(solution)/shard_map/ppermute | solution.py:40
  75.3 0.8 collective-permute-start.20
  76.1 1.4 %collective-permute-done.19.refs_3_ = bf16[12,240,128]{2,1,0:T(8,128)(2,1)S(1)} collective-permute-done((bf16[12,240,128]{2,1,0:T(8,128)(2,1)S(1)}, bf16[12,240,128]{2,1,0:T(8,128)(2,1)S(1)}, u32[]{:S(2)}, u32[]{:S(2)}) %collective-permute-start.19) | collective-permute-done | bytes 737312 | tf_op jit(solution)/shard_map/ppermute | solution.py:40
  77.5 0.9 %shard_map.162 = (f32[384,1920]{1,0:T(8,128)S(1)}, f32[8,128]{1,0:T(8,128)S(1)}) custom-call(s32[1]{0:T(128)} %bitcast.here_ref, bf16[384,256]{1,0:T(8,128)(2,1)S(1)} %copy-done.3, f32[8,128]{1,0:T(8,128)S(1)} %get-tuple-element.134.gate_ref.near_ref, bf16[4,240,128]{2,1,0:T(8,128)(2,1)S(1)} %get-tuple-element.125.refs_0_, ...), custom_call_target="tpu_custom_call" | custom-call | flops 1 | bytes 1 | tf_op jit(solution)/shard_map/pallas_call | solution.py:714
  78.4 1.7 %collective-permute-done.20 = f32[2,8,256]{2,1,0:T(8,128)S(1)} collective-permute-done((f32[2,8,256]{2,1,0:T(8,128)S(1)}, f32[2,8,256]{2,1,0:T(8,128)S(1)}, u32[]{:S(2)}, u32[]{:S(2)}) %collective-permute-start.20) | collective-permute-done | bytes 16416 | tf_op jit(solution)/shard_map/ppermute | solution.py:40
  80.1 1.2 %collective-permute-start.21 = (f32[1,8,256]{2,1,0:T(8,128)S(1)}, f32[1,8,256]{2,1,0:T(8,128)S(1)}, u32[]{:S(2)}, u32[]{:S(2)}) collective-permute-start(f32[1,8,256]{2,1,0:T(8,128)S(1)} %get-tuple-element.156), channel_id=1, source_target_pairs={{0,2},{2,0},{4,6},{6,4},{8,10},{10,8},{12,14},{14,12},{1,3},{3,1},... | collective-permute-start | bytes 24584 | tf_op jit(solution)/shard_map/ppermute | solution.py:40
  81.3 2.2 %shard_map.163 = (bf16[384,1920]{1,0:T(8,128)(2,1)}, f32[8,128]{1,0:T(8,128)S(1)}) custom-call(s32[1]{0:T(128)} %bitcast.here_ref, bf16[384,256]{1,0:T(8,128)(2,1)S(1)} %collective-permute-done.refs_1_.cot_ref, f32[384,1920]{1,0:T(8,128)S(1)} %get-tuple-element.137.near_ref, bf16[4,240,128]{2,1,0:T(8,128)(2,1)S(1)} %get-tuple-element.125.refs_0_, ...), custom_call_target="tpu_custom_call" | custom-call | flops 1 | bytes 1 | tf_op jit(solution)/shard_map/pallas_call | solution.py:732
  83.5 0.2 collective-permute-done.21.other_ref
  83.8 1.1 %shard_map.164 = (bf16[1,8,256]{2,1,0:T(8,128)(2,1)}, bf16[1,8,2048]{2,1,0:T(8,128)(2,1)}) custom-call(bf16[1,8,2048]{2,1,0:T(8,128)(2,1)S(1)} %copy-done.6, f32[1,8,256]{2,1,0:T(8,128)S(1)} %get-tuple-element.157.keep_ref, f32[1,8,256]{2,1,0:T(8,128)S(1)} %collective-permute-done.21.other_ref, bf16[1,8,256]{2,1,0:T(8,128)(2,1)S(1)} %copy-done.7, ...), custom_call_target="tpu_custom_call" | custom-call | flops 1 | bytes 1 | tf_op jit(solution)/shard_map/pallas_call | solution.py:569
  (34 shorter events, 0.3 us)
Async XLA Ops:
  0.6 9.6 %collective-permute-start = (bf16[384,256]{1,0:T(8,128)(2,1)}, bf16[384,256]{1,0:T(8,128)(2,1)S(1)}, u32[]{:S(2)}, u32[]{:S(2)}) collective-permute-start(bf16[384,256]{1,0:T(8,128)(2,1)} %cot_ref.1), channel_id=1, source_target_pairs={{0,1},{1,0},{2,3},{3,2},{4,5},{5,4},{6,7},{7,6},{8,9},{9,8},{10,11... | collective-permute-start | bytes 589832 | tf_op jit(solution)/shard_map/ppermute | solution.py:40
  5.0 9.7 %copy-start.4 = (bf16[1,1024,256]{2,1,0:T(8,128)(2,1)S(1)}, bf16[1,1024,256]{2,1,0:T(8,128)(2,1)}, u32[]{:S(2)}) copy-start(bf16[1,1024,256]{2,1,0:T(8,128)(2,1)} %keys_ref.1) | copy-start | bytes 1572868
  5.0 9.7 %copy-start.5 = (bf16[1,1024,256]{2,1,0:T(8,128)(2,1)S(1)}, bf16[1,1024,256]{2,1,0:T(8,128)(2,1)}, u32[]{:S(2)}) copy-start(bf16[1,1024,256]{2,1,0:T(8,128)(2,1)} %values_ref.2) | copy-start | bytes 1572868
  5.0 9.7 %copy-start.6 = (bf16[1,8,2048]{2,1,0:T(8,128)(2,1)S(1)}, bf16[1,8,2048]{2,1,0:T(8,128)(2,1)}, u32[]{:S(2)}) copy-start(bf16[1,8,2048]{2,1,0:T(8,128)(2,1)} %query_ref.3) | copy-start | bytes 98308
  5.0 20.9 %collective-permute-start.1 = (bf16[1440,128]{1,0:T(8,128)(2,1)S(1)}, bf16[1440,128]{1,0:T(8,128)(2,1)S(1)}, u32[]{:S(2)}, u32[]{:S(2)}) collective-permute-start(bf16[1440,128]{1,0:T(8,128)(2,1)S(1)} %get-tuple-element.85), channel_id=1, source_target_pairs={{0,8},{2,10},{4,12},{6,14},{8,0},{10,2},{12,4},{14,6},{1,9},{3,11}... | collective-permute-start | bytes 1105928 | tf_op jit(solution)/shard_map/ppermute | solution.py:40
  8.7 17.4 %collective-permute-start.2 = (bf16[1440,128]{1,0:T(8,128)(2,1)S(1)}, bf16[1440,128]{1,0:T(8,128)(2,1)S(1)}, u32[]{:S(2)}, u32[]{:S(2)}) collective-permute-start(bf16[1440,128]{1,0:T(8,128)(2,1)S(1)} %get-tuple-element.87), channel_id=1, source_target_pairs={{0,4},{2,6},{4,0},{6,2},{8,12},{10,14},{12,8},{14,10},{1,5},{3,7},... | collective-permute-start | bytes 1105928 | tf_op jit(solution)/shard_map/ppermute | solution.py:40
  11.9 14.2 %collective-permute-start.4 = (bf16[1024,128]{1,0:T(8,128)(2,1)S(1)}, bf16[1024,128]{1,0:T(8,128)(2,1)S(1)}, u32[]{:S(2)}, u32[]{:S(2)}) collective-permute-start(bf16[1024,128]{1,0:T(8,128)(2,1)S(1)} %get-tuple-element.89), channel_id=1, source_target_pairs={{0,2},{2,0},{4,6},{6,4},{8,10},{10,8},{12,14},{14,12},{1,3},{3,1},... | collective-permute-start | bytes 786440 | tf_op jit(solution)/shard_map/ppermute | solution.py:40
  13.5 12.7 %collective-permute-start.3 = (bf16[960,128]{1,0:T(8,128)(2,1)S(1)}, bf16[960,128]{1,0:T(8,128)(2,1)S(1)}, u32[]{:S(2)}, u32[]{:S(2)}) collective-permute-start(bf16[960,128]{1,0:T(8,128)(2,1)S(1)} %get-tuple-element.88), channel_id=1, source_target_pairs={{0,2},{2,0},{4,6},{6,4},{8,10},{10,8},{12,14},{14,12},{1,3},{3,1},... | collective-permute-start | bytes 737288 | tf_op jit(solution)/shard_map/ppermute | solution.py:40
  26.5 19.7 %collective-permute-start.5 = (bf16[1504,128]{1,0:T(8,128)(2,1)S(1)}, bf16[1504,128]{1,0:T(8,128)(2,1)S(1)}, u32[]{:S(2)}, u32[]{:S(2)}) collective-permute-start(bf16[1504,128]{1,0:T(8,128)(2,1)S(1)} %get-tuple-element.98), channel_id=1, source_target_pairs={{0,8},{2,10},{4,12},{6,14},{8,0},{10,2},{12,4},{14,6},{1,9},{3,11}... | collective-permute-start | bytes 1155080 | tf_op jit(solution)/shard_map/ppermute | solution.py:40
  27.9 16.0 %collective-permute-start.6 = (bf16[1440,128]{1,0:T(8,128)(2,1)S(1)}, bf16[1440,128]{1,0:T(8,128)(2,1)S(1)}, u32[]{:S(2)}, u32[]{:S(2)}) collective-permute-start(bf16[1440,128]{1,0:T(8,128)(2,1)S(1)} %get-tuple-element.99), channel_id=1, source_target_pairs={{0,4},{2,6},{4,0},{6,2},{8,12},{10,14},{12,8},{14,10},{1,5},{3,7},... | collective-permute-start | bytes 1105928 | tf_op jit(solution)/shard_map/ppermute | solution.py:40
  30.4 7.4 %collective-permute-start.7 = (bf16[960,128]{1,0:T(8,128)(2,1)S(1)}, bf16[960,128]{1,0:T(8,128)(2,1)S(1)}, u32[]{:S(2)}, u32[]{:S(2)}) collective-permute-start(bf16[960,128]{1,0:T(8,128)(2,1)S(1)} %get-tuple-element.100), channel_id=1, source_target_pairs={{0,2},{2,0},{4,6},{6,4},{8,10},{10,8},{12,14},{14,12},{1,3},{3,1},... | collective-permute-start | bytes 737288 | tf_op jit(solution)/shard_map/ppermute | solution.py:40
  46.2 23.1 %copy-start = (f32[240,512]{1,0:T(8,128)S(1)}, f32[240,512]{1,0:T(8,128)}, u32[]{:S(2)}) copy-start(f32[240,512]{1,0:T(8,128)} %master_ref.3) | copy-start | bytes 1474564
  46.2 23.1 %copy-start.1 = (f32[240,512]{1,0:T(8,128)S(1)}, f32[240,512]{1,0:T(8,128)}, u32[]{:S(2)}) copy-start(f32[240,512]{1,0:T(8,128)} %first_ref.3) | copy-start | bytes 1474564
  46.2 23.1 %copy-start.2 = (f32[240,512]{1,0:T(8,128)S(1)}, f32[240,512]{1,0:T(8,128)}, u32[]{:S(2)}) copy-start(f32[240,512]{1,0:T(8,128)} %second_ref.3) | copy-start | bytes 1474564
  47.0 7.7 %collective-permute-start.8 = (bf16[480,128]{1,0:T(8,128)(2,1)S(1)}, bf16[480,128]{1,0:T(8,128)(2,1)S(1)}, u32[]{:S(2)}, u32[]{:S(2)}) collective-permute-start(bf16[480,128]{1,0:T(8,128)(2,1)S(1)} %get-tuple-element.110), channel_id=1, source_target_pairs={{0,8},{2,10},{4,12},{6,14},{8,0},{10,2},{12,4},{14,6},{1,9},{3,11}... | collective-permute-start | bytes 368648 | tf_op jit(solution)/shard_map/ppermute | solution.py:40
  48.3 6.0 %collective-permute-start.9 = (bf16[304,128]{1,0:T(8,128)(2,1)S(1)}, bf16[304,128]{1,0:T(8,128)(2,1)S(1)}, u32[]{:S(2)}, u32[]{:S(2)}) collective-permute-start(bf16[304,128]{1,0:T(8,128)(2,1)S(1)} %get-tuple-element.111), channel_id=1, source_target_pairs={{0,4},{2,6},{4,0},{6,2},{8,12},{10,14},{12,8},{14,10},{1,5},{3,7},... | collective-permute-start | bytes 233480 | tf_op jit(solution)/shard_map/ppermute | solution.py:40
  50.1 4.2 %collective-permute-start.10 = (bf16[240,128]{1,0:T(8,128)(2,1)S(1)}, bf16[240,128]{1,0:T(8,128)(2,1)S(1)}, u32[]{:S(2)}, u32[]{:S(2)}) collective-permute-start(bf16[240,128]{1,0:T(8,128)(2,1)S(1)} %get-tuple-element.112), channel_id=1, source_target_pairs={{0,2},{2,0},{4,6},{6,4},{8,10},{10,8},{12,14},{14,12},{1,3},{3,1},... | collective-permute-start | bytes 184328 | tf_op jit(solution)/shard_map/ppermute | solution.py:40
  55.0 3.7 %collective-permute-start.11 = (f32[8,128]{1,0:T(8,128)S(1)}, f32[8,128]{1,0:T(8,128)S(1)}, u32[]{:S(2)}, u32[]{:S(2)}) collective-permute-start(f32[8,128]{1,0:T(8,128)S(1)} %get-tuple-element.117), channel_id=1, source_target_pairs={{0,2},{2,0},{4,6},{6,4},{8,10},{10,8},{12,14},{14,12},{1,3},{3,1},... | collective-permute-start | bytes 12296 | tf_op jit(solution)/shard_map/ppermute | solution.py:40
  56.2 3.6 %collective-permute-start.12 = (f32[8,128]{1,0:T(8,128)S(1)}, f32[8,128]{1,0:T(8,128)S(1)}, u32[]{:S(2)}, u32[]{:S(2)}) collective-permute-start(f32[8,128]{1,0:T(8,128)S(1)} %get-tuple-element.117), channel_id=1, source_target_pairs={{0,4},{2,6},{4,0},{6,2},{8,12},{10,14},{12,8},{14,10},{1,5},{3,7},... | collective-permute-start | bytes 12296 | tf_op jit(solution)/shard_map/ppermute | solution.py:40
  56.7 4.5 %collective-permute-start.13 = (f32[8,128]{1,0:T(8,128)S(1)}, f32[8,128]{1,0:T(8,128)S(1)}, u32[]{:S(2)}, u32[]{:S(2)}) collective-permute-start(f32[8,128]{1,0:T(8,128)S(1)} %get-tuple-element.117), channel_id=1, source_target_pairs={{0,6},{2,4},{4,2},{6,0},{8,14},{10,12},{12,10},{14,8},{1,7},{3,5},... | collective-permute-start | bytes 12296 | tf_op jit(solution)/shard_map/ppermute | solution.py:40
  61.2 8.2 %collective-permute-start.16 = (bf16[4,240,128]{2,1,0:T(8,128)(2,1)S(1)}, bf16[4,240,128]{2,1,0:T(8,128)(2,1)S(1)}, u32[]{:S(2)}, u32[]{:S(2)}) collective-permute-start(bf16[4,240,128]{2,1,0:T(8,128)(2,1)S(1)} %get-tuple-element.125.refs_0_), channel_id=1, source_target_pairs={{0,4},{2,6},{4,0},{6,2},{8,12},{10,14},{12,8},{14,10},{1,5},{3,7},... | collective-permute-start | bytes 737288 | tf_op jit(solution)/shard_map/ppermute | solution.py:40
  62.7 14.8 %collective-permute-start.19 = (bf16[12,240,128]{2,1,0:T(8,128)(2,1)S(1)}, bf16[12,240,128]{2,1,0:T(8,128)(2,1)S(1)}, u32[]{:S(2)}, u32[]{:S(2)}) collective-permute-start(bf16[12,240,128]{2,1,0:T(8,128)(2,1)S(1)} %get-tuple-element.135.refs_1_), channel_id=1, source_target_pairs={{0,2},{2,0},{4,6},{6,4},{8,10},{10,8},{12,14},{14,12},{1,3},{3,1},... | collective-permute-start | bytes 2211848 | tf_op jit(solution)/shard_map/ppermute | solution.py:40
  63.7 1.2 %collective-permute-start.14 = (f32[8,128]{1,0:T(8,128)S(1)}, f32[8,128]{1,0:T(8,128)S(1)}, u32[]{:S(2)}, u32[]{:S(2)}) collective-permute-start(f32[8,128]{1,0:T(8,128)S(1)} %add_add_fusion), channel_id=1, source_target_pairs={{0,1},{1,0},{2,3},{3,2},{4,5},{5,4},{6,7},{7,6},{8,9},{9,8},{10,11... | collective-permute-start | bytes 12296 | tf_op jit(solution)/shard_map/ppermute | solution.py:40
  64.8 4.5 %collective-permute-start.15 = (f32[8,128]{1,0:T(8,128)S(1)}, f32[8,128]{1,0:T(8,128)S(1)}, u32[]{:S(2)}, u32[]{:S(2)}) collective-permute-start(f32[8,128]{1,0:T(8,128)S(1)} %add.24.square_ref), channel_id=1, source_target_pairs={{0,8},{2,10},{4,12},{6,14},{8,0},{10,2},{12,4},{14,6},{1,9},{3,11}... | collective-permute-start | bytes 12296 | tf_op jit(solution)/shard_map/ppermute | solution.py:40
  70.0 7.6 %copy-start.3 = (bf16[384,256]{1,0:T(8,128)(2,1)S(1)}, bf16[384,256]{1,0:T(8,128)(2,1)}, u32[]{:S(2)}) copy-start(bf16[384,256]{1,0:T(8,128)(2,1)} %cot_ref.1) | copy-start | bytes 589828
  70.0 1.3 %collective-permute-start.17 = (f32[8,8,256]{2,1,0:T(8,128)S(1)}, f32[8,8,256]{2,1,0:T(8,128)S(1)}, u32[]{:S(2)}, u32[]{:S(2)}) collective-permute-start(f32[8,8,256]{2,1,0:T(8,128)S(1)} %get-tuple-element.131), channel_id=1, source_target_pairs={{0,1},{1,0},{2,3},{3,2},{4,5},{5,4},{6,7},{7,6},{8,9},{9,8},{10,11... | collective-permute-start | bytes 196616 | tf_op jit(solution)/shard_map/ppermute | solution.py:40
  71.3 4.0 %collective-permute-start.18 = (f32[4,8,256]{2,1,0:T(8,128)S(1)}, f32[4,8,256]{2,1,0:T(8,128)S(1)}, u32[]{:S(2)}, u32[]{:S(2)}) collective-permute-start(f32[4,8,256]{2,1,0:T(8,128)S(1)} %pad_maximum_fusion), channel_id=1, source_target_pairs={{0,4},{2,6},{4,0},{6,2},{8,12},{10,14},{12,8},{14,10},{1,5},{3,7},... | collective-permute-start | bytes 98312 | tf_op jit(solution)/shard_map/ppermute | solution.py:40
  75.3 4.7 %collective-permute-start.20 = (f32[2,8,256]{2,1,0:T(8,128)S(1)}, f32[2,8,256]{2,1,0:T(8,128)S(1)}, u32[]{:S(2)}, u32[]{:S(2)}) collective-permute-start(f32[2,8,256]{2,1,0:T(8,128)S(1)} %stack.28), channel_id=1, source_target_pairs={{0,8},{2,10},{4,12},{6,14},{8,0},{10,2},{12,4},{14,6},{1,9},{3,11}... | collective-permute-start | bytes 49160 | tf_op jit(solution)/shard_map/ppermute | solution.py:40
  80.1 3.7 %collective-permute-start.21 = (f32[1,8,256]{2,1,0:T(8,128)S(1)}, f32[1,8,256]{2,1,0:T(8,128)S(1)}, u32[]{:S(2)}, u32[]{:S(2)}) collective-permute-start(f32[1,8,256]{2,1,0:T(8,128)S(1)} %get-tuple-element.156), channel_id=1, source_target_pairs={{0,2},{2,0},{4,6},{6,4},{8,10},{10,8},{12,14},{14,12},{1,3},{3,1},... | collective-permute-start | bytes 24584 | tf_op jit(solution)/shard_map/ppermute | solution.py:40
  81.3 2.5 %copy-start.7 = (bf16[1,8,256]{2,1,0:T(8,128)(2,1)S(1)}, bf16[1,8,256]{2,1,0:T(8,128)(2,1)}, u32[]{:S(2)}) copy-start(bf16[1,8,256]{2,1,0:T(8,128)(2,1)} %values_ref.3) | copy-start | bytes 12292

commit v5 on v4

--- a/solution.py
+++ b/solution.py
@@ -48,19 +48,19 @@
     return jnp.stack([blocks[i] for i, name in enumerate(names) if (name >> bit) & 1 == value])
 
 
-units = (1, 1, 2)
+units = (2, 2)
 widths = (1, 1, 1, 1)
 
 
 def sum_orders(bits):
     if bits == 3:
-        return [[2, 0, 1], [1, 2, 0], [0, 1, 2]]
-    return [[(c * max(1, bits // 3) + s) % bits for s in range(bits)] for c in range(3)]
+        return [[1, 0, 2], [0, 2, 1]]
+    return [list(range(1, bits)) + [0], list(range(bits))]
 
 
 def gather_orders(bits):
     up = list(range(1, bits))
-    return [up[-1:] + [0] + up[:-1], up[::-1] + [0], up + [0], up + [0]]
+    return [up[-1:] + [0] + up[:-1]] + [up[::-1] + [0]] * 3
 
 
 def sum_names(order, stage):
@@ -111,7 +111,7 @@
 
 
 def row_bits(bits):
-    return [0, 2, 1] if bits == 3 else list(range(bits))
+    return [0, 1, 2] if bits == 3 else list(range(bits))
 
 
 def carrier(bits, stage):
@@ -603,8 +603,8 @@
         add = [came[m][i * rows : (i + 1) * rows, :] for m, i in where]
         add = add[0] if len(add) == 1 else jnp.concatenate(add, axis=1)
         pieces.append(keeps[c][0] + add.astype(jnp.float32))
-    near = jnp.concatenate(pieces[:2], axis=1)
-    far = pieces[2]
+    whole = jnp.concatenate(pieces, axis=1)
+    near, far = whole[:, :half], whole[:, half:]
     here = here_ref[0]
     grad_ref[:, :half] = jnp.where(here == 0, near, far)
     grad_ref[:, half:] = jnp.where(here == 0, far, near)

time: 85 us -> 79.8 us (0.939)
  waiting for transfers between devices: 41.9 us -> 36.5 us
    ppermute x22 -> x21, waiting for transfers between devices: 41.9 us -> 36.5 us  [swap_with(): return lax.ppermute(value, axis, [(i, i ^ mask) for i in range(size)])]
    ppermute x22 -> x21, starting transfers between devices: 27.4 us -> 27.6 us  [swap_with(): return lax.ppermute(value, axis, [(i, i ^ mask) for i in range(size)])]
  transfers between devices with their start and end apart: 22 -> 21, of which waited for: 17 -> 15; matrix products, arithmetic and copies ran while one was open for 0% -> 0% of each run, Pallas kernels for 14% -> 10%
where the time goes in v5:
time: 79.8 us; the launch traced here: 79.7 us
  waiting for transfers between devices  36.5 us (46%)
  starting transfers between devices  27.6 us (35%)
  Pallas kernels  14 us (18%)
  between operations  1.47 us (2%)
    ppermute x21, waiting for transfers between devices, swap_with(): return lax.ppermute(value, axis, [(i, i ^ mask) for i in range(size)])  36.5 us
    ppermute x21, starting transfers between devices, swap_with(): return lax.ppermute(value, axis, [(i, i ^ mask) for i in range(size)])  27.6 us
    pallas_call x2, Pallas kernels, first_stage(): pl.pallas_call(functools.partial(first_kernel, bits, cuts, unit, over, sl...  5.36 us
    pallas_call x1, Pallas kernels, input_far(): pl.pallas_call(functools.partial(far_kernel, bits, unit, (2, 3)), out_sha...  2.24 us
    pallas_call x1, Pallas kernels, updated(): pl.pallas_call(functools.partial(update_kernel, limit), out_shape=[jax.Sh...  1.66 us
  transfers between devices with their start and end apart: 21, of which 15 were waited for; matrix products, arithmetic and copies ran while one was open for 0% of the time, Pallas kernels for 10%

profile of v5, /device:TPU:0, one launch (start us, length us, event | category | flops | bytes accessed | tf_op | source)
XLA Modules:
  0.0 79.7 jit_solution(107157892424907670)
XLA Ops:
  0.6 0.0 copy-start.3
  0.6 0.1 pad_add_fusion.where_ref
  0.7 3.7 %shard_map.154 = (bf16[960,128]{1,0:T(8,128)(2,1)S(1)}, bf16[1920,128]{1,0:T(8,128)(2,1)S(1)}, f32[4,240,256]{2,1,0:T(8,128)S(1)}, bf16[384,1920]{1,0:T(8,128)(2...) custom-call(s32[2]{0:T(128)S(1)} %pad_add_fusion.where_ref, ...), custom_call_target="tpu_custom_call" | custom-call | flops 1 | bytes 1 | tf_op jit(solution)/shard_map/pallas_call | solution.py:360
  4.5 0.0 copy-start.4
  4.5 0.0 copy-start.5
  4.5 3.1 %collective-permute-start.2 = (bf16[1920,128]{1,0:T(8,128)(2,1)S(1)}, bf16[1920,128]{1,0:T(8,128)(2,1)S(1)}, u32[]{:S(2)}, u32[]{:S(2)}) collective-permute-start(bf16[1920,128]{1,0:T(8,128)(2,1)S(1)} %get-tuple-element.83), channel_id=1, source_target_pairs={{0,4},{2,6},{4,0},{6,2},{8,12},{10,14},{12,8},{14,10},{1,5},{3,7},... | collective-permute-start | bytes 1474568 | tf_op jit(solution)/shard_map/ppermute | solution.py:40
  7.6 1.4 %collective-permute-done.refs_1_.cot_ref = bf16[384,256]{1,0:T(8,128)(2,1)S(1)} collective-permute-done((bf16[384,256]{1,0:T(8,128)(2,1)S(1)}, bf16[384,256]{1,0:T(8,128)(2,1)S(1)}, u32[]{:S(2)}, u32[]{:S(2)}) %collective-permute-start) | collective-permute-done | bytes 196640 | tf_op jit(solution)/shard_map/ppermute | solution.py:40
  9.0 1.6 %shard_map.155 = (bf16[960,128]{1,0:T(8,128)(2,1)S(1)}, bf16[1024,128]{1,0:T(8,128)(2,1)S(1)}, f32[4,240,256]{2,1,0:T(8,128)S(1)}, bf16[1,240,128]{2,1,0:T(8,128...) custom-call(s32[2]{0:T(128)S(1)} %pad_add_fusion.where_ref, ...), custom_call_target="tpu_custom_call" | custom-call | flops 1 | bytes 1 | tf_op jit(solution)/shard_map/pallas_call | solution.py:360
  10.7 1.6 %collective-permute-start.4 = (bf16[1024,128]{1,0:T(8,128)(2,1)S(1)}, bf16[1024,128]{1,0:T(8,128)(2,1)S(1)}, u32[]{:S(2)}, u32[]{:S(2)}) collective-permute-start(bf16[1024,128]{1,0:T(8,128)(2,1)S(1)} %get-tuple-element.85), channel_id=1, source_target_pairs={{0,2},{2,0},{4,6},{6,4},{8,10},{10,8},{12,14},{14,12},{1,3},{3,1},... | collective-permute-start | bytes 786440 | tf_op jit(solution)/shard_map/ppermute | solution.py:40
  12.2 2.6 %collective-permute-start.1 = (bf16[960,128]{1,0:T(8,128)(2,1)S(1)}, bf16[960,128]{1,0:T(8,128)(2,1)S(1)}, u32[]{:S(2)}, u32[]{:S(2)}) collective-permute-start(bf16[960,128]{1,0:T(8,128)(2,1)S(1)} %get-tuple-element.81), channel_id=1, source_target_pairs={{0,8},{2,10},{4,12},{6,14},{8,0},{10,2},{12,4},{14,6},{1,9},{3,11}... | collective-permute-start | bytes 737288 | tf_op jit(solution)/shard_map/ppermute | solution.py:40
  14.8 0.5 collective-permute-start.3
  16.0 0.8 shard_map.156
  16.8 6.6 %collective-permute-done.1.refs_0_ = bf16[960,128]{1,0:T(8,128)(2,1)S(1)} collective-permute-done((bf16[960,128]{1,0:T(8,128)(2,1)S(1)}, bf16[960,128]{1,0:T(8,128)(2,1)S(1)}, u32[]{:S(2)}, u32[]{:S(2)}) %collective-permute-start.1) | collective-permute-done | bytes 245792 | tf_op jit(solution)/shard_map/ppermute | solution.py:40
  23.4 1.0 %collective-permute-done.3.refs_2_ = bf16[960,128]{1,0:T(8,128)(2,1)S(1)} collective-permute-done((bf16[960,128]{1,0:T(8,128)(2,1)S(1)}, bf16[960,128]{1,0:T(8,128)(2,1)S(1)}, u32[]{:S(2)}, u32[]{:S(2)}) %collective-permute-start.3) | collective-permute-done | bytes 245792 | tf_op jit(solution)/shard_map/ppermute | solution.py:40
  24.4 0.4 shard_map.157
  24.7 2.6 %collective-permute-start.6 = (bf16[1504,128]{1,0:T(8,128)(2,1)S(1)}, bf16[1504,128]{1,0:T(8,128)(2,1)S(1)}, u32[]{:S(2)}, u32[]{:S(2)}) collective-permute-start(bf16[1504,128]{1,0:T(8,128)(2,1)S(1)} %get-tuple-element.94), channel_id=1, source_target_pairs={{0,4},{2,6},{4,0},{6,2},{8,12},{10,14},{12,8},{14,10},{1,5},{3,7},... | collective-permute-start | bytes 1155080 | tf_op jit(solution)/shard_map/ppermute | solution.py:40
  27.3 1.5 %collective-permute-start.7 = (bf16[1440,128]{1,0:T(8,128)(2,1)S(1)}, bf16[1440,128]{1,0:T(8,128)(2,1)S(1)}, u32[]{:S(2)}, u32[]{:S(2)}) collective-permute-start(bf16[1440,128]{1,0:T(8,128)(2,1)S(1)} %get-tuple-element.95), channel_id=1, source_target_pairs={{0,2},{2,0},{4,6},{6,4},{8,10},{10,8},{12,14},{14,12},{1,3},{3,1},... | collective-permute-start | bytes 1105928 | tf_op jit(solution)/shard_map/ppermute | solution.py:40
  28.8 1.6 %collective-permute-start.5 = (bf16[960,128]{1,0:T(8,128)(2,1)S(1)}, bf16[960,128]{1,0:T(8,128)(2,1)S(1)}, u32[]{:S(2)}, u32[]{:S(2)}) collective-permute-start(bf16[960,128]{1,0:T(8,128)(2,1)S(1)} %get-tuple-element.93), channel_id=1, source_target_pairs={{0,8},{2,10},{4,12},{6,14},{8,0},{10,2},{12,4},{14,6},{1,9},{3,11}... | collective-permute-start | bytes 737288 | tf_op jit(solution)/shard_map/ppermute | solution.py:40
  30.3 9.5 %collective-permute-done.5.refs_0_ = bf16[960,128]{1,0:T(8,128)(2,1)S(1)} collective-permute-done((bf16[960,128]{1,0:T(8,128)(2,1)S(1)}, bf16[960,128]{1,0:T(8,128)(2,1)S(1)}, u32[]{:S(2)}, u32[]{:S(2)}) %collective-permute-start.5) | collective-permute-done | bytes 245792 | tf_op jit(solution)/shard_map/ppermute | solution.py:40
  39.9 0.7 collective-permute-done.6.refs_1_
  40.6 0.8 shard_map.158
  41.4 2.7 %collective-permute-start.8 = (bf16[544,128]{1,0:T(8,128)(2,1)S(1)}, bf16[544,128]{1,0:T(8,128)(2,1)S(1)}, u32[]{:S(2)}, u32[]{:S(2)}) collective-permute-start(bf16[544,128]{1,0:T(8,128)(2,1)S(1)} %get-tuple-element.104), channel_id=1, source_target_pairs={{0,8},{2,10},{4,12},{6,14},{8,0},{10,2},{12,4},{14,6},{1,9},{3,11}... | collective-permute-start | bytes 417800 | tf_op jit(solution)/shard_map/ppermute | solution.py:40
  44.1 4.9 %collective-permute-done.9.refs_1_ = bf16[480,128]{1,0:T(8,128)(2,1)S(1)} collective-permute-done((bf16[480,128]{1,0:T(8,128)(2,1)S(1)}, bf16[480,128]{1,0:T(8,128)(2,1)S(1)}, u32[]{:S(2)}, u32[]{:S(2)}) %collective-permute-start.9) | collective-permute-done | bytes 122912 | tf_op jit(solution)/shard_map/ppermute | solution.py:40
  49.0 0.2 collective-permute-done.8.refs_0_
  49.2 0.3 shard_map.159
  49.5 1.8 %collective-permute-start.10 = (f32[8,128]{1,0:T(8,128)S(1)}, f32[8,128]{1,0:T(8,128)S(1)}, u32[]{:S(2)}, u32[]{:S(2)}) collective-permute-start(f32[8,128]{1,0:T(8,128)S(1)} %get-tuple-element.109), channel_id=1, source_target_pairs={{0,2},{2,0},{4,6},{6,4},{8,10},{10,8},{12,14},{14,12},{1,3},{3,1},... | collective-permute-start | bytes 12296 | tf_op jit(solution)/shard_map/ppermute | solution.py:40
  51.2 1.1 %collective-permute-start.11 = (f32[8,128]{1,0:T(8,128)S(1)}, f32[8,128]{1,0:T(8,128)S(1)}, u32[]{:S(2)}, u32[]{:S(2)}) collective-permute-start(f32[8,128]{1,0:T(8,128)S(1)} %get-tuple-element.109), channel_id=1, source_target_pairs={{0,4},{2,6},{4,0},{6,2},{8,12},{10,14},{12,8},{14,10},{1,5},{3,7},... | collective-permute-start | bytes 12296 | tf_op jit(solution)/shard_map/ppermute | solution.py:40
  52.3 0.7 collective-permute-start.12
  53.0 0.1 collective-permute-done.10
  53.1 1.7 %collective-permute-done.11 = f32[8,128]{1,0:T(8,128)S(1)} collective-permute-done((f32[8,128]{1,0:T(8,128)S(1)}, f32[8,128]{1,0:T(8,128)S(1)}, u32[]{:S(2)}, u32[]{:S(2)}) %collective-permute-start.11) | collective-permute-done | bytes 4128 | tf_op jit(solution)/shard_map/ppermute | solution.py:40
  54.9 2.1 %collective-permute-done.12 = f32[8,128]{1,0:T(8,128)S(1)} collective-permute-done((f32[8,128]{1,0:T(8,128)S(1)}, f32[8,128]{1,0:T(8,128)S(1)}, u32[]{:S(2)}, u32[]{:S(2)}) %collective-permute-start.12) | collective-permute-done | bytes 4128 | tf_op jit(solution)/shard_map/ppermute | solution.py:40
  56.9 0.9 %collective-permute-start.15 = (bf16[4,240,128]{2,1,0:T(8,128)(2,1)S(1)}, bf16[4,240,128]{2,1,0:T(8,128)(2,1)S(1)}, u32[]{:S(2)}, u32[]{:S(2)}) collective-permute-start(bf16[4,240,128]{2,1,0:T(8,128)(2,1)S(1)} %get-tuple-element.117.refs_0_), channel_id=1, source_target_pairs={{0,4},{2,6},{4,0},{6,2},{8,12},{10,14},{12,8},{14,10},{1,5},{3,7},... | collective-permute-start | bytes 737288 | tf_op jit(solution)/shard_map/ppermute | solution.py:40
  57.9 0.3 collective-permute-start.18
  58.2 1.2 %collective-permute-done.13 = f32[8,128]{1,0:T(8,128)S(1)} collective-permute-done((f32[8,128]{1,0:T(8,128)S(1)}, f32[8,128]{1,0:T(8,128)S(1)}, u32[]{:S(2)}, u32[]{:S(2)}) %collective-permute-start.13) | collective-permute-done | bytes 4128 | tf_op jit(solution)/shard_map/ppermute | solution.py:40
  59.3 1.8 %collective-permute-start.14 = (f32[8,128]{1,0:T(8,128)S(1)}, f32[8,128]{1,0:T(8,128)S(1)}, u32[]{:S(2)}, u32[]{:S(2)}) collective-permute-start(f32[8,128]{1,0:T(8,128)S(1)} %add.24.square_ref), channel_id=1, source_target_pairs={{0,8},{2,10},{4,12},{6,14},{8,0},{10,2},{12,4},{14,6},{1,9},{3,11}... | collective-permute-start | bytes 12296 | tf_op jit(solution)/shard_map/ppermute | solution.py:40
  61.1 2.7 %collective-permute-done.14.other_ref = f32[8,128]{1,0:T(8,128)S(1)} collective-permute-done((f32[8,128]{1,0:T(8,128)S(1)}, f32[8,128]{1,0:T(8,128)S(1)}, u32[]{:S(2)}, u32[]{:S(2)}) %collective-permute-start.14) | collective-permute-done | bytes 4128 | tf_op jit(solution)/shard_map/ppermute | solution.py:40
  63.9 0.6 shard_map.160
  64.5 0.1 collective-permute-start.16
  64.6 1.2 %collective-permute-done.16 = f32[8,8,256]{2,1,0:T(8,128)S(1)} collective-permute-done((f32[8,8,256]{2,1,0:T(8,128)S(1)}, f32[8,8,256]{2,1,0:T(8,128)S(1)}, u32[]{:S(2)}, u32[]{:S(2)}) %collective-permute-start.16) | collective-permute-done | bytes 65568 | tf_op jit(solution)/shard_map/ppermute | solution.py:40
  65.9 1.3 %collective-permute-start.17 = (f32[4,8,256]{2,1,0:T(8,128)S(1)}, f32[4,8,256]{2,1,0:T(8,128)S(1)}, u32[]{:S(2)}, u32[]{:S(2)}) collective-permute-start(f32[4,8,256]{2,1,0:T(8,128)S(1)} %pad_maximum_fusion), channel_id=1, source_target_pairs={{0,4},{2,6},{4,0},{6,2},{8,12},{10,14},{12,8},{14,10},{1,5},{3,7},... | collective-permute-start | bytes 98312 | tf_op jit(solution)/shard_map/ppermute | solution.py:40
  67.2 1.7 %shard_map.161 = (f32[240,512]{1,0:T(8,128)}, f32[240,512]{1,0:T(8,128)}, f32[240,512]{1,0:T(8,128)}, f32[8,128]{1,0:T(8,128)S(1)}) custom-call(f32[8,128]{1,0:T(8,128)S(1)} %add.24.square_ref, f32[8,128]{1,0:T(8,128)S(1)} %collective-permute-done.14.other_ref, f32[240,512]{1,0:T(8,128)S(1)} %get-tuple-element.124.grad_ref, f32[240,512]{1,0:T(8,128)S(1)} %copy-done, ...), custom_call_target="tpu_custom_call" | custom-call | flops 1 | bytes 1 | tf_op jit(solution)/shard_map/pallas_call | solution.py:816
  68.8 1.0 %collective-permute-done.17 = f32[4,8,256]{2,1,0:T(8,128)S(1)} collective-permute-done((f32[4,8,256]{2,1,0:T(8,128)S(1)}, f32[4,8,256]{2,1,0:T(8,128)S(1)}, u32[]{:S(2)}, u32[]{:S(2)}) %collective-permute-start.17) | collective-permute-done | bytes 32800 | tf_op jit(solution)/shard_map/ppermute | solution.py:40
  69.8 1.8 %collective-permute-start.19 = (f32[2,8,256]{2,1,0:T(8,128)S(1)}, f32[2,8,256]{2,1,0:T(8,128)S(1)}, u32[]{:S(2)}, u32[]{:S(2)}) collective-permute-start(f32[2,8,256]{2,1,0:T(8,128)S(1)} %stack.28), channel_id=1, source_target_pairs={{0,8},{2,10},{4,12},{6,14},{8,0},{10,2},{12,4},{14,6},{1,9},{3,11}... | collective-permute-start | bytes 49160 | tf_op jit(solution)/shard_map/ppermute | solution.py:40
  71.7 0.9 %shard_map.162 = (f32[384,1920]{1,0:T(8,128)S(1)}, f32[8,128]{1,0:T(8,128)S(1)}) custom-call(s32[1]{0:T(128)} %bitcast.here_ref, bf16[384,256]{1,0:T(8,128)(2,1)S(1)} %copy-done.3, f32[8,128]{1,0:T(8,128)S(1)} %get-tuple-element.126.gate_ref.near_ref, bf16[4,240,128]{2,1,0:T(8,128)(2,1)S(1)} %get-tuple-element.117.refs_0_, ...), custom_call_target="tpu_custom_call" | custom-call | flops 1 | bytes 1 | tf_op jit(solution)/shard_map/pallas_call | solution.py:714
  72.5 2.0 %collective-permute-done.19 = f32[2,8,256]{2,1,0:T(8,128)S(1)} collective-permute-done((f32[2,8,256]{2,1,0:T(8,128)S(1)}, f32[2,8,256]{2,1,0:T(8,128)S(1)}, u32[]{:S(2)}, u32[]{:S(2)}) %collective-permute-start.19) | collective-permute-done | bytes 16416 | tf_op jit(solution)/shard_map/ppermute | solution.py:40
  74.6 1.8 %collective-permute-start.20 = (f32[1,8,256]{2,1,0:T(8,128)S(1)}, f32[1,8,256]{2,1,0:T(8,128)S(1)}, u32[]{:S(2)}, u32[]{:S(2)}) collective-permute-start(f32[1,8,256]{2,1,0:T(8,128)S(1)} %get-tuple-element.148), channel_id=1, source_target_pairs={{0,2},{2,0},{4,6},{6,4},{8,10},{10,8},{12,14},{14,12},{1,3},{3,1},... | collective-permute-start | bytes 24584 | tf_op jit(solution)/shard_map/ppermute | solution.py:40
  76.3 2.2 %shard_map.163 = (bf16[384,1920]{1,0:T(8,128)(2,1)}, f32[8,128]{1,0:T(8,128)S(1)}) custom-call(s32[1]{0:T(128)} %bitcast.here_ref, bf16[384,256]{1,0:T(8,128)(2,1)S(1)} %collective-permute-done.refs_1_.cot_ref, f32[384,1920]{1,0:T(8,128)S(1)} %get-tuple-element.129.near_ref, bf16[4,240,128]{2,1,0:T(8,128)(2,1)S(1)} %get-tuple-element.117.refs_0_, ...), custom_call_target="tpu_custom_call" | custom-call | flops 1 | bytes 1 | tf_op jit(solution)/shard_map/pallas_call | solution.py:732
  78.6 1.1 %shard_map.164 = (bf16[1,8,256]{2,1,0:T(8,128)(2,1)}, bf16[1,8,2048]{2,1,0:T(8,128)(2,1)}) custom-call(bf16[1,8,2048]{2,1,0:T(8,128)(2,1)S(1)} %copy-done.6, f32[1,8,256]{2,1,0:T(8,128)S(1)} %get-tuple-element.149.keep_ref, f32[1,8,256]{2,1,0:T(8,128)S(1)} %collective-permute-done.20.other_ref, bf16[1,8,256]{2,1,0:T(8,128)(2,1)S(1)} %copy-done.7, ...), custom_call_target="tpu_custom_call" | custom-call | flops 1 | bytes 1 | tf_op jit(solution)/shard_map/pallas_call | solution.py:569
  (32 shorter events, 0.1 us)
Async XLA Ops:
  0.6 7.0 %copy-start.3 = (bf16[384,256]{1,0:T(8,128)(2,1)S(1)}, bf16[384,256]{1,0:T(8,128)(2,1)}, u32[]{:S(2)}) copy-start(bf16[384,256]{1,0:T(8,128)(2,1)} %cot_ref.1) | copy-start | bytes 589828
  4.5 11.5 %copy-start.4 = (bf16[1,1024,256]{2,1,0:T(8,128)(2,1)S(1)}, bf16[1,1024,256]{2,1,0:T(8,128)(2,1)}, u32[]{:S(2)}) copy-start(bf16[1,1024,256]{2,1,0:T(8,128)(2,1)} %keys_ref.1) | copy-start | bytes 1572868
  4.5 11.5 %copy-start.5 = (bf16[1,1024,256]{2,1,0:T(8,128)(2,1)S(1)}, bf16[1,1024,256]{2,1,0:T(8,128)(2,1)}, u32[]{:S(2)}) copy-start(bf16[1,1024,256]{2,1,0:T(8,128)(2,1)} %values_ref.2) | copy-start | bytes 1572868
  4.5 11.5 %copy-start.6 = (bf16[1,8,2048]{2,1,0:T(8,128)(2,1)S(1)}, bf16[1,8,2048]{2,1,0:T(8,128)(2,1)}, u32[]{:S(2)}) copy-start(bf16[1,8,2048]{2,1,0:T(8,128)(2,1)} %query_ref.3) | copy-start | bytes 98308
  4.5 19.8 %collective-permute-start.2 = (bf16[1920,128]{1,0:T(8,128)(2,1)S(1)}, bf16[1920,128]{1,0:T(8,128)(2,1)S(1)}, u32[]{:S(2)}, u32[]{:S(2)}) collective-permute-start(bf16[1920,128]{1,0:T(8,128)(2,1)S(1)} %get-tuple-element.83), channel_id=1, source_target_pairs={{0,4},{2,6},{4,0},{6,2},{8,12},{10,14},{12,8},{14,10},{1,5},{3,7},... | collective-permute-start | bytes 1474568 | tf_op jit(solution)/shard_map/ppermute | solution.py:40
  7.6 1.4 %collective-permute-start = (bf16[384,256]{1,0:T(8,128)(2,1)S(1)}, bf16[384,256]{1,0:T(8,128)(2,1)S(1)}, u32[]{:S(2)}, u32[]{:S(2)}) collective-permute-start(bf16[384,256]{1,0:T(8,128)(2,1)S(1)} %copy-done.3), channel_id=1, source_target_pairs={{0,1},{1,0},{2,3},{3,2},{4,5},{5,4},{6,7},{7,6},{8,9},{9,8},{10,11... | collective-permute-start | bytes 589832 | tf_op jit(solution)/shard_map/ppermute | solution.py:40
  10.7 13.7 %collective-permute-start.4 = (bf16[1024,128]{1,0:T(8,128)(2,1)S(1)}, bf16[1024,128]{1,0:T(8,128)(2,1)S(1)}, u32[]{:S(2)}, u32[]{:S(2)}) collective-permute-start(bf16[1024,128]{1,0:T(8,128)(2,1)S(1)} %get-tuple-element.85), channel_id=1, source_target_pairs={{0,2},{2,0},{4,6},{6,4},{8,10},{10,8},{12,14},{14,12},{1,3},{3,1},... | collective-permute-start | bytes 786440 | tf_op jit(solution)/shard_map/ppermute | solution.py:40
  12.2 11.2 %collective-permute-start.1 = (bf16[960,128]{1,0:T(8,128)(2,1)S(1)}, bf16[960,128]{1,0:T(8,128)(2,1)S(1)}, u32[]{:S(2)}, u32[]{:S(2)}) collective-permute-start(bf16[960,128]{1,0:T(8,128)(2,1)S(1)} %get-tuple-element.81), channel_id=1, source_target_pairs={{0,8},{2,10},{4,12},{6,14},{8,0},{10,2},{12,4},{14,6},{1,9},{3,11}... | collective-permute-start | bytes 737288 | tf_op jit(solution)/shard_map/ppermute | solution.py:40
  14.8 9.5 %collective-permute-start.3 = (bf16[960,128]{1,0:T(8,128)(2,1)S(1)}, bf16[960,128]{1,0:T(8,128)(2,1)S(1)}, u32[]{:S(2)}, u32[]{:S(2)}) collective-permute-start(bf16[960,128]{1,0:T(8,128)(2,1)S(1)} %get-tuple-element.84), channel_id=1, source_target_pairs={{0,2},{2,0},{4,6},{6,4},{8,10},{10,8},{12,14},{14,12},{1,3},{3,1},... | collective-permute-start | bytes 737288 | tf_op jit(solution)/shard_map/ppermute | solution.py:40
  24.7 15.9 %collective-permute-start.6 = (bf16[1504,128]{1,0:T(8,128)(2,1)S(1)}, bf16[1504,128]{1,0:T(8,128)(2,1)S(1)}, u32[]{:S(2)}, u32[]{:S(2)}) collective-permute-start(bf16[1504,128]{1,0:T(8,128)(2,1)S(1)} %get-tuple-element.94), channel_id=1, source_target_pairs={{0,4},{2,6},{4,0},{6,2},{8,12},{10,14},{12,8},{14,10},{1,5},{3,7},... | collective-permute-start | bytes 1155080 | tf_op jit(solution)/shard_map/ppermute | solution.py:40
  27.3 12.6 %collective-permute-start.7 = (bf16[1440,128]{1,0:T(8,128)(2,1)S(1)}, bf16[1440,128]{1,0:T(8,128)(2,1)S(1)}, u32[]{:S(2)}, u32[]{:S(2)}) collective-permute-start(bf16[1440,128]{1,0:T(8,128)(2,1)S(1)} %get-tuple-element.95), channel_id=1, source_target_pairs={{0,2},{2,0},{4,6},{6,4},{8,10},{10,8},{12,14},{14,12},{1,3},{3,1},... | collective-permute-start | bytes 1105928 | tf_op jit(solution)/shard_map/ppermute | solution.py:40
  28.8 11.1 %collective-permute-start.5 = (bf16[960,128]{1,0:T(8,128)(2,1)S(1)}, bf16[960,128]{1,0:T(8,128)(2,1)S(1)}, u32[]{:S(2)}, u32[]{:S(2)}) collective-permute-start(bf16[960,128]{1,0:T(8,128)(2,1)S(1)} %get-tuple-element.93), channel_id=1, source_target_pairs={{0,8},{2,10},{4,12},{6,14},{8,0},{10,2},{12,4},{14,6},{1,9},{3,11}... | collective-permute-start | bytes 737288 | tf_op jit(solution)/shard_map/ppermute | solution.py:40
  40.6 23.2 %copy-start = (f32[240,512]{1,0:T(8,128)S(1)}, f32[240,512]{1,0:T(8,128)}, u32[]{:S(2)}) copy-start(f32[240,512]{1,0:T(8,128)} %master_ref.3) | copy-start | bytes 1474564
  40.6 23.2 %copy-start.1 = (f32[240,512]{1,0:T(8,128)S(1)}, f32[240,512]{1,0:T(8,128)}, u32[]{:S(2)}) copy-start(f32[240,512]{1,0:T(8,128)} %first_ref.3) | copy-start | bytes 1474564
  40.6 23.2 %copy-start.2 = (f32[240,512]{1,0:T(8,128)S(1)}, f32[240,512]{1,0:T(8,128)}, u32[]{:S(2)}) copy-start(f32[240,512]{1,0:T(8,128)} %second_ref.3) | copy-start | bytes 1474564
  41.4 7.8 %collective-permute-start.8 = (bf16[544,128]{1,0:T(8,128)(2,1)S(1)}, bf16[544,128]{1,0:T(8,128)(2,1)S(1)}, u32[]{:S(2)}, u32[]{:S(2)}) collective-permute-start(bf16[544,128]{1,0:T(8,128)(2,1)S(1)} %get-tuple-element.104), channel_id=1, source_target_pairs={{0,8},{2,10},{4,12},{6,14},{8,0},{10,2},{12,4},{14,6},{1,9},{3,11}... | collective-permute-start | bytes 417800 | tf_op jit(solution)/shard_map/ppermute | solution.py:40
  44.1 4.9 %collective-permute-start.9 = (bf16[480,128]{1,0:T(8,128)(2,1)S(1)}, bf16[480,128]{1,0:T(8,128)(2,1)S(1)}, u32[]{:S(2)}, u32[]{:S(2)}) collective-permute-start(bf16[480,128]{1,0:T(8,128)(2,1)S(1)} %get-tuple-element.105), channel_id=1, source_target_pairs={{0,4},{2,6},{4,0},{6,2},{8,12},{10,14},{12,8},{14,10},{1,5},{3,7},... | collective-permute-start | bytes 368648 | tf_op jit(solution)/shard_map/ppermute | solution.py:40
  49.5 3.7 %collective-permute-start.10 = (f32[8,128]{1,0:T(8,128)S(1)}, f32[8,128]{1,0:T(8,128)S(1)}, u32[]{:S(2)}, u32[]{:S(2)}) collective-permute-start(f32[8,128]{1,0:T(8,128)S(1)} %get-tuple-element.109), channel_id=1, source_target_pairs={{0,2},{2,0},{4,6},{6,4},{8,10},{10,8},{12,14},{14,12},{1,3},{3,1},... | collective-permute-start | bytes 12296 | tf_op jit(solution)/shard_map/ppermute | solution.py:40
  51.2 3.6 %collective-permute-start.11 = (f32[8,128]{1,0:T(8,128)S(1)}, f32[8,128]{1,0:T(8,128)S(1)}, u32[]{:S(2)}, u32[]{:S(2)}) collective-permute-start(f32[8,128]{1,0:T(8,128)S(1)} %get-tuple-element.109), channel_id=1, source_target_pairs={{0,4},{2,6},{4,0},{6,2},{8,12},{10,14},{12,8},{14,10},{1,5},{3,7},... | collective-permute-start | bytes 12296 | tf_op jit(solution)/shard_map/ppermute | solution.py:40
  52.3 4.6 %collective-permute-start.12 = (f32[8,128]{1,0:T(8,128)S(1)}, f32[8,128]{1,0:T(8,128)S(1)}, u32[]{:S(2)}, u32[]{:S(2)}) collective-permute-start(f32[8,128]{1,0:T(8,128)S(1)} %get-tuple-element.109), channel_id=1, source_target_pairs={{0,6},{2,4},{4,2},{6,0},{8,14},{10,12},{12,10},{14,8},{1,7},{3,5},... | collective-permute-start | bytes 12296 | tf_op jit(solution)/shard_map/ppermute | solution.py:40
  56.9 6.9 %collective-permute-start.15 = (bf16[4,240,128]{2,1,0:T(8,128)(2,1)S(1)}, bf16[4,240,128]{2,1,0:T(8,128)(2,1)S(1)}, u32[]{:S(2)}, u32[]{:S(2)}) collective-permute-start(bf16[4,240,128]{2,1,0:T(8,128)(2,1)S(1)} %get-tuple-element.117.refs_0_), channel_id=1, source_target_pairs={{0,4},{2,6},{4,0},{6,2},{8,12},{10,14},{12,8},{14,10},{1,5},{3,7},... | collective-permute-start | bytes 737288 | tf_op jit(solution)/shard_map/ppermute | solution.py:40
  57.9 13.8 %collective-permute-start.18 = (bf16[12,240,128]{2,1,0:T(8,128)(2,1)S(1)}, bf16[12,240,128]{2,1,0:T(8,128)(2,1)S(1)}, u32[]{:S(2)}, u32[]{:S(2)}) collective-permute-start(bf16[12,240,128]{2,1,0:T(8,128)(2,1)S(1)} %get-tuple-element.127.refs_1_), channel_id=1, source_target_pairs={{0,2},{2,0},{4,6},{6,4},{8,10},{10,8},{12,14},{14,12},{1,3},{3,1},... | collective-permute-start | bytes 2211848 | tf_op jit(solution)/shard_map/ppermute | solution.py:40
  58.2 1.2 %collective-permute-start.13 = (f32[8,128]{1,0:T(8,128)S(1)}, f32[8,128]{1,0:T(8,128)S(1)}, u32[]{:S(2)}, u32[]{:S(2)}) collective-permute-start(f32[8,128]{1,0:T(8,128)S(1)} %add_add_fusion), channel_id=1, source_target_pairs={{0,1},{1,0},{2,3},{3,2},{4,5},{5,4},{6,7},{7,6},{8,9},{9,8},{10,11... | collective-permute-start | bytes 12296 | tf_op jit(solution)/shard_map/ppermute | solution.py:40
  59.3 4.5 %collective-permute-start.14 = (f32[8,128]{1,0:T(8,128)S(1)}, f32[8,128]{1,0:T(8,128)S(1)}, u32[]{:S(2)}, u32[]{:S(2)}) collective-permute-start(f32[8,128]{1,0:T(8,128)S(1)} %add.24.square_ref), channel_id=1, source_target_pairs={{0,8},{2,10},{4,12},{6,14},{8,0},{10,2},{12,4},{14,6},{1,9},{3,11}... | collective-permute-start | bytes 12296 | tf_op jit(solution)/shard_map/ppermute | solution.py:40
  64.5 1.3 %collective-permute-start.16 = (f32[8,8,256]{2,1,0:T(8,128)S(1)}, f32[8,8,256]{2,1,0:T(8,128)S(1)}, u32[]{:S(2)}, u32[]{:S(2)}) collective-permute-start(f32[8,8,256]{2,1,0:T(8,128)S(1)} %get-tuple-element.123), channel_id=1, source_target_pairs={{0,1},{1,0},{2,3},{3,2},{4,5},{5,4},{6,7},{7,6},{8,9},{9,8},{10,11... | collective-permute-start | bytes 196616 | tf_op jit(solution)/shard_map/ppermute | solution.py:40
  65.9 4.0 %collective-permute-start.17 = (f32[4,8,256]{2,1,0:T(8,128)S(1)}, f32[4,8,256]{2,1,0:T(8,128)S(1)}, u32[]{:S(2)}, u32[]{:S(2)}) collective-permute-start(f32[4,8,256]{2,1,0:T(8,128)S(1)} %pad_maximum_fusion), channel_id=1, source_target_pairs={{0,4},{2,6},{4,0},{6,2},{8,12},{10,14},{12,8},{14,10},{1,5},{3,7},... | collective-permute-start | bytes 98312 | tf_op jit(solution)/shard_map/ppermute | solution.py:40
  69.8 4.7 %collective-permute-start.19 = (f32[2,8,256]{2,1,0:T(8,128)S(1)}, f32[2,8,256]{2,1,0:T(8,128)S(1)}, u32[]{:S(2)}, u32[]{:S(2)}) collective-permute-start(f32[2,8,256]{2,1,0:T(8,128)S(1)} %stack.28), channel_id=1, source_target_pairs={{0,8},{2,10},{4,12},{6,14},{8,0},{10,2},{12,4},{14,6},{1,9},{3,11}... | collective-permute-start | bytes 49160 | tf_op jit(solution)/shard_map/ppermute | solution.py:40
  74.6 4.0 %collective-permute-start.20 = (f32[1,8,256]{2,1,0:T(8,128)S(1)}, f32[1,8,256]{2,1,0:T(8,128)S(1)}, u32[]{:S(2)}, u32[]{:S(2)}) collective-permute-start(f32[1,8,256]{2,1,0:T(8,128)S(1)} %get-tuple-element.148), channel_id=1, source_target_pairs={{0,2},{2,0},{4,6},{6,4},{8,10},{10,8},{12,14},{14,12},{1,3},{3,1},... | collective-permute-start | bytes 24584 | tf_op jit(solution)/shard_map/ppermute | solution.py:40
  76.3 2.3 %copy-start.7 = (bf16[1,8,256]{2,1,0:T(8,128)(2,1)S(1)}, bf16[1,8,256]{2,1,0:T(8,128)(2,1)}, u32[]{:S(2)}) copy-start(bf16[1,8,256]{2,1,0:T(8,128)(2,1)} %values_ref.3) | copy-start | bytes 12292

commit v6 on v5

--- a/solution.py
+++ b/solution.py
@@ -661,20 +661,20 @@
 
 
 def near_kernel(bits, unit, which, here_ref, cot_ref, gate_ref, *refs):
-    blocks, out_ref, token_ref, weight = refs[:-3], refs[-3], refs[-2], refs[-1]
+    blocks, out_ref, far_ref, token_ref, weight = refs[:-4], *refs[-4:]
     token_ref[...] = jnp.zeros(token_ref.shape, jnp.float32)
     columns = out_ref.shape[1]
-    lay_out(bits, unit, which, here_ref[0], columns >> bits, block_reader(bits, blocks), weight)
+    held = block_reader(bits, blocks)
+    lay_out(bits, unit, which[0], here_ref[0], columns >> bits, held, weight)
+    lay_out(bits, unit, which[1], here_ref[0], columns >> bits, held, far_ref)
     tile = 384 if columns % 384 == 0 else columns
     for at in range(0, columns, tile):
         out_ref[:, at : at + tile] = contract_last(cot_ref[...], weight[at : at + tile, :])
 
 
-def far_kernel(bits, unit, which, here_ref, cot_ref, near_ref, *refs):
-    blocks, out_ref, token_ref, weight, result, done = refs[:-5], *refs[-5:]
+def far_kernel(cot_ref, near_ref, weight, out_ref, token_ref, result, done):
     token_ref[...] = jnp.zeros(token_ref.shape, jnp.float32)
-    count, columns = result.shape
-    lay_out(bits, unit, which, here_ref[0], columns >> bits, block_reader(bits, blocks), weight)
+    count = result.shape[0]
     tile = count // done.shape[0]
     copies = []
     for i in range(done.shape[0]):
@@ -710,38 +710,37 @@
     columns = owned << bits
     if owned % 16 != 0:
         product = contract_last(cot, gathered_columns(bits, (0, 1), blocks))
-        return product, gate
+        return product, gathered_columns(bits, (2, 3), blocks), gate
     return pl.pallas_call(
-        functools.partial(near_kernel, bits, unit, (0, 1)),
-        out_shape=[jax.ShapeDtypeStruct((cot.shape[0], columns), jnp.float32), TOKEN],
+        functools.partial(near_kernel, bits, unit, ((0, 1), (2, 3))),
+        out_shape=[
+            jax.ShapeDtypeStruct((cot.shape[0], columns), jnp.float32),
+            jax.ShapeDtypeStruct((columns, 2 * unit), jnp.bfloat16),
+            TOKEN,
+        ],
         in_specs=[SMEM] + [VMEM] * (2 + len(blocks)),
-        out_specs=[VMEM] * 2,
+        out_specs=[VMEM] * 3,
         scratch_shapes=[pltpu.VMEM((columns, 2 * unit), jnp.bfloat16)],
         compiler_params=INPUT,
         cost_estimate=TINY,
     )(lax.axis_index("fsdp").astype(jnp.int32).reshape(1), cot, gate, *blocks)
 
 
-def input_far(bits, owned, unit, cot, near, blocks):
-    columns = owned << bits
-    if owned % 16 != 0:
-        product = near + contract_last(cot, gathered_columns(bits, (2, 3), blocks))
-        return (unit_scale * product).astype(jnp.bfloat16), jnp.zeros(TOKEN.shape, TOKEN.dtype)
-    tokens = cot.shape[0]
+def input_far(cot, near, weight):
+    tokens, columns = near.shape
     pieces = 4 if tokens % 64 == 0 else 1
     return pl.pallas_call(
-        functools.partial(far_kernel, bits, unit, (2, 3)),
+        far_kernel,
         out_shape=[jax.ShapeDtypeStruct((tokens, columns), jnp.bfloat16), TOKEN],
-        in_specs=[SMEM] + [VMEM] * (2 + len(blocks)),
+        in_specs=[VMEM] * 3,
         out_specs=[pl.BlockSpec(memory_space=pl.ANY), VMEM],
         scratch_shapes=[
-            pltpu.VMEM((columns, 2 * unit), jnp.bfloat16),
             pltpu.VMEM((tokens, columns), jnp.bfloat16),
             pltpu.SemaphoreType.DMA((pieces,)),
         ],
         compiler_params=INPUT,
         cost_estimate=TINY,
-    )(lax.axis_index("fsdp").astype(jnp.int32).reshape(1), cot, near, *blocks)
+    )(cot, near, weight)
 
 
 def adamw(factor, grad, master, first, second):
@@ -924,14 +923,14 @@
         names = [name for name in names if not (name >> bit) & 1]
         come = swap(give, "fsdp", bit)
         if bit == 1:
-            come, updated_token = tied(come, updated_token)
+            pass
         if bit == 2:
-            near_sum, near_token = input_near(
+            near_sum, far_weight, near_token = input_near(
                 bits, owned, unit, learn_grad_out, blocks + late, updated_token
             )
-            come, near_token = tied(come, near_token)
+            come, near_token, updated_token = tied(come, near_token, updated_token)
         if bit == 0:
-            grad_in, far_token = input_far(bits, owned, unit, other_cot, near_sum, blocks + late)
+            grad_in, far_token = input_far(other_cot, near_sum, far_weight)
         projected = keep + come
     shape = (row_count, steps, column_count)
     step_keys, attention = attend_fresh(

time: 79.8 us -> 79.3 us (level)
  starting transfers between devices: 27.6 us -> 26.6 us
    ppermute x21, starting transfers between devices: 27.6 us -> 26.6 us  [swap_with(): return lax.ppermute(value, axis, [(i, i ^ mask) for i in range(size)])]
where the time goes in v6:
time: 79.3 us; the launch traced here: 79.1 us
  waiting for transfers between devices  37 us (47%)
  starting transfers between devices  26.6 us (34%)
  Pallas kernels  13.9 us (18%)
  between operations  1.45 us (2%)
    ppermute x21, waiting for transfers between devices, swap_with(): return lax.ppermute(value, axis, [(i, i ^ mask) for i in range(size)])  37 us
    ppermute x21, starting transfers between devices, swap_with(): return lax.ppermute(value, axis, [(i, i ^ mask) for i in range(size)])  26.6 us
    pallas_call x2, Pallas kernels, first_stage(): pl.pallas_call(functools.partial(first_kernel, bits, cuts, unit, over, sl...  5.36 us
    pallas_call x1, Pallas kernels, input_far(): pl.pallas_call(far_kernel, out_shape=[jax.ShapeDtypeStruct((tokens, colum...  2.03 us
    pallas_call x1, Pallas kernels, updated(): pl.pallas_call(functools.partial(update_kernel, limit), out_shape=[jax.Sh...  1.65 us
  transfers between devices with their start and end apart: 21, of which 15 were waited for; matrix products, arithmetic and copies ran while one was open for 0% of the time, Pallas kernels for 10%

profile of v6, /device:TPU:0, one launch (start us, length us, event | category | flops | bytes accessed | tf_op | source)
XLA Modules:
  0.0 79.1 jit_solution(10217250735519127160)
XLA Ops:
  0.6 0.1 pad_add_fusion.where_ref
  0.7 3.7 %shard_map.154 = (bf16[960,128]{1,0:T(8,128)(2,1)S(1)}, bf16[1920,128]{1,0:T(8,128)(2,1)S(1)}, f32[4,240,256]{2,1,0:T(8,128)S(1)}, bf16[384,1920]{1,0:T(8,128)(2...) custom-call(s32[2]{0:T(128)S(1)} %pad_add_fusion.where_ref, ...), custom_call_target="tpu_custom_call" | custom-call | flops 1 | bytes 1 | tf_op jit(solution)/shard_map/pallas_call | solution.py:360
  4.5 0.0 copy-start.4
  4.5 0.0 copy-start.5
  4.5 3.1 %collective-permute-start.2 = (bf16[1920,128]{1,0:T(8,128)(2,1)S(1)}, bf16[1920,128]{1,0:T(8,128)(2,1)S(1)}, u32[]{:S(2)}, u32[]{:S(2)}) collective-permute-start(bf16[1920,128]{1,0:T(8,128)(2,1)S(1)} %get-tuple-element.83), channel_id=1, source_target_pairs={{0,4},{2,6},{4,0},{6,2},{8,12},{10,14},{12,8},{14,10},{1,5},{3,7},... | collective-permute-start | bytes 1474568 | tf_op jit(solution)/shard_map/ppermute | solution.py:40
  7.6 1.4 %collective-permute-done.refs_1_.cot_ref = bf16[384,256]{1,0:T(8,128)(2,1)S(1)} collective-permute-done((bf16[384,256]{1,0:T(8,128)(2,1)S(1)}, bf16[384,256]{1,0:T(8,128)(2,1)S(1)}, u32[]{:S(2)}, u32[]{:S(2)}) %collective-permute-start) | collective-permute-done | bytes 196640 | tf_op jit(solution)/shard_map/ppermute | solution.py:40
  9.0 1.6 %shard_map.155 = (bf16[960,128]{1,0:T(8,128)(2,1)S(1)}, bf16[1024,128]{1,0:T(8,128)(2,1)S(1)}, f32[4,240,256]{2,1,0:T(8,128)S(1)}, bf16[1,240,128]{2,1,0:T(8,128...) custom-call(s32[2]{0:T(128)S(1)} %pad_add_fusion.where_ref, ...), custom_call_target="tpu_custom_call" | custom-call | flops 1 | bytes 1 | tf_op jit(solution)/shard_map/pallas_call | solution.py:360
  10.7 1.6 %collective-permute-start.4 = (bf16[1024,128]{1,0:T(8,128)(2,1)S(1)}, bf16[1024,128]{1,0:T(8,128)(2,1)S(1)}, u32[]{:S(2)}, u32[]{:S(2)}) collective-permute-start(bf16[1024,128]{1,0:T(8,128)(2,1)S(1)} %get-tuple-element.85), channel_id=1, source_target_pairs={{0,2},{2,0},{4,6},{6,4},{8,10},{10,8},{12,14},{14,12},{1,3},{3,1},... | collective-permute-start | bytes 786440 | tf_op jit(solution)/shard_map/ppermute | solution.py:40
  12.2 2.6 %collective-permute-start.1 = (bf16[960,128]{1,0:T(8,128)(2,1)S(1)}, bf16[960,128]{1,0:T(8,128)(2,1)S(1)}, u32[]{:S(2)}, u32[]{:S(2)}) collective-permute-start(bf16[960,128]{1,0:T(8,128)(2,1)S(1)} %get-tuple-element.81), channel_id=1, source_target_pairs={{0,8},{2,10},{4,12},{6,14},{8,0},{10,2},{12,4},{14,6},{1,9},{3,11}... | collective-permute-start | bytes 737288 | tf_op jit(solution)/shard_map/ppermute | solution.py:40
  14.8 0.5 collective-permute-start.3
  16.0 0.8 %shard_map.156 = (f32[1,2,64,128]{3,2,1,0:T(8,128)S(1)}, f32[1,2,64,128]{3,2,1,0:T(8,128)S(1)}, f32[1,2,64,128]{3,2,1,0:T(8,128)S(1)}) custom-call(s32[1]{0:T(128)S(6)} %copy.17.length_ref, bf16[1,8,2048]{2,1,0:T(8,128)(2,1)S(1)} %copy-done.6, bf16[1,1024,256]{2,1,0:T(8,128)(2,1)S(1)} %copy-done.4, bf16[1,1024,256]{2,1,0:T(8,128)(2,1)S(1)} %copy-done.5, ...), custom_call_target="tpu_custom_call" | custom-call | flops 1 | bytes 1 | tf_op jit(solution)/shard_map/pallas_call | solution.py:521
  16.8 6.6 %collective-permute-done.1.refs_0_ = bf16[960,128]{1,0:T(8,128)(2,1)S(1)} collective-permute-done((bf16[960,128]{1,0:T(8,128)(2,1)S(1)}, bf16[960,128]{1,0:T(8,128)(2,1)S(1)}, u32[]{:S(2)}, u32[]{:S(2)}) %collective-permute-start.1) | collective-permute-done | bytes 245792 | tf_op jit(solution)/shard_map/ppermute | solution.py:40
  23.4 1.0 %collective-permute-done.3.refs_2_ = bf16[960,128]{1,0:T(8,128)(2,1)S(1)} collective-permute-done((bf16[960,128]{1,0:T(8,128)(2,1)S(1)}, bf16[960,128]{1,0:T(8,128)(2,1)S(1)}, u32[]{:S(2)}, u32[]{:S(2)}) %collective-permute-start.3) | collective-permute-done | bytes 245792 | tf_op jit(solution)/shard_map/ppermute | solution.py:40
  24.4 0.4 shard_map.157
  24.7 2.6 %collective-permute-start.6 = (bf16[1504,128]{1,0:T(8,128)(2,1)S(1)}, bf16[1504,128]{1,0:T(8,128)(2,1)S(1)}, u32[]{:S(2)}, u32[]{:S(2)}) collective-permute-start(bf16[1504,128]{1,0:T(8,128)(2,1)S(1)} %get-tuple-element.94), channel_id=1, source_target_pairs={{0,4},{2,6},{4,0},{6,2},{8,12},{10,14},{12,8},{14,10},{1,5},{3,7},... | collective-permute-start | bytes 1155080 | tf_op jit(solution)/shard_map/ppermute | solution.py:40
  27.3 1.5 %collective-permute-start.7 = (bf16[1440,128]{1,0:T(8,128)(2,1)S(1)}, bf16[1440,128]{1,0:T(8,128)(2,1)S(1)}, u32[]{:S(2)}, u32[]{:S(2)}) collective-permute-start(bf16[1440,128]{1,0:T(8,128)(2,1)S(1)} %get-tuple-element.95), channel_id=1, source_target_pairs={{0,2},{2,0},{4,6},{6,4},{8,10},{10,8},{12,14},{14,12},{1,3},{3,1},... | collective-permute-start | bytes 1105928 | tf_op jit(solution)/shard_map/ppermute | solution.py:40
  28.8 1.6 %collective-permute-start.5 = (bf16[960,128]{1,0:T(8,128)(2,1)S(1)}, bf16[960,128]{1,0:T(8,128)(2,1)S(1)}, u32[]{:S(2)}, u32[]{:S(2)}) collective-permute-start(bf16[960,128]{1,0:T(8,128)(2,1)S(1)} %get-tuple-element.93), channel_id=1, source_target_pairs={{0,8},{2,10},{4,12},{6,14},{8,0},{10,2},{12,4},{14,6},{1,9},{3,11}... | collective-permute-start | bytes 737288 | tf_op jit(solution)/shard_map/ppermute | solution.py:40
  30.3 9.5 %collective-permute-done.5.refs_0_ = bf16[960,128]{1,0:T(8,128)(2,1)S(1)} collective-permute-done((bf16[960,128]{1,0:T(8,128)(2,1)S(1)}, bf16[960,128]{1,0:T(8,128)(2,1)S(1)}, u32[]{:S(2)}, u32[]{:S(2)}) %collective-permute-start.5) | collective-permute-done | bytes 245792 | tf_op jit(solution)/shard_map/ppermute | solution.py:40
  39.9 0.7 collective-permute-done.6.refs_1_
  40.6 0.8 shard_map.158
  41.4 2.7 %collective-permute-start.8 = (bf16[544,128]{1,0:T(8,128)(2,1)S(1)}, bf16[544,128]{1,0:T(8,128)(2,1)S(1)}, u32[]{:S(2)}, u32[]{:S(2)}) collective-permute-start(bf16[544,128]{1,0:T(8,128)(2,1)S(1)} %get-tuple-element.104), channel_id=1, source_target_pairs={{0,8},{2,10},{4,12},{6,14},{8,0},{10,2},{12,4},{14,6},{1,9},{3,11}... | collective-permute-start | bytes 417800 | tf_op jit(solution)/shard_map/ppermute | solution.py:40
  44.1 4.9 %collective-permute-done.9.refs_1_ = bf16[480,128]{1,0:T(8,128)(2,1)S(1)} collective-permute-done((bf16[480,128]{1,0:T(8,128)(2,1)S(1)}, bf16[480,128]{1,0:T(8,128)(2,1)S(1)}, u32[]{:S(2)}, u32[]{:S(2)}) %collective-permute-start.9) | collective-permute-done | bytes 122912 | tf_op jit(solution)/shard_map/ppermute | solution.py:40
  49.0 0.2 collective-permute-done.8.refs_0_
  49.2 0.3 shard_map.159
  49.4 2.4 %collective-permute-start.12 = (f32[8,128]{1,0:T(8,128)S(1)}, f32[8,128]{1,0:T(8,128)S(1)}, u32[]{:S(2)}, u32[]{:S(2)}) collective-permute-start(f32[8,128]{1,0:T(8,128)S(1)} %get-tuple-element.109), channel_id=1, source_target_pairs={{0,6},{2,4},{4,2},{6,0},{8,14},{10,12},{12,10},{14,8},{1,7},{3,5},... | collective-permute-start | bytes 12296 | tf_op jit(solution)/shard_map/ppermute | solution.py:40
  51.8 0.9 %collective-permute-start.11 = (f32[8,128]{1,0:T(8,128)S(1)}, f32[8,128]{1,0:T(8,128)S(1)}, u32[]{:S(2)}, u32[]{:S(2)}) collective-permute-start(f32[8,128]{1,0:T(8,128)S(1)} %get-tuple-element.109), channel_id=1, source_target_pairs={{0,4},{2,6},{4,0},{6,2},{8,12},{10,14},{12,8},{14,10},{1,5},{3,7},... | collective-permute-start | bytes 12296 | tf_op jit(solution)/shard_map/ppermute | solution.py:40
  52.7 0.3 collective-permute-start.10
  53.0 1.1 %collective-permute-done.12 = f32[8,128]{1,0:T(8,128)S(1)} collective-permute-done((f32[8,128]{1,0:T(8,128)S(1)}, f32[8,128]{1,0:T(8,128)S(1)}, u32[]{:S(2)}, u32[]{:S(2)}) %collective-permute-start.12) | collective-permute-done | bytes 4128 | tf_op jit(solution)/shard_map/ppermute | solution.py:40
  54.1 1.5 %collective-permute-done.11 = f32[8,128]{1,0:T(8,128)S(1)} collective-permute-done((f32[8,128]{1,0:T(8,128)S(1)}, f32[8,128]{1,0:T(8,128)S(1)}, u32[]{:S(2)}, u32[]{:S(2)}) %collective-permute-start.11) | collective-permute-done | bytes 4128 | tf_op jit(solution)/shard_map/ppermute | solution.py:40
  55.5 0.9 %collective-permute-done.10 = f32[8,128]{1,0:T(8,128)S(1)} collective-permute-done((f32[8,128]{1,0:T(8,128)S(1)}, f32[8,128]{1,0:T(8,128)S(1)}, u32[]{:S(2)}, u32[]{:S(2)}) %collective-permute-start.10) | collective-permute-done | bytes 4128 | tf_op jit(solution)/shard_map/ppermute | solution.py:40
  56.4 1.2 %collective-permute-start.15 = (bf16[4,240,128]{2,1,0:T(8,128)(2,1)S(1)}, bf16[4,240,128]{2,1,0:T(8,128)(2,1)S(1)}, u32[]{:S(2)}, u32[]{:S(2)}) collective-permute-start(bf16[4,240,128]{2,1,0:T(8,128)(2,1)S(1)} %get-tuple-element.117.refs_0_), channel_id=1, source_target_pairs={{0,4},{2,6},{4,0},{6,2},{8,12},{10,14},{12,8},{14,10},{1,5},{3,7},... | collective-permute-start | bytes 737288 | tf_op jit(solution)/shard_map/ppermute | solution.py:40
  57.6 0.4 collective-permute-start.16
  58.0 1.2 %collective-permute-done.13 = f32[8,128]{1,0:T(8,128)S(1)} collective-permute-done((f32[8,128]{1,0:T(8,128)S(1)}, f32[8,128]{1,0:T(8,128)S(1)}, u32[]{:S(2)}, u32[]{:S(2)}) %collective-permute-start.13) | collective-permute-done | bytes 4128 | tf_op jit(solution)/shard_map/ppermute | solution.py:40
  59.2 1.4 %collective-permute-start.14 = (f32[8,128]{1,0:T(8,128)S(1)}, f32[8,128]{1,0:T(8,128)S(1)}, u32[]{:S(2)}, u32[]{:S(2)}) collective-permute-start(f32[8,128]{1,0:T(8,128)S(1)} %add.24.square_ref), channel_id=1, source_target_pairs={{0,8},{2,10},{4,12},{6,14},{8,0},{10,2},{12,4},{14,6},{1,9},{3,11}... | collective-permute-start | bytes 12296 | tf_op jit(solution)/shard_map/ppermute | solution.py:40
  60.6 3.1 %collective-permute-done.14.other_ref = f32[8,128]{1,0:T(8,128)S(1)} collective-permute-done((f32[8,128]{1,0:T(8,128)S(1)}, f32[8,128]{1,0:T(8,128)S(1)}, u32[]{:S(2)}, u32[]{:S(2)}) %collective-permute-start.14) | collective-permute-done | bytes 4128 | tf_op jit(solution)/shard_map/ppermute | solution.py:40
  63.7 0.6 shard_map.160
  64.3 0.1 collective-permute-start.17
  64.4 1.2 %collective-permute-done.17 = f32[8,8,256]{2,1,0:T(8,128)S(1)} collective-permute-done((f32[8,8,256]{2,1,0:T(8,128)S(1)}, f32[8,8,256]{2,1,0:T(8,128)S(1)}, u32[]{:S(2)}, u32[]{:S(2)}) %collective-permute-start.17) | collective-permute-done | bytes 65568 | tf_op jit(solution)/shard_map/ppermute | solution.py:40
  65.7 0.8 %collective-permute-start.18 = (f32[4,8,256]{2,1,0:T(8,128)S(1)}, f32[4,8,256]{2,1,0:T(8,128)S(1)}, u32[]{:S(2)}, u32[]{:S(2)}) collective-permute-start(f32[4,8,256]{2,1,0:T(8,128)S(1)} %pad_maximum_fusion), channel_id=1, source_target_pairs={{0,4},{2,6},{4,0},{6,2},{8,12},{10,14},{12,8},{14,10},{1,5},{3,7},... | collective-permute-start | bytes 98312 | tf_op jit(solution)/shard_map/ppermute | solution.py:40
  66.5 3.2 %collective-permute-done.18 = f32[4,8,256]{2,1,0:T(8,128)S(1)} collective-permute-done((f32[4,8,256]{2,1,0:T(8,128)S(1)}, f32[4,8,256]{2,1,0:T(8,128)S(1)}, u32[]{:S(2)}, u32[]{:S(2)}) %collective-permute-start.18) | collective-permute-done | bytes 32800 | tf_op jit(solution)/shard_map/ppermute | solution.py:40
  69.6 1.5 %collective-permute-start.19 = (f32[2,8,256]{2,1,0:T(8,128)S(1)}, f32[2,8,256]{2,1,0:T(8,128)S(1)}, u32[]{:S(2)}, u32[]{:S(2)}) collective-permute-start(f32[2,8,256]{2,1,0:T(8,128)S(1)} %stack.28), channel_id=1, source_target_pairs={{0,8},{2,10},{4,12},{6,14},{8,0},{10,2},{12,4},{14,6},{1,9},{3,11}... | collective-permute-start | bytes 49160 | tf_op jit(solution)/shard_map/ppermute | solution.py:40
  71.1 1.6 %shard_map.161 = (f32[240,512]{1,0:T(8,128)}, f32[240,512]{1,0:T(8,128)}, f32[240,512]{1,0:T(8,128)}, f32[8,128]{1,0:T(8,128)S(1)}) custom-call(f32[8,128]{1,0:T(8,128)S(1)} %add.24.square_ref, f32[8,128]{1,0:T(8,128)S(1)} %collective-permute-done.14.other_ref, f32[240,512]{1,0:T(8,128)S(1)} %get-tuple-element.122.grad_ref, f32[240,512]{1,0:T(8,128)S(1)} %copy-done, ...), custom_call_target="tpu_custom_call" | custom-call | flops 1 | bytes 1 | tf_op jit(solution)/shard_map/pallas_call | solution.py:815
  72.8 1.0 %shard_map.162 = (f32[384,1920]{1,0:T(8,128)S(1)}, bf16[1920,256]{1,0:T(8,128)(2,1)S(1)}, f32[8,128]{1,0:T(8,128)S(1)}) custom-call(s32[1]{0:T(128)} %bitcast.here_ref, bf16[384,256]{1,0:T(8,128)(2,1)S(1)} %copy-done.3, f32[8,128]{1,0:T(8,128)S(1)} %get-tuple-element.139.gate_ref.near_ref, bf16[4,240,128]{2,1,0:T(8,128)(2,1)S(1)} %get-tuple-element.117.refs_0_, ...), custom_call_target="tpu_custom_call" | custom-call | flops 1 | bytes 1 | tf_op jit(solution)/shard_map/pallas_call | solution.py:714
  73.8 0.6 collective-permute-done.19
  74.4 1.6 %collective-permute-start.20 = (f32[1,8,256]{2,1,0:T(8,128)S(1)}, f32[1,8,256]{2,1,0:T(8,128)S(1)}, u32[]{:S(2)}, u32[]{:S(2)}) collective-permute-start(f32[1,8,256]{2,1,0:T(8,128)S(1)} %get-tuple-element.148), channel_id=1, source_target_pairs={{0,2},{2,0},{4,6},{6,4},{8,10},{10,8},{12,14},{14,12},{1,3},{3,1},... | collective-permute-start | bytes 24584 | tf_op jit(solution)/shard_map/ppermute | solution.py:40
  76.0 2.0 %shard_map.163 = (bf16[384,1920]{1,0:T(8,128)(2,1)}, f32[8,128]{1,0:T(8,128)S(1)}) custom-call(bf16[384,256]{1,0:T(8,128)(2,1)S(1)} %collective-permute-done.refs_1_.cot_ref, f32[384,1920]{1,0:T(8,128)S(1)} %get-tuple-element.126.near_ref, bf16[1920,256]{1,0:T(8,128)(2,1)S(1)} %get-tuple-element.127.weight), custom_call_target="tpu_custom_call" | custom-call | flops 1 | bytes 1 | tf_op jit(solution)/shard_map/pallas_call | solution.py:732
  78.0 0.0 collective-permute-done.20.other_ref
  78.1 1.1 %shard_map.164 = (bf16[1,8,256]{2,1,0:T(8,128)(2,1)}, bf16[1,8,2048]{2,1,0:T(8,128)(2,1)}) custom-call(bf16[1,8,2048]{2,1,0:T(8,128)(2,1)S(1)} %copy-done.6, f32[1,8,256]{2,1,0:T(8,128)S(1)} %get-tuple-element.149.keep_ref, f32[1,8,256]{2,1,0:T(8,128)S(1)} %collective-permute-done.20.other_ref, bf16[1,8,256]{2,1,0:T(8,128)(2,1)S(1)} %copy-done.7, ...), custom_call_target="tpu_custom_call" | custom-call | flops 1 | bytes 1 | tf_op jit(solution)/shard_map/pallas_call | solution.py:569
  (32 shorter events, 0.1 us)
Async XLA Ops:
  0.6 7.0 %copy-start.3 = (bf16[384,256]{1,0:T(8,128)(2,1)S(1)}, bf16[384,256]{1,0:T(8,128)(2,1)}, u32[]{:S(2)}) copy-start(bf16[384,256]{1,0:T(8,128)(2,1)} %cot_ref.1) | copy-start | bytes 589828
  4.5 11.5 %copy-start.4 = (bf16[1,1024,256]{2,1,0:T(8,128)(2,1)S(1)}, bf16[1,1024,256]{2,1,0:T(8,128)(2,1)}, u32[]{:S(2)}) copy-start(bf16[1,1024,256]{2,1,0:T(8,128)(2,1)} %keys_ref.1) | copy-start | bytes 1572868
  4.5 11.5 %copy-start.5 = (bf16[1,1024,256]{2,1,0:T(8,128)(2,1)S(1)}, bf16[1,1024,256]{2,1,0:T(8,128)(2,1)}, u32[]{:S(2)}) copy-start(bf16[1,1024,256]{2,1,0:T(8,128)(2,1)} %values_ref.2) | copy-start | bytes 1572868
  4.5 11.5 %copy-start.6 = (bf16[1,8,2048]{2,1,0:T(8,128)(2,1)S(1)}, bf16[1,8,2048]{2,1,0:T(8,128)(2,1)}, u32[]{:S(2)}) copy-start(bf16[1,8,2048]{2,1,0:T(8,128)(2,1)} %query_ref.3) | copy-start | bytes 98308
  4.5 19.8 %collective-permute-start.2 = (bf16[1920,128]{1,0:T(8,128)(2,1)S(1)}, bf16[1920,128]{1,0:T(8,128)(2,1)S(1)}, u32[]{:S(2)}, u32[]{:S(2)}) collective-permute-start(bf16[1920,128]{1,0:T(8,128)(2,1)S(1)} %get-tuple-element.83), channel_id=1, source_target_pairs={{0,4},{2,6},{4,0},{6,2},{8,12},{10,14},{12,8},{14,10},{1,5},{3,7},... | collective-permute-start | bytes 1474568 | tf_op jit(solution)/shard_map/ppermute | solution.py:40
  7.6 1.4 %collective-permute-start = (bf16[384,256]{1,0:T(8,128)(2,1)S(1)}, bf16[384,256]{1,0:T(8,128)(2,1)S(1)}, u32[]{:S(2)}, u32[]{:S(2)}) collective-permute-start(bf16[384,256]{1,0:T(8,128)(2,1)S(1)} %copy-done.3), channel_id=1, source_target_pairs={{0,1},{1,0},{2,3},{3,2},{4,5},{5,4},{6,7},{7,6},{8,9},{9,8},{10,11... | collective-permute-start | bytes 589832 | tf_op jit(solution)/shard_map/ppermute | solution.py:40
  10.7 13.7 %collective-permute-start.4 = (bf16[1024,128]{1,0:T(8,128)(2,1)S(1)}, bf16[1024,128]{1,0:T(8,128)(2,1)S(1)}, u32[]{:S(2)}, u32[]{:S(2)}) collective-permute-start(bf16[1024,128]{1,0:T(8,128)(2,1)S(1)} %get-tuple-element.85), channel_id=1, source_target_pairs={{0,2},{2,0},{4,6},{6,4},{8,10},{10,8},{12,14},{14,12},{1,3},{3,1},... | collective-permute-start | bytes 786440 | tf_op jit(solution)/shard_map/ppermute | solution.py:40
  12.2 11.2 %collective-permute-start.1 = (bf16[960,128]{1,0:T(8,128)(2,1)S(1)}, bf16[960,128]{1,0:T(8,128)(2,1)S(1)}, u32[]{:S(2)}, u32[]{:S(2)}) collective-permute-start(bf16[960,128]{1,0:T(8,128)(2,1)S(1)} %get-tuple-element.81), channel_id=1, source_target_pairs={{0,8},{2,10},{4,12},{6,14},{8,0},{10,2},{12,4},{14,6},{1,9},{3,11}... | collective-permute-start | bytes 737288 | tf_op jit(solution)/shard_map/ppermute | solution.py:40
  14.8 9.5 %collective-permute-start.3 = (bf16[960,128]{1,0:T(8,128)(2,1)S(1)}, bf16[960,128]{1,0:T(8,128)(2,1)S(1)}, u32[]{:S(2)}, u32[]{:S(2)}) collective-permute-start(bf16[960,128]{1,0:T(8,128)(2,1)S(1)} %get-tuple-element.84), channel_id=1, source_target_pairs={{0,2},{2,0},{4,6},{6,4},{8,10},{10,8},{12,14},{14,12},{1,3},{3,1},... | collective-permute-start | bytes 737288 | tf_op jit(solution)/shard_map/ppermute | solution.py:40
  24.7 15.9 %collective-permute-start.6 = (bf16[1504,128]{1,0:T(8,128)(2,1)S(1)}, bf16[1504,128]{1,0:T(8,128)(2,1)S(1)}, u32[]{:S(2)}, u32[]{:S(2)}) collective-permute-start(bf16[1504,128]{1,0:T(8,128)(2,1)S(1)} %get-tuple-element.94), channel_id=1, source_target_pairs={{0,4},{2,6},{4,0},{6,2},{8,12},{10,14},{12,8},{14,10},{1,5},{3,7},... | collective-permute-start | bytes 1155080 | tf_op jit(solution)/shard_map/ppermute | solution.py:40
  27.3 12.6 %collective-permute-start.7 = (bf16[1440,128]{1,0:T(8,128)(2,1)S(1)}, bf16[1440,128]{1,0:T(8,128)(2,1)S(1)}, u32[]{:S(2)}, u32[]{:S(2)}) collective-permute-start(bf16[1440,128]{1,0:T(8,128)(2,1)S(1)} %get-tuple-element.95), channel_id=1, source_target_pairs={{0,2},{2,0},{4,6},{6,4},{8,10},{10,8},{12,14},{14,12},{1,3},{3,1},... | collective-permute-start | bytes 1105928 | tf_op jit(solution)/shard_map/ppermute | solution.py:40
  28.8 11.1 %collective-permute-start.5 = (bf16[960,128]{1,0:T(8,128)(2,1)S(1)}, bf16[960,128]{1,0:T(8,128)(2,1)S(1)}, u32[]{:S(2)}, u32[]{:S(2)}) collective-permute-start(bf16[960,128]{1,0:T(8,128)(2,1)S(1)} %get-tuple-element.93), channel_id=1, source_target_pairs={{0,8},{2,10},{4,12},{6,14},{8,0},{10,2},{12,4},{14,6},{1,9},{3,11}... | collective-permute-start | bytes 737288 | tf_op jit(solution)/shard_map/ppermute | solution.py:40
  40.6 23.1 %copy-start = (f32[240,512]{1,0:T(8,128)S(1)}, f32[240,512]{1,0:T(8,128)}, u32[]{:S(2)}) copy-start(f32[240,512]{1,0:T(8,128)} %master_ref.3) | copy-start | bytes 1474564
  40.6 23.1 %copy-start.1 = (f32[240,512]{1,0:T(8,128)S(1)}, f32[240,512]{1,0:T(8,128)}, u32[]{:S(2)}) copy-start(f32[240,512]{1,0:T(8,128)} %first_ref.3) | copy-start | bytes 1474564
  40.6 23.1 %copy-start.2 = (f32[240,512]{1,0:T(8,128)S(1)}, f32[240,512]{1,0:T(8,128)}, u32[]{:S(2)}) copy-start(f32[240,512]{1,0:T(8,128)} %second_ref.3) | copy-start | bytes 1474564
  41.4 7.8 %collective-permute-start.8 = (bf16[544,128]{1,0:T(8,128)(2,1)S(1)}, bf16[544,128]{1,0:T(8,128)(2,1)S(1)}, u32[]{:S(2)}, u32[]{:S(2)}) collective-permute-start(bf16[544,128]{1,0:T(8,128)(2,1)S(1)} %get-tuple-element.104), channel_id=1, source_target_pairs={{0,8},{2,10},{4,12},{6,14},{8,0},{10,2},{12,4},{14,6},{1,9},{3,11}... | collective-permute-start | bytes 417800 | tf_op jit(solution)/shard_map/ppermute | solution.py:40
  44.1 4.9 %collective-permute-start.9 = (bf16[480,128]{1,0:T(8,128)(2,1)S(1)}, bf16[480,128]{1,0:T(8,128)(2,1)S(1)}, u32[]{:S(2)}, u32[]{:S(2)}) collective-permute-start(bf16[480,128]{1,0:T(8,128)(2,1)S(1)} %get-tuple-element.105), channel_id=1, source_target_pairs={{0,4},{2,6},{4,0},{6,2},{8,12},{10,14},{12,8},{14,10},{1,5},{3,7},... | collective-permute-start | bytes 368648 | tf_op jit(solution)/shard_map/ppermute | solution.py:40
  49.4 4.6 %collective-permute-start.12 = (f32[8,128]{1,0:T(8,128)S(1)}, f32[8,128]{1,0:T(8,128)S(1)}, u32[]{:S(2)}, u32[]{:S(2)}) collective-permute-start(f32[8,128]{1,0:T(8,128)S(1)} %get-tuple-element.109), channel_id=1, source_target_pairs={{0,6},{2,4},{4,2},{6,0},{8,14},{10,12},{12,10},{14,8},{1,7},{3,5},... | collective-permute-start | bytes 12296 | tf_op jit(solution)/shard_map/ppermute | solution.py:40
  51.8 3.7 %collective-permute-start.11 = (f32[8,128]{1,0:T(8,128)S(1)}, f32[8,128]{1,0:T(8,128)S(1)}, u32[]{:S(2)}, u32[]{:S(2)}) collective-permute-start(f32[8,128]{1,0:T(8,128)S(1)} %get-tuple-element.109), channel_id=1, source_target_pairs={{0,4},{2,6},{4,0},{6,2},{8,12},{10,14},{12,8},{14,10},{1,5},{3,7},... | collective-permute-start | bytes 12296 | tf_op jit(solution)/shard_map/ppermute | solution.py:40
  52.7 3.7 %collective-permute-start.10 = (f32[8,128]{1,0:T(8,128)S(1)}, f32[8,128]{1,0:T(8,128)S(1)}, u32[]{:S(2)}, u32[]{:S(2)}) collective-permute-start(f32[8,128]{1,0:T(8,128)S(1)} %get-tuple-element.109), channel_id=1, source_target_pairs={{0,2},{2,0},{4,6},{6,4},{8,10},{10,8},{12,14},{14,12},{1,3},{3,1},... | collective-permute-start | bytes 12296 | tf_op jit(solution)/shard_map/ppermute | solution.py:40
  56.4 7.3 %collective-permute-start.15 = (bf16[4,240,128]{2,1,0:T(8,128)(2,1)S(1)}, bf16[4,240,128]{2,1,0:T(8,128)(2,1)S(1)}, u32[]{:S(2)}, u32[]{:S(2)}) collective-permute-start(bf16[4,240,128]{2,1,0:T(8,128)(2,1)S(1)} %get-tuple-element.117.refs_0_), channel_id=1, source_target_pairs={{0,4},{2,6},{4,0},{6,2},{8,12},{10,14},{12,8},{14,10},{1,5},{3,7},... | collective-permute-start | bytes 737288 | tf_op jit(solution)/shard_map/ppermute | solution.py:40
  57.6 15.2 %collective-permute-start.16 = (bf16[12,240,128]{2,1,0:T(8,128)(2,1)S(1)}, bf16[12,240,128]{2,1,0:T(8,128)(2,1)S(1)}, u32[]{:S(2)}, u32[]{:S(2)}) collective-permute-start(bf16[12,240,128]{2,1,0:T(8,128)(2,1)S(1)} %get-tuple-element.124.refs_1_), channel_id=1, source_target_pairs={{0,2},{2,0},{4,6},{6,4},{8,10},{10,8},{12,14},{14,12},{1,3},{3,1},... | collective-permute-start | bytes 2211848 | tf_op jit(solution)/shard_map/ppermute | solution.py:40
  58.0 1.2 %collective-permute-start.13 = (f32[8,128]{1,0:T(8,128)S(1)}, f32[8,128]{1,0:T(8,128)S(1)}, u32[]{:S(2)}, u32[]{:S(2)}) collective-permute-start(f32[8,128]{1,0:T(8,128)S(1)} %add_add_fusion), channel_id=1, source_target_pairs={{0,1},{1,0},{2,3},{3,2},{4,5},{5,4},{6,7},{7,6},{8,9},{9,8},{10,11... | collective-permute-start | bytes 12296 | tf_op jit(solution)/shard_map/ppermute | solution.py:40
  59.2 4.5 %collective-permute-start.14 = (f32[8,128]{1,0:T(8,128)S(1)}, f32[8,128]{1,0:T(8,128)S(1)}, u32[]{:S(2)}, u32[]{:S(2)}) collective-permute-start(f32[8,128]{1,0:T(8,128)S(1)} %add.24.square_ref), channel_id=1, source_target_pairs={{0,8},{2,10},{4,12},{6,14},{8,0},{10,2},{12,4},{14,6},{1,9},{3,11}... | collective-permute-start | bytes 12296 | tf_op jit(solution)/shard_map/ppermute | solution.py:40
  64.3 1.3 %collective-permute-start.17 = (f32[8,8,256]{2,1,0:T(8,128)S(1)}, f32[8,8,256]{2,1,0:T(8,128)S(1)}, u32[]{:S(2)}, u32[]{:S(2)}) collective-permute-start(f32[8,8,256]{2,1,0:T(8,128)S(1)} %get-tuple-element.133), channel_id=1, source_target_pairs={{0,1},{1,0},{2,3},{3,2},{4,5},{5,4},{6,7},{7,6},{8,9},{9,8},{10,11... | collective-permute-start | bytes 196616 | tf_op jit(solution)/shard_map/ppermute | solution.py:40
  65.7 4.0 %collective-permute-start.18 = (f32[4,8,256]{2,1,0:T(8,128)S(1)}, f32[4,8,256]{2,1,0:T(8,128)S(1)}, u32[]{:S(2)}, u32[]{:S(2)}) collective-permute-start(f32[4,8,256]{2,1,0:T(8,128)S(1)} %pad_maximum_fusion), channel_id=1, source_target_pairs={{0,4},{2,6},{4,0},{6,2},{8,12},{10,14},{12,8},{14,10},{1,5},{3,7},... | collective-permute-start | bytes 98312 | tf_op jit(solution)/shard_map/ppermute | solution.py:40
  69.6 4.7 %collective-permute-start.19 = (f32[2,8,256]{2,1,0:T(8,128)S(1)}, f32[2,8,256]{2,1,0:T(8,128)S(1)}, u32[]{:S(2)}, u32[]{:S(2)}) collective-permute-start(f32[2,8,256]{2,1,0:T(8,128)S(1)} %stack.28), channel_id=1, source_target_pairs={{0,8},{2,10},{4,12},{6,14},{8,0},{10,2},{12,4},{14,6},{1,9},{3,11}... | collective-permute-start | bytes 49160 | tf_op jit(solution)/shard_map/ppermute | solution.py:40
  74.4 3.7 %collective-permute-start.20 = (f32[1,8,256]{2,1,0:T(8,128)S(1)}, f32[1,8,256]{2,1,0:T(8,128)S(1)}, u32[]{:S(2)}, u32[]{:S(2)}) collective-permute-start(f32[1,8,256]{2,1,0:T(8,128)S(1)} %get-tuple-element.148), channel_id=1, source_target_pairs={{0,2},{2,0},{4,6},{6,4},{8,10},{10,8},{12,14},{14,12},{1,3},{3,1},... | collective-permute-start | bytes 24584 | tf_op jit(solution)/shard_map/ppermute | solution.py:40
  76.0 2.1 %copy-start.7 = (bf16[1,8,256]{2,1,0:T(8,128)(2,1)S(1)}, bf16[1,8,256]{2,1,0:T(8,128)(2,1)}, u32[]{:S(2)}) copy-start(bf16[1,8,256]{2,1,0:T(8,128)(2,1)} %values_ref.3) | copy-start | bytes 12292

commit v7 on v6

--- a/solution.py
+++ b/solution.py
@@ -728,7 +728,7 @@
 
 def input_far(cot, near, weight):
     tokens, columns = near.shape
-    pieces = 4 if tokens % 64 == 0 else 1
+    pieces = 2 if tokens % 32 == 0 else 1
     return pl.pallas_call(
         far_kernel,
         out_shape=[jax.ShapeDtypeStruct((tokens, columns), jnp.bfloat16), TOKEN],

time: 79.3 us -> 79.3 us (level)
  transfers between devices with their start and end apart: 21 -> 21, of which waited for: 15 -> 16; matrix products, arithmetic and copies ran while one was open for 0% -> 0% of each run, Pallas kernels for 10% -> 9%
where the time goes in v7:
time: 79.3 us; the launch traced here: 79.1 us
  waiting for transfers between devices  37.4 us (47%)
  starting transfers between devices  26.6 us (34%)
  Pallas kernels  13.5 us (17%)
  between operations  1.45 us (2%)
    ppermute x21, waiting for transfers between devices, swap_with(): return lax.ppermute(value, axis, [(i, i ^ mask) for i in range(size)])  37.4 us
    ppermute x21, starting transfers between devices, swap_with(): return lax.ppermute(value, axis, [(i, i ^ mask) for i in range(size)])  26.6 us
    pallas_call x2, Pallas kernels, first_stage(): pl.pallas_call(functools.partial(first_kernel, bits, cuts, unit, over, sl...  5.36 us
    pallas_call x1, Pallas kernels, input_far(): pl.pallas_call(far_kernel, out_shape=[jax.ShapeDtypeStruct((tokens, colum...  1.66 us
    pallas_call x1, Pallas kernels, updated(): pl.pallas_call(functools.partial(update_kernel, limit), out_shape=[jax.Sh...  1.65 us
  transfers between devices with their start and end apart: 21, of which 16 were waited for; matrix products, arithmetic and copies ran while one was open for 0% of the time, Pallas kernels for 9%

profile of v7, /device:TPU:0, one launch (start us, length us, event | category | flops | bytes accessed | tf_op | source)
XLA Modules:
  0.0 79.1 jit_solution(2007098937865056362)
XLA Ops:
  0.6 0.1 pad_add_fusion.where_ref
  0.7 3.7 %shard_map.154 = (bf16[960,128]{1,0:T(8,128)(2,1)S(1)}, bf16[1920,128]{1,0:T(8,128)(2,1)S(1)}, f32[4,240,256]{2,1,0:T(8,128)S(1)}, bf16[384,1920]{1,0:T(8,128)(2...) custom-call(s32[2]{0:T(128)S(1)} %pad_add_fusion.where_ref, ...), custom_call_target="tpu_custom_call" | custom-call | flops 1 | bytes 1 | tf_op jit(solution)/shard_map/pallas_call | solution.py:360
  4.5 0.0 copy-start.4
  4.5 0.0 copy-start.5
  4.5 3.1 %collective-permute-start.2 = (bf16[1920,128]{1,0:T(8,128)(2,1)S(1)}, bf16[1920,128]{1,0:T(8,128)(2,1)S(1)}, u32[]{:S(2)}, u32[]{:S(2)}) collective-permute-start(bf16[1920,128]{1,0:T(8,128)(2,1)S(1)} %get-tuple-element.83), channel_id=1, source_target_pairs={{0,4},{2,6},{4,0},{6,2},{8,12},{10,14},{12,8},{14,10},{1,5},{3,7},... | collective-permute-start | bytes 1474568 | tf_op jit(solution)/shard_map/ppermute | solution.py:40
  7.6 1.4 %collective-permute-done.refs_1_.cot_ref = bf16[384,256]{1,0:T(8,128)(2,1)S(1)} collective-permute-done((bf16[384,256]{1,0:T(8,128)(2,1)S(1)}, bf16[384,256]{1,0:T(8,128)(2,1)S(1)}, u32[]{:S(2)}, u32[]{:S(2)}) %collective-permute-start) | collective-permute-done | bytes 196640 | tf_op jit(solution)/shard_map/ppermute | solution.py:40
  9.0 1.6 %shard_map.155 = (bf16[960,128]{1,0:T(8,128)(2,1)S(1)}, bf16[1024,128]{1,0:T(8,128)(2,1)S(1)}, f32[4,240,256]{2,1,0:T(8,128)S(1)}, bf16[1,240,128]{2,1,0:T(8,128...) custom-call(s32[2]{0:T(128)S(1)} %pad_add_fusion.where_ref, ...), custom_call_target="tpu_custom_call" | custom-call | flops 1 | bytes 1 | tf_op jit(solution)/shard_map/pallas_call | solution.py:360
  10.7 1.6 %collective-permute-start.4 = (bf16[1024,128]{1,0:T(8,128)(2,1)S(1)}, bf16[1024,128]{1,0:T(8,128)(2,1)S(1)}, u32[]{:S(2)}, u32[]{:S(2)}) collective-permute-start(bf16[1024,128]{1,0:T(8,128)(2,1)S(1)} %get-tuple-element.85), channel_id=1, source_target_pairs={{0,2},{2,0},{4,6},{6,4},{8,10},{10,8},{12,14},{14,12},{1,3},{3,1},... | collective-permute-start | bytes 786440 | tf_op jit(solution)/shard_map/ppermute | solution.py:40
  12.2 2.6 %collective-permute-start.1 = (bf16[960,128]{1,0:T(8,128)(2,1)S(1)}, bf16[960,128]{1,0:T(8,128)(2,1)S(1)}, u32[]{:S(2)}, u32[]{:S(2)}) collective-permute-start(bf16[960,128]{1,0:T(8,128)(2,1)S(1)} %get-tuple-element.81), channel_id=1, source_target_pairs={{0,8},{2,10},{4,12},{6,14},{8,0},{10,2},{12,4},{14,6},{1,9},{3,11}... | collective-permute-start | bytes 737288 | tf_op jit(solution)/shard_map/ppermute | solution.py:40
  14.8 0.5 collective-permute-start.3
  16.0 0.8 %shard_map.156 = (f32[1,2,64,128]{3,2,1,0:T(8,128)S(1)}, f32[1,2,64,128]{3,2,1,0:T(8,128)S(1)}, f32[1,2,64,128]{3,2,1,0:T(8,128)S(1)}) custom-call(s32[1]{0:T(128)S(6)} %copy.17.length_ref, bf16[1,8,2048]{2,1,0:T(8,128)(2,1)S(1)} %copy-done.6, bf16[1,1024,256]{2,1,0:T(8,128)(2,1)S(1)} %copy-done.4, bf16[1,1024,256]{2,1,0:T(8,128)(2,1)S(1)} %copy-done.5, ...), custom_call_target="tpu_custom_call" | custom-call | flops 1 | bytes 1 | tf_op jit(solution)/shard_map/pallas_call | solution.py:521
  16.8 6.6 %collective-permute-done.1.refs_0_ = bf16[960,128]{1,0:T(8,128)(2,1)S(1)} collective-permute-done((bf16[960,128]{1,0:T(8,128)(2,1)S(1)}, bf16[960,128]{1,0:T(8,128)(2,1)S(1)}, u32[]{:S(2)}, u32[]{:S(2)}) %collective-permute-start.1) | collective-permute-done | bytes 245792 | tf_op jit(solution)/shard_map/ppermute | solution.py:40
  23.4 1.0 %collective-permute-done.3.refs_2_ = bf16[960,128]{1,0:T(8,128)(2,1)S(1)} collective-permute-done((bf16[960,128]{1,0:T(8,128)(2,1)S(1)}, bf16[960,128]{1,0:T(8,128)(2,1)S(1)}, u32[]{:S(2)}, u32[]{:S(2)}) %collective-permute-start.3) | collective-permute-done | bytes 245792 | tf_op jit(solution)/shard_map/ppermute | solution.py:40
  24.4 0.4 shard_map.157
  24.7 2.6 %collective-permute-start.6 = (bf16[1504,128]{1,0:T(8,128)(2,1)S(1)}, bf16[1504,128]{1,0:T(8,128)(2,1)S(1)}, u32[]{:S(2)}, u32[]{:S(2)}) collective-permute-start(bf16[1504,128]{1,0:T(8,128)(2,1)S(1)} %get-tuple-element.94), channel_id=1, source_target_pairs={{0,4},{2,6},{4,0},{6,2},{8,12},{10,14},{12,8},{14,10},{1,5},{3,7},... | collective-permute-start | bytes 1155080 | tf_op jit(solution)/shard_map/ppermute | solution.py:40
  27.3 1.5 %collective-permute-start.7 = (bf16[1440,128]{1,0:T(8,128)(2,1)S(1)}, bf16[1440,128]{1,0:T(8,128)(2,1)S(1)}, u32[]{:S(2)}, u32[]{:S(2)}) collective-permute-start(bf16[1440,128]{1,0:T(8,128)(2,1)S(1)} %get-tuple-element.95), channel_id=1, source_target_pairs={{0,2},{2,0},{4,6},{6,4},{8,10},{10,8},{12,14},{14,12},{1,3},{3,1},... | collective-permute-start | bytes 1105928 | tf_op jit(solution)/shard_map/ppermute | solution.py:40
  28.8 1.6 %collective-permute-start.5 = (bf16[960,128]{1,0:T(8,128)(2,1)S(1)}, bf16[960,128]{1,0:T(8,128)(2,1)S(1)}, u32[]{:S(2)}, u32[]{:S(2)}) collective-permute-start(bf16[960,128]{1,0:T(8,128)(2,1)S(1)} %get-tuple-element.93), channel_id=1, source_target_pairs={{0,8},{2,10},{4,12},{6,14},{8,0},{10,2},{12,4},{14,6},{1,9},{3,11}... | collective-permute-start | bytes 737288 | tf_op jit(solution)/shard_map/ppermute | solution.py:40
  30.3 9.5 %collective-permute-done.5.refs_0_ = bf16[960,128]{1,0:T(8,128)(2,1)S(1)} collective-permute-done((bf16[960,128]{1,0:T(8,128)(2,1)S(1)}, bf16[960,128]{1,0:T(8,128)(2,1)S(1)}, u32[]{:S(2)}, u32[]{:S(2)}) %collective-permute-start.5) | collective-permute-done | bytes 245792 | tf_op jit(solution)/shard_map/ppermute | solution.py:40
  39.9 0.7 collective-permute-done.6.refs_1_
  40.6 0.8 shard_map.158
  41.4 2.7 %collective-permute-start.8 = (bf16[544,128]{1,0:T(8,128)(2,1)S(1)}, bf16[544,128]{1,0:T(8,128)(2,1)S(1)}, u32[]{:S(2)}, u32[]{:S(2)}) collective-permute-start(bf16[544,128]{1,0:T(8,128)(2,1)S(1)} %get-tuple-element.104), channel_id=1, source_target_pairs={{0,8},{2,10},{4,12},{6,14},{8,0},{10,2},{12,4},{14,6},{1,9},{3,11}... | collective-permute-start | bytes 417800 | tf_op jit(solution)/shard_map/ppermute | solution.py:40
  44.1 4.9 %collective-permute-done.9.refs_1_ = bf16[480,128]{1,0:T(8,128)(2,1)S(1)} collective-permute-done((bf16[480,128]{1,0:T(8,128)(2,1)S(1)}, bf16[480,128]{1,0:T(8,128)(2,1)S(1)}, u32[]{:S(2)}, u32[]{:S(2)}) %collective-permute-start.9) | collective-permute-done | bytes 122912 | tf_op jit(solution)/shard_map/ppermute | solution.py:40
  49.0 0.2 collective-permute-done.8.refs_0_
  49.2 0.3 shard_map.159
  49.4 2.4 %collective-permute-start.12 = (f32[8,128]{1,0:T(8,128)S(1)}, f32[8,128]{1,0:T(8,128)S(1)}, u32[]{:S(2)}, u32[]{:S(2)}) collective-permute-start(f32[8,128]{1,0:T(8,128)S(1)} %get-tuple-element.109), channel_id=1, source_target_pairs={{0,6},{2,4},{4,2},{6,0},{8,14},{10,12},{12,10},{14,8},{1,7},{3,5},... | collective-permute-start | bytes 12296 | tf_op jit(solution)/shard_map/ppermute | solution.py:40
  51.8 0.9 %collective-permute-start.11 = (f32[8,128]{1,0:T(8,128)S(1)}, f32[8,128]{1,0:T(8,128)S(1)}, u32[]{:S(2)}, u32[]{:S(2)}) collective-permute-start(f32[8,128]{1,0:T(8,128)S(1)} %get-tuple-element.109), channel_id=1, source_target_pairs={{0,4},{2,6},{4,0},{6,2},{8,12},{10,14},{12,8},{14,10},{1,5},{3,7},... | collective-permute-start | bytes 12296 | tf_op jit(solution)/shard_map/ppermute | solution.py:40
  52.7 0.3 collective-permute-start.10
  53.0 1.1 %collective-permute-done.12 = f32[8,128]{1,0:T(8,128)S(1)} collective-permute-done((f32[8,128]{1,0:T(8,128)S(1)}, f32[8,128]{1,0:T(8,128)S(1)}, u32[]{:S(2)}, u32[]{:S(2)}) %collective-permute-start.12) | collective-permute-done | bytes 4128 | tf_op jit(solution)/shard_map/ppermute | solution.py:40
  54.1 1.5 %collective-permute-done.11 = f32[8,128]{1,0:T(8,128)S(1)} collective-permute-done((f32[8,128]{1,0:T(8,128)S(1)}, f32[8,128]{1,0:T(8,128)S(1)}, u32[]{:S(2)}, u32[]{:S(2)}) %collective-permute-start.11) | collective-permute-done | bytes 4128 | tf_op jit(solution)/shard_map/ppermute | solution.py:40
  55.5 0.9 %collective-permute-done.10 = f32[8,128]{1,0:T(8,128)S(1)} collective-permute-done((f32[8,128]{1,0:T(8,128)S(1)}, f32[8,128]{1,0:T(8,128)S(1)}, u32[]{:S(2)}, u32[]{:S(2)}) %collective-permute-start.10) | collective-permute-done | bytes 4128 | tf_op jit(solution)/shard_map/ppermute | solution.py:40
  56.4 1.2 %collective-permute-start.15 = (bf16[4,240,128]{2,1,0:T(8,128)(2,1)S(1)}, bf16[4,240,128]{2,1,0:T(8,128)(2,1)S(1)}, u32[]{:S(2)}, u32[]{:S(2)}) collective-permute-start(bf16[4,240,128]{2,1,0:T(8,128)(2,1)S(1)} %get-tuple-element.117.refs_0_), channel_id=1, source_target_pairs={{0,4},{2,6},{4,0},{6,2},{8,12},{10,14},{12,8},{14,10},{1,5},{3,7},... | collective-permute-start | bytes 737288 | tf_op jit(solution)/shard_map/ppermute | solution.py:40
  57.6 0.4 collective-permute-start.16
  58.0 1.2 %collective-permute-done.13 = f32[8,128]{1,0:T(8,128)S(1)} collective-permute-done((f32[8,128]{1,0:T(8,128)S(1)}, f32[8,128]{1,0:T(8,128)S(1)}, u32[]{:S(2)}, u32[]{:S(2)}) %collective-permute-start.13) | collective-permute-done | bytes 4128 | tf_op jit(solution)/shard_map/ppermute | solution.py:40
  59.2 1.4 %collective-permute-start.14 = (f32[8,128]{1,0:T(8,128)S(1)}, f32[8,128]{1,0:T(8,128)S(1)}, u32[]{:S(2)}, u32[]{:S(2)}) collective-permute-start(f32[8,128]{1,0:T(8,128)S(1)} %add.24.square_ref), channel_id=1, source_target_pairs={{0,8},{2,10},{4,12},{6,14},{8,0},{10,2},{12,4},{14,6},{1,9},{3,11}... | collective-permute-start | bytes 12296 | tf_op jit(solution)/shard_map/ppermute | solution.py:40
  60.6 3.1 %collective-permute-done.14.other_ref = f32[8,128]{1,0:T(8,128)S(1)} collective-permute-done((f32[8,128]{1,0:T(8,128)S(1)}, f32[8,128]{1,0:T(8,128)S(1)}, u32[]{:S(2)}, u32[]{:S(2)}) %collective-permute-start.14) | collective-permute-done | bytes 4128 | tf_op jit(solution)/shard_map/ppermute | solution.py:40
  63.7 0.6 shard_map.160
  64.3 0.1 collective-permute-start.17
  64.4 1.2 %collective-permute-done.17 = f32[8,8,256]{2,1,0:T(8,128)S(1)} collective-permute-done((f32[8,8,256]{2,1,0:T(8,128)S(1)}, f32[8,8,256]{2,1,0:T(8,128)S(1)}, u32[]{:S(2)}, u32[]{:S(2)}) %collective-permute-start.17) | collective-permute-done | bytes 65568 | tf_op jit(solution)/shard_map/ppermute | solution.py:40
  65.7 0.8 %collective-permute-start.18 = (f32[4,8,256]{2,1,0:T(8,128)S(1)}, f32[4,8,256]{2,1,0:T(8,128)S(1)}, u32[]{:S(2)}, u32[]{:S(2)}) collective-permute-start(f32[4,8,256]{2,1,0:T(8,128)S(1)} %pad_maximum_fusion), channel_id=1, source_target_pairs={{0,4},{2,6},{4,0},{6,2},{8,12},{10,14},{12,8},{14,10},{1,5},{3,7},... | collective-permute-start | bytes 98312 | tf_op jit(solution)/shard_map/ppermute | solution.py:40
  66.5 3.2 %collective-permute-done.18 = f32[4,8,256]{2,1,0:T(8,128)S(1)} collective-permute-done((f32[4,8,256]{2,1,0:T(8,128)S(1)}, f32[4,8,256]{2,1,0:T(8,128)S(1)}, u32[]{:S(2)}, u32[]{:S(2)}) %collective-permute-start.18) | collective-permute-done | bytes 32800 | tf_op jit(solution)/shard_map/ppermute | solution.py:40
  69.6 1.5 %collective-permute-start.19 = (f32[2,8,256]{2,1,0:T(8,128)S(1)}, f32[2,8,256]{2,1,0:T(8,128)S(1)}, u32[]{:S(2)}, u32[]{:S(2)}) collective-permute-start(f32[2,8,256]{2,1,0:T(8,128)S(1)} %stack.28), channel_id=1, source_target_pairs={{0,8},{2,10},{4,12},{6,14},{8,0},{10,2},{12,4},{14,6},{1,9},{3,11}... | collective-permute-start | bytes 49160 | tf_op jit(solution)/shard_map/ppermute | solution.py:40
  71.1 1.6 %shard_map.161 = (f32[240,512]{1,0:T(8,128)}, f32[240,512]{1,0:T(8,128)}, f32[240,512]{1,0:T(8,128)}, f32[8,128]{1,0:T(8,128)S(1)}) custom-call(f32[8,128]{1,0:T(8,128)S(1)} %add.24.square_ref, f32[8,128]{1,0:T(8,128)S(1)} %collective-permute-done.14.other_ref, f32[240,512]{1,0:T(8,128)S(1)} %get-tuple-element.122.grad_ref, f32[240,512]{1,0:T(8,128)S(1)} %copy-done, ...), custom_call_target="tpu_custom_call" | custom-call | flops 1 | bytes 1 | tf_op jit(solution)/shard_map/pallas_call | solution.py:815
  72.8 1.0 %shard_map.162 = (f32[384,1920]{1,0:T(8,128)S(1)}, bf16[1920,256]{1,0:T(8,128)(2,1)S(1)}, f32[8,128]{1,0:T(8,128)S(1)}) custom-call(s32[1]{0:T(128)} %bitcast.here_ref, bf16[384,256]{1,0:T(8,128)(2,1)S(1)} %copy-done.3, f32[8,128]{1,0:T(8,128)S(1)} %get-tuple-element.139.gate_ref.near_ref, bf16[4,240,128]{2,1,0:T(8,128)(2,1)S(1)} %get-tuple-element.117.refs_0_, ...), custom_call_target="tpu_custom_call" | custom-call | flops 1 | bytes 1 | tf_op jit(solution)/shard_map/pallas_call | solution.py:714
  73.8 0.6 collective-permute-done.19
  74.4 1.6 %collective-permute-start.20 = (f32[1,8,256]{2,1,0:T(8,128)S(1)}, f32[1,8,256]{2,1,0:T(8,128)S(1)}, u32[]{:S(2)}, u32[]{:S(2)}) collective-permute-start(f32[1,8,256]{2,1,0:T(8,128)S(1)} %get-tuple-element.148), channel_id=1, source_target_pairs={{0,2},{2,0},{4,6},{6,4},{8,10},{10,8},{12,14},{14,12},{1,3},{3,1},... | collective-permute-start | bytes 24584 | tf_op jit(solution)/shard_map/ppermute | solution.py:40
  76.0 1.7 %shard_map.163 = (bf16[384,1920]{1,0:T(8,128)(2,1)}, f32[8,128]{1,0:T(8,128)S(1)}) custom-call(bf16[384,256]{1,0:T(8,128)(2,1)S(1)} %collective-permute-done.refs_1_.cot_ref, f32[384,1920]{1,0:T(8,128)S(1)} %get-tuple-element.126.near_ref, bf16[1920,256]{1,0:T(8,128)(2,1)S(1)} %get-tuple-element.127.weight), custom_call_target="tpu_custom_call" | custom-call | flops 1 | bytes 1 | tf_op jit(solution)/shard_map/pallas_call | solution.py:732
  77.7 0.4 collective-permute-done.20.other_ref
  78.1 1.1 %shard_map.164 = (bf16[1,8,256]{2,1,0:T(8,128)(2,1)}, bf16[1,8,2048]{2,1,0:T(8,128)(2,1)}) custom-call(bf16[1,8,2048]{2,1,0:T(8,128)(2,1)S(1)} %copy-done.6, f32[1,8,256]{2,1,0:T(8,128)S(1)} %get-tuple-element.149.keep_ref, f32[1,8,256]{2,1,0:T(8,128)S(1)} %collective-permute-done.20.other_ref, bf16[1,8,256]{2,1,0:T(8,128)(2,1)S(1)} %copy-done.7, ...), custom_call_target="tpu_custom_call" | custom-call | flops 1 | bytes 1 | tf_op jit(solution)/shard_map/pallas_call | solution.py:569
  (32 shorter events, 0.1 us)
Async XLA Ops:
  0.6 7.0 %copy-start.3 = (bf16[384,256]{1,0:T(8,128)(2,1)S(1)}, bf16[384,256]{1,0:T(8,128)(2,1)}, u32[]{:S(2)}) copy-start(bf16[384,256]{1,0:T(8,128)(2,1)} %cot_ref.1) | copy-start | bytes 589828
  4.5 11.5 %copy-start.4 = (bf16[1,1024,256]{2,1,0:T(8,128)(2,1)S(1)}, bf16[1,1024,256]{2,1,0:T(8,128)(2,1)}, u32[]{:S(2)}) copy-start(bf16[1,1024,256]{2,1,0:T(8,128)(2,1)} %keys_ref.1) | copy-start | bytes 1572868
  4.5 11.5 %copy-start.5 = (bf16[1,1024,256]{2,1,0:T(8,128)(2,1)S(1)}, bf16[1,1024,256]{2,1,0:T(8,128)(2,1)}, u32[]{:S(2)}) copy-start(bf16[1,1024,256]{2,1,0:T(8,128)(2,1)} %values_ref.2) | copy-start | bytes 1572868
  4.5 11.5 %copy-start.6 = (bf16[1,8,2048]{2,1,0:T(8,128)(2,1)S(1)}, bf16[1,8,2048]{2,1,0:T(8,128)(2,1)}, u32[]{:S(2)}) copy-start(bf16[1,8,2048]{2,1,0:T(8,128)(2,1)} %query_ref.3) | copy-start | bytes 98308
  4.5 19.8 %collective-permute-start.2 = (bf16[1920,128]{1,0:T(8,128)(2,1)S(1)}, bf16[1920,128]{1,0:T(8,128)(2,1)S(1)}, u32[]{:S(2)}, u32[]{:S(2)}) collective-permute-start(bf16[1920,128]{1,0:T(8,128)(2,1)S(1)} %get-tuple-element.83), channel_id=1, source_target_pairs={{0,4},{2,6},{4,0},{6,2},{8,12},{10,14},{12,8},{14,10},{1,5},{3,7},... | collective-permute-start | bytes 1474568 | tf_op jit(solution)/shard_map/ppermute | solution.py:40
  7.6 1.4 %collective-permute-start = (bf16[384,256]{1,0:T(8,128)(2,1)S(1)}, bf16[384,256]{1,0:T(8,128)(2,1)S(1)}, u32[]{:S(2)}, u32[]{:S(2)}) collective-permute-start(bf16[384,256]{1,0:T(8,128)(2,1)S(1)} %copy-done.3), channel_id=1, source_target_pairs={{0,1},{1,0},{2,3},{3,2},{4,5},{5,4},{6,7},{7,6},{8,9},{9,8},{10,11... | collective-permute-start | bytes 589832 | tf_op jit(solution)/shard_map/ppermute | solution.py:40
  10.7 13.7 %collective-permute-start.4 = (bf16[1024,128]{1,0:T(8,128)(2,1)S(1)}, bf16[1024,128]{1,0:T(8,128)(2,1)S(1)}, u32[]{:S(2)}, u32[]{:S(2)}) collective-permute-start(bf16[1024,128]{1,0:T(8,128)(2,1)S(1)} %get-tuple-element.85), channel_id=1, source_target_pairs={{0,2},{2,0},{4,6},{6,4},{8,10},{10,8},{12,14},{14,12},{1,3},{3,1},... | collective-permute-start | bytes 786440 | tf_op jit(solution)/shard_map/ppermute | solution.py:40
  12.2 11.2 %collective-permute-start.1 = (bf16[960,128]{1,0:T(8,128)(2,1)S(1)}, bf16[960,128]{1,0:T(8,128)(2,1)S(1)}, u32[]{:S(2)}, u32[]{:S(2)}) collective-permute-start(bf16[960,128]{1,0:T(8,128)(2,1)S(1)} %get-tuple-element.81), channel_id=1, source_target_pairs={{0,8},{2,10},{4,12},{6,14},{8,0},{10,2},{12,4},{14,6},{1,9},{3,11}... | collective-permute-start | bytes 737288 | tf_op jit(solution)/shard_map/ppermute | solution.py:40
  14.8 9.5 %collective-permute-start.3 = (bf16[960,128]{1,0:T(8,128)(2,1)S(1)}, bf16[960,128]{1,0:T(8,128)(2,1)S(1)}, u32[]{:S(2)}, u32[]{:S(2)}) collective-permute-start(bf16[960,128]{1,0:T(8,128)(2,1)S(1)} %get-tuple-element.84), channel_id=1, source_target_pairs={{0,2},{2,0},{4,6},{6,4},{8,10},{10,8},{12,14},{14,12},{1,3},{3,1},... | collective-permute-start | bytes 737288 | tf_op jit(solution)/shard_map/ppermute | solution.py:40
  24.7 15.9 %collective-permute-start.6 = (bf16[1504,128]{1,0:T(8,128)(2,1)S(1)}, bf16[1504,128]{1,0:T(8,128)(2,1)S(1)}, u32[]{:S(2)}, u32[]{:S(2)}) collective-permute-start(bf16[1504,128]{1,0:T(8,128)(2,1)S(1)} %get-tuple-element.94), channel_id=1, source_target_pairs={{0,4},{2,6},{4,0},{6,2},{8,12},{10,14},{12,8},{14,10},{1,5},{3,7},... | collective-permute-start | bytes 1155080 | tf_op jit(solution)/shard_map/ppermute | solution.py:40
  27.3 12.6 %collective-permute-start.7 = (bf16[1440,128]{1,0:T(8,128)(2,1)S(1)}, bf16[1440,128]{1,0:T(8,128)(2,1)S(1)}, u32[]{:S(2)}, u32[]{:S(2)}) collective-permute-start(bf16[1440,128]{1,0:T(8,128)(2,1)S(1)} %get-tuple-element.95), channel_id=1, source_target_pairs={{0,2},{2,0},{4,6},{6,4},{8,10},{10,8},{12,14},{14,12},{1,3},{3,1},... | collective-permute-start | bytes 1105928 | tf_op jit(solution)/shard_map/ppermute | solution.py:40
  28.8 11.1 %collective-permute-start.5 = (bf16[960,128]{1,0:T(8,128)(2,1)S(1)}, bf16[960,128]{1,0:T(8,128)(2,1)S(1)}, u32[]{:S(2)}, u32[]{:S(2)}) collective-permute-start(bf16[960,128]{1,0:T(8,128)(2,1)S(1)} %get-tuple-element.93), channel_id=1, source_target_pairs={{0,8},{2,10},{4,12},{6,14},{8,0},{10,2},{12,4},{14,6},{1,9},{3,11}... | collective-permute-start | bytes 737288 | tf_op jit(solution)/shard_map/ppermute | solution.py:40
  40.6 23.1 %copy-start = (f32[240,512]{1,0:T(8,128)S(1)}, f32[240,512]{1,0:T(8,128)}, u32[]{:S(2)}) copy-start(f32[240,512]{1,0:T(8,128)} %master_ref.3) | copy-start | bytes 1474564
  40.6 23.1 %copy-start.1 = (f32[240,512]{1,0:T(8,128)S(1)}, f32[240,512]{1,0:T(8,128)}, u32[]{:S(2)}) copy-start(f32[240,512]{1,0:T(8,128)} %first_ref.3) | copy-start | bytes 1474564
  40.6 23.1 %copy-start.2 = (f32[240,512]{1,0:T(8,128)S(1)}, f32[240,512]{1,0:T(8,128)}, u32[]{:S(2)}) copy-start(f32[240,512]{1,0:T(8,128)} %second_ref.3) | copy-start | bytes 1474564
  41.4 7.8 %collective-permute-start.8 = (bf16[544,128]{1,0:T(8,128)(2,1)S(1)}, bf16[544,128]{1,0:T(8,128)(2,1)S(1)}, u32[]{:S(2)}, u32[]{:S(2)}) collective-permute-start(bf16[544,128]{1,0:T(8,128)(2,1)S(1)} %get-tuple-element.104), channel_id=1, source_target_pairs={{0,8},{2,10},{4,12},{6,14},{8,0},{10,2},{12,4},{14,6},{1,9},{3,11}... | collective-permute-start | bytes 417800 | tf_op jit(solution)/shard_map/ppermute | solution.py:40
  44.1 4.9 %collective-permute-start.9 = (bf16[480,128]{1,0:T(8,128)(2,1)S(1)}, bf16[480,128]{1,0:T(8,128)(2,1)S(1)}, u32[]{:S(2)}, u32[]{:S(2)}) collective-permute-start(bf16[480,128]{1,0:T(8,128)(2,1)S(1)} %get-tuple-element.105), channel_id=1, source_target_pairs={{0,4},{2,6},{4,0},{6,2},{8,12},{10,14},{12,8},{14,10},{1,5},{3,7},... | collective-permute-start | bytes 368648 | tf_op jit(solution)/shard_map/ppermute | solution.py:40
  49.4 4.6 %collective-permute-start.12 = (f32[8,128]{1,0:T(8,128)S(1)}, f32[8,128]{1,0:T(8,128)S(1)}, u32[]{:S(2)}, u32[]{:S(2)}) collective-permute-start(f32[8,128]{1,0:T(8,128)S(1)} %get-tuple-element.109), channel_id=1, source_target_pairs={{0,6},{2,4},{4,2},{6,0},{8,14},{10,12},{12,10},{14,8},{1,7},{3,5},... | collective-permute-start | bytes 12296 | tf_op jit(solution)/shard_map/ppermute | solution.py:40
  51.8 3.7 %collective-permute-start.11 = (f32[8,128]{1,0:T(8,128)S(1)}, f32[8,128]{1,0:T(8,128)S(1)}, u32[]{:S(2)}, u32[]{:S(2)}) collective-permute-start(f32[8,128]{1,0:T(8,128)S(1)} %get-tuple-element.109), channel_id=1, source_target_pairs={{0,4},{2,6},{4,0},{6,2},{8,12},{10,14},{12,8},{14,10},{1,5},{3,7},... | collective-permute-start | bytes 12296 | tf_op jit(solution)/shard_map/ppermute | solution.py:40
  52.7 3.7 %collective-permute-start.10 = (f32[8,128]{1,0:T(8,128)S(1)}, f32[8,128]{1,0:T(8,128)S(1)}, u32[]{:S(2)}, u32[]{:S(2)}) collective-permute-start(f32[8,128]{1,0:T(8,128)S(1)} %get-tuple-element.109), channel_id=1, source_target_pairs={{0,2},{2,0},{4,6},{6,4},{8,10},{10,8},{12,14},{14,12},{1,3},{3,1},... | collective-permute-start | bytes 12296 | tf_op jit(solution)/shard_map/ppermute | solution.py:40
  56.4 7.3 %collective-permute-start.15 = (bf16[4,240,128]{2,1,0:T(8,128)(2,1)S(1)}, bf16[4,240,128]{2,1,0:T(8,128)(2,1)S(1)}, u32[]{:S(2)}, u32[]{:S(2)}) collective-permute-start(bf16[4,240,128]{2,1,0:T(8,128)(2,1)S(1)} %get-tuple-element.117.refs_0_), channel_id=1, source_target_pairs={{0,4},{2,6},{4,0},{6,2},{8,12},{10,14},{12,8},{14,10},{1,5},{3,7},... | collective-permute-start | bytes 737288 | tf_op jit(solution)/shard_map/ppermute | solution.py:40
  57.6 15.2 %collective-permute-start.16 = (bf16[12,240,128]{2,1,0:T(8,128)(2,1)S(1)}, bf16[12,240,128]{2,1,0:T(8,128)(2,1)S(1)}, u32[]{:S(2)}, u32[]{:S(2)}) collective-permute-start(bf16[12,240,128]{2,1,0:T(8,128)(2,1)S(1)} %get-tuple-element.124.refs_1_), channel_id=1, source_target_pairs={{0,2},{2,0},{4,6},{6,4},{8,10},{10,8},{12,14},{14,12},{1,3},{3,1},... | collective-permute-start | bytes 2211848 | tf_op jit(solution)/shard_map/ppermute | solution.py:40
  58.0 1.2 %collective-permute-start.13 = (f32[8,128]{1,0:T(8,128)S(1)}, f32[8,128]{1,0:T(8,128)S(1)}, u32[]{:S(2)}, u32[]{:S(2)}) collective-permute-start(f32[8,128]{1,0:T(8,128)S(1)} %add_add_fusion), channel_id=1, source_target_pairs={{0,1},{1,0},{2,3},{3,2},{4,5},{5,4},{6,7},{7,6},{8,9},{9,8},{10,11... | collective-permute-start | bytes 12296 | tf_op jit(solution)/shard_map/ppermute | solution.py:40
  59.2 4.5 %collective-permute-start.14 = (f32[8,128]{1,0:T(8,128)S(1)}, f32[8,128]{1,0:T(8,128)S(1)}, u32[]{:S(2)}, u32[]{:S(2)}) collective-permute-start(f32[8,128]{1,0:T(8,128)S(1)} %add.24.square_ref), channel_id=1, source_target_pairs={{0,8},{2,10},{4,12},{6,14},{8,0},{10,2},{12,4},{14,6},{1,9},{3,11}... | collective-permute-start | bytes 12296 | tf_op jit(solution)/shard_map/ppermute | solution.py:40
  64.3 1.3 %collective-permute-start.17 = (f32[8,8,256]{2,1,0:T(8,128)S(1)}, f32[8,8,256]{2,1,0:T(8,128)S(1)}, u32[]{:S(2)}, u32[]{:S(2)}) collective-permute-start(f32[8,8,256]{2,1,0:T(8,128)S(1)} %get-tuple-element.133), channel_id=1, source_target_pairs={{0,1},{1,0},{2,3},{3,2},{4,5},{5,4},{6,7},{7,6},{8,9},{9,8},{10,11... | collective-permute-start | bytes 196616 | tf_op jit(solution)/shard_map/ppermute | solution.py:40
  65.7 4.0 %collective-permute-start.18 = (f32[4,8,256]{2,1,0:T(8,128)S(1)}, f32[4,8,256]{2,1,0:T(8,128)S(1)}, u32[]{:S(2)}, u32[]{:S(2)}) collective-permute-start(f32[4,8,256]{2,1,0:T(8,128)S(1)} %pad_maximum_fusion), channel_id=1, source_target_pairs={{0,4},{2,6},{4,0},{6,2},{8,12},{10,14},{12,8},{14,10},{1,5},{3,7},... | collective-permute-start | bytes 98312 | tf_op jit(solution)/shard_map/ppermute | solution.py:40
  69.6 4.7 %collective-permute-start.19 = (f32[2,8,256]{2,1,0:T(8,128)S(1)}, f32[2,8,256]{2,1,0:T(8,128)S(1)}, u32[]{:S(2)}, u32[]{:S(2)}) collective-permute-start(f32[2,8,256]{2,1,0:T(8,128)S(1)} %stack.28), channel_id=1, source_target_pairs={{0,8},{2,10},{4,12},{6,14},{8,0},{10,2},{12,4},{14,6},{1,9},{3,11}... | collective-permute-start | bytes 49160 | tf_op jit(solution)/shard_map/ppermute | solution.py:40
  74.4 3.7 %collective-permute-start.20 = (f32[1,8,256]{2,1,0:T(8,128)S(1)}, f32[1,8,256]{2,1,0:T(8,128)S(1)}, u32[]{:S(2)}, u32[]{:S(2)}) collective-permute-start(f32[1,8,256]{2,1,0:T(8,128)S(1)} %get-tuple-element.148), channel_id=1, source_target_pairs={{0,2},{2,0},{4,6},{6,4},{8,10},{10,8},{12,14},{14,12},{1,3},{3,1},... | collective-permute-start | bytes 24584 | tf_op jit(solution)/shard_map/ppermute | solution.py:40
  76.0 2.1 %copy-start.7 = (bf16[1,8,256]{2,1,0:T(8,128)(2,1)S(1)}, bf16[1,8,256]{2,1,0:T(8,128)(2,1)}, u32[]{:S(2)}) copy-start(bf16[1,8,256]{2,1,0:T(8,128)(2,1)} %values_ref.3) | copy-start | bytes 12292
